TPU v7x, 128 devices: a whole 4x4x4 slice. The times are simulated.
128 devices in a mesh: section: 2 (over x_lo), shard: 16 (over z, x_hi, core), replica: 4 (over y).
Axes of the slice: x: 4 (x_hi: 2, x_lo: 2; x = x_hi * 2 + x_lo), y: 4, z: 4, core: 2. Of those that a mesh axis runs over, the one named last changes fastest.
Arguments:
- inputs: bfloat16 [2, 4, 1024, 1024], P(None, 'replica', 'shard'), may hold values from -6 to 6
- segments: int32 [2, 4, 1024], P(None, 'replica', 'shard'), may hold values from 0 to 2, as said below
- cotangent: bfloat16 [2, 4, 1024, 1024], P(None, 'replica', 'shard'), may hold values from -6 to 6
- attend_weight: bfloat16 [2, 1024, 3072], P('section', 'shard'), may hold values from -0.1875 to 0.1875
- output_weight: bfloat16 [2, 1024, 1024], P('section', 'shard'), may hold values from -2 to 2
- expand_weight: bfloat16 [2, 1024, 4096], P('section', 'shard'), may hold values from -0.1875 to 0.1875
- contract_weight: bfloat16 [2, 4096, 1024], P('section', 'shard'), may hold values from -0.09375 to 0.09375
- biases: bfloat16 [2, 6, 1024], P('section', None, 'shard'), may hold values from -1.5 to 1.5
- hidden_bias: bfloat16 [2, 4096], P('section', 'shard'), may hold values from -1.5 to 1.5
- gains: bfloat16 [2, 2, 1024], P('section', None, 'shard'), may hold values from 0.5 to 1.5
Outputs:
- layer_output: bfloat16 [2, 2, 4, 1024, 1024], P('section', None, 'replica', 'shard')
- input_grad: float32 [2, 2, 4, 1024, 1024], P('section', None, 'replica', 'shard')
- attend_grad: float32 [2, 1024, 3072], P('section', 'shard')
- output_grad: float32 [2, 1024, 1024], P('section', 'shard')
- expand_grad: float32 [2, 1024, 4096], P('section', 'shard')
- contract_grad: float32 [2, 4096, 1024], P('section', 'shard')
- biases_grad: float32 [2, 6, 1024], P('section', None, 'shard')
- hidden_grad: float32 [2, 4096], P('section', 'shard')
- gains_grad: float32 [2, 2, 1024], P('section', None, 'shard')
Inputs may be any that keep to these rules, and one draw needn't show every extreme that they name: `segments`: along each sequence the numbers start at 0 and rise by one where a document starts; a sequence holds one to three documents, one of them longer than half the sequence, every other one of 204 tokens or more. A token attends to the tokens of its own sequence that carry the same number.
All inputs are finite; a program needn't handle non-finite values.
Results may differ from a plain program's by a relative error of at most 0.019.
Values may be sent and summed in bfloat16 or wider, within the bound.
No kernel may reach another device: no remote copies, remote signals or barrier semaphores. Data moves between devices by JAX's collectives and lax.ppermute only.
A program may use at most 192 MiB of HBM per device.

v0:
```python
import math

import jax
import jax.numpy as jnp
from jax import lax
from jax.sharding import PartitionSpec as P

HEADS = 16
HEAD_DIM = 64


NEGATIVE = -1e30
EPSILON = 1e-05


def from_behind(value, axis, by):
    peers = lax.axis_size(axis)
    pairs = [(i, i + by) for i in range(peers) if 0 <= i + by < peers]
    return lax.ppermute(value, axis, pairs)


def layer_norm(value, gain, shift):
    mean_value = jnp.mean(value, -1, keepdims=True)
    centred = value - mean_value
    spread = jnp.mean(centred * centred, -1, keepdims=True)
    return centred * lax.rsqrt(spread + EPSILON) * gain + shift


def gelu_exact(value):
    return jax.nn.gelu(value, approximate=False)


def matmul(left, right):
    return jnp.dot(left, right, preferred_element_type=jnp.float32)


def times_transposed(left, right):
    return lax.dot_general(
        left, right, (((1,), (1,)), ((), ())), preferred_element_type=jnp.float32
    )


def transposed_times(left, right):
    return lax.dot_general(
        left, right, (((0,), (0,)), ((), ())), preferred_element_type=jnp.float32
    )


def fetch_each(
    attend_weight, output_weight, expand_weight, contract_weight, biases, hidden_bias, gains
):
    gathered = (
        lax.all_gather(attend_weight, "shard", axis=1, tiled=True),
        lax.all_gather(output_weight, "shard", axis=1, tiled=True),
        lax.all_gather(expand_weight, "shard", axis=1, tiled=True),
        lax.all_gather(contract_weight, "shard", axis=1, tiled=True),
        lax.all_gather(biases, "shard", axis=2, tiled=True),
        lax.all_gather(hidden_bias, "shard", axis=1, tiled=True),
        lax.all_gather(gains, "shard", axis=2, tiled=True),
    )
    return tuple((piece[0] for piece in gathered))


def attention_scores(queries, key_rows, seg_local, seg_whole):
    sequences, length, features = key_rows.shape
    local_rows = seg_local.shape[1]
    query_heads = queries.reshape(sequences, local_rows, HEADS, HEAD_DIM)
    key_heads = key_rows.reshape(sequences, length, HEADS, HEAD_DIM)
    scaled = jnp.einsum(
        "sqhd,skhd->shqk", query_heads, key_heads, preferred_element_type=jnp.float32
    ) * (1.0 / math.sqrt(HEAD_DIM))
    matching = seg_local[:, None, :, None] == seg_whole[:, None, None, :]
    return jnp.where(matching, scaled, NEGATIVE)


def forward_layer(layer_input, seg_local, seg_whole, params):
    attend_weight, output_weight, expand_weight, contract_weight, biases, hidden_bias, gains = (
        params
    )
    sequences, local_rows, features = layer_input.shape
    flat_input = layer_input.reshape(sequences * local_rows, features)
    packed_bias = jnp.concatenate([biases[0], jnp.zeros_like(biases[0]), biases[1]]).astype(
        jnp.float32
    )
    packed = (matmul(flat_input, attend_weight) + packed_bias).astype(jnp.bfloat16)
    queries = packed[:, :features]
    key_local = packed[:, features : 2 * features].reshape(sequences, local_rows, features)
    value_local = packed[:, 2 * features :].reshape(sequences, local_rows, features)
    key_rows, value_rows = (
        lax.all_gather(key_local, "shard", axis=1, tiled=True),
        lax.all_gather(value_local, "shard", axis=1, tiled=True),
    )
    scores = attention_scores(queries, key_rows, seg_local, seg_whole)
    highest = jnp.max(scores, -1, keepdims=True)
    exponent = jnp.exp(scores - highest)
    totals = jnp.sum(exponent, -1, keepdims=True)
    soft_weights = (exponent / totals).astype(jnp.bfloat16)
    log_totals = highest + jnp.log(totals)
    length = key_rows.shape[1]
    value_heads = value_rows.reshape(sequences, length, HEADS, HEAD_DIM)
    context = jnp.einsum(
        "shqk,skhd->sqhd", soft_weights, value_heads, preferred_element_type=jnp.float32
    )
    context = context.reshape(sequences * local_rows, features).astype(jnp.bfloat16)
    attention = matmul(context, output_weight) + biases[2].astype(jnp.float32)
    residual = flat_input.astype(jnp.float32) + attention
    first = layer_norm(residual, gains[0].astype(jnp.float32), biases[3].astype(jnp.float32))
    first_low = first.astype(jnp.bfloat16)
    inner = matmul(first_low, expand_weight) + hidden_bias.astype(jnp.float32)
    activation = gelu_exact(inner).astype(jnp.bfloat16)
    mlp_out = matmul(activation, contract_weight) + biases[4].astype(jnp.float32)
    second = first + mlp_out
    output = layer_norm(second, gains[1].astype(jnp.float32), biases[5].astype(jnp.float32))
    saved = (
        flat_input,
        queries,
        key_rows,
        value_rows,
        log_totals,
        context,
        residual,
        first_low,
        inner,
        activation,
        second,
    )
    return (output.astype(jnp.bfloat16).reshape(sequences, local_rows, features), saved)


def backward_layer(grad_output, saved, seg_local, seg_whole, params):
    attend_weight, output_weight, expand_weight, contract_weight, biases, hidden_bias, gains = (
        params
    )
    (
        flat_input,
        queries,
        key_rows,
        value_rows,
        log_totals,
        context,
        residual,
        first_low,
        inner,
        activation,
        second,
    ) = saved
    sequences, length, features = key_rows.shape
    local_rows = queries.shape[0] // sequences
    unused, norm_back_two = jax.vjp(
        layer_norm, second, gains[1].astype(jnp.float32), biases[5].astype(jnp.float32)
    )
    grad_second, grad_gain_two, grad_shift_two = norm_back_two(grad_output)
    grad_mlp = grad_second.astype(jnp.bfloat16)
    unused, gelu_back = jax.vjp(gelu_exact, inner)
    grad_inner = gelu_back(times_transposed(grad_mlp, contract_weight))[0].astype(jnp.bfloat16)
    grad_first = grad_second + times_transposed(grad_inner, expand_weight)
    unused, norm_back_one = jax.vjp(
        layer_norm, residual, gains[0].astype(jnp.float32), biases[3].astype(jnp.float32)
    )
    grad_residual, grad_gain_one, grad_shift_one = norm_back_one(grad_first)
    grad_attn = grad_residual.astype(jnp.bfloat16)
    grad_context = times_transposed(grad_attn, output_weight).astype(jnp.bfloat16)
    grad_context = grad_context.reshape(sequences, local_rows, HEADS, HEAD_DIM)
    scores = attention_scores(queries, key_rows, seg_local, seg_whole)
    soft_full = jnp.exp(scores - log_totals)
    query_heads = queries.reshape(sequences, local_rows, HEADS, HEAD_DIM)
    key_heads = key_rows.reshape(sequences, length, HEADS, HEAD_DIM)
    value_heads = value_rows.reshape(sequences, length, HEADS, HEAD_DIM)
    grad_soft = jnp.einsum(
        "sqhd,skhd->shqk", grad_context, value_heads, preferred_element_type=jnp.float32
    )
    row_total = jnp.sum(soft_full * grad_soft, -1, keepdims=True)
    grad_scores = (soft_full * (grad_soft - row_total)).astype(jnp.bfloat16)
    scale_factor = 1.0 / math.sqrt(HEAD_DIM)
    grad_query = (
        jnp.einsum("shqk,skhd->sqhd", grad_scores, key_heads, preferred_element_type=jnp.float32)
        * scale_factor
    )
    grad_key = (
        jnp.einsum("shqk,sqhd->skhd", grad_scores, query_heads, preferred_element_type=jnp.float32)
        * scale_factor
    )
    grad_value = jnp.einsum(
        "shqk,sqhd->skhd",
        soft_full.astype(jnp.bfloat16),
        grad_context,
        preferred_element_type=jnp.float32,
    )
    grad_key_own, grad_value_own = (
        lax.psum_scatter(
            grad_key.reshape(sequences, length, features).astype(jnp.bfloat16),
            "shard",
            scatter_dimension=1,
            tiled=True,
        ).astype(jnp.float32),
        lax.psum_scatter(
            grad_value.reshape(sequences, length, features).astype(jnp.bfloat16),
            "shard",
            scatter_dimension=1,
            tiled=True,
        ).astype(jnp.float32),
    )
    grad_packed = jnp.concatenate(
        [
            grad_query.reshape(sequences * local_rows, features),
            grad_key_own.reshape(sequences * local_rows, features),
            grad_value_own.reshape(sequences * local_rows, features),
        ],
        1,
    ).astype(jnp.bfloat16)
    grad_input = grad_residual + times_transposed(grad_packed, attend_weight)
    records = (
        grad_packed,
        grad_attn,
        grad_inner,
        grad_mlp,
        grad_gain_one,
        grad_gain_two,
        grad_shift_one,
        grad_shift_two,
    )
    return (grad_input, records)


def stack_pieces(*pieces):
    return jnp.stack(pieces)


def on_device(
    inputs,
    segments,
    cotangent,
    attend_weight,
    output_weight,
    expand_weight,
    contract_weight,
    biases,
    hidden_bias,
    gains,
):
    section_index = lax.axis_index("section")
    section_count = lax.axis_size("section")
    micro_count = inputs.shape[0]
    sequences, local_rows, features = (inputs.shape[1], inputs.shape[2], inputs.shape[3])
    turns = section_count + micro_count - 1
    seg_whole_all = lax.all_gather(segments, "shard", axis=2, tiled=True)
    params = None
    incoming = jnp.zeros((sequences, local_rows, features), jnp.bfloat16)
    saved_list = []
    output_list = []
    for turn_index in range(turns):
        micro_index = jnp.clip(turn_index - section_index, 0, micro_count - 1)
        own_input = lax.dynamic_index_in_dim(inputs, micro_index, 0, keepdims=False)
        layer_input = jnp.where(section_index == 0, own_input, incoming)
        seg_local = lax.dynamic_index_in_dim(segments, micro_index, 0, keepdims=False)
        seg_whole = lax.dynamic_index_in_dim(seg_whole_all, micro_index, 0, keepdims=False)
        params = fetch_each(
            attend_weight, output_weight, expand_weight, contract_weight, biases, hidden_bias, gains
        )
        output, saved = forward_layer(layer_input, seg_local, seg_whole, params)
        saved_list.append(saved)
        output_list.append(output)
        if turn_index + 1 < turns:
            incoming = from_behind(output, "section", 1)
    saved_stack = jax.tree.map(stack_pieces, *saved_list)
    output_stack = jnp.stack(output_list)
    layer_output = jnp.stack(
        [
            lax.dynamic_index_in_dim(output_stack, micro_step + section_index, 0, keepdims=False)
            for micro_step in range(micro_count)
        ]
    )[None]
    incoming_grad = jnp.zeros((sequences, local_rows, features), jnp.bfloat16)
    record_list = []
    grad_list = []
    for turn_index in range(turns):
        micro_index = jnp.clip(turn_index - (section_count - 1 - section_index), 0, micro_count - 1)
        forward_turn = micro_index + section_index
        saved = jax.tree.map(
            lambda stacked: lax.dynamic_index_in_dim(stacked, forward_turn, 0, keepdims=False),
            saved_stack,
        )
        own_grad = lax.dynamic_index_in_dim(cotangent, micro_index, 0, keepdims=False)
        grad_output = jnp.where(section_index == section_count - 1, own_grad, incoming_grad)
        grad_output = grad_output.astype(jnp.float32).reshape(sequences * local_rows, features)
        seg_local = lax.dynamic_index_in_dim(segments, micro_index, 0, keepdims=False)
        seg_whole = lax.dynamic_index_in_dim(seg_whole_all, micro_index, 0, keepdims=False)
        params = fetch_each(
            attend_weight, output_weight, expand_weight, contract_weight, biases, hidden_bias, gains
        )
        grad_input, records = backward_layer(grad_output, saved, seg_local, seg_whole, params)
        grad_input = grad_input.reshape(sequences, local_rows, features)
        grad_list.append(grad_input)
        record_list.append(records)
        if turn_index + 1 < turns:
            incoming_grad = from_behind(grad_input.astype(jnp.bfloat16), "section", -1)
    grad_stack = jnp.stack(grad_list)
    input_grad = jnp.stack(
        [
            lax.dynamic_index_in_dim(
                grad_stack, micro_step + section_count - 1 - section_index, 0, keepdims=False
            )
            for micro_step in range(micro_count)
        ]
    )[None]
    record_stack = jax.tree.map(stack_pieces, *record_list)
    picked_saved = [
        jax.tree.map(
            lambda stacked: lax.dynamic_index_in_dim(
                stacked, micro_step + section_index, 0, keepdims=False
            ),
            saved_stack,
        )
        for micro_step in range(micro_count)
    ]
    picked_records = [
        jax.tree.map(
            lambda stacked: lax.dynamic_index_in_dim(
                stacked, micro_step + section_count - 1 - section_index, 0, keepdims=False
            ),
            record_stack,
        )
        for micro_step in range(micro_count)
    ]

    def joined(source, position):
        return jnp.concatenate([item[position] for item in source], 0)

    def summed_over(source, position):
        return sum((item[position] for item in source))

    rows_input = joined(picked_saved, 0)
    rows_context = joined(picked_saved, 5)
    rows_first = joined(picked_saved, 7)
    rows_active = joined(picked_saved, 9)
    grad_packed = joined(picked_records, 0)
    grad_attn = joined(picked_records, 1)
    grad_inner = joined(picked_records, 2)
    grad_mlp = joined(picked_records, 3)
    attend_total = transposed_times(rows_input, grad_packed)
    output_total = transposed_times(rows_context, grad_attn)
    expand_total = transposed_times(rows_first, grad_inner)
    contract_total = transposed_times(rows_active, grad_mlp)
    packed_sums = jnp.sum(grad_packed.astype(jnp.float32), 0)
    biases_total = jnp.stack(
        [
            packed_sums[:features],
            packed_sums[2 * features :],
            jnp.sum(grad_attn.astype(jnp.float32), 0),
            summed_over(picked_records, 6),
            jnp.sum(grad_mlp.astype(jnp.float32), 0),
            summed_over(picked_records, 7),
        ]
    )
    hidden_total = jnp.sum(grad_inner.astype(jnp.float32), 0)
    gains_total = jnp.stack([summed_over(picked_records, 4), summed_over(picked_records, 5)])
    owned = (
        lax.psum_scatter(
            attend_total[None].astype(jnp.bfloat16), "shard", scatter_dimension=1, tiled=True
        ).astype(jnp.float32),
        lax.psum_scatter(
            output_total[None].astype(jnp.bfloat16), "shard", scatter_dimension=1, tiled=True
        ).astype(jnp.float32),
        lax.psum_scatter(
            expand_total[None].astype(jnp.bfloat16), "shard", scatter_dimension=1, tiled=True
        ).astype(jnp.float32),
        lax.psum_scatter(
            contract_total[None].astype(jnp.bfloat16), "shard", scatter_dimension=1, tiled=True
        ).astype(jnp.float32),
        lax.psum_scatter(
            biases_total[None].astype(jnp.bfloat16), "shard", scatter_dimension=2, tiled=True
        ).astype(jnp.float32),
        lax.psum_scatter(
            hidden_total[None].astype(jnp.bfloat16), "shard", scatter_dimension=1, tiled=True
        ).astype(jnp.float32),
        lax.psum_scatter(
            gains_total[None].astype(jnp.bfloat16), "shard", scatter_dimension=2, tiled=True
        ).astype(jnp.float32),
    )
    totals = (
        lax.psum(owned[0].astype(jnp.bfloat16), "replica").astype(jnp.float32),
        lax.psum(owned[1].astype(jnp.bfloat16), "replica").astype(jnp.float32),
        lax.psum(owned[2].astype(jnp.bfloat16), "replica").astype(jnp.float32),
        lax.psum(owned[3].astype(jnp.bfloat16), "replica").astype(jnp.float32),
        lax.psum(owned[4].astype(jnp.bfloat16), "replica").astype(jnp.float32),
        lax.psum(owned[5].astype(jnp.bfloat16), "replica").astype(jnp.float32),
        lax.psum(owned[6].astype(jnp.bfloat16), "replica").astype(jnp.float32),
    )
    return (
        layer_output,
        input_grad,
        totals[0],
        totals[1],
        totals[2],
        totals[3],
        totals[4],
        totals[5],
        totals[6],
    )


def solution(mesh):
    placed = (
        P(None, "replica", "shard", None),
        P(None, "replica", "shard"),
        P(None, "replica", "shard", None),
        P("section", "shard", None),
        P("section", "shard", None),
        P("section", "shard", None),
        P("section", "shard", None),
        P("section", None, "shard"),
        P("section", "shard"),
        P("section", None, "shard"),
    )
    return jax.shard_map(
        on_device,
        mesh=mesh,
        in_specs=placed,
        out_specs=(
            P("section", None, "replica", "shard", None),
            P("section", None, "replica", "shard", None),
            P("section", "shard", None),
            P("section", "shard", None),
            P("section", "shard", None),
            P("section", "shard", None),
            P("section", None, "shard"),
            P("section", "shard"),
            P("section", None, "shard"),
        ),
        check_vma=False,
    )
```

profile of v0, /device:TPU:1, one launch (start us, length us, event | category | flops | bytes accessed | tf_op | source)
XLA Modules:
  0.0 1872.4 jit_solution(10554834604788595752)
XLA Ops:
  8.8 30.6 %all_gather.29 = bf16[1,6,1024]{1,0,2:T(2,128)(2,1)S(1)} all-gather(bf16[1,6,64]{1,0,2:T(2,128)(2,1)S(1)} %copy.100), channel_id=1, replica_groups=mesh['section'=2,'shard'=16,'replica'=4] {'shard'}, dimensions={2}, use_global_device_ids=true | all-gather | bytes 13056 | tf_op jit(solution)/shard_map/all_gather | solution.py:57
  46.8 33.0 %all-gather.17.cloned.1.call-done = bf16[1,1024,3072]{2,1,0:T(8,128)(2,1)} async-done(((bf16[1,64,3072]{2,1,0:T(8,128)(2,1)}), bf16[1,1024,3072]{2,1,0:T(8,128)(2,1)}) %all-gather.17.cloned.1.call-update) | async-done | bytes 6291472 | tf_op jit(solution)/shard_map/all_gather | solution.py:53
  87.3 19.8 %all_gather.36 = bf16[1,4096]{1,0:T(2,128)(2,1)S(1)} all-gather(bf16[1,256]{1,0:T(2,128)(2,1)S(1)} %copy-done.161), channel_id=1, replica_groups=mesh['section'=2,'shard'=16,'replica'=4] {'shard'}, dimensions={1}, use_global_device_ids=true | all-gather | bytes 8704 | tf_op jit(solution)/shard_map/all_gather | solution.py:58
  107.2 24.5 %all_gather.34 = bf16[1,2,1024]{1,0,2:T(2,128)(2,1)S(1)} all-gather(bf16[1,2,64]{1,0,2:T(2,128)(2,1)S(1)} %copy.105), channel_id=1, replica_groups=mesh['section'=2,'shard'=16,'replica'=4] {'shard'}, dimensions={2}, use_global_device_ids=true | all-gather | bytes 4352 | tf_op jit(solution)/shard_map/all_gather | solution.py:59
  131.8 23.2 %all_gather.31 = s32[2,1,1024]{0,1,2:T(1,128)S(1)} all-gather(s32[2,1,64]{0,1,2:T(1,128)S(1)} %copy.102), channel_id=1, replica_groups=mesh['section'=2,'shard'=16,'replica'=4] {'shard'}, dimensions={2}, use_global_device_ids=true | all-gather | bytes 8704 | tf_op jit(solution)/shard_map/all_gather | solution.py:246
  155.6 154.9 %dynamic-slice_reduce_fusion.2 = (s32[1024]{0:T(1024)}, s32[1024]{0:T(1024)}, s32[1024]{0:T(1024)}, s32[1024]{0:T(1024)}, s32[1024]{0:T(1024)S(1)}, /*index=5*/s32[1024]{0:T(1024)S(1)}) fusion(s32[2,1,1024]{0,1,2:T(1,128)S(1)} %all_gather.31, s32[]{:T(128)S(6)} %min.24, s32[]{:T(128)S(6)} %min.23, s32[]{:T(128)S(6)} %min.22, s32[]{:T(128)S(6)} %min.21, ...), kind=kLoop, calls=%fused_computation.354 | loop fusion | bytes 49176 | tf_op jit(solution)/shard_map/jit(dynamic_index_in_dim)/dynamic_slice | solution.py:287
  316.8 20.0 %fusion.312 = (f32[1024]{0:T(1024)S(1)}, f32[1024]{0:T(1024)S(1)}, f32[1024]{0:T(1024)S(1)}, f32[1024]{0:T(1024)S(1)}) fusion(bf16[1,6,1024]{1,0,2:T(2,128)(2,1)S(1)} %all_gather.29), kind=kLoop, calls=%fused_computation.338 | loop fusion | flops 4096 | bytes 24576 | tf_op jit(solution)/shard_map/convert_element_type | solution.py:113
  358.6 19.1 %all-gather.23.cloned.1.call-done = bf16[1,4096,1024]{2,1,0:T(8,128)(2,1)} async-done(((bf16[1,256,1024]{2,1,0:T(8,128)(2,1)}), bf16[1,4096,1024]{2,1,0:T(8,128)(2,1)}) %all-gather.23.cloned.1.call-update) | async-done | bytes 8388624 | tf_op jit(solution)/shard_map/all_gather | solution.py:56
  394.0 47.1 %all-gather.31.cloned.1.call-done = bf16[1024,1024]{1,0:T(8,128)(2,1)} async-done(((bf16[64,1024]{1,0:T(8,128)(2,1)}), bf16[1024,1024]{1,0:T(8,128)(2,1)}) %all-gather.31.cloned.1.call-update) | async-done | bytes 2097168 | tf_op jit(solution)/shard_map/all_gather | solution.py:90
  448.5 42.0 %all-gather.29.cloned.1.call-done = bf16[1024,1024]{1,0:T(8,128)(2,1)} async-done(((bf16[64,1024]{1,0:T(8,128)(2,1)}), bf16[1024,1024]{1,0:T(8,128)(2,1)}) %all-gather.29.cloned.1.call-update) | async-done | bytes 2097168 | tf_op jit(solution)/shard_map/all_gather | solution.py:91
  499.9 8.6 fusion.185
  524.7 42.1 %all-gather.35.cloned.1.call-done = bf16[1024,1024]{1,0:T(8,128)(2,1)} async-done(((bf16[64,1024]{1,0:T(8,128)(2,1)}), bf16[1024,1024]{1,0:T(8,128)(2,1)}) %all-gather.35.cloned.1.call-update) | async-done | bytes 2097168 | tf_op jit(solution)/shard_map/all_gather | solution.py:90
  577.5 38.1 %all-gather.33.cloned.1.call-done = bf16[1024,1024]{1,0:T(8,128)(2,1)} async-done(((bf16[64,1024]{1,0:T(8,128)(2,1)}), bf16[1024,1024]{1,0:T(8,128)(2,1)}) %all-gather.33.cloned.1.call-update) | async-done | bytes 2097168 | tf_op jit(solution)/shard_map/all_gather | solution.py:91
  670.0 10.9 copy.134
  698.7 10.9 copy.132
  727.3 25.6 %reduce-scatter.42.cloned.1.call-done = bf16[64,1024]{1,0:T(8,128)(2,1)} async-done(((bf16[1024,1024]{1,0:T(8,128)(2,1)}), bf16[64,1024]{1,0:T(8,128)(2,1)}) %reduce-scatter.42.cloned.1.call-update) | async-done | bytes 131088
  755.8 71.5 %reduce-scatter.40.cloned.1.call-done = bf16[64,1024]{1,0:T(8,128)(2,1)} async-done(((bf16[1024,1024]{1,0:T(8,128)(2,1)}), bf16[64,1024]{1,0:T(8,128)(2,1)}) %reduce-scatter.40.cloned.1.call-update) | async-done | bytes 131088
  864.2 10.9 copy.138
  893.1 11.0 copy.136
  920.5 30.3 %reduce-scatter.46.cloned.1.call-done = bf16[64,1024]{1,0:T(8,128)(2,1)} async-done(((bf16[1024,1024]{1,0:T(8,128)(2,1)}), bf16[64,1024]{1,0:T(8,128)(2,1)}) %reduce-scatter.46.cloned.1.call-update) | async-done | bytes 131088
  954.4 70.7 %reduce-scatter.44.cloned.1.call-done = bf16[64,1024]{1,0:T(8,128)(2,1)} async-done(((bf16[1024,1024]{1,0:T(8,128)(2,1)}), bf16[64,1024]{1,0:T(8,128)(2,1)}) %reduce-scatter.44.cloned.1.call-update) | async-done | bytes 131088
  1119.7 22.9 %reduce-scatter.50.cloned.1.call-done = bf16[64,1024]{1,0:T(8,128)(2,1)} async-done(((bf16[1024,1024]{1,0:T(8,128)(2,1)}), bf16[64,1024]{1,0:T(8,128)(2,1)}) %reduce-scatter.50.cloned.1.call-update) | async-done | bytes 131088
  1143.9 73.0 %reduce-scatter.48.cloned.1.call-done = bf16[64,1024]{1,0:T(8,128)(2,1)} async-done(((bf16[1024,1024]{1,0:T(8,128)(2,1)}), bf16[64,1024]{1,0:T(8,128)(2,1)}) %reduce-scatter.48.cloned.1.call-update) | async-done | bytes 131088
  1237.1 53.7 %reduce-scatter.34.cloned.1.call-done = bf16[1,64,1024]{2,1,0:T(8,128)(2,1)} async-done(((bf16[1,1024,1024]{2,1,0:T(8,128)(2,1)}), bf16[1,64,1024]{2,1,0:T(8,128)(2,1)}) %reduce-scatter.34.cloned.1.call-update) | async-done | bytes 131088 | tf_op jit(solution)/shard_map/reduce_scatter | solution.py:361
  1290.8 107.0 %reduce-scatter.36.cloned.1.call-done = bf16[1,64,4096]{2,1,0:T(8,128)(2,1)} async-done(((bf16[1,1024,4096]{2,1,0:T(8,128)(2,1)}), bf16[1,64,4096]{2,1,0:T(8,128)(2,1)}) %reduce-scatter.36.cloned.1.call-update) | async-done | bytes 524304 | tf_op jit(solution)/shard_map/reduce_scatter | solution.py:364
  1397.7 106.1 %reduce-scatter.38.cloned.1.call-done = bf16[1,256,1024]{2,1,0:T(8,128)(2,1)} async-done(((bf16[1,4096,1024]{2,1,0:T(8,128)(2,1)}), bf16[1,256,1024]{2,1,0:T(8,128)(2,1)}) %reduce-scatter.38.cloned.1.call-update) | async-done | bytes 524304 | tf_op jit(solution)/shard_map/reduce_scatter | solution.py:367
  1503.9 93.1 %reduce-scatter.32.cloned.1.call-done = bf16[1,64,3072]{2,1,0:T(8,128)(2,1)} async-done(((bf16[1,1024,3072]{2,1,0:T(8,128)(2,1)}), bf16[1,64,3072]{2,1,0:T(8,128)(2,1)}) %reduce-scatter.32.cloned.1.call-update) | async-done | bytes 393232 | tf_op jit(solution)/shard_map/reduce_scatter | solution.py:358
  1599.5 64.5 %reduce-scatter.56.cloned.1.call-done = bf16[64,2]{1,0:T(8,128)(2,1)} async-done(((bf16[1024,2]{1,0:T(8,128)(2,1)}), bf16[64,2]{1,0:T(8,128)(2,1)}) %reduce-scatter.56.cloned.1.call-update) | async-done | bytes 272
  1664.8 69.5 %reduce-scatter.54.cloned.1.call-done = bf16[256,1]{1,0:T(8,128)(2,1)} async-done(((bf16[4096,1]{1,0:T(8,128)(2,1)}), bf16[256,1]{1,0:T(8,128)(2,1)}) %reduce-scatter.54.cloned.1.call-update) | async-done | bytes 528
  1741.1 62.2 %reduce-scatter.52.cloned.1.call-done = bf16[64,6]{1,0:T(8,128)(2,1)} async-done(((bf16[1024,6]{1,0:T(8,128)(2,1)}), bf16[64,6]{1,0:T(8,128)(2,1)}) %reduce-scatter.52.cloned.1.call-update) | async-done | bytes 784
  1804.3 8.6 all-reduce
  1814.6 42.9 %all-reduce.4.cloned.1.call-done = (bf16[1,64,3072]{2,1,0:T(8,128)(2,1)}, bf16[1,64,1024]{2,1,0:T(8,128)(2,1)}, bf16[1,64,4096]{2,1,0:T(8,128)(2,1)}, bf16[1,256,1024]{2,1,0:T(8,128)(2,1)}) async-done(((bf16[1,64,3072]{2,1,0:T(8,128)(2,1)}, bf16[1,64,1024]{2,1,0:T(8,128)(2,1)}, bf16[1,64,4096]{2,1,0:T(8,128)(2,1)}, bf16[1,256,1024]{2,1,0:T(8,128)(2,1)}), (bf16[1,64,3072]{2,1,0:T(8,128)(2,1)}, ...) | async-done | bytes 1572880 | tf_op jit(solution)/shard_map/psum | solution.py:381
  (676 shorter events, 406.4 us)
Async XLA Ops:
  7.2 72.6 %all-gather.17.cloned.1.call-start = ((), (), s32[]{:S(2)}) async-start(), calls=%async_computation.13 | async-start | bytes 6684672 | tf_op jit(solution)/shard_map/all_gather | solution.py:53
  7.9 329.2 %all-gather.25.cloned.1.call-start = ((), (), s32[]{:S(2)}) async-start(), calls=%async_computation.21 | async-start | bytes 2228224 | tf_op jit(solution)/shard_map/all_gather | solution.py:91
  84.6 256.4 %all-gather.27.cloned.1.call-start = ((), (), s32[]{:S(2)}) async-start(), calls=%async_computation.22 | async-start | bytes 2228224 | tf_op jit(solution)/shard_map/all_gather | solution.py:90
  85.4 262.7 %all-gather.19.cloned.1.call-start = ((), (), s32[]{:S(2)}) async-start(), calls=%async_computation.14 | async-start | bytes 2228224 | tf_op jit(solution)/shard_map/all_gather | solution.py:54
  86.0 264.6 %all-gather.21.cloned.1.call-start = ((), (), s32[]{:S(2)}) async-start(), calls=%async_computation.15 | async-start | bytes 8912896 | tf_op jit(solution)/shard_map/all_gather | solution.py:55
  86.5 291.2 %all-gather.23.cloned.1.call-start = ((), (), s32[]{:S(2)}) async-start(), calls=%async_computation.16 | async-start | bytes 8912896 | tf_op jit(solution)/shard_map/all_gather | solution.py:56
  87.1 354.0 %all-gather.31.cloned.1.call-start = ((), (), s32[]{:S(2)}) async-start(), calls=%async_computation.24 | async-start | bytes 2228224 | tf_op jit(solution)/shard_map/all_gather | solution.py:90
  383.2 4.8 collective-permute-start
  392.9 97.7 %all-gather.29.cloned.1.call-start = ((), (), s32[]{:S(2)}) async-start(), calls=%async_computation.23 | async-start | bytes 2228224 | tf_op jit(solution)/shard_map/all_gather | solution.py:91
  393.7 173.2 %all-gather.35.cloned.1.call-start = ((), (), s32[]{:S(2)}) async-start(), calls=%async_computation.26 | async-start | bytes 2228224 | tf_op jit(solution)/shard_map/all_gather | solution.py:90
  510.6 4.8 collective-permute-start.1
  517.6 98.0 %all-gather.33.cloned.1.call-start = ((), (), s32[]{:S(2)}) async-start(), calls=%async_computation.25 | async-start | bytes 2228224 | tf_op jit(solution)/shard_map/all_gather | solution.py:91
  518.1 234.7 %reduce-scatter.42.cloned.1.call-start = ((), (), s32[]{:S(2)}) async-start(), calls=%async_computation.28 | async-start | bytes 2228224
  685.2 142.1 %reduce-scatter.40.cloned.1.call-start = ((), (), s32[]{:S(2)}) async-start(), calls=%async_computation.27 | async-start | bytes 2228224
  714.1 236.7 %reduce-scatter.46.cloned.1.call-start = ((), (), s32[]{:S(2)}) async-start(), calls=%async_computation.30 | async-start | bytes 2228224
  836.1 5.7 collective-permute-start.2
  879.4 145.6 %reduce-scatter.44.cloned.1.call-start = ((), (), s32[]{:S(2)}) async-start(), calls=%async_computation.29 | async-start | bytes 2228224
  908.4 234.2 %reduce-scatter.50.cloned.1.call-start = ((), (), s32[]{:S(2)}) async-start(), calls=%async_computation.32 | async-start | bytes 2228224
  1033.9 5.7 collective-permute-start.3
  1071.2 145.7 %reduce-scatter.48.cloned.1.call-start = ((), (), s32[]{:S(2)}) async-start(), calls=%async_computation.31 | async-start | bytes 2228224
  1094.2 196.6 %reduce-scatter.34.cloned.1.call-start = ((), (), s32[]{:S(2)}) async-start(), calls=%async_computation.18 | async-start | bytes 2228224 | tf_op jit(solution)/shard_map/reduce_scatter | solution.py:361
  1097.6 300.1 %reduce-scatter.36.cloned.1.call-start = ((), (), s32[]{:S(2)}) async-start(), calls=%async_computation.19 | async-start | bytes 8912896 | tf_op jit(solution)/shard_map/reduce_scatter | solution.py:364
  1105.5 398.4 %reduce-scatter.38.cloned.1.call-start = ((), (), s32[]{:S(2)}) async-start(), calls=%async_computation.20 | async-start | bytes 8912896 | tf_op jit(solution)/shard_map/reduce_scatter | solution.py:367
  1113.7 483.3 %reduce-scatter.32.cloned.1.call-start = ((), (), s32[]{:S(2)}) async-start(), calls=%async_computation.17 | async-start | bytes 6684672 | tf_op jit(solution)/shard_map/reduce_scatter | solution.py:358
  1228.4 435.6 %reduce-scatter.56.cloned.1.call-start = ((), (), s32[]{:S(2)}) async-start(), calls=%async_computation.35 | async-start | bytes 278528
  1230.6 503.8 %reduce-scatter.54.cloned.1.call-start = ((), (), s32[]{:S(2)}) async-start(), calls=%async_computation.34 | async-start | bytes 1114112
  1232.3 571.0 %reduce-scatter.52.cloned.1.call-start = ((), (), s32[]{:S(2)}) async-start(), calls=%async_computation.33 | async-start | bytes 278528
  1232.6 502.7 %copy-start.45 = (bf16[1,64,1024]{1,2,0:T(8,128)(2,1)S(1)}, bf16[1,64,1024]{1,2,0:T(8,128)(2,1)}, u32[]{:S(2)}) copy-start(bf16[1,64,1024]{1,2,0:T(8,128)(2,1)} %copy-done.44) | copy-start | bytes 393220
  1232.6 502.7 %copy-start.47 = (bf16[1,64,1024]{1,2,0:T(8,128)(2,1)S(1)}, bf16[1,64,1024]{1,2,0:T(8,128)(2,1)}, u32[]{:S(2)}) copy-start(bf16[1,64,1024]{1,2,0:T(8,128)(2,1)} %copy-done.46) | copy-start | bytes 393220
  1232.6 502.7 %copy-start.138 = (f32[64]{0:T(128)S(1)}, f32[64]{0:T(128)}, u32[]{:S(2)}) copy-start(f32[64]{0:T(128)} %copy-done.137) | copy-start | bytes 772
  1236.2 499.2 %copy-start.74 = (bf16[16,64,64]{2,1,0:T(8,128)(2,1)S(1)}, bf16[16,64,64]{2,1,0:T(8,128)(2,1)}, u32[]{:S(2)}) copy-start(bf16[16,64,64]{2,1,0:T(8,128)(2,1)} %fusion.119) | copy-start | bytes 393220
  1236.2 621.3 %all-reduce.4.cloned.1.call-start = ((), (), s32[]{:S(2)}) async-start(), calls=%async_computation.36 | async-start | bytes 3145728 | tf_op jit(solution)/shard_map/psum | solution.py:381
  (176 other events, 4373.6 us)
Sparse Core Ops, SparseCore 0:
  10.5 69.2 all-gather.16
  84.8 46.4 all-gather.24
  134.3 47.1 all-gather.26
  183.9 46.3 all-gather.18
  232.6 71.8 all-gather.20
  306.9 70.8 all-gather.22
  393.0 48.0 all-gather.30
  444.1 46.3 all-gather.28
  517.7 49.1 all-gather.34
  569.1 46.3 all-gather.32
  685.3 67.5 reduce-scatter.41
  757.1 70.0 reduce-scatter.39
  879.5 71.2 reduce-scatter.45
  955.0 69.9 reduce-scatter.43
  1071.3 71.2 reduce-scatter.49
  1146.9 70.0 reduce-scatter.47
  1220.7 70.0 reduce-scatter.33
  1295.5 102.2 reduce-scatter.35
  1402.6 101.2 reduce-scatter.37
  1508.5 88.4 reduce-scatter.31
  1600.7 63.2 reduce-scatter.55
  1668.4 65.9 reduce-scatter.53
  1739.1 64.2 reduce-scatter.51
  1805.9 51.5 all-reduce.3
where the time goes:
time: 1880 us; the launch traced here: 1870 us
  waiting for transfers between devices  1130 us (60%)
  local copies, waits for them, and re-layouts  351 us (19%)
  matrix products  175 us (9%)
  blocking collectives  107 us (6%)
  other arithmetic  80.1 us (4%)
    unnamed x33, waiting for transfers between devices  495 us
    dynamic_slice x1, local copies, waits for them, and re-layouts, on_device(): lax.dynamic_index_in_dim(seg_whole_all, micro_index, 0, keepdims=False)  155 us
    unnamed x401, local copies, waits for them, and re-layouts  126 us
    reduce_scatter x1, waiting for transfers between devices, on_device(): lax.psum_scatter(expand_total[None].astype(jnp.bfloat16), 'shard', scatte...  107 us
    reduce_scatter x1, waiting for transfers between devices, on_device(): lax.psum_scatter(contract_total[None].astype(jnp.bfloat16), 'shard', scat...  106 us
    reduce_scatter x1, waiting for transfers between devices, on_device(): lax.psum_scatter(attend_total[None].astype(jnp.bfloat16), 'shard', scatte...  93.1 us
    all_gather x3, waiting for transfers between devices, forward_layer(): lax.all_gather(key_local, 'shard', axis=1, tiled=True)  89.2 us
    all_gather x3, waiting for transfers between devices, forward_layer(): lax.all_gather(value_local, 'shard', axis=1, tiled=True)  80.1 us
  transfers between devices with their start and end apart: 28, of which 24 were waited for; matrix products, arithmetic and copies ran while one was open for 21% of the time, Pallas kernels for 0%

commit v1 on v0

v1 whole, which is shorter than its diff:
```python
import math

import jax
import jax.numpy as jnp
from jax import lax
from jax.sharding import PartitionSpec as P

HEADS = 16
HEAD_DIM = 64
NEGATIVE = -1e30
EPSILON = 1e-05
SCALE = 1.0 / math.sqrt(HEAD_DIM)
LOW = jnp.bfloat16
ALL = ("section", "shard")
REST = ("shard", "replica")


def layer_norm(value, gain, shift):
    mean_value = jnp.mean(value, -1, keepdims=True)
    centred = value - mean_value
    spread = jnp.mean(centred * centred, -1, keepdims=True)
    return centred * lax.rsqrt(spread + EPSILON) * gain + shift


def gelu_exact(value):
    return jax.nn.gelu(value, approximate=False)


def matmul(left, right):
    return jnp.dot(left, right, preferred_element_type=jnp.float32)


def times_transposed(left, right):
    return lax.dot_general(
        left, right, (((1,), (1,)), ((), ())), preferred_element_type=jnp.float32
    )


def transposed_times(left, right):
    return lax.dot_general(
        left, right, (((0,), (0,)), ((), ())), preferred_element_type=jnp.float32
    )


def exchange(value, axes):
    return lax.all_to_all(value, axes, 0, 0, tiled=True)


def swap_cores(value):
    return lax.ppermute(value, "shard", [(i, i ^ 1) for i in range(16)])


def whole_sequence(tokens):
    core = lax.axis_index("shard") % 2
    micros, rows, features = tokens.shape
    half = rows // 2
    sends = jnp.broadcast_to(
        tokens.reshape(micros, 1, 2, half, features), (micros, 4, 2, half, features)
    ).reshape(16, half, features)
    mine = exchange(sends, "shard")
    other = swap_cores(mine)
    lower = jnp.where(core == 0, mine, other)
    upper = jnp.where(core == 0, other, mine)
    return jnp.stack([lower, upper], 1).reshape(16 * rows, features)


def to_tokens(value, parts):
    width = parts * HEAD_DIM
    sends = jnp.broadcast_to(value.reshape(1, 16, 64, width), (2, 16, 64, width))
    got = exchange(sends.reshape(32, 64, width), ALL)
    got = got.reshape(2, 2, 8, 64, parts, HEAD_DIM).transpose(1, 3, 4, 0, 2, 5)
    return got.reshape(128, parts * 1024)


def to_head(value, layer):
    sends = value.reshape(2, 64, 2, 8, HEAD_DIM).transpose(2, 0, 3, 1, 4).reshape(32, 64, HEAD_DIM)
    got = exchange(sends, ALL)
    return got[16 * layer : 16 * layer + 16].reshape(1024, HEAD_DIM)


def masked_scores(queries, keys, seg):
    scores = times_transposed(queries, keys) * SCALE
    return jnp.where(seg[:, None] == seg[None, :], scores, NEGATIVE)


def attend(packed, seg):
    queries, keys, values = jnp.split(packed, 3, 1)
    scores = masked_scores(queries, keys, seg)
    highest = jnp.max(scores, -1, keepdims=True)
    exponent = jnp.exp(scores - highest)
    totals = jnp.sum(exponent, -1, keepdims=True)
    context = matmul((exponent / totals).astype(LOW), values).astype(LOW)
    return context, highest + jnp.log(totals)


def attend_back(packed, log_totals, seg, grad_context):
    queries, keys, values = jnp.split(packed, 3, 1)
    soft = jnp.exp(masked_scores(queries, keys, seg) - log_totals)
    grad_soft = times_transposed(grad_context, values)
    row_total = jnp.sum(soft * grad_soft, -1, keepdims=True)
    grad_scores = (soft * (grad_soft - row_total)).astype(LOW)
    return jnp.concatenate(
        [
            matmul(grad_scores, keys) * SCALE,
            transposed_times(grad_scores, queries) * SCALE,
            transposed_times(soft.astype(LOW), grad_context),
        ],
        1,
    ).astype(LOW)


def block_forward(tokens, context, weights, biases, hidden_bias, gains):
    output_weight, expand_weight, contract_weight = weights
    residual = tokens.astype(jnp.float32) + (matmul(context, output_weight) + biases[2])
    first = layer_norm(residual, gains[0], biases[3])
    first_low = first.astype(LOW)
    inner = jnp.concatenate([matmul(first_low, part) for part in expand_weight], 1) + hidden_bias
    activation = gelu_exact(inner).astype(LOW)
    second = first + (matmul(activation, contract_weight) + biases[4])
    output = layer_norm(second, gains[1], biases[5]).astype(LOW)
    return output, (residual, first_low, inner, second)


def block_back(grad, saved, weights, biases, gains):
    output_weight, expand_weight, contract_weight = weights
    residual, first_low, inner, second = saved
    unused, norm_back_two = jax.vjp(layer_norm, second, gains[1], biases[5])
    grad_second, grad_gain_two, grad_shift_two = norm_back_two(grad)
    grad_mlp = grad_second.astype(LOW)
    unused, gelu_back = jax.vjp(gelu_exact, inner)
    grad_inner = gelu_back(times_transposed(grad_mlp, contract_weight))[0].astype(LOW)
    grad_first = grad_second
    for part, piece in zip(expand_weight, jnp.split(grad_inner, 4, 1)):
        grad_first = grad_first + times_transposed(piece, part)
    unused, norm_back_one = jax.vjp(layer_norm, residual, gains[0], biases[3])
    grad_residual, grad_gain_one, grad_shift_one = norm_back_one(grad_first)
    grad_attn = grad_residual.astype(LOW)
    grad_context = times_transposed(grad_attn, output_weight).astype(LOW)
    attn_sum = jnp.sum(grad_attn.astype(jnp.float32), 0)
    sums = jnp.stack([grad_gain_one, grad_gain_two, attn_sum, grad_shift_one, grad_shift_two])
    return grad_mlp, grad_residual, grad_attn, grad_context, sums


def on_device(
    inputs,
    segments,
    cotangent,
    attend_weight,
    output_weight,
    expand_weight,
    contract_weight,
    biases,
    hidden_bias,
    gains,
):
    section = lax.axis_index("section")
    shard = lax.axis_index("shard")
    on_first = section == 0
    micro = shard // 8
    head = section * 8 + shard % 8
    inputs = inputs[:, 0]

    with jax.named_scope("gather_block_weights"):
        rows = jnp.concatenate(
            [output_weight[0]] + jnp.split(expand_weight[0], 4, 1) + [contract_weight[0]], 0
        )
        gathered = lax.all_gather(rows, "shard", axis=0, tiled=False)
        weights = (
            gathered[:, :64].reshape(1024, 1024),
            [gathered[:, 64 + 64 * q : 128 + 64 * q].reshape(1024, 1024) for q in range(4)],
            gathered[:, 320:576].reshape(4096, 1024),
        )

    with jax.named_scope("head_weights"):
        by_head = attend_weight[0].reshape(64, 3, HEADS, HEAD_DIM).transpose(2, 0, 1, 3)
        small = jnp.concatenate(
            [
                biases.reshape(384),
                gains.reshape(128),
                hidden_bias.reshape(256),
                segments.reshape(128).astype(LOW),
                jnp.zeros((16 * 192 - 896,), LOW),
            ]
        ).reshape(1, 16, 192)
        block = jnp.concatenate(
            [by_head.reshape(HEADS, 64, 192), jnp.broadcast_to(small, (HEADS, 16, 192))], 1
        )
        block = jnp.broadcast_to(block.reshape(2, 1, 8, 80, 192), (2, 2, 8, 80, 192))
        got = exchange(block.reshape(32, 80, 192), ALL).reshape(2, 16, 80, 192)
        head_weight = got[:, :, :64].reshape(2, 1024, 192)
        small = got[:, :, 64:69].reshape(2, 16, 960)
        all_biases = small[:, :, :384].reshape(2, 16, 6, 64).transpose(0, 2, 1, 3)
        all_biases = all_biases.reshape(2, 6, 1024).astype(jnp.float32)
        all_gains = small[:, :, 384:512].reshape(2, 16, 2, 64).transpose(0, 2, 1, 3)
        all_gains = all_gains.reshape(2, 2, 1024).astype(jnp.float32)
        all_hidden = small[:, :, 512:768].reshape(2, 4096).astype(jnp.float32)
        seg = small[0, :, 768:896].reshape(16, 2, 64)
        seg = jnp.where(micro == 0, seg[:, 0], seg[:, 1]).reshape(1024)
        own_biases = jnp.where(on_first, all_biases[0], all_biases[1])
        own_gains = jnp.where(on_first, all_gains[0], all_gains[1])
        own_hidden = jnp.where(on_first, all_hidden[0], all_hidden[1])
        head_bias = lax.dynamic_slice_in_dim(
            all_biases.reshape(2, 6, HEADS, HEAD_DIM), head, 1, 2
        )[:, :, 0]
        head_bias = jnp.concatenate(
            [head_bias[:, 0], jnp.zeros_like(head_bias[:, 0]), head_bias[:, 1]], 1
        )

    def attention(layer, tokens):
        with jax.named_scope("sequence_tokens"):
            whole = whole_sequence(tokens)
        with jax.named_scope("attention"):
            packed = (matmul(whole, head_weight[layer]) + head_bias[layer]).astype(LOW)
            context, log_totals = attend(packed, seg)
        with jax.named_scope("context_out"):
            context = to_tokens(context, 1)
        return context, (whole, packed, log_totals)

    def attention_back(layer, grad_context, kept):
        whole, packed, log_totals = kept
        with jax.named_scope("grad_context_in"):
            grad_context = to_head(grad_context, layer)
        with jax.named_scope("attention_back"):
            grad_packed = attend_back(packed, log_totals, seg, grad_context)
            grad_weight = transposed_times(whole, grad_packed)
            grad_sums = jnp.sum(grad_packed.astype(jnp.float32), 0)
        return grad_packed, grad_weight, grad_sums

    context_0, kept_0 = attention(0, inputs)
    tokens_0 = inputs.reshape(128, 1024)
    with jax.named_scope("block_0"):
        output, unused = block_forward(
            tokens_0, context_0, weights, own_biases, own_hidden, own_gains
        )
    with jax.named_scope("to_next_section"):
        tokens_1 = jnp.where(
            on_first, output, lax.ppermute(output, "section", [(0, 1)])
        )
    with jax.named_scope("gather_attend_weight"):
        late_weight, unused = lax.optimization_barrier((attend_weight[0], output))
        whole_attend = lax.all_gather(late_weight, "shard", axis=0, tiled=True)
    context_1, kept_1 = attention(1, tokens_1.reshape(2, 64, 1024))
    own_tokens = jnp.where(on_first, tokens_0, tokens_1)
    own_context = jnp.where(on_first, context_0, context_1)
    with jax.named_scope("block_1"):
        output, saved = block_forward(
            own_tokens, own_context, weights, own_biases, own_hidden, own_gains
        )
    layer_output = output.reshape(1, 2, 1, 64, 1024)
    with jax.named_scope("gather_first"):
        first_all = lax.all_gather(saved[1], "shard", axis=0, tiled=True)

    last_grad = cotangent.reshape(128, 1024)
    with jax.named_scope("block_back_1"):
        unused, grad_residual, unused, grad_context, unused = block_back(
            last_grad.astype(jnp.float32), saved, weights, own_biases, own_gains
        )
    grad_packed, grad_attend_1, grad_sums_1 = attention_back(1, grad_context, kept_1)
    with jax.named_scope("grad_tokens_1"):
        grad_tokens_1 = grad_residual + times_transposed(to_tokens(grad_packed, 3), whole_attend)
    with jax.named_scope("to_previous_section"):
        arrived = lax.ppermute(grad_tokens_1.astype(LOW), "section", [(1, 0)])
        own_grad = jnp.where(on_first, arrived, last_grad)
    with jax.named_scope("block_back_0"):
        grad_mlp, grad_residual, grad_attn, grad_context, norm_sums = block_back(
            own_grad.astype(jnp.float32), saved, weights, own_biases, own_gains
        )
    with jax.named_scope("gather_grad_mlp"):
        grad_mlp_all = lax.all_gather(grad_mlp, "shard", axis=0, tiled=True)
    grad_packed, grad_attend_0, grad_sums_0 = attention_back(0, grad_context, kept_0)

    with jax.named_scope("swap_attend_grad"):
        grad_attend_0 = grad_attend_0.astype(LOW)
        grad_attend_1 = grad_attend_1.astype(LOW)
        sums = jnp.stack([grad_sums_0, grad_sums_1]).astype(LOW)
        pad = jnp.zeros((15, 192), LOW)
        part_0 = jnp.concatenate([grad_attend_0, sums[0:1], pad], 0)
        part_1 = jnp.concatenate([grad_attend_1, sums[1:2], pad], 0)
        keep = jnp.where(on_first, part_0, part_1)
        give = jnp.where(on_first, part_1, part_0)
        take = lax.ppermute(give, "section", [(0, 1), (1, 0)])
        lower = jnp.where(on_first, keep, take)
        upper = jnp.where(on_first, take, keep)
        attend_part = jnp.concatenate([lower[:1024], upper[:1024]], 1)
        sums = jnp.stack([lower[1024], upper[1024]]).reshape(2, 3, HEAD_DIM)
    with jax.named_scope("block_weight_grads"):
        quarter = lax.dynamic_index_in_dim(
            jnp.stack([part for part in weights[1]]), shard // 4, 0, keepdims=False
        )
        expand_part = lax.dynamic_slice_in_dim(quarter, (shard % 4) * 256, 256, 1)
        hidden_part = lax.dynamic_slice_in_dim(own_hidden, shard * 256, 256, 0)
        inner = matmul(first_all, expand_part) + hidden_part
        activation, gelu_back = jax.vjp(gelu_exact, inner)
        grad_inner = gelu_back(times_transposed(grad_mlp_all, contract_weight[0]))[0].astype(LOW)
        expand_grad = transposed_times(first_all, grad_inner)
        contract_grad = transposed_times(activation.astype(LOW), grad_mlp_all)
        output_grad = transposed_times(own_context, grad_attn)
        hidden_sum = jnp.sum(grad_inner.astype(jnp.float32), 0)
        mlp_sum = jnp.sum(grad_mlp_all.astype(jnp.float32), 0)
    with jax.named_scope("sum_contract"):
        rows = jnp.concatenate(
            [
                contract_grad,
                jnp.concatenate([hidden_sum, jnp.zeros((768,), jnp.float32)])[None],
                mlp_sum[None],
                jnp.zeros((14, 1024), jnp.float32),
            ],
            0,
        ).astype(LOW)
        contract_total = lax.psum(rows, "replica").astype(jnp.float32)
    with jax.named_scope("sum_weight_grads"):
        norm_rows = norm_sums.reshape(5, 16, 64).transpose(1, 0, 2)
        mine = jnp.arange(8) == shard % 8
        head_rows = jnp.where(
            mine[None, :, None, None], sums[:, None, ::2].astype(jnp.float32), 0.0
        ).reshape(16, 2, 64)
        vectors = jnp.pad(
            jnp.concatenate([norm_rows, head_rows], 1), ((0, 0), (0, 9), (0, 64))
        )
        vectors = jnp.broadcast_to(vectors[:, None], (16, 4, 16, 128)).reshape(1024, 128)
        parts = jnp.concatenate(
            [
                attend_part,
                output_grad.astype(LOW),
                expand_grad.astype(LOW),
                vectors.astype(LOW),
            ],
            1,
        )
        got = exchange(parts.reshape(64, 16, 1792), REST).astype(jnp.float32)
        got_attend = got[:, :, :384].reshape(2, 8, 4, 16, 2, 3, 64).sum((0, 2))
        got_attend = got_attend.transpose(1, 3, 2, 0, 4).reshape(16, 3072)
        got_output = got[:, :, 384:1408].sum(0)
        got_expand = got[:, :, 1408:1664].reshape(16, 4, 16, 256).sum(1)
        got_expand = got_expand.transpose(1, 0, 2).reshape(16, 4096)
        got_vectors = got[:, :7, 1664:1728].sum(0)
        owned = jnp.concatenate([got_attend, got_output, got_expand], 1).astype(LOW)
    with jax.named_scope("gather_weight_grads"):
        totals = lax.all_gather(owned, "replica", axis=0, tiled=True)
        totals = totals.astype(jnp.float32)
    with jax.named_scope("grad_tokens_0"):
        late_packed, unused = lax.optimization_barrier((grad_packed, owned))
        grad_tokens_0 = grad_residual + times_transposed(to_tokens(late_packed, 3), whole_attend)
    input_grad = jnp.where(on_first, grad_tokens_0, grad_tokens_1).reshape(1, 2, 1, 64, 1024)
    mlp_own = lax.dynamic_slice_in_dim(contract_total[257], shard * 64, 64, 0)
    biases_grad = jnp.stack(
        [
            got_vectors[5],
            got_vectors[6],
            got_vectors[2],
            got_vectors[3],
            mlp_own,
            got_vectors[4],
        ]
    )
    return (
        layer_output,
        input_grad,
        totals[None, :, :3072],
        totals[None, :, 3072:4096],
        totals[None, :, 4096:],
        contract_total[None, :256],
        biases_grad[None],
        contract_total[None, 256, :256],
        got_vectors[None, :2],
    )


def solution(mesh):
    placed = (
        P(None, "replica", "shard", None),
        P(None, "replica", "shard"),
        P(None, "replica", "shard", None),
        P("section", "shard", None),
        P("section", "shard", None),
        P("section", "shard", None),
        P("section", "shard", None),
        P("section", None, "shard"),
        P("section", "shard"),
        P("section", None, "shard"),
    )
    return jax.shard_map(
        on_device,
        mesh=mesh,
        in_specs=placed,
        out_specs=(
            P("section", None, "replica", "shard", None),
            P("section", None, "replica", "shard", None),
            P("section", "shard", None),
            P("section", "shard", None),
            P("section", "shard", None),
            P("section", "shard", None),
            P("section", None, "shard"),
            P("section", "shard"),
            P("section", None, "shard"),
        ),
        check_vma=False,
    )
```

time: 1880 us -> 611 us (0.33)
  waiting for transfers between devices: 1130 us -> 214 us
  local copies, waits for them, and re-layouts: 351 us -> 125 us
  matrix products: 175 us -> 110 us
  blocking collectives: 107 us -> 43.6 us
  starting transfers between devices: 9.13 us -> 56.3 us
  other arithmetic: 80.1 us -> 35.8 us
    unnamed x33 -> x6, waiting for transfers between devices: 495 us -> 0.1 us
    reduce_scatter x4 -> x0, waiting for transfers between devices: 360 us -> none  [the longest x1 107 us: on_device(): lax.psum_scatter(expand_total[None].astype(jnp.bfloat16), 'shard', scatte...]
    all_gather x10 -> x5, waiting for transfers between devices: 222 us -> 22.9 us  [the longest x1 16.7 us: on_device(): gathered = lax.all_gather(rows, 'shard', axis=0, tiled=False)]
    dynamic_slice x11 -> x2, local copies, waits for them, and re-layouts: 184 us -> 0.65 us  [the longest x1 0.57 us: on_device(): hidden_part = lax.dynamic_slice_in_dim(own_hidden, shard * 256, 256, 0)]
    all_to_all x0 -> x8, waiting for transfers between devices: none -> 154 us  [exchange(): return lax.all_to_all(value, axes, 0, 0, tiled=True)]
    all_gather x4 -> x0, blocking collectives: 98.2 us -> none  [the longest x1 30.6 us: fetch_each(): lax.all_gather(biases, 'shard', axis=2, tiled=True)]
    unnamed x401 -> x202, local copies, waits for them, and re-layouts: 126 us -> 40.2 us
    dot_general x21 -> x0, matrix products: 63.1 us -> none  [the longest x6 14.7 us: attention_scores(): jnp.einsum('sqhd,skhd->shqk', query_heads, key_heads, preferred_element_t...]
  transfers between devices with their start and end apart: 28 -> 19, of which waited for: 24 -> 16; matrix products, arithmetic and copies ran while one was open for 21% -> 32% of each run, Pallas kernels for 0% -> 0%
where the time goes in v1:
time: 611 us; the launch traced here: 601 us
  waiting for transfers between devices  214 us (35%)
  local copies, waits for them, and re-layouts  125 us (20%)
  matrix products  110 us (18%)
  starting transfers between devices  56.3 us (9%)
  blocking collectives  43.6 us (7%)
  other arithmetic  35.8 us (6%)
  between operations  16.2 us (3%)
    all_to_all x8, waiting for transfers between devices, exchange(): return lax.all_to_all(value, axes, 0, 0, tiled=True)  154 us
    dot_general x19, matrix products, times_transposed(): lax.dot_general(left, right, (((1,), (1,)), ((), ())), preferred_element_...  54 us
    all_to_all x8, starting transfers between devices, exchange(): return lax.all_to_all(value, axes, 0, 0, tiled=True)  48.1 us
    all_to_all x2, blocking collectives, exchange(): return lax.all_to_all(value, axes, 0, 0, tiled=True)  43.6 us
    unnamed x202, local copies, waits for them, and re-layouts  40.2 us
    dot_general x19, matrix products, matmul(): return jnp.dot(left, right, preferred_element_type=jnp.float32)  35.9 us
    dot_general x9, matrix products, transposed_times(): lax.dot_general(left, right, (((0,), (0,)), ((), ())), preferred_element_...  20.4 us
    ppermute x1, waiting for transfers between devices, on_device(): take = lax.ppermute(give, 'section', [(0, 1), (1, 0)])  19.9 us
  transfers between devices with their start and end apart: 19, of which 16 were waited for; matrix products, arithmetic and copies ran while one was open for 32% of the time, Pallas kernels for 0%

profile of v1, /device:TPU:1, one launch (start us, length us, event | category | flops | bytes accessed | tf_op | source)
XLA Modules:
  0.0 601.2 jit_solution(795445649647818464)
XLA Ops:
  19.1 9.4 %all-to-all-start = ((bf16[32,80,192]{2,1,0:T(8,128)(2,1)}), bf16[32,80,192]{2,1,0:T(8,128)(2,1)S(1)}, u32[]{:S(2)}, u32[]{:S(2)}) async-start(bf16[32,80,192]{2,1,0:T(8,128)(2,1)} %bitcast.4), calls=%async_computation | async-start | bytes 2621440 | tf_op jit(solution)/shard_map/head_weights/all_to_all | solution.py:46
  28.7 32.4 %all-to-all-done = bf16[32,80,192]{2,1,0:T(8,128)(2,1)S(1)} async-done(((bf16[32,80,192]{2,1,0:T(8,128)(2,1)}), bf16[32,80,192]{2,1,0:T(8,128)(2,1)S(1)}, u32[]{:S(2)}, u32[]{:S(2)}) %all-to-all-start) | async-done | bytes 983072 | tf_op jit(solution)/shard_map/head_weights/all_to_all | solution.py:46
  66.3 18.3 %all-to-all-done.1 = bf16[16,32,1024]{2,1,0:T(8,128)(2,1)S(1)} async-done(((bf16[16,32,1024]{2,1,0:T(8,128)(2,1)}), bf16[16,32,1024]{2,1,0:T(8,128)(2,1)S(1)}, u32[]{:S(2)}, u32[]{:S(2)}) %all-to-all-start.1) | async-done | bytes 1048608 | tf_op jit(solution)/shard_map/sequence_tokens/all_to_all | solution.py:46
  102.7 33.9 %all-to-all-done.2 = bf16[32,2,2048]{2,1,0:T(2,128)(2,1)S(1)} async-done(((bf16[32,2,2048]{2,1,0:T(2,128)(2,1)}), bf16[32,2,2048]{2,1,0:T(2,128)(2,1)S(1)}, u32[]{:S(2)}, u32[]{:S(2)}) %all-to-all-start.2) | async-done | bytes 262176 | tf_op jit(solution)/shard_map/context_out/all_to_all | solution.py:46
  137.6 16.7 %all-gather.15.cloned.1.call-done = bf16[9216,1024]{1,0:T(8,128)(2,1)} async-done(((bf16[576,1024]{1,0:T(8,128)(2,1)}), bf16[9216,1024]{1,0:T(8,128)(2,1)}) %all-gather.15.cloned.1.call-update) | async-done | bytes 18874384 | tf_op jit(solution)/shard_map/gather_block_weights/all_gather | solution.py:167
  154.3 7.1 %fusion.185 = (bf16[16,64,1024]{2,1,0:T(8,128)(2,1)S(1)}, bf16[16,64,1024]{2,1,0:T(8,128)(2,1)S(1)}, bf16[16,64,1024]{2,1,0:T(8,128)(2,1)}, bf16[16,64,1024]{2,1,0:T(8,128)(2,1)}, bf16[16,64,1024]{2,1,0:T(8,128)(2,1)}) fusion(bf16[16,576,1024]{2,1,0:T(8,128)(2,1)} %bitcast.267), kind=kLoop, calls=%fused_computation.359 | loop fusion | bytes 20971520 | tf_op jit(solution)/shard_map/gather_block_weights/slice | solution.py:170
  161.4 8.9 %slice.266 = bf16[16,256,1024]{2,1,0:T(8,128)(2,1)} slice(bf16[16,576,1024]{2,1,0:T(8,128)(2,1)} %bitcast.268), slice={[0:16], [320:576], [0:1024]} | slice | bytes 16777216 | tf_op jit(solution)/shard_map/gather_block_weights/slice | solution.py:171
  175.9 8.4 %fusion.193 = (f32[128]{0:T(128)S(1)}, f32[128,1024]{1,0:T(8,128)S(1)}) fusion(f32[1024]{0:T(1024)S(1)} %bitcast.353, bf16[4096,1024]{1,0:T(8,128)(2,1)} %bitcast.272, f32[128,1024]{1,0:T(8,128)S(1)} %fusion.201, f32[128,1024]{1,0:T(8,128)S(1)} %fusion.200, f32[128,1024]{1,0:T(8,128)S(1)} %fusion.199, f32[128,1024]{1,0:T(8,128)S(1)} %fusion.198, ...), kind=kOutput, calls=%fused_computation.367 | convolution fusion | flops 1110835072 | bytes 11564544 | tf_op jit(solution)/shard_map/block_0/dot_general | solution.py:30
  187.9 4.7 collective-permute-done.1
  192.9 24.8 %all_to_all.50 = bf16[16,32,1024]{2,1,0:T(8,128)(2,1)S(1)} all-to-all(bf16[16,32,1024]{2,1,0:T(8,128)(2,1)S(1)} %bitcast.289), channel_id=1, replica_groups=mesh['section'=2,'shard'=16,'replica'=4] {'shard'}, dimensions={0} | all-to-all | bytes 2097152 | tf_op jit(solution)/shard_map/sequence_tokens/all_to_all | solution.py:46
  230.1 18.9 %all_to_all.51 = bf16[32,2,2048]{2,1,0:T(2,128)(2,1)} all-to-all(bf16[32,2,2048]{2,1,0:T(2,128)(2,1)} %reshape.502), channel_id=1, replica_groups=mesh['section'=2,'shard'=16,'replica'=4] {'section','shard'}, dimensions={0} | all-to-all | bytes 524288 | tf_op jit(solution)/shard_map/context_out/all_to_all | solution.py:46
  261.1 4.4 fusion.7
  265.5 5.8 fusion.195
  293.6 5.9 all-to-all-start.5
  299.6 8.8 %all-to-all-done.5 = bf16[32,2,2048]{2,1,0:T(2,128)(2,1)} async-done(((bf16[32,2,2048]{2,1,0:T(2,128)(2,1)}), bf16[32,2,2048]{2,1,0:T(2,128)(2,1)}, u32[]{:S(2)}, u32[]{:S(2)}) %all-to-all-start.5) | async-done | bytes 262176 | tf_op jit(solution)/shard_map/grad_context_in/all_to_all | solution.py:46
  336.3 4.7 all-to-all-start.6
  351.1 7.2 %all-to-all-done.6 = bf16[32,64,192]{2,1,0:T(8,128)(2,1)} async-done(((bf16[32,64,192]{2,1,0:T(8,128)(2,1)}), bf16[32,64,192]{2,1,0:T(8,128)(2,1)}, u32[]{:S(2)}, u32[]{:S(2)}) %all-to-all-start.6) | async-done | bytes 786464 | tf_op jit(solution)/shard_map/grad_tokens_1/all_to_all | solution.py:46
  366.9 6.3 %fusion.196 = (bf16[128,1024]{1,0:T(8,128)(2,1)}, f32[128,1024]{1,0:T(8,128)}) fusion(bf16[128,3072]{1,0:T(8,128)(2,1)} %reshape.475, bf16[1024,3072]{1,0:T(8,128)(2,1)} %all-gather.7.cloned.1.call-done, f32[128,1024]{1,0:T(8,128)} %copy-done.26, f32[128]{0:T(128)} %copy-done.78), kind=kOutput, calls=%fused_computation.370 | convolution fusion | flops 805699584 | bytes 8389120 | tf_op jit(solution)/shard_map/grad_tokens_1/dot_general | solution.py:34
  378.0 5.4 collective-permute-done.3
  387.4 8.9 %add_convert_fusion.1 = bf16[128,4096]{1,0:T(8,128)(2,1)} fusion(f32[128,4096]{1,0:T(8,128)} %copy-done.37, f32[4096]{0:T(1024)S(1)} %bitcast.340, f32[128,1024]{1,0:T(8,128)} %copy-done.39, f32[128,1024]{1,0:T(8,128)} %copy-done.40, f32[128,1024]{1,0:T(8,128)} %copy-done.41, f32[128,1024]{1,0:T(8,128)} %copy-done.42, ...), kind=kOutput, calls=%fused_computation.52 | convolution fusion | flops 1083179008 | bytes 13910016 | tf_op jit(solution)/shard_map/block_back_0/dot_general | solution.py:34
  406.7 4.6 all-to-all-start.7
  411.4 5.4 convolution_add_fusion
  429.7 19.9 %collective-permute-done.4 = bf16[1040,192]{0,1:T(8,128)(2,1)S(1)} collective-permute-done((bf16[1040,192]{0,1:T(8,128)(2,1)S(1)}, bf16[1040,192]{0,1:T(8,128)(2,1)S(1)}, u32[]{:S(2)}, u32[]{:S(2)}) %collective-permute-start.4) | collective-permute-done | bytes 399392 | tf_op jit(solution)/shard_map/swap_attend_grad/ppermute | solution.py:281
  454.1 6.2 %all-gather.11.cloned.1.call-done = bf16[2048,1024]{1,0:T(8,128)(2,1)} async-done(((bf16[128,1024]{1,0:T(8,128)(2,1)}), bf16[2048,1024]{1,0:T(8,128)(2,1)}) %all-gather.11.cloned.1.call-update) | async-done | bytes 4194320 | tf_op jit(solution)/shard_map/gather_grad_mlp/all_gather | solution.py:269
  460.3 7.9 %fusion.197 = (bf16[256]{0:T(256)(128)(2,1)S(1)}, bf16[2048,256]{1,0:T(8,128)(2,1)S(1)}) fusion(f32[2048,256]{1,0:T(8,128)} %convolution_add_fusion, bf16[2048,1024]{1,0:T(8,128)(2,1)} %all-gather.11.cloned.1.call-done, bf16[1,256,1024]{2,1,0:T(8,128)(2,1)S(1)} %copy-done.57), kind=kOutput, calls=%fused_computation.371 | convolution fusion | flops 1112014592 | bytes 7864832 | tf_op jit(solution)/shard_map/block_weight_grads/dot_general | solution.py:34
  471.1 5.9 copy.143
  477.0 6.1 %all-to-all-start.8 = ((bf16[64,16,1792]{2,1,0:T(8,128)(2,1)}), bf16[64,16,1792]{2,1,0:T(8,128)(2,1)}, u32[]{:S(2)}, u32[]{:S(2)}) async-start(bf16[64,16,1792]{2,1,0:T(8,128)(2,1)} %bitcast.271), calls=%async_computation.8 | async-start | bytes 7340032 | tf_op jit(solution)/shard_map/sum_weight_grads/all_to_all | solution.py:46
  486.3 8.1 %convolution_convert_fusion = bf16[256,1024]{1,0:T(8,128)(2,1)S(1)} fusion(bf16[2048,1024]{1,0:T(8,128)(2,1)} %all-gather.11.cloned.1.call-done, f32[2048,256]{1,0:T(8,128)} %convolution_add_fusion), kind=kOutput, calls=%fused_computation.88 | convolution fusion | flops 1108082688 | bytes 6815744 | tf_op jit(solution)/shard_map/block_weight_grads/dot_general | solution.py:40
  495.5 37.7 %all-to-all-done.8 = bf16[64,16,1792]{2,1,0:T(8,128)(2,1)} async-done(((bf16[64,16,1792]{2,1,0:T(8,128)(2,1)}), bf16[64,16,1792]{2,1,0:T(8,128)(2,1)}, u32[]{:S(2)}, u32[]{:S(2)}) %all-to-all-start.8) | async-done | bytes 3670048 | tf_op jit(solution)/shard_map/sum_weight_grads/all_to_all | solution.py:46
  554.1 9.8 %all-to-all-start.9 = ((bf16[32,64,192]{2,1,0:T(8,128)(2,1)}), bf16[32,64,192]{2,1,0:T(8,128)(2,1)S(1)}, u32[]{:S(2)}, u32[]{:S(2)}) async-start(bf16[32,64,192]{2,1,0:T(8,128)(2,1)} %bitcast.79), calls=%async_computation.9 | async-start | bytes 2097152 | tf_op jit(solution)/shard_map/grad_tokens_0/all_to_all | solution.py:46
  568.0 12.9 %all-to-all-done.9 = bf16[32,64,192]{2,1,0:T(8,128)(2,1)S(1)} async-done(((bf16[32,64,192]{2,1,0:T(8,128)(2,1)}), bf16[32,64,192]{2,1,0:T(8,128)(2,1)S(1)}, u32[]{:S(2)}, u32[]{:S(2)}) %all-to-all-start.9) | async-done | bytes 786464 | tf_op jit(solution)/shard_map/grad_tokens_0/all_to_all | solution.py:46
  584.3 5.8 fusion.42
  (453 shorter events, 214.0 us)
Async XLA Ops:
  7.2 147.1 %all-gather.15.cloned.1.call-start = ((), (), s32[]{:S(2)}) async-start(), calls=%async_computation.15 | async-start | bytes 20054016 | tf_op jit(solution)/shard_map/gather_block_weights/all_gather | solution.py:167
  17.9 43.1 %copy-start.30 = (bf16[2,1,64,1024]{3,2,1,0:T(8,128)(2,1)S(1)}, bf16[2,1,64,1024]{3,2,1,0:T(8,128)(2,1)}, u32[]{:S(2)}) copy-start(bf16[2,1,64,1024]{3,2,1,0:T(8,128)(2,1)} %param.10) | copy-start | bytes 786436
  19.1 42.0 %all-to-all-start = ((bf16[32,80,192]{2,1,0:T(8,128)(2,1)}), bf16[32,80,192]{2,1,0:T(8,128)(2,1)S(1)}, u32[]{:S(2)}, u32[]{:S(2)}) async-start(bf16[32,80,192]{2,1,0:T(8,128)(2,1)} %bitcast.4), calls=%async_computation | async-start | bytes 2621440 | tf_op jit(solution)/shard_map/head_weights/all_to_all | solution.py:46
  62.2 22.4 %all-to-all-start.1 = ((bf16[16,32,1024]{2,1,0:T(8,128)(2,1)}), bf16[16,32,1024]{2,1,0:T(8,128)(2,1)S(1)}, u32[]{:S(2)}, u32[]{:S(2)}) async-start(bf16[16,32,1024]{2,1,0:T(8,128)(2,1)} %bitcast.7), calls=%async_computation.1 | async-start | bytes 2097152 | tf_op jit(solution)/shard_map/sequence_tokens/all_to_all | solution.py:46
  84.6 4.3 collective-permute-start
  98.3 38.2 %all-to-all-start.2 = ((bf16[32,2,2048]{2,1,0:T(2,128)(2,1)}), bf16[32,2,2048]{2,1,0:T(2,128)(2,1)S(1)}, u32[]{:S(2)}, u32[]{:S(2)}) async-start(bf16[32,2,2048]{2,1,0:T(2,128)(2,1)} %reshape.500), calls=%async_computation.2 | async-start | bytes 524288 | tf_op jit(solution)/shard_map/context_out/all_to_all | solution.py:46
  102.2 264.7 %all-gather.7.cloned.1.call-start = ((), (), s32[]{:S(2)}) async-start(), calls=%async_computation.10 | async-start | bytes 6684672 | tf_op jit(solution)/shard_map/gather_attend_weight/all_gather | solution.py:241
  102.7 73.3 %copy-start.58 = (f32[2,2,8,128]{3,1,2,0:T(2,128)}, f32[2,2,8,128]{3,1,2,0:T(2,128)S(1)}, u32[]{:S(2)}) copy-start(f32[2,2,8,128]{3,1,2,0:T(2,128)S(1)} %copy.157) | copy-start | bytes 49156
  102.7 67.6 %copy-start.61 = (f32[1,1,1024]{2,0,1:T(1,128)}, f32[1,1,1024]{2,0,1:T(1,128)S(1)}, u32[]{:S(2)}) copy-start(f32[1,1,1024]{2,0,1:T(1,128)S(1)} %get-tuple-element.104) | copy-start | bytes 12292
  102.7 73.2 %copy-start.76 = (f32[1,1,1024]{2,0,1:T(1,128)}, f32[1,1,1024]{2,0,1:T(1,128)S(1)}, u32[]{:S(2)}) copy-start(f32[1,1,1024]{2,0,1:T(1,128)S(1)} %get-tuple-element.102) | copy-start | bytes 12292
  137.6 32.6 %copy-start.34 = (bf16[128,1024]{1,0:T(8,128)(2,1)}, bf16[128,1024]{1,0:T(8,128)(2,1)S(1)}, u32[]{:S(2)}) copy-start(bf16[128,1024]{1,0:T(8,128)(2,1)S(1)} %reshape.457) | copy-start | bytes 786436
  184.8 7.8 %collective-permute-start.1 = (bf16[128,1024]{1,0:T(8,128)(2,1)S(1)}, bf16[128,1024]{1,0:T(8,128)(2,1)}, u32[]{:S(2)}, u32[]{:S(2)}) collective-permute-start(bf16[128,1024]{1,0:T(8,128)(2,1)S(1)} %add_convert_fusion.4), channel_id=1, source_target_pairs={{0,64},{1,65},{2,66},{3,67},{4,68},{5,69},{6,70},{7,71},{8,72},{9,... | collective-permute-start | bytes 786440 | tf_op jit(solution)/shard_map/to_next_section/ppermute | solution.py:237
  187.9 223.6 %all-gather.9.cloned.1.call-start = ((), (), s32[]{:S(2)}) async-start(), calls=%async_computation.11 | async-start | bytes 4456448 | tf_op jit(solution)/shard_map/gather_first/all_gather | solution.py:251
  217.7 2.9 collective-permute-start.2
  255.5 29.3 %copy-start.70 = (f32[128]{0:T(128)}, f32[128]{0:T(128)S(1)}, u32[]{:S(2)}) copy-start(f32[128]{0:T(128)S(1)} %fusion.139) | copy-start | bytes 1540
  258.0 14.3 %copy-start.39 = (f32[128,1024]{1,0:T(8,128)}, f32[128,1024]{1,0:T(8,128)S(1)}, u32[]{:S(2)}) copy-start(f32[128,1024]{1,0:T(8,128)S(1)} %fusion.205) | copy-start | bytes 1572868
  259.9 12.5 %copy-start.40 = (f32[128,1024]{1,0:T(8,128)}, f32[128,1024]{1,0:T(8,128)S(1)}, u32[]{:S(2)}) copy-start(f32[128,1024]{1,0:T(8,128)S(1)} %fusion.204) | copy-start | bytes 1572868
  287.4 12.2 %copy-start.67 = (f32[1024]{0:T(1024)S(1)}, f32[1024]{0:T(1024)}, u32[]{:S(2)}) copy-start(f32[1024]{0:T(1024)} %copy-done.66) | copy-start | bytes 12292
  287.4 12.2 %copy-start.69 = (f32[1024]{0:T(1024)S(1)}, f32[1024]{0:T(1024)}, u32[]{:S(2)}) copy-start(f32[1024]{0:T(1024)} %copy-done.68) | copy-start | bytes 12292
  293.6 14.8 %all-to-all-start.5 = ((bf16[32,2,2048]{2,1,0:T(2,128)(2,1)}), bf16[32,2,2048]{2,1,0:T(2,128)(2,1)}, u32[]{:S(2)}, u32[]{:S(2)}) async-start(bf16[32,2,2048]{2,1,0:T(2,128)(2,1)} %reshape.504), calls=%async_computation.5 | async-start | bytes 524288 | tf_op jit(solution)/shard_map/grad_context_in/all_to_all | solution.py:46
  336.3 21.9 %all-to-all-start.6 = ((bf16[32,64,192]{2,1,0:T(8,128)(2,1)}), bf16[32,64,192]{2,1,0:T(8,128)(2,1)}, u32[]{:S(2)}, u32[]{:S(2)}) async-start(bf16[32,64,192]{2,1,0:T(8,128)(2,1)} %bitcast.290), calls=%async_computation.6 | async-start | bytes 2097152 | tf_op jit(solution)/shard_map/grad_tokens_1/all_to_all | solution.py:46
  341.0 119.3 %all-gather.11.cloned.1.call-start = ((), (), s32[]{:S(2)}) async-start(), calls=%async_computation.12 | async-start | bytes 4456448 | tf_op jit(solution)/shard_map/gather_grad_mlp/all_gather | solution.py:269
  373.3 10.2 %collective-permute-start.3 = (bf16[128,1024]{1,0:T(8,128)(2,1)}, bf16[128,1024]{1,0:T(8,128)(2,1)}, u32[]{:S(2)}, u32[]{:S(2)}) collective-permute-start(bf16[128,1024]{1,0:T(8,128)(2,1)} %get-tuple-element.133), channel_id=1, source_target_pairs={{64,0},{65,1},{66,2},{67,3},{68,4},{69,5},{70,6},{71,7},{72,8},{73... | collective-permute-start | bytes 786440 | tf_op jit(solution)/shard_map/to_previous_section/ppermute | solution.py:262
  406.7 13.3 %all-to-all-start.7 = ((bf16[32,2,2048]{2,1,0:T(2,128)(2,1)}), bf16[32,2,2048]{2,1,0:T(2,128)(2,1)S(1)}, u32[]{:S(2)}, u32[]{:S(2)}) async-start(bf16[32,2,2048]{2,1,0:T(2,128)(2,1)} %reshape.506), calls=%async_computation.7 | async-start | bytes 524288 | tf_op jit(solution)/shard_map/grad_context_in/all_to_all | solution.py:46
  429.0 21.1 %copy-start.81 = (pred[16]{0:T(512)(128)(4,1)S(1)}, pred[16]{0:T(512)(128)(4,1)}, u32[]{:S(2)}) copy-start(pred[16]{0:T(512)(128)(4,1)} %broadcast_in_dim.209) | copy-start | bytes 52
  429.1 20.6 %collective-permute-start.4 = (bf16[1040,192]{0,1:T(8,128)(2,1)S(1)}, bf16[1040,192]{0,1:T(8,128)(2,1)S(1)}, u32[]{:S(2)}, u32[]{:S(2)}) collective-permute-start(bf16[1040,192]{0,1:T(8,128)(2,1)S(1)} %broadcast_select_fusion.3), channel_id=1, source_target_pairs={{0,64},{64,0},{1,65},{65,1},{2,66},{66,2},{3,67},{67,3},{4,68},{68... | collective-permute-start | bytes 1198088 | tf_op jit(solution)/shard_map/swap_attend_grad/ppermute | solution.py:281
  429.7 22.4 %copy-start.35 = (bf16[128,1024]{1,0:T(8,128)(2,1)S(1)}, bf16[128,1024]{1,0:T(8,128)(2,1)}, u32[]{:S(2)}) copy-start(bf16[128,1024]{1,0:T(8,128)(2,1)} %copy-done.34) | copy-start | bytes 786436
  429.7 22.4 %copy-start.51 = (bf16[128,1024]{1,0:T(8,128)(2,1)S(1)}, bf16[128,1024]{1,0:T(8,128)(2,1)}, u32[]{:S(2)}) copy-start(bf16[128,1024]{1,0:T(8,128)(2,1)} %reshape.479) | copy-start | bytes 786436
  477.0 56.2 %all-to-all-start.8 = ((bf16[64,16,1792]{2,1,0:T(8,128)(2,1)}), bf16[64,16,1792]{2,1,0:T(8,128)(2,1)}, u32[]{:S(2)}, u32[]{:S(2)}) async-start(bf16[64,16,1792]{2,1,0:T(8,128)(2,1)} %bitcast.271), calls=%async_computation.8 | async-start | bytes 7340032 | tf_op jit(solution)/shard_map/sum_weight_grads/all_to_all | solution.py:46
  483.1 69.0 %all-reduce.4.cloned.1.call-start = ((), (), s32[]{:S(2)}) async-start(), calls=%async_computation.14 | async-start | bytes 1114112 | tf_op jit(solution)/shard_map/sum_contract/psum | solution.py:310
  495.4 94.7 %all-gather.13.cloned.1.call-start = ((), (), s32[]{:S(2)}) async-start(), calls=%async_computation.13 | async-start | bytes 1310720 | tf_op jit(solution)/shard_map/gather_weight_grads/all_gather | solution.py:339
  554.1 26.8 %all-to-all-start.9 = ((bf16[32,64,192]{2,1,0:T(8,128)(2,1)}), bf16[32,64,192]{2,1,0:T(8,128)(2,1)S(1)}, u32[]{:S(2)}, u32[]{:S(2)}) async-start(bf16[32,64,192]{2,1,0:T(8,128)(2,1)} %bitcast.79), calls=%async_computation.9 | async-start | bytes 2097152 | tf_op jit(solution)/shard_map/grad_tokens_0/all_to_all | solution.py:46
  (75 other events, 333.7 us)
Sparse Core Ops, SparseCore 0:
  14.2 140.0 all-gather.14
  188.0 72.4 all-gather.6
  279.0 56.4 all-gather.8
  396.4 63.8 all-gather.10
  495.5 56.5 all-reduce.3
  554.3 25.5 all-gather.12

commit v2 on v1

--- a/solution.py
+++ b/solution.py
@@ -64,18 +64,30 @@
     return jnp.stack([lower, upper], 1).reshape(16 * rows, features)
 
 
-def to_tokens(value, parts):
+def send_tokens(value, parts):
+    core = lax.axis_index("shard") % 2
     width = parts * HEAD_DIM
-    sends = jnp.broadcast_to(value.reshape(1, 16, 64, width), (2, 16, 64, width))
-    got = exchange(sends.reshape(32, 64, width), ALL)
-    got = got.reshape(2, 2, 8, 64, parts, HEAD_DIM).transpose(1, 3, 4, 0, 2, 5)
-    return got.reshape(128, parts * 1024)
+    halves = value.reshape(16, 2, 32, width)
+    keep = jnp.where(core == 0, halves[:, 0], halves[:, 1])
+    take = swap_cores(jnp.where(core == 0, halves[:, 1], halves[:, 0]))
+    lower = jnp.split(jnp.where(core == 0, keep, take), parts, 2)
+    upper = jnp.split(jnp.where(core == 0, take, keep), parts, 2)
+    pair = jnp.concatenate([piece for both in zip(lower, upper) for piece in both], 2)
+    sends = jnp.broadcast_to(pair[None], (2, 16, 32, 2 * width)).reshape(32, 32, 2 * width)
+    return exchange(sends, ALL).reshape(2, 2, 4, 2, 32, 2 * width)
+
+
+def as_rows(got):
+    return got.transpose(1, 3, 4, 0, 2, 5).reshape(128, 8 * got.shape[-1])
 
 
 def to_head(value, layer):
-    sends = value.reshape(2, 64, 2, 8, HEAD_DIM).transpose(2, 0, 3, 1, 4).reshape(32, 64, HEAD_DIM)
+    core = lax.axis_index("shard") % 2
+    sends = value.reshape(2, 64, 2, 4, 128).transpose(2, 0, 3, 1, 4)[:, :, :, None]
+    sends = jnp.broadcast_to(sends, (2, 2, 4, 2, 64, 128)).reshape(32, 64, 128)
     got = exchange(sends, ALL)
-    return got[16 * layer : 16 * layer + 16].reshape(1024, HEAD_DIM)
+    got = got[16 * layer : 16 * layer + 16].reshape(1024, 128)
+    return jnp.where(core == 0, got[:, :HEAD_DIM], got[:, HEAD_DIM:])
 
 
 def masked_scores(queries, keys, seg):
@@ -141,6 +153,19 @@
     return grad_mlp, grad_residual, grad_attn, grad_context, sums
 
 
+def unpack_weights(gathered):
+    return (
+        gathered[:, :64].reshape(1024, 1024),
+        [gathered[:, 64 + 64 * q : 128 + 64 * q].reshape(1024, 1024) for q in range(4)],
+        gathered[:, 320:576].reshape(4096, 1024),
+    )
+
+
+def with_sums(grad, sums):
+    rows = jnp.concatenate([sums[None], jnp.zeros((15, sums.shape[0]), jnp.float32)], 0)
+    return jnp.concatenate([grad.astype(LOW), rows.astype(LOW)], 0)
+
+
 def on_device(
     inputs,
     segments,
@@ -164,12 +189,9 @@
         rows = jnp.concatenate(
             [output_weight[0]] + jnp.split(expand_weight[0], 4, 1) + [contract_weight[0]], 0
         )
-        gathered = lax.all_gather(rows, "shard", axis=0, tiled=False)
-        weights = (
-            gathered[:, :64].reshape(1024, 1024),
-            [gathered[:, 64 + 64 * q : 128 + 64 * q].reshape(1024, 1024) for q in range(4)],
-            gathered[:, 320:576].reshape(4096, 1024),
-        )
+        quarter = lax.dynamic_slice_in_dim(rows, lax.axis_index("replica") * 144, 144, 0)
+        gathered = lax.all_gather(quarter, REST, axis=0, tiled=False).reshape(16, 576, 1024)
+        weights = unpack_weights(gathered)
 
     with jax.named_scope("head_weights"):
         by_head = attend_weight[0].reshape(64, 3, HEADS, HEAD_DIM).transpose(2, 0, 1, 3)
@@ -213,7 +235,7 @@
             packed = (matmul(whole, head_weight[layer]) + head_bias[layer]).astype(LOW)
             context, log_totals = attend(packed, seg)
         with jax.named_scope("context_out"):
-            context = to_tokens(context, 1)
+            context = as_rows(send_tokens(context, 1))
         return context, (whole, packed, log_totals)
 
     def attention_back(layer, grad_context, kept):
@@ -237,7 +259,8 @@
             on_first, output, lax.ppermute(output, "section", [(0, 1)])
         )
     with jax.named_scope("gather_attend_weight"):
-        late_weight, unused = lax.optimization_barrier((attend_weight[0], output))
+        by_pair = attend_weight[0].reshape(64, 3, 8, 128).transpose(0, 2, 1, 3).reshape(64, 3072)
+        late_weight, unused = lax.optimization_barrier((by_pair, output))
         whole_attend = lax.all_gather(late_weight, "shard", axis=0, tiled=True)
     context_1, kept_1 = attention(1, tokens_1.reshape(2, 64, 1024))
     own_tokens = jnp.where(on_first, tokens_0, tokens_1)
@@ -256,8 +279,11 @@
             last_grad.astype(jnp.float32), saved, weights, own_biases, own_gains
         )
     grad_packed, grad_attend_1, grad_sums_1 = attention_back(1, grad_context, kept_1)
+    with jax.named_scope("swap_attend_grad"):
+        part_1 = with_sums(grad_attend_1, grad_sums_1)
+        take_1 = lax.ppermute(part_1, "section", [(0, 1)])
     with jax.named_scope("grad_tokens_1"):
-        grad_tokens_1 = grad_residual + times_transposed(to_tokens(grad_packed, 3), whole_attend)
+        grad_tokens_1 = grad_residual + times_transposed(as_rows(send_tokens(grad_packed, 3)), whole_attend)
     with jax.named_scope("to_previous_section"):
         arrived = lax.ppermute(grad_tokens_1.astype(LOW), "section", [(1, 0)])
         own_grad = jnp.where(on_first, arrived, last_grad)
@@ -269,46 +295,14 @@
         grad_mlp_all = lax.all_gather(grad_mlp, "shard", axis=0, tiled=True)
     grad_packed, grad_attend_0, grad_sums_0 = attention_back(0, grad_context, kept_0)
 
-    with jax.named_scope("swap_attend_grad"):
-        grad_attend_0 = grad_attend_0.astype(LOW)
-        grad_attend_1 = grad_attend_1.astype(LOW)
-        sums = jnp.stack([grad_sums_0, grad_sums_1]).astype(LOW)
-        pad = jnp.zeros((15, 192), LOW)
-        part_0 = jnp.concatenate([grad_attend_0, sums[0:1], pad], 0)
-        part_1 = jnp.concatenate([grad_attend_1, sums[1:2], pad], 0)
-        keep = jnp.where(on_first, part_0, part_1)
-        give = jnp.where(on_first, part_1, part_0)
-        take = lax.ppermute(give, "section", [(0, 1), (1, 0)])
-        lower = jnp.where(on_first, keep, take)
-        upper = jnp.where(on_first, take, keep)
+    with jax.named_scope("sum_attend_grads"):
+        part_0 = with_sums(grad_attend_0, grad_sums_0)
+        take_0 = lax.ppermute(part_0, "section", [(1, 0)])
+        lower = jnp.where(on_first, part_0, take_1)
+        upper = jnp.where(on_first, take_0, part_1)
         attend_part = jnp.concatenate([lower[:1024], upper[:1024]], 1)
         sums = jnp.stack([lower[1024], upper[1024]]).reshape(2, 3, HEAD_DIM)
-    with jax.named_scope("block_weight_grads"):
-        quarter = lax.dynamic_index_in_dim(
-            jnp.stack([part for part in weights[1]]), shard // 4, 0, keepdims=False
-        )
-        expand_part = lax.dynamic_slice_in_dim(quarter, (shard % 4) * 256, 256, 1)
-        hidden_part = lax.dynamic_slice_in_dim(own_hidden, shard * 256, 256, 0)
-        inner = matmul(first_all, expand_part) + hidden_part
-        activation, gelu_back = jax.vjp(gelu_exact, inner)
-        grad_inner = gelu_back(times_transposed(grad_mlp_all, contract_weight[0]))[0].astype(LOW)
-        expand_grad = transposed_times(first_all, grad_inner)
-        contract_grad = transposed_times(activation.astype(LOW), grad_mlp_all)
-        output_grad = transposed_times(own_context, grad_attn)
-        hidden_sum = jnp.sum(grad_inner.astype(jnp.float32), 0)
-        mlp_sum = jnp.sum(grad_mlp_all.astype(jnp.float32), 0)
-    with jax.named_scope("sum_contract"):
-        rows = jnp.concatenate(
-            [
-                contract_grad,
-                jnp.concatenate([hidden_sum, jnp.zeros((768,), jnp.float32)])[None],
-                mlp_sum[None],
-                jnp.zeros((14, 1024), jnp.float32),
-            ],
-            0,
-        ).astype(LOW)
-        contract_total = lax.psum(rows, "replica").astype(jnp.float32)
-    with jax.named_scope("sum_weight_grads"):
+        output_grad = transposed_times(own_context, grad_attn).astype(LOW)
         norm_rows = norm_sums.reshape(5, 16, 64).transpose(1, 0, 2)
         mine = jnp.arange(8) == shard % 8
         head_rows = jnp.where(
@@ -318,31 +312,60 @@
             jnp.concatenate([norm_rows, head_rows], 1), ((0, 0), (0, 9), (0, 64))
         )
         vectors = jnp.broadcast_to(vectors[:, None], (16, 4, 16, 128)).reshape(1024, 128)
-        parts = jnp.concatenate(
+        parts = jnp.concatenate([attend_part, output_grad, vectors.astype(LOW)], 1)
+        got = exchange(parts.reshape(64, 16, 1536), REST)
+    with jax.named_scope("block_weight_grads"):
+        quarter = lax.dynamic_index_in_dim(
+            jnp.stack([part for part in weights[1]]), shard // 4, 0, keepdims=False
+        )
+        expand_part = lax.dynamic_slice_in_dim(quarter, (shard % 4) * 256, 256, 1)
+        hidden_part = lax.dynamic_slice_in_dim(own_hidden, shard * 256, 256, 0)
+        inner = matmul(first_all, expand_part) + hidden_part
+        activation, gelu_back = jax.vjp(gelu_exact, inner)
+        grad_inner = gelu_back(times_transposed(grad_mlp_all, contract_weight[0]))[0].astype(LOW)
+        expand_grad = transposed_times(first_all, grad_inner).astype(LOW)
+        contract_grad = transposed_times(activation.astype(LOW), grad_mlp_all).astype(LOW)
+        hidden_sum = jnp.sum(grad_inner.astype(jnp.float32), 0)
+        mlp_sum = jnp.sum(grad_mlp_all.astype(jnp.float32), 0)
+        extra = jnp.concatenate(
             [
-                attend_part,
-                output_grad.astype(LOW),
-                expand_grad.astype(LOW),
-                vectors.astype(LOW),
+                jnp.concatenate([hidden_sum, jnp.zeros((768,), jnp.float32)])[None],
+                mlp_sum[None],
+                jnp.zeros((14, 1024), jnp.float32),
             ],
-            1,
-        )
-        got = exchange(parts.reshape(64, 16, 1792), REST).astype(jnp.float32)
-        got_attend = got[:, :, :384].reshape(2, 8, 4, 16, 2, 3, 64).sum((0, 2))
-        got_attend = got_attend.transpose(1, 3, 2, 0, 4).reshape(16, 3072)
-        got_output = got[:, :, 384:1408].sum(0)
-        got_expand = got[:, :, 1408:1664].reshape(16, 4, 16, 256).sum(1)
+            0,
+        ).astype(LOW)
+        rows = jnp.concatenate(
+            [contract_grad.reshape(4, 64, 1024), jnp.broadcast_to(extra, (4, 16, 1024))], 1
+        )
+    got, expand_grad, rows = lax.optimization_barrier((got, expand_grad, rows))
+    with jax.named_scope("sum_expand"):
+        got_expand = exchange(expand_grad.reshape(64, 16, 256), REST).reshape(16, 4, 16, 256)
+        got_expand = got_expand.astype(jnp.float32).sum(1).astype(LOW)
         got_expand = got_expand.transpose(1, 0, 2).reshape(16, 4096)
-        got_vectors = got[:, :7, 1664:1728].sum(0)
-        owned = jnp.concatenate([got_attend, got_output, got_expand], 1).astype(LOW)
+    with jax.named_scope("sum_contract"):
+        got_contract = exchange(rows, "replica").astype(jnp.float32).sum(0)
+    with jax.named_scope("sum_attend_grads"):
+        got_attend = got[:, :, :384].astype(jnp.float32).reshape(2, 8, 4, 16, 384).sum((0, 2))
+        got_output = got[:, :, 384:1408].astype(jnp.float32).sum(0).astype(LOW)
+        got_vectors = got[:, :7, 1408:1472].astype(jnp.float32).sum(0)
+        got_attend, got_output = lax.optimization_barrier((got_attend.astype(LOW), got_output))
+        got_attend = got_attend.reshape(8, 16, 2, 3, 64).transpose(1, 3, 2, 0, 4)
+        got_attend = got_attend.reshape(16, 3072)
+    with jax.named_scope("gather_weight_grads"):
+        contract_rows = got_contract[:64].astype(LOW).reshape(4, 16, 1024)
+        owned = jnp.concatenate([got_attend, got_output, got_expand, *contract_rows], 1)
+    with jax.named_scope("grad_tokens_0"):
+        late_packed, owned = lax.optimization_barrier((grad_packed, owned))
+        packed_rows = as_rows(send_tokens(late_packed, 3))
+        grad_tokens_0 = grad_residual + times_transposed(packed_rows, whole_attend)
     with jax.named_scope("gather_weight_grads"):
         totals = lax.all_gather(owned, "replica", axis=0, tiled=True)
-        totals = totals.astype(jnp.float32)
-    with jax.named_scope("grad_tokens_0"):
-        late_packed, unused = lax.optimization_barrier((grad_packed, owned))
-        grad_tokens_0 = grad_residual + times_transposed(to_tokens(late_packed, 3), whole_attend)
+        contract_total = totals[:, 8192:].reshape(4, 16, 4, 1024).transpose(0, 2, 1, 3)
+        contract_total = contract_total.reshape(1, 256, 1024).astype(jnp.float32)
+        totals = totals[None, :, :8192].astype(jnp.float32)
     input_grad = jnp.where(on_first, grad_tokens_0, grad_tokens_1).reshape(1, 2, 1, 64, 1024)
-    mlp_own = lax.dynamic_slice_in_dim(contract_total[257], shard * 64, 64, 0)
+    mlp_own = lax.dynamic_slice_in_dim(got_contract[65], shard * 64, 64, 0)
     biases_grad = jnp.stack(
         [
             got_vectors[5],
@@ -356,12 +379,12 @@
     return (
         layer_output,
         input_grad,
-        totals[None, :, :3072],
-        totals[None, :, 3072:4096],
-        totals[None, :, 4096:],
-        contract_total[None, :256],
+        totals[:, :, :3072],
+        totals[:, :, 3072:4096],
+        totals[:, :, 4096:],
+        contract_total,
         biases_grad[None],
-        contract_total[None, 256, :256],
+        got_contract[None, 64, :256],
         got_vectors[None, :2],
     )
 

time: 611 us -> 593 us (0.971)
  waiting for transfers between devices: 214 us -> 180 us
  starting transfers between devices: 56.3 us -> 75.8 us
  local copies, waits for them, and re-layouts: 125 us -> 115 us
    all_to_all x8 -> x10, waiting for transfers between devices: 154 us -> 113 us  [exchange(): return lax.all_to_all(value, axes, 0, 0, tiled=True)]
    all_gather x1, waiting for transfers between devices: 16.7 us -> 39 us  [on_device(): lax.all_gather(quarter, REST, axis=0, tiled=False).reshape(16, 576, 1024)]
    all_to_all x8 -> x10, starting transfers between devices: 48.1 us -> 60.3 us  [exchange(): return lax.all_to_all(value, axes, 0, 0, tiled=True)]
    unnamed x202 -> x211, local copies, waits for them, and re-layouts: 40.2 us -> 33.7 us
    concatenate x9 -> x5, local copies, waits for them, and re-layouts: 14.9 us -> 8.34 us  [the longest x2 3.42 us: send_tokens(): jnp.concatenate([piece for both in zip(lower, upper) for piece in both], 2)]
    all_gather x1, waiting for transfers between devices: 6.18 us -> 0.02 us  [on_device(): grad_mlp_all = lax.all_gather(grad_mlp, 'shard', axis=0, tiled=True)]
    ppermute x1 -> x2, starting transfers between devices: 0.57 us -> 6.71 us  [the longest x1 5.29 us: on_device(): take_1 = lax.ppermute(part_1, 'section', [(0, 1)])]
    ppermute x1 -> x2, waiting for transfers between devices: 19.9 us -> 15.6 us  [the longest x1 15.6 us: on_device(): take_0 = lax.ppermute(part_0, 'section', [(1, 0)])]
  transfers between devices with their start and end apart: 19 -> 25, of which waited for: 16 -> 18; matrix products, arithmetic and copies ran while one was open for 32% -> 35% of each run, Pallas kernels for 0% -> 0%
where the time goes in v2:
time: 593 us; the launch traced here: 582 us
  waiting for transfers between devices  180 us (30%)
  local copies, waits for them, and re-layouts  115 us (19%)
  matrix products  111 us (19%)
  starting transfers between devices  75.8 us (13%)
  blocking collectives  44.5 us (8%)
  other arithmetic  39.6 us (7%)
  between operations  16.2 us (3%)
    all_to_all x10, waiting for transfers between devices, exchange(): return lax.all_to_all(value, axes, 0, 0, tiled=True)  113 us
    all_to_all x10, starting transfers between devices, exchange(): return lax.all_to_all(value, axes, 0, 0, tiled=True)  60.3 us
    dot_general x19, matrix products, times_transposed(): lax.dot_general(left, right, (((1,), (1,)), ((), ())), preferred_element_...  57 us
    all_to_all x2, blocking collectives, exchange(): return lax.all_to_all(value, axes, 0, 0, tiled=True)  44.5 us
    all_gather x1, waiting for transfers between devices, on_device(): lax.all_gather(quarter, REST, axis=0, tiled=False).reshape(16, 576, 1024)  39 us
    unnamed x211, local copies, waits for them, and re-layouts  33.7 us
    dot_general x19, matrix products, matmul(): return jnp.dot(left, right, preferred_element_type=jnp.float32)  31.4 us
    dot_general x9, matrix products, transposed_times(): lax.dot_general(left, right, (((0,), (0,)), ((), ())), preferred_element_...  22.1 us
  transfers between devices with their start and end apart: 25, of which 18 were waited for; matrix products, arithmetic and copies ran while one was open for 35% of the time, Pallas kernels for 0%

profile of v2, /device:TPU:1, one launch (start us, length us, event | category | flops | bytes accessed | tf_op | source)
XLA Modules:
  0.0 582.1 jit_solution(5407254878257515325)
XLA Ops:
  18.9 9.4 %all-to-all-start = ((bf16[32,80,192]{2,1,0:T(8,128)(2,1)}), bf16[32,80,192]{2,1,0:T(8,128)(2,1)S(1)}, u32[]{:S(2)}, u32[]{:S(2)}) async-start(bf16[32,80,192]{2,1,0:T(8,128)(2,1)} %bitcast.5), calls=%async_computation | async-start | bytes 2621440 | tf_op jit(solution)/shard_map/head_weights/all_to_all | solution.py:46
  28.4 21.9 %all-to-all-done = bf16[32,80,192]{2,1,0:T(8,128)(2,1)S(1)} async-done(((bf16[32,80,192]{2,1,0:T(8,128)(2,1)}), bf16[32,80,192]{2,1,0:T(8,128)(2,1)S(1)}, u32[]{:S(2)}, u32[]{:S(2)}) %all-to-all-start) | async-done | bytes 983072 | tf_op jit(solution)/shard_map/head_weights/all_to_all | solution.py:46
  51.4 4.6 all-to-all-start.1
  56.4 23.6 %all-to-all-done.1 = bf16[16,32,1024]{2,1,0:T(8,128)(2,1)S(1)} async-done(((bf16[16,32,1024]{2,1,0:T(8,128)(2,1)}), bf16[16,32,1024]{2,1,0:T(8,128)(2,1)S(1)}, u32[]{:S(2)}, u32[]{:S(2)}) %all-to-all-start.1) | async-done | bytes 1048608 | tf_op jit(solution)/shard_map/sequence_tokens/all_to_all | solution.py:46
  100.7 10.4 %all-to-all-done.2 = bf16[32,32,128]{2,1,0:T(8,128)(2,1)S(1)} async-done(((bf16[32,32,128]{2,1,0:T(8,128)(2,1)}), bf16[32,32,128]{2,1,0:T(8,128)(2,1)S(1)}, u32[]{:S(2)}, u32[]{:S(2)}) %all-to-all-start.2) | async-done | bytes 262176 | tf_op jit(solution)/shard_map/context_out/all_to_all | solution.py:46
  111.5 39.0 %all-gather.15.cloned.1.call-done = bf16[9216,1024]{1,0:T(8,128)(2,1)} async-done(((bf16[144,1024]{1,0:T(8,128)(2,1)}), bf16[9216,1024]{1,0:T(8,128)(2,1)}) %all-gather.15.cloned.1.call-update) | async-done | bytes 18874384 | tf_op jit(solution)/shard_map/gather_block_weights/all_gather | solution.py:193
  150.5 8.1 %slice.332 = bf16[16,256,1024]{2,1,0:T(8,128)(2,1)} slice(bf16[16,576,1024]{2,1,0:T(8,128)(2,1)} %bitcast.336), slice={[0:16], [320:576], [0:1024]} | slice | bytes 16777216 | tf_op jit(solution)/shard_map/gather_block_weights/slice | solution.py:160
  158.6 4.7 fusion.193
  169.7 5.6 fusion.205
  178.0 5.4 collective-permute-done.2
  183.7 23.8 %all_to_all.60 = bf16[16,32,1024]{2,1,0:T(8,128)(2,1)} all-to-all(bf16[16,32,1024]{2,1,0:T(8,128)(2,1)S(1)} %bitcast.355), channel_id=1, replica_groups=mesh['section'=2,'shard'=16,'replica'=4] {'shard'}, dimensions={0} | all-to-all | bytes 2097152 | tf_op jit(solution)/shard_map/sequence_tokens/all_to_all | solution.py:46
  221.8 20.7 %all_to_all.61 = bf16[32,32,128]{2,1,0:T(8,128)(2,1)S(1)} all-to-all(bf16[32,32,128]{2,1,0:T(8,128)(2,1)S(1)} %bitcast.387), channel_id=1, replica_groups=mesh['section'=2,'shard'=16,'replica'=4] {'section','shard'}, dimensions={0} | all-to-all | bytes 524288 | tf_op jit(solution)/shard_map/context_out/all_to_all | solution.py:46
  255.3 5.9 %fusion.207 = (f32[128]{0:T(128)S(1)}, f32[128,1024]{1,0:T(8,128)S(1)}) fusion(f32[1024]{0:T(1024)S(1)} %bitcast.436, bf16[4096,1024]{1,0:T(8,128)(2,1)} %bitcast.340, f32[128,4096]{1,0:T(8,128)S(1)} %fusion.7, f32[4096]{0:T(1024)S(1)} %bitcast.420, f32[128,1024]{1,0:T(8,128)S(1)} %fusion.217, f32[128,1024]{1,0:T(8,128)S(1)} %fusion.216, ...), kind=kOutput, calls=%fused_computation.408 | convolution fusion | flops 1078198144 | bytes 13661184 | tf_op jit(solution)/shard_map/block_1/dot_general | solution.py:30
  262.3 6.1 %add_convert_fusion.2 = bf16[128,4096]{1,0:T(8,128)(2,1)} fusion(f32[128,4096]{1,0:T(8,128)S(1)} %fusion.7, bf16[4096,1024]{1,0:T(8,128)(2,1)S(1)} %bitcast.347, f32[128,1024]{1,0:T(8,128)S(1)} %get-tuple-element.92, f32[128]{0:T(128)S(1)} %negate_multiply_fusion.6, f32[4096]{0:T(1024)S(1)} %bitcast.421, f32[128,1024]{1,0:T(8,128)} %copy-done.36, ...), kind=kOutput, calls=%fused_computation.54 | convolution fusion | flops 1083441152 | bytes 14172672 | tf_op jit(solution)/shard_map/block_back_1/dot_general | solution.py:34
  282.3 5.0 all-to-all-start.5
  287.3 11.5 %all-to-all-done.5 = bf16[32,64,128]{2,1,0:T(8,128)(2,1)} async-done(((bf16[32,64,128]{2,1,0:T(8,128)(2,1)}), bf16[32,64,128]{2,1,0:T(8,128)(2,1)}, u32[]{:S(2)}, u32[]{:S(2)}) %all-to-all-start.5) | async-done | bytes 524320 | tf_op jit(solution)/shard_map/grad_context_in/all_to_all | solution.py:46
  324.6 5.1 all-to-all-start.6
  349.0 6.2 %fusion.208 = (bf16[128,1024]{1,0:T(8,128)(2,1)S(1)}, f32[128,1024]{1,0:T(8,128)}) fusion(bf16[128,3072]{1,0:T(8,128)(2,1)} %reshape.529, bf16[1024,3072]{1,0:T(8,128)(2,1)} %all-gather.7.cloned.1.call-done, f32[128,1024]{1,0:T(8,128)} %copy-done.23, f32[128]{0:T(128)} %copy-done.78), kind=kOutput, calls=%fused_computation.409 | convolution fusion | flops 805699584 | bytes 8389120 | tf_op jit(solution)/shard_map/grad_tokens_1/dot_general | solution.py:34
  357.7 5.3 collective-permute-start.7
  367.3 8.8 %add_convert_fusion.1 = bf16[128,4096]{1,0:T(8,128)(2,1)} fusion(f32[128,4096]{1,0:T(8,128)} %copy-done.34, f32[4096]{0:T(1024)S(1)} %bitcast.422, f32[128,1024]{1,0:T(8,128)} %copy-done.36, f32[128,1024]{1,0:T(8,128)} %copy-done.37, f32[128,1024]{1,0:T(8,128)} %copy-done.38, f32[128,1024]{1,0:T(8,128)} %copy-done.39, ...), kind=kOutput, calls=%fused_computation.52 | convolution fusion | flops 1083179008 | bytes 13910016 | tf_op jit(solution)/shard_map/block_back_0/dot_general | solution.py:34
  386.2 4.8 all-to-all-start.7
  391.1 5.4 convolution_add_fusion
  396.9 5.6 all-to-all-done.7
  415.2 15.6 %collective-permute-done.8 = bf16[1040,192]{0,1:T(8,128)(2,1)S(1)} collective-permute-done((bf16[1040,192]{0,1:T(8,128)(2,1)S(1)}, bf16[1040,192]{0,1:T(8,128)(2,1)S(1)}, u32[]{:S(2)}, u32[]{:S(2)}) %collective-permute-start.8) | collective-permute-done | bytes 399392 | tf_op jit(solution)/shard_map/sum_attend_grads/ppermute | solution.py:300
  438.1 10.4 %all-to-all-start.8 = ((bf16[64,16,1536]{2,1,0:T(8,128)(2,1)}), bf16[64,16,1536]{2,1,0:T(8,128)(2,1)S(1)}, u32[]{:S(2)}, u32[]{:S(2)}) async-start(bf16[64,16,1536]{2,1,0:T(8,128)(2,1)} %bitcast.81), calls=%async_computation.8 | async-start | bytes 6291456 | tf_op jit(solution)/shard_map/sum_attend_grads/all_to_all | solution.py:46
  448.6 8.7 %fusion.209 = (bf16[256]{0:T(256)(128)(2,1)S(1)}, bf16[2048,256]{1,0:T(8,128)(2,1)}) fusion(f32[2048,256]{1,0:T(8,128)} %convolution_add_fusion, bf16[2048,1024]{1,0:T(8,128)(2,1)} %all-gather.11.cloned.1.call-done, bf16[1,256,1024]{2,1,0:T(8,128)(2,1)} %param.16), kind=kOutput, calls=%fused_computation.410 | convolution fusion | flops 1112014592 | bytes 7864832 | tf_op jit(solution)/shard_map/block_weight_grads/dot_general | solution.py:34
  460.2 8.2 %convolution_convert_fusion.1 = bf16[256,1024]{1,0:T(8,128)(2,1)S(1)} fusion(bf16[2048,1024]{1,0:T(8,128)(2,1)} %all-gather.11.cloned.1.call-done, f32[2048,256]{1,0:T(8,128)} %convolution_add_fusion), kind=kOutput, calls=%fused_computation.90 | convolution fusion | flops 1108082688 | bytes 6815744 | tf_op jit(solution)/shard_map/block_weight_grads/dot_general | solution.py:40
  471.5 16.8 %all-to-all-done.8 = bf16[64,16,1536]{2,1,0:T(8,128)(2,1)S(1)} async-done(((bf16[64,16,1536]{2,1,0:T(8,128)(2,1)}), bf16[64,16,1536]{2,1,0:T(8,128)(2,1)S(1)}, u32[]{:S(2)}, u32[]{:S(2)}) %all-to-all-start.8) | async-done | bytes 3145760 | tf_op jit(solution)/shard_map/sum_attend_grads/all_to_all | solution.py:46
  501.8 8.4 %all-to-all-start.9 = ((bf16[64,16,256]{2,1,0:T(8,128)(2,1)}), bf16[64,16,256]{2,1,0:T(8,128)(2,1)}, u32[]{:S(2)}, u32[]{:S(2)}) async-start(bf16[64,16,256]{2,1,0:T(8,128)(2,1)} %bitcast.397), calls=%async_computation.9 | async-start | bytes 1048576 | tf_op jit(solution)/shard_map/sum_expand/all_to_all | solution.py:46
  515.8 7.7 %all-to-all-done.9 = bf16[64,16,256]{2,1,0:T(8,128)(2,1)} async-done(((bf16[64,16,256]{2,1,0:T(8,128)(2,1)}), bf16[64,16,256]{2,1,0:T(8,128)(2,1)}, u32[]{:S(2)}, u32[]{:S(2)}) %all-to-all-start.9) | async-done | bytes 524320 | tf_op jit(solution)/shard_map/sum_expand/all_to_all | solution.py:46
  548.4 11.1 %all-to-all-done.11 = bf16[32,32,384]{2,1,0:T(8,128)(2,1)} async-done(((bf16[32,32,384]{2,1,0:T(8,128)(2,1)}), bf16[32,32,384]{2,1,0:T(8,128)(2,1)}, u32[]{:S(2)}, u32[]{:S(2)}) %all-to-all-start.11) | async-done | bytes 786464 | tf_op jit(solution)/shard_map/grad_tokens_0/all_to_all | solution.py:46
  561.9 5.8 fusion.41
  (495 shorter events, 226.3 us)
Async XLA Ops:
  7.2 143.3 %all-gather.15.cloned.1.call-start = ((), (), s32[]{:S(2)}) async-start(), calls=%async_computation.16 | async-start | bytes 19169280 | tf_op jit(solution)/shard_map/gather_block_weights/all_gather | solution.py:193
  17.7 32.6 %copy-start.26 = (bf16[2,1,64,1024]{3,2,1,0:T(8,128)(2,1)S(1)}, bf16[2,1,64,1024]{3,2,1,0:T(8,128)(2,1)}, u32[]{:S(2)}) copy-start(bf16[2,1,64,1024]{3,2,1,0:T(8,128)(2,1)} %param.10) | copy-start | bytes 786436
  18.9 31.4 %all-to-all-start = ((bf16[32,80,192]{2,1,0:T(8,128)(2,1)}), bf16[32,80,192]{2,1,0:T(8,128)(2,1)S(1)}, u32[]{:S(2)}, u32[]{:S(2)}) async-start(bf16[32,80,192]{2,1,0:T(8,128)(2,1)} %bitcast.5), calls=%async_computation | async-start | bytes 2621440 | tf_op jit(solution)/shard_map/head_weights/all_to_all | solution.py:46
  51.4 28.6 %all-to-all-start.1 = ((bf16[16,32,1024]{2,1,0:T(8,128)(2,1)}), bf16[16,32,1024]{2,1,0:T(8,128)(2,1)S(1)}, u32[]{:S(2)}, u32[]{:S(2)}) async-start(bf16[16,32,1024]{2,1,0:T(8,128)(2,1)} %bitcast.8), calls=%async_computation.1 | async-start | bytes 2097152 | tf_op jit(solution)/shard_map/sequence_tokens/all_to_all | solution.py:46
  80.0 5.4 collective-permute-start
  93.1 1.4 collective-permute-start.1
  95.4 15.7 %all-to-all-start.2 = ((bf16[32,32,128]{2,1,0:T(8,128)(2,1)}), bf16[32,32,128]{2,1,0:T(8,128)(2,1)S(1)}, u32[]{:S(2)}, u32[]{:S(2)}) async-start(bf16[32,32,128]{2,1,0:T(8,128)(2,1)} %bitcast.22), calls=%async_computation.2 | async-start | bytes 524288 | tf_op jit(solution)/shard_map/context_out/all_to_all | solution.py:46
  99.1 249.9 %all-gather.7.cloned.1.call-start = ((), (), s32[]{:S(2)}) async-start(), calls=%async_computation.12 | async-start | bytes 6684672 | tf_op jit(solution)/shard_map/gather_attend_weight/all_gather | solution.py:264
  111.5 51.8 %copy-start.31 = (bf16[128,1024]{1,0:T(8,128)(2,1)}, bf16[128,1024]{1,0:T(8,128)(2,1)S(1)}, u32[]{:S(2)}) copy-start(bf16[128,1024]{1,0:T(8,128)(2,1)S(1)} %reshape.509) | copy-start | bytes 786436
  175.7 7.6 %collective-permute-start.2 = (bf16[128,1024]{1,0:T(8,128)(2,1)S(1)}, bf16[128,1024]{1,0:T(8,128)(2,1)S(1)}, u32[]{:S(2)}, u32[]{:S(2)}) collective-permute-start(bf16[128,1024]{1,0:T(8,128)(2,1)S(1)} %add_convert_fusion.4), channel_id=1, source_target_pairs={{0,64},{1,65},{2,66},{3,67},{4,68},{5,69},{6,70},{7,71},{8,72},{9,... | collective-permute-start | bytes 786440 | tf_op jit(solution)/shard_map/to_next_section/ppermute | solution.py:259
  207.5 4.3 collective-permute-start.3
  211.8 179.3 %all-gather.9.cloned.1.call-start = ((), (), s32[]{:S(2)}) async-start(), calls=%async_computation.13 | async-start | bytes 4456448 | tf_op jit(solution)/shard_map/gather_first/all_gather | solution.py:274
  220.1 22.8 %copy-start.65 = (f32[1,1,1024]{2,0,1:T(1,128)S(1)}, f32[1,1,1024]{2,0,1:T(1,128)}, u32[]{:S(2)}) copy-start(f32[1,1,1024]{2,0,1:T(1,128)} %get-tuple-element.136) | copy-start | bytes 12292
  220.1 1.4 collective-permute-start.4
  245.3 29.7 %copy-start.69 = (f32[128]{0:T(128)}, f32[128]{0:T(128)S(1)}, u32[]{:S(2)}) copy-start(f32[128]{0:T(128)S(1)} %fusion.147) | copy-start | bytes 1540
  282.3 16.5 %all-to-all-start.5 = ((bf16[32,64,128]{2,1,0:T(8,128)(2,1)}), bf16[32,64,128]{2,1,0:T(8,128)(2,1)}, u32[]{:S(2)}, u32[]{:S(2)}) async-start(bf16[32,64,128]{2,1,0:T(8,128)(2,1)} %bitcast.376), calls=%async_computation.5 | async-start | bytes 1048576 | tf_op jit(solution)/shard_map/grad_context_in/all_to_all | solution.py:46
  318.0 1.6 collective-permute-start.5
  324.6 19.4 %all-to-all-start.6 = ((bf16[32,32,384]{2,1,0:T(8,128)(2,1)}), bf16[32,32,384]{2,1,0:T(8,128)(2,1)}, u32[]{:S(2)}, u32[]{:S(2)}) async-start(bf16[32,32,384]{2,1,0:T(8,128)(2,1)} %bitcast.359), calls=%async_computation.6 | async-start | bytes 1572864 | tf_op jit(solution)/shard_map/grad_tokens_1/all_to_all | solution.py:46
  329.7 118.8 %all-gather.11.cloned.1.call-start = ((), (), s32[]{:S(2)}) async-start(), calls=%async_computation.14 | async-start | bytes 4456448 | tf_op jit(solution)/shard_map/gather_grad_mlp/all_gather | solution.py:295
  355.2 9.7 %collective-permute-start.6 = (bf16[128,1024]{1,0:T(8,128)(2,1)S(1)}, bf16[128,1024]{1,0:T(8,128)(2,1)S(1)}, u32[]{:S(2)}, u32[]{:S(2)}) collective-permute-start(bf16[128,1024]{1,0:T(8,128)(2,1)S(1)} %get-tuple-element.165), channel_id=1, source_target_pairs={{64,0},{65,1},{66,2},{67,3},{68,4},{69,5},{70,6},{71,7},{72,8},{73... | collective-permute-start | bytes 786440 | tf_op jit(solution)/shard_map/to_previous_section/ppermute | solution.py:288
  357.7 52.9 %collective-permute-start.7 = (bf16[1040,192]{0,1:T(8,128)(2,1)}, bf16[1040,192]{0,1:T(8,128)(2,1)}, u32[]{:S(2)}, u32[]{:S(2)}) collective-permute-start(bf16[1040,192]{0,1:T(8,128)(2,1)} %fusion.106), channel_id=1, source_target_pairs={{0,64},{1,65},{2,66},{3,67},{4,68},{5,69},{6,70},{7,71},{8,72},{9,... | collective-permute-start | bytes 1198088 | tf_op jit(solution)/shard_map/swap_attend_grad/ppermute | solution.py:284
  386.2 16.3 %all-to-all-start.7 = ((bf16[32,64,128]{2,1,0:T(8,128)(2,1)}), bf16[32,64,128]{2,1,0:T(8,128)(2,1)S(1)}, u32[]{:S(2)}, u32[]{:S(2)}) async-start(bf16[32,64,128]{2,1,0:T(8,128)(2,1)} %bitcast.75), calls=%async_computation.7 | async-start | bytes 1048576 | tf_op jit(solution)/shard_map/grad_context_in/all_to_all | solution.py:46
  410.8 20.1 %copy-start.45 = (bf16[1024,192]{0,1:T(8,128)(2,1)S(1)}, bf16[1024,192]{0,1:T(8,128)(2,1)}, u32[]{:S(2)}) copy-start(bf16[1024,192]{0,1:T(8,128)(2,1)} %convolution_convert_fusion.3) | copy-start | bytes 1179652
  410.8 20.0 %copy-start.57 = (bf16[1,192]{0,1:T(8,128)(2,1)S(1)}, bf16[1,192]{0,1:T(8,128)(2,1)}, u32[]{:S(2)}) copy-start(bf16[1,192]{0,1:T(8,128)(2,1)} %copy-done.56) | copy-start | bytes 1156
  410.8 20.0 %collective-permute-start.8 = (bf16[1040,192]{0,1:T(8,128)(2,1)S(1)}, bf16[1040,192]{0,1:T(8,128)(2,1)S(1)}, u32[]{:S(2)}, u32[]{:S(2)}) collective-permute-start(bf16[1040,192]{0,1:T(8,128)(2,1)S(1)} %get-tuple-element.114), channel_id=1, source_target_pairs={{64,0},{65,1},{66,2},{67,3},{68,4},{69,5},{70,6},{71,7},{72,8},{73... | collective-permute-start | bytes 1198088 | tf_op jit(solution)/shard_map/sum_attend_grads/ppermute | solution.py:300
  414.3 17.7 %copy-start.83 = (pred[16]{0:T(512)(128)(4,1)S(1)}, pred[16]{0:T(512)(128)(4,1)}, u32[]{:S(2)}) copy-start(pred[16]{0:T(512)(128)(4,1)} %broadcast_in_dim.217) | copy-start | bytes 52
  438.1 50.2 %all-to-all-start.8 = ((bf16[64,16,1536]{2,1,0:T(8,128)(2,1)}), bf16[64,16,1536]{2,1,0:T(8,128)(2,1)S(1)}, u32[]{:S(2)}, u32[]{:S(2)}) async-start(bf16[64,16,1536]{2,1,0:T(8,128)(2,1)} %bitcast.81), calls=%async_computation.8 | async-start | bytes 6291456 | tf_op jit(solution)/shard_map/sum_attend_grads/all_to_all | solution.py:46
  488.3 13.5 %all-to-all-start.10 = ((bf16[4,80,1024]{2,1,0:T(8,128)(2,1)}), bf16[4,80,1024]{2,1,0:T(8,128)(2,1)}, u32[]{:S(2)}, u32[]{:S(2)}) async-start(bf16[4,80,1024]{2,1,0:T(8,128)(2,1)} %pad_maximum_fusion.3), calls=%async_computation.10 | async-start | bytes 1310720 | tf_op jit(solution)/shard_map/sum_contract/all_to_all | solution.py:46
  501.8 21.7 %all-to-all-start.9 = ((bf16[64,16,256]{2,1,0:T(8,128)(2,1)}), bf16[64,16,256]{2,1,0:T(8,128)(2,1)}, u32[]{:S(2)}, u32[]{:S(2)}) async-start(bf16[64,16,256]{2,1,0:T(8,128)(2,1)} %bitcast.397), calls=%async_computation.9 | async-start | bytes 1048576 | tf_op jit(solution)/shard_map/sum_expand/all_to_all | solution.py:46
  510.2 57.4 %all-gather.13.cloned.1.call-start = ((), (), s32[]{:S(2)}) async-start(), calls=%async_computation.15 | async-start | bytes 1966080 | tf_op jit(solution)/shard_map/gather_weight_grads/all_gather | solution.py:363
  532.9 2.5 collective-permute-start.9
  540.5 19.0 %all-to-all-start.11 = ((bf16[32,32,384]{2,1,0:T(8,128)(2,1)}), bf16[32,32,384]{2,1,0:T(8,128)(2,1)}, u32[]{:S(2)}, u32[]{:S(2)}) async-start(bf16[32,32,384]{2,1,0:T(8,128)(2,1)} %bitcast.360), calls=%async_computation.11 | async-start | bytes 1572864 | tf_op jit(solution)/shard_map/grad_tokens_0/all_to_all | solution.py:46
  (87 other events, 437.9 us)
Sparse Core Ops, SparseCore 0:
  13.9 136.5 all-gather.14
  211.9 60.4 all-gather.6
  275.1 57.0 all-gather.8
  376.3 55.5 all-gather.10
  532.0 22.2 all-gather.12

commit v3 on v2

--- a/solution.py
+++ b/solution.py
@@ -3,6 +3,8 @@
 import jax
 import jax.numpy as jnp
 from jax import lax
+from jax.experimental import pallas as pl
+from jax.experimental.pallas import tpu as pltpu
 from jax.sharding import PartitionSpec as P
 
 HEADS = 16
@@ -13,17 +15,6 @@
 LOW = jnp.bfloat16
 ALL = ("section", "shard")
 REST = ("shard", "replica")
-
-
-def layer_norm(value, gain, shift):
-    mean_value = jnp.mean(value, -1, keepdims=True)
-    centred = value - mean_value
-    spread = jnp.mean(centred * centred, -1, keepdims=True)
-    return centred * lax.rsqrt(spread + EPSILON) * gain + shift
-
-
-def gelu_exact(value):
-    return jax.nn.gelu(value, approximate=False)
 
 
 def matmul(left, right):
@@ -121,44 +112,231 @@
     ).astype(LOW)
 
 
-def block_forward(tokens, context, weights, biases, hidden_bias, gains):
-    output_weight, expand_weight, contract_weight = weights
-    residual = tokens.astype(jnp.float32) + (matmul(context, output_weight) + biases[2])
-    first = layer_norm(residual, gains[0], biases[3])
-    first_low = first.astype(LOW)
-    inner = jnp.concatenate([matmul(first_low, part) for part in expand_weight], 1) + hidden_bias
-    activation = gelu_exact(inner).astype(LOW)
-    second = first + (matmul(activation, contract_weight) + biases[4])
-    output = layer_norm(second, gains[1], biases[5]).astype(LOW)
-    return output, (residual, first_low, inner, second)
-
-
-def block_back(grad, saved, weights, biases, gains):
-    output_weight, expand_weight, contract_weight = weights
-    residual, first_low, inner, second = saved
-    unused, norm_back_two = jax.vjp(layer_norm, second, gains[1], biases[5])
-    grad_second, grad_gain_two, grad_shift_two = norm_back_two(grad)
-    grad_mlp = grad_second.astype(LOW)
-    unused, gelu_back = jax.vjp(gelu_exact, inner)
-    grad_inner = gelu_back(times_transposed(grad_mlp, contract_weight))[0].astype(LOW)
-    grad_first = grad_second
-    for part, piece in zip(expand_weight, jnp.split(grad_inner, 4, 1)):
-        grad_first = grad_first + times_transposed(piece, part)
-    unused, norm_back_one = jax.vjp(layer_norm, residual, gains[0], biases[3])
-    grad_residual, grad_gain_one, grad_shift_one = norm_back_one(grad_first)
-    grad_attn = grad_residual.astype(LOW)
-    grad_context = times_transposed(grad_attn, output_weight).astype(LOW)
-    attn_sum = jnp.sum(grad_attn.astype(jnp.float32), 0)
-    sums = jnp.stack([grad_gain_one, grad_gain_two, attn_sum, grad_shift_one, grad_shift_two])
-    return grad_mlp, grad_residual, grad_attn, grad_context, sums
-
-
-def unpack_weights(gathered):
+def normed(value):
+    mean_value = jnp.mean(value, -1, keepdims=True)
+    centred = value - mean_value
+    spread = jnp.mean(centred * centred, -1, keepdims=True)
+    scale = lax.rsqrt(spread + EPSILON)
+    return centred * scale, scale
+
+
+def normed_back(grad, value, gain):
+    unit, scale = normed(value)
+    weighted = grad * gain
+    inner_mean = jnp.mean(weighted * unit, -1, keepdims=True)
+    grad_value = scale * (weighted - jnp.mean(weighted, -1, keepdims=True) - unit * inner_mean)
     return (
-        gathered[:, :64].reshape(1024, 1024),
-        [gathered[:, 64 + 64 * q : 128 + 64 * q].reshape(1024, 1024) for q in range(4)],
-        gathered[:, 320:576].reshape(4096, 1024),
-    )
+        grad_value,
+        jnp.sum(grad * unit, 0, keepdims=True),
+        jnp.sum(grad, 0, keepdims=True),
+    )
+
+
+def gelu_share(value):
+    return 0.5 * (1.0 + lax.erf(value * math.sqrt(0.5)))
+
+
+def gelu_slope(value):
+    return gelu_share(value) + value * jnp.exp(-0.5 * value * value) * (0.5 / math.pi) ** 0.5
+
+
+PARTS = 4
+WIDTH = 1024
+
+
+def this_part(j):
+    return jnp.minimum(j, PARTS - 1)
+
+
+def part_before(j):
+    return jnp.maximum(j - 1, 0)
+
+
+def weight_specs(expand_at, contract_at):
+    return [
+        pl.BlockSpec((16, 64, 1024), lambda j: (0, 4, 0)),
+        pl.BlockSpec((16, 64, WIDTH), lambda j: (0, 5 + expand_at(j), 0)),
+        pl.BlockSpec((4, 256, 1024), lambda j: (contract_at(j), 0, 0)),
+    ]
+
+
+def full(*shape):
+    return pl.BlockSpec(shape, lambda j: (0,) * len(shape))
+
+
+ROWS_F32 = jax.ShapeDtypeStruct((128, 1024), jnp.float32)
+ROWS_LOW = jax.ShapeDtypeStruct((128, 1024), LOW)
+BLOCK_PARAMS = pltpu.CompilerParams(
+    dimension_semantics=("arbitrary",), vmem_limit_bytes=48 * 1024 * 1024
+)
+BLOCK_COST = pl.CostEstimate(
+    flops=2 * 128 * 1024 * 9216, bytes_accessed=24 * 1024 * 1024, transcendentals=128 * 4096
+)
+
+
+def forward_kernel(
+    tokens,
+    context,
+    output_weight,
+    expand_weight,
+    contract_weight,
+    params,
+    hidden,
+    output,
+    residual,
+    first_low,
+    inner,
+    second,
+    first,
+    total,
+    before,
+):
+    step = pl.program_id(0)
+
+    @pl.when(step == 0)
+    def start():
+        attention = matmul(context[...], output_weight[...].reshape(1024, 1024))
+        summed = tokens[...].astype(jnp.float32) + (attention + params[0:1])
+        residual[...] = summed
+        after = normed(summed)[0] * params[4:5] + params[1:2]
+        first[...] = after
+        first_low[...] = after.astype(LOW)
+        total[...] = jnp.zeros_like(total)
+        before[...] = jnp.zeros_like(before)
+
+    last_part = before[...]
+    inner_part = matmul(first_low[...], expand_weight[...].reshape(1024, WIDTH)) + hidden[0]
+    inner[...] = inner_part
+    activation = (last_part * gelu_share(last_part)).astype(LOW)
+    total[...] += matmul(activation, contract_weight[...].reshape(WIDTH, 1024))
+    before[...] = inner_part
+
+    @pl.when(step == PARTS)
+    def finish():
+        summed = first[...] + (total[...] + params[2:3])
+        second[...] = summed
+        output[...] = (normed(summed)[0] * params[5:6] + params[3:4]).astype(LOW)
+
+
+def block_forward(tokens, context, gathered, params, hidden):
+    output, *saved = pl.pallas_call(
+        forward_kernel,
+        grid=(PARTS + 1,),
+        in_specs=[
+            full(128, 1024),
+            full(128, 1024),
+            *weight_specs(this_part, part_before),
+            full(8, 1024),
+            pl.BlockSpec((1, 1, WIDTH), lambda j: (this_part(j), 0, 0)),
+        ],
+        out_specs=[
+            full(128, 1024),
+            full(128, 1024),
+            full(128, 1024),
+            pl.BlockSpec((128, WIDTH), lambda j: (0, this_part(j))),
+            full(128, 1024),
+        ],
+        out_shape=[
+            ROWS_LOW,
+            ROWS_F32,
+            ROWS_LOW,
+            jax.ShapeDtypeStruct((128, 4096), jnp.float32),
+            ROWS_F32,
+        ],
+        scratch_shapes=[
+            pltpu.VMEM((128, 1024), jnp.float32),
+            pltpu.VMEM((128, 1024), jnp.float32),
+            pltpu.VMEM((128, WIDTH), jnp.float32),
+        ],
+        compiler_params=BLOCK_PARAMS,
+        cost_estimate=BLOCK_COST,
+    )(tokens, context, gathered, gathered, gathered, params, hidden)
+    return output, saved
+
+
+def backward_kernel(
+    grad,
+    output_weight,
+    expand_weight,
+    contract_weight,
+    params,
+    residual,
+    inner,
+    second,
+    grad_mlp,
+    grad_residual,
+    grad_attn,
+    grad_context,
+    sums,
+    grad_second,
+    total,
+    before,
+):
+    step = pl.program_id(0)
+
+    @pl.when(step == 0)
+    def start():
+        by_value, by_gain, by_shift = normed_back(
+            grad[...].astype(jnp.float32), second[...], params[5:6]
+        )
+        grad_second[...] = by_value
+        grad_mlp[...] = by_value.astype(LOW)
+        sums[1:2] = by_gain
+        sums[4:5] = by_shift
+        total[...] = jnp.zeros_like(total)
+        before[...] = jnp.zeros_like(before)
+
+    last_part = before[...]
+    before[...] = times_transposed(grad_mlp[...], contract_weight[...].reshape(WIDTH, 1024))
+    grad_inner = (last_part * gelu_slope(inner[...])).astype(LOW)
+    total[...] += times_transposed(grad_inner, expand_weight[...].reshape(1024, WIDTH))
+
+    @pl.when(step == PARTS)
+    def finish():
+        by_value, by_gain, by_shift = normed_back(
+            grad_second[...] + total[...], residual[...], params[4:5]
+        )
+        grad_residual[...] = by_value
+        rounded = by_value.astype(LOW)
+        grad_attn[...] = rounded
+        grad_context[...] = times_transposed(
+            rounded, output_weight[...].reshape(1024, 1024)
+        ).astype(LOW)
+        sums[0:1] = by_gain
+        sums[2:3] = jnp.sum(rounded.astype(jnp.float32), 0, keepdims=True)
+        sums[3:4] = by_shift
+        sums[5:8] = jnp.zeros((3, 1024), jnp.float32)
+
+
+def block_back(grad, saved, gathered, params):
+    residual, unused, inner, second = saved
+    return pl.pallas_call(
+        backward_kernel,
+        grid=(PARTS + 1,),
+        in_specs=[
+            full(128, 1024),
+            *weight_specs(part_before, this_part),
+            full(8, 1024),
+            full(128, 1024),
+            pl.BlockSpec((128, WIDTH), lambda j: (0, part_before(j))),
+            full(128, 1024),
+        ],
+        out_specs=[full(128, 1024)] * 4 + [full(8, 1024)],
+        out_shape=[
+            ROWS_LOW,
+            ROWS_F32,
+            ROWS_LOW,
+            ROWS_LOW,
+            jax.ShapeDtypeStruct((8, 1024), jnp.float32),
+        ],
+        scratch_shapes=[
+            pltpu.VMEM((128, 1024), jnp.float32),
+            pltpu.VMEM((128, 1024), jnp.float32),
+            pltpu.VMEM((128, WIDTH), jnp.float32),
+        ],
+        compiler_params=BLOCK_PARAMS,
+        cost_estimate=BLOCK_COST,
+    )(grad, gathered, gathered, gathered, params, residual, inner, second)
 
 
 def with_sums(grad, sums):
@@ -187,11 +365,10 @@
 
     with jax.named_scope("gather_block_weights"):
         rows = jnp.concatenate(
-            [output_weight[0]] + jnp.split(expand_weight[0], 4, 1) + [contract_weight[0]], 0
+            [contract_weight[0], output_weight[0]] + jnp.split(expand_weight[0], 4, 1), 0
         )
         quarter = lax.dynamic_slice_in_dim(rows, lax.axis_index("replica") * 144, 144, 0)
         gathered = lax.all_gather(quarter, REST, axis=0, tiled=False).reshape(16, 576, 1024)
-        weights = unpack_weights(gathered)
 
     with jax.named_scope("head_weights"):
         by_head = attend_weight[0].reshape(64, 3, HEADS, HEAD_DIM).transpose(2, 0, 1, 3)
@@ -220,7 +397,8 @@
         seg = jnp.where(micro == 0, seg[:, 0], seg[:, 1]).reshape(1024)
         own_biases = jnp.where(on_first, all_biases[0], all_biases[1])
         own_gains = jnp.where(on_first, all_gains[0], all_gains[1])
-        own_hidden = jnp.where(on_first, all_hidden[0], all_hidden[1])
+        own_hidden = jnp.where(on_first, all_hidden[0], all_hidden[1]).reshape(PARTS, 1, WIDTH)
+        params = jnp.concatenate([own_biases[2:], own_gains, jnp.zeros((2, 1024))], 0)
         head_bias = lax.dynamic_slice_in_dim(
             all_biases.reshape(2, 6, HEADS, HEAD_DIM), head, 1, 2
         )[:, :, 0]
@@ -251,9 +429,7 @@
     context_0, kept_0 = attention(0, inputs)
     tokens_0 = inputs.reshape(128, 1024)
     with jax.named_scope("block_0"):
-        output, unused = block_forward(
-            tokens_0, context_0, weights, own_biases, own_hidden, own_gains
-        )
+        output, unused = block_forward(tokens_0, context_0, gathered, params, own_hidden)
     with jax.named_scope("to_next_section"):
         tokens_1 = jnp.where(
             on_first, output, lax.ppermute(output, "section", [(0, 1)])
@@ -266,9 +442,7 @@
     own_tokens = jnp.where(on_first, tokens_0, tokens_1)
     own_context = jnp.where(on_first, context_0, context_1)
     with jax.named_scope("block_1"):
-        output, saved = block_forward(
-            own_tokens, own_context, weights, own_biases, own_hidden, own_gains
-        )
+        output, saved = block_forward(own_tokens, own_context, gathered, params, own_hidden)
     layer_output = output.reshape(1, 2, 1, 64, 1024)
     with jax.named_scope("gather_first"):
         first_all = lax.all_gather(saved[1], "shard", axis=0, tiled=True)
@@ -276,7 +450,7 @@
     last_grad = cotangent.reshape(128, 1024)
     with jax.named_scope("block_back_1"):
         unused, grad_residual, unused, grad_context, unused = block_back(
-            last_grad.astype(jnp.float32), saved, weights, own_biases, own_gains
+            last_grad, saved, gathered, params
         )
     grad_packed, grad_attend_1, grad_sums_1 = attention_back(1, grad_context, kept_1)
     with jax.named_scope("swap_attend_grad"):
@@ -289,21 +463,23 @@
         own_grad = jnp.where(on_first, arrived, last_grad)
     with jax.named_scope("block_back_0"):
         grad_mlp, grad_residual, grad_attn, grad_context, norm_sums = block_back(
-            own_grad.astype(jnp.float32), saved, weights, own_biases, own_gains
+            own_grad, saved, gathered, params
         )
     with jax.named_scope("gather_grad_mlp"):
         grad_mlp_all = lax.all_gather(grad_mlp, "shard", axis=0, tiled=True)
     grad_packed, grad_attend_0, grad_sums_0 = attention_back(0, grad_context, kept_0)
 
-    with jax.named_scope("sum_attend_grads"):
+    with jax.named_scope("sum_output_grad"):
+        output_grad = transposed_times(own_context, grad_attn).astype(LOW)
+        output_got = exchange(output_grad.reshape(64, 16, 1024), REST)
+    with jax.named_scope("swap_attend_grad"):
         part_0 = with_sums(grad_attend_0, grad_sums_0)
         take_0 = lax.ppermute(part_0, "section", [(1, 0)])
         lower = jnp.where(on_first, part_0, take_1)
         upper = jnp.where(on_first, take_0, part_1)
         attend_part = jnp.concatenate([lower[:1024], upper[:1024]], 1)
         sums = jnp.stack([lower[1024], upper[1024]]).reshape(2, 3, HEAD_DIM)
-        output_grad = transposed_times(own_context, grad_attn).astype(LOW)
-        norm_rows = norm_sums.reshape(5, 16, 64).transpose(1, 0, 2)
+        norm_rows = norm_sums[:5].reshape(5, 16, 64).transpose(1, 0, 2)
         mine = jnp.arange(8) == shard % 8
         head_rows = jnp.where(
             mine[None, :, None, None], sums[:, None, ::2].astype(jnp.float32), 0.0
@@ -312,17 +488,16 @@
             jnp.concatenate([norm_rows, head_rows], 1), ((0, 0), (0, 9), (0, 64))
         )
         vectors = jnp.broadcast_to(vectors[:, None], (16, 4, 16, 128)).reshape(1024, 128)
-        parts = jnp.concatenate([attend_part, output_grad, vectors.astype(LOW)], 1)
-        got = exchange(parts.reshape(64, 16, 1536), REST)
+        vectors = vectors.astype(LOW)
     with jax.named_scope("block_weight_grads"):
-        quarter = lax.dynamic_index_in_dim(
-            jnp.stack([part for part in weights[1]]), shard // 4, 0, keepdims=False
-        )
-        expand_part = lax.dynamic_slice_in_dim(quarter, (shard % 4) * 256, 256, 1)
-        hidden_part = lax.dynamic_slice_in_dim(own_hidden, shard * 256, 256, 0)
+        expand_part = lax.dynamic_slice(
+            gathered, (0, 320 + shard // 4 * 64, shard % 4 * 256), (16, 64, 256)
+        ).reshape(1024, 256)
+        hidden_part = lax.dynamic_slice_in_dim(own_hidden.reshape(4096), shard * 256, 256, 0)
         inner = matmul(first_all, expand_part) + hidden_part
-        activation, gelu_back = jax.vjp(gelu_exact, inner)
-        grad_inner = gelu_back(times_transposed(grad_mlp_all, contract_weight[0]))[0].astype(LOW)
+        activation = inner * gelu_share(inner)
+        grad_inner = times_transposed(grad_mlp_all, contract_weight[0]) * gelu_slope(inner)
+        grad_inner = grad_inner.astype(LOW)
         expand_grad = transposed_times(first_all, grad_inner).astype(LOW)
         contract_grad = transposed_times(activation.astype(LOW), grad_mlp_all).astype(LOW)
         hidden_sum = jnp.sum(grad_inner.astype(jnp.float32), 0)
@@ -338,17 +513,21 @@
         rows = jnp.concatenate(
             [contract_grad.reshape(4, 64, 1024), jnp.broadcast_to(extra, (4, 16, 1024))], 1
         )
-    got, expand_grad, rows = lax.optimization_barrier((got, expand_grad, rows))
-    with jax.named_scope("sum_expand"):
-        got_expand = exchange(expand_grad.reshape(64, 16, 256), REST).reshape(16, 4, 16, 256)
-        got_expand = got_expand.astype(jnp.float32).sum(1).astype(LOW)
-        got_expand = got_expand.transpose(1, 0, 2).reshape(16, 4096)
+    output_got, attend_part, expand_grad, vectors, rows = lax.optimization_barrier(
+        (output_got, attend_part, expand_grad, vectors, rows)
+    )
+    with jax.named_scope("sum_attend_expand_grads"):
+        parts = jnp.concatenate([attend_part, expand_grad, vectors], 1)
+        got = exchange(parts.reshape(64, 16, 768), REST)
+        got, rows = lax.optimization_barrier((got, rows))
     with jax.named_scope("sum_contract"):
         got_contract = exchange(rows, "replica").astype(jnp.float32).sum(0)
-    with jax.named_scope("sum_attend_grads"):
+    with jax.named_scope("sum_attend_expand_grads"):
+        got_output = output_got.astype(jnp.float32).sum(0).astype(LOW)
         got_attend = got[:, :, :384].astype(jnp.float32).reshape(2, 8, 4, 16, 384).sum((0, 2))
-        got_output = got[:, :, 384:1408].astype(jnp.float32).sum(0).astype(LOW)
-        got_vectors = got[:, :7, 1408:1472].astype(jnp.float32).sum(0)
+        got_expand = got[:, :, 384:640].astype(jnp.float32).reshape(16, 4, 16, 256).sum(1)
+        got_expand = got_expand.astype(LOW).transpose(1, 0, 2).reshape(16, 4096)
+        got_vectors = got[:, :7, 640:704].astype(jnp.float32).sum(0)
         got_attend, got_output = lax.optimization_barrier((got_attend.astype(LOW), got_output))
         got_attend = got_attend.reshape(8, 16, 2, 3, 64).transpose(1, 3, 2, 0, 4)
         got_attend = got_attend.reshape(16, 3072)

time: 593 us -> 572 us (0.965)
  matrix products: 111 us -> 50.9 us
  Pallas kernels: 0 us -> 50.7 us
  local copies, waits for them, and re-layouts: 115 us -> 71.2 us
  blocking collectives: 44.5 us -> 70 us
  waiting for transfers between devices: 180 us -> 205 us
  other arithmetic: 39.6 us -> 26.8 us
    pallas_call x0 -> x4, Pallas kernels: none -> 50.7 us  [the longest x2 27.4 us: block_back(): pl.pallas_call(backward_kernel, grid=(PARTS + 1,), in_specs=[full(128, 10...]
    dot_general x19 -> x7, matrix products: 57 us -> 25.2 us  [times_transposed(): lax.dot_general(left, right, (((1,), (1,)), ((), ())), preferred_element_...]
    all_to_all x2 -> x3, blocking collectives: 44.5 us -> 70 us  [exchange(): return lax.all_to_all(value, axes, 0, 0, tiled=True)]
    dot_general x19 -> x7, matrix products: 31.4 us -> 11.4 us  [matmul(): return jnp.dot(left, right, preferred_element_type=jnp.float32)]
    all_gather x1, waiting for transfers between devices: 0.02 us -> 17.8 us  [on_device(): grad_mlp_all = lax.all_gather(grad_mlp, 'shard', axis=0, tiled=True)]
    slice x4 -> x2, local copies, waits for them, and re-layouts: 13.4 us -> 0.01 us  [the longest x1 0.01 us: on_device(): own_biases[2:]]
    unnamed x211 -> x106, local copies, waits for them, and re-layouts: 33.7 us -> 21.6 us
    ppermute x1, waiting for transfers between devices: 15.6 us -> 6.41 us  [on_device(): take_0 = lax.ppermute(part_0, 'section', [(1, 0)])]
  transfers between devices with their start and end apart: 25 -> 24, of which waited for: 18 -> 19; matrix products, arithmetic and copies ran while one was open for 35% -> 20% of each run, Pallas kernels for 0% -> 7%
where the time goes in v3:
time: 572 us; the launch traced here: 562 us
  waiting for transfers between devices  205 us (36%)
  starting transfers between devices  72.4 us (13%)
  local copies, waits for them, and re-layouts  71.2 us (12%)
  blocking collectives  70 us (12%)
  matrix products  50.9 us (9%)
  Pallas kernels  50.7 us (9%)
  other arithmetic  26.8 us (5%)
  between operations  15.4 us (3%)
    all_to_all x9, waiting for transfers between devices, exchange(): return lax.all_to_all(value, axes, 0, 0, tiled=True)  118 us
    all_to_all x3, blocking collectives, exchange(): return lax.all_to_all(value, axes, 0, 0, tiled=True)  70 us
    all_to_all x9, starting transfers between devices, exchange(): return lax.all_to_all(value, axes, 0, 0, tiled=True)  57.3 us
    all_gather x1, waiting for transfers between devices, on_device(): lax.all_gather(quarter, REST, axis=0, tiled=False).reshape(16, 576, 1024)  39.8 us
    pallas_call x2, Pallas kernels, block_back(): pl.pallas_call(backward_kernel, grid=(PARTS + 1,), in_specs=[full(128, 10...  27.4 us
    dot_general x7, matrix products, times_transposed(): lax.dot_general(left, right, (((1,), (1,)), ((), ())), preferred_element_...  25.2 us
    pallas_call x2, Pallas kernels, block_forward(): pl.pallas_call(forward_kernel, grid=(PARTS + 1,), in_specs=[full(128, 102...  23.3 us
    unnamed x106, local copies, waits for them, and re-layouts  21.6 us
  transfers between devices with their start and end apart: 24, of which 19 were waited for; matrix products, arithmetic and copies ran while one was open for 20% of the time, Pallas kernels for 7%

profile of v3, /device:TPU:1, one launch (start us, length us, event | category | flops | bytes accessed | tf_op | source)
XLA Modules:
  0.0 562.3 jit_solution(4602900112377114219)
XLA Ops:
  18.9 9.6 %all-to-all-start = ((bf16[32,80,192]{2,1,0:T(8,128)(2,1)}), bf16[32,80,192]{2,1,0:T(8,128)(2,1)S(1)}, u32[]{:S(2)}, u32[]{:S(2)}) async-start(bf16[32,80,192]{2,1,0:T(8,128)(2,1)} %bitcast.5), calls=%async_computation | async-start | bytes 2621440 | tf_op jit(solution)/shard_map/head_weights/all_to_all | solution.py:37
  30.0 20.3 %all-to-all-done = bf16[32,80,192]{2,1,0:T(8,128)(2,1)S(1)} async-done(((bf16[32,80,192]{2,1,0:T(8,128)(2,1)}), bf16[32,80,192]{2,1,0:T(8,128)(2,1)S(1)}, u32[]{:S(2)}, u32[]{:S(2)}) %all-to-all-start) | async-done | bytes 983072 | tf_op jit(solution)/shard_map/head_weights/all_to_all | solution.py:37
  51.4 4.7 all-to-all-start.1
  56.6 23.6 %all-to-all-done.1 = bf16[16,32,1024]{2,1,0:T(8,128)(2,1)S(1)} async-done(((bf16[16,32,1024]{2,1,0:T(8,128)(2,1)}), bf16[16,32,1024]{2,1,0:T(8,128)(2,1)S(1)}, u32[]{:S(2)}, u32[]{:S(2)}) %all-to-all-start.1) | async-done | bytes 1048608 | tf_op jit(solution)/shard_map/sequence_tokens/all_to_all | solution.py:37
  94.3 3.9 all-to-all-start.2
  98.7 11.6 %all-to-all-done.2 = bf16[32,32,128]{2,1,0:T(8,128)(2,1)S(1)} async-done(((bf16[32,32,128]{2,1,0:T(8,128)(2,1)}), bf16[32,32,128]{2,1,0:T(8,128)(2,1)S(1)}, u32[]{:S(2)}, u32[]{:S(2)}) %all-to-all-start.2) | async-done | bytes 262176 | tf_op jit(solution)/shard_map/context_out/all_to_all | solution.py:37
  110.7 39.8 %all-gather.15.cloned.1.call-done = bf16[9216,1024]{1,0:T(8,128)(2,1)} async-done(((bf16[144,1024]{1,0:T(8,128)(2,1)}), bf16[9216,1024]{1,0:T(8,128)(2,1)}) %all-gather.15.cloned.1.call-update) | async-done | bytes 18874384 | tf_op jit(solution)/shard_map/gather_block_weights/all_gather | solution.py:371
  150.5 11.9 %block_0.1 = (bf16[128,1024]{1,0:T(8,128)(2,1)S(1)}, f32[128,1024]{1,0:T(8,128)}, bf16[128,1024]{1,0:T(8,128)(2,1)}, f32[128,4096]{1,0:T(8,128)}, f32[128,1024]{1,0:T(8,128)}) custom-call(bf16[128,1024]{1,0:T(8,128)(2,1)S(1)} %bitcast.247, bf16[128,1024]{1,0:T(8,128)(2,1)S(1)} %reshape.377.context, bf16[16,576,1024]{2,1,0:T(8,128)(2,1)} %bitcast.249, ...), custom_call_target="tpu_custom_call" | custom-call | flops 2415919104 | bytes 25165824 | tf_op jit(solution)/shard_map/block_0/pallas_call | solution.py:222
  164.7 5.5 collective-permute-done.2
  171.1 25.1 %all_to_all.60 = bf16[16,32,1024]{2,1,0:T(8,128)(2,1)S(1)} all-to-all(bf16[16,32,1024]{2,1,0:T(8,128)(2,1)S(1)} %bitcast.272), channel_id=1, replica_groups=mesh['section'=2,'shard'=16,'replica'=4] {'shard'}, dimensions={0} | all-to-all | bytes 2097152 | tf_op jit(solution)/shard_map/sequence_tokens/all_to_all | solution.py:37
  207.3 16.4 %all_to_all.61 = bf16[32,32,128]{2,1,0:T(8,128)(2,1)S(1)} all-to-all(bf16[32,32,128]{2,1,0:T(8,128)(2,1)S(1)} %bitcast.301), channel_id=1, replica_groups=mesh['section'=2,'shard'=16,'replica'=4] {'section','shard'}, dimensions={0} | all-to-all | bytes 524288 | tf_op jit(solution)/shard_map/context_out/all_to_all | solution.py:37
  225.0 11.4 %block_1.1 = (bf16[128,1024]{1,0:T(8,128)(2,1)}, f32[128,1024]{1,0:T(8,128)S(1)}, bf16[128,1024]{1,0:T(8,128)(2,1)S(1)}, f32[128,4096]{1,0:T(8,128)S(1)}, f32[128,1024]{1,0:T(8,128)S(1)}) custom-call(bf16[128,1024]{1,0:T(8,128)(2,1)S(1)} %copy-done.1, bf16[128,1024]{1,0:T(8,128)(2,1)S(1)} %broadcast_select_fusion.6.context, ...), custom_call_target="tpu_custom_call" | custom-call | flops 2415919104 | bytes 25165824 | tf_op jit(solution)/shard_map/block_1/pallas_call | solution.py:222
  238.1 14.1 %block_back_1.1 = (bf16[128,1024]{1,0:T(8,128)(2,1)}, f32[128,1024]{1,0:T(8,128)S(1)}, bf16[128,1024]{1,0:T(8,128)(2,1)}, bf16[128,1024]{1,0:T(8,128)(2,1)S(1)}, f32[8,1024]{1,0:T(8,128)}) custom-call(bf16[128,1024]{1,0:T(8,128)(2,1)S(1)} %bitcast.248, bf16[16,576,1024]{2,1,0:T(8,128)(2,1)} %bitcast.255, bf16[16,576,1024]{2,1,0:T(8,128)(2,1)} %bitcast.256, ...), custom_call_target="tpu_custom_call" | custom-call | flops 2415919104 | bytes 25165824 | tf_op jit(solution)/shard_map/block_back_1/pallas_call | solution.py:313
  257.4 5.7 %all-to-all-start.5 = ((bf16[32,64,128]{2,1,0:T(8,128)(2,1)}), bf16[32,64,128]{2,1,0:T(8,128)(2,1)}, u32[]{:S(2)}, u32[]{:S(2)}) async-start(bf16[32,64,128]{2,1,0:T(8,128)(2,1)} %bitcast.288), calls=%async_computation.5 | async-start | bytes 1048576 | tf_op jit(solution)/shard_map/grad_context_in/all_to_all | solution.py:37
  263.3 11.5 %all-to-all-done.5 = bf16[32,64,128]{2,1,0:T(8,128)(2,1)} async-done(((bf16[32,64,128]{2,1,0:T(8,128)(2,1)}), bf16[32,64,128]{2,1,0:T(8,128)(2,1)}, u32[]{:S(2)}, u32[]{:S(2)}) %all-to-all-start.5) | async-done | bytes 524320 | tf_op jit(solution)/shard_map/grad_context_in/all_to_all | solution.py:37
  303.7 28.5 %all_to_all.62 = bf16[32,32,384]{2,1,0:T(8,128)(2,1)S(1)} all-to-all(bf16[32,32,384]{2,1,0:T(8,128)(2,1)S(1)} %bitcast.276), channel_id=1, replica_groups=mesh['section'=2,'shard'=16,'replica'=4] {'section','shard'}, dimensions={0} | all-to-all | bytes 1572864 | tf_op jit(solution)/shard_map/grad_tokens_1/all_to_all | solution.py:37
  336.1 6.1 %fusion.68 = (bf16[128,1024]{1,0:T(8,128)(2,1)S(1)}, f32[128,1024]{1,0:T(8,128)}) fusion(f32[128,1024]{1,0:T(8,128)} %copy-done.6, bf16[128,3072]{1,0:T(8,128)(2,1)} %reshape.392, bf16[1024,3072]{1,0:T(8,128)(2,1)} %all-gather.7.cloned.1.call-done), kind=kOutput, calls=%fused_computation.184 | convolution fusion | flops 805568512 | bytes 8388608 | tf_op jit(solution)/shard_map/grad_tokens_1/dot_general | solution.py:25
  343.5 8.3 %collective-permute-done.6 = bf16[128,1024]{1,0:T(8,128)(2,1)S(1)} collective-permute-done((bf16[128,1024]{1,0:T(8,128)(2,1)S(1)}, bf16[128,1024]{1,0:T(8,128)(2,1)S(1)}, u32[]{:S(2)}, u32[]{:S(2)}) %collective-permute-start.6) | collective-permute-done | bytes 262176 | tf_op jit(solution)/shard_map/to_previous_section/ppermute | solution.py:462
  351.9 13.3 %block_back_0.1 = (bf16[128,1024]{1,0:T(8,128)(2,1)S(1)}, f32[128,1024]{1,0:T(8,128)S(1)}, bf16[128,1024]{1,0:T(8,128)(2,1)S(1)}, bf16[128,1024]{1,0:T(8,128)(2,1)S(1)}, f32[8,1024]{1,0:T(8,128)S(1)}) custom-call(bf16[128,1024]{1,0:T(8,128)(2,1)S(1)} %broadcast_select_fusion.5.grad, bf16[16,576,1024]{2,1,0:T(8,128)(2,1)} %bitcast.258, ...), custom_call_target="tpu_custom_call" | custom-call | flops 2415919104 | bytes 25165824 | tf_op jit(solution)/shard_map/block_back_0/pallas_call | solution.py:313
  372.9 5.6 all-to-all-start.7
  383.4 7.8 %all-to-all-done.7 = bf16[32,64,128]{2,1,0:T(8,128)(2,1)} async-done(((bf16[32,64,128]{2,1,0:T(8,128)(2,1)}), bf16[32,64,128]{2,1,0:T(8,128)(2,1)}, u32[]{:S(2)}, u32[]{:S(2)}) %all-to-all-start.7) | async-done | bytes 524320 | tf_op jit(solution)/shard_map/grad_context_in/all_to_all | solution.py:37
  402.4 4.8 convolution_add_fusion
  409.2 7.4 %all-to-all-start.8 = ((bf16[64,16,1024]{2,1,0:T(8,128)(2,1)}), bf16[64,16,1024]{2,1,0:T(8,128)(2,1)S(1)}, u32[]{:S(2)}, u32[]{:S(2)}) async-start(bf16[64,16,1024]{2,1,0:T(8,128)(2,1)} %bitcast.65), calls=%async_computation.8 | async-start | bytes 4194304 | tf_op jit(solution)/shard_map/sum_output_grad/all_to_all | solution.py:37
  417.6 6.4 %collective-permute-done.8 = bf16[1040,192]{0,1:T(8,128)(2,1)} collective-permute-done((bf16[1040,192]{0,1:T(8,128)(2,1)}, bf16[1040,192]{0,1:T(8,128)(2,1)}, u32[]{:S(2)}, u32[]{:S(2)}) %collective-permute-start.8) | collective-permute-done | bytes 399392 | tf_op jit(solution)/shard_map/swap_attend_grad/ppermute | solution.py:477
  428.4 17.8 %all-gather.11.cloned.1.call-done = bf16[2048,1024]{1,0:T(8,128)(2,1)} async-done(((bf16[128,1024]{1,0:T(8,128)(2,1)}), bf16[2048,1024]{1,0:T(8,128)(2,1)}) %all-gather.11.cloned.1.call-update) | async-done | bytes 4194320 | tf_op jit(solution)/shard_map/gather_grad_mlp/all_gather | solution.py:469
  449.1 5.4 fusion.69
  464.4 7.5 %all-to-all-start.9 = ((bf16[64,16,768]{2,1,0:T(8,128)(2,1)}), bf16[64,16,768]{2,1,0:T(8,128)(2,1)}, u32[]{:S(2)}, u32[]{:S(2)}) async-start(bf16[64,16,768]{2,1,0:T(8,128)(2,1)} %bitcast.266), calls=%async_computation.9 | async-start | bytes 3145728 | tf_op jit(solution)/shard_map/sum_attend_expand_grads/all_to_all | solution.py:37
  472.2 23.4 %all-to-all-done.9 = bf16[64,16,768]{2,1,0:T(8,128)(2,1)} async-done(((bf16[64,16,768]{2,1,0:T(8,128)(2,1)}), bf16[64,16,768]{2,1,0:T(8,128)(2,1)}, u32[]{:S(2)}, u32[]{:S(2)}) %all-to-all-start.9) | async-done | bytes 1572896 | tf_op jit(solution)/shard_map/sum_attend_expand_grads/all_to_all | solution.py:37
  502.2 8.9 %all-to-all-done.10 = bf16[4,80,1024]{2,1,0:T(8,128)(2,1)S(1)} async-done(((bf16[4,80,1024]{2,1,0:T(8,128)(2,1)}), bf16[4,80,1024]{2,1,0:T(8,128)(2,1)S(1)}, u32[]{:S(2)}, u32[]{:S(2)}) %all-to-all-start.10) | async-done | bytes 655392 | tf_op jit(solution)/shard_map/sum_contract/all_to_all | solution.py:37
  517.3 9.4 %all-to-all-start.11 = ((bf16[32,32,384]{2,1,0:T(8,128)(2,1)}), bf16[32,32,384]{2,1,0:T(8,128)(2,1)S(1)}, u32[]{:S(2)}, u32[]{:S(2)}) async-start(bf16[32,32,384]{2,1,0:T(8,128)(2,1)} %bitcast.80), calls=%async_computation.11 | async-start | bytes 1572864 | tf_op jit(solution)/shard_map/grad_tokens_0/all_to_all | solution.py:37
  529.5 11.4 %all-to-all-done.11 = bf16[32,32,384]{2,1,0:T(8,128)(2,1)S(1)} async-done(((bf16[32,32,384]{2,1,0:T(8,128)(2,1)}), bf16[32,32,384]{2,1,0:T(8,128)(2,1)S(1)}, u32[]{:S(2)}, u32[]{:S(2)}) %all-to-all-start.11) | async-done | bytes 786464 | tf_op jit(solution)/shard_map/grad_tokens_0/all_to_all | solution.py:37
  542.1 5.1 fusion.70
  (336 shorter events, 154.7 us)
Async XLA Ops:
  7.2 143.3 %all-gather.15.cloned.1.call-start = ((), (), s32[]{:S(2)}) async-start(), calls=%async_computation.16 | async-start | bytes 19169280 | tf_op jit(solution)/shard_map/gather_block_weights/all_gather | solution.py:371
  18.9 31.5 %copy-start = (bf16[2,1,64,1024]{3,2,1,0:T(8,128)(2,1)S(1)}, bf16[2,1,64,1024]{3,2,1,0:T(8,128)(2,1)}, u32[]{:S(2)}) copy-start(bf16[2,1,64,1024]{3,2,1,0:T(8,128)(2,1)} %param.10) | copy-start | bytes 786436
  18.9 31.5 %all-to-all-start = ((bf16[32,80,192]{2,1,0:T(8,128)(2,1)}), bf16[32,80,192]{2,1,0:T(8,128)(2,1)S(1)}, u32[]{:S(2)}, u32[]{:S(2)}) async-start(bf16[32,80,192]{2,1,0:T(8,128)(2,1)} %bitcast.5), calls=%async_computation | async-start | bytes 2621440 | tf_op jit(solution)/shard_map/head_weights/all_to_all | solution.py:37
  51.4 28.8 %all-to-all-start.1 = ((bf16[16,32,1024]{2,1,0:T(8,128)(2,1)}), bf16[16,32,1024]{2,1,0:T(8,128)(2,1)S(1)}, u32[]{:S(2)}, u32[]{:S(2)}) async-start(bf16[16,32,1024]{2,1,0:T(8,128)(2,1)} %bitcast.271), calls=%async_computation.1 | async-start | bytes 2097152 | tf_op jit(solution)/shard_map/sequence_tokens/all_to_all | solution.py:37
  80.2 4.3 collective-permute-start
  92.0 1.4 collective-permute-start.1
  94.3 16.0 %all-to-all-start.2 = ((bf16[32,32,128]{2,1,0:T(8,128)(2,1)}), bf16[32,32,128]{2,1,0:T(8,128)(2,1)S(1)}, u32[]{:S(2)}, u32[]{:S(2)}) async-start(bf16[32,32,128]{2,1,0:T(8,128)(2,1)} %bitcast.22), calls=%async_computation.2 | async-start | bytes 524288 | tf_op jit(solution)/shard_map/context_out/all_to_all | solution.py:37
  98.2 237.8 %all-gather.7.cloned.1.call-start = ((), (), s32[]{:S(2)}) async-start(), calls=%async_computation.12 | async-start | bytes 6684672 | tf_op jit(solution)/shard_map/gather_attend_weight/all_gather | solution.py:440
  162.4 239.9 %all-gather.9.cloned.1.call-start = ((), (), s32[]{:S(2)}) async-start(), calls=%async_computation.13 | async-start | bytes 4456448 | tf_op jit(solution)/shard_map/gather_first/all_gather | solution.py:448
  162.5 7.7 %collective-permute-start.2 = (bf16[128,1024]{1,0:T(8,128)(2,1)S(1)}, bf16[128,1024]{1,0:T(8,128)(2,1)S(1)}, u32[]{:S(2)}, u32[]{:S(2)}) collective-permute-start(bf16[128,1024]{1,0:T(8,128)(2,1)S(1)} %get-tuple-element.34), channel_id=1, source_target_pairs={{0,64},{1,65},{2,66},{3,67},{4,68},{5,69},{6,70},{7,71},{8,72},{9,... | collective-permute-start | bytes 786440 | tf_op jit(solution)/shard_map/to_next_section/ppermute | solution.py:435
  196.2 2.7 collective-permute-start.3
  205.6 1.4 collective-permute-start.4
  257.4 17.3 %all-to-all-start.5 = ((bf16[32,64,128]{2,1,0:T(8,128)(2,1)}), bf16[32,64,128]{2,1,0:T(8,128)(2,1)}, u32[]{:S(2)}, u32[]{:S(2)}) async-start(bf16[32,64,128]{2,1,0:T(8,128)(2,1)} %bitcast.288), calls=%async_computation.5 | async-start | bytes 1048576 | tf_op jit(solution)/shard_map/grad_context_in/all_to_all | solution.py:37
  263.2 183.0 %all-gather.11.cloned.1.call-start = ((), (), s32[]{:S(2)}) async-start(), calls=%async_computation.14 | async-start | bytes 4456448 | tf_op jit(solution)/shard_map/gather_grad_mlp/all_gather | solution.py:469
  298.0 1.6 collective-permute-start.5
  336.1 15.7 %copy-start.3 = (bf16[2,1,64,1024]{3,2,1,0:T(8,128)(2,1)S(1)}, bf16[2,1,64,1024]{3,2,1,0:T(8,128)(2,1)}, u32[]{:S(2)}) copy-start(bf16[2,1,64,1024]{3,2,1,0:T(8,128)(2,1)} %param.12) | copy-start | bytes 786436
  342.2 9.6 %collective-permute-start.6 = (bf16[128,1024]{1,0:T(8,128)(2,1)S(1)}, bf16[128,1024]{1,0:T(8,128)(2,1)S(1)}, u32[]{:S(2)}, u32[]{:S(2)}) collective-permute-start(bf16[128,1024]{1,0:T(8,128)(2,1)S(1)} %get-tuple-element.151), channel_id=1, source_target_pairs={{64,0},{65,1},{66,2},{67,3},{68,4},{69,5},{70,6},{71,7},{72,8},{73... | collective-permute-start | bytes 786440 | tf_op jit(solution)/shard_map/to_previous_section/ppermute | solution.py:462
  368.4 10.1 %copy-start.22 = (bf16[16,2,32,1024]{3,2,1,0:T(8,128)(2,1)S(1)}, bf16[16,2,32,1024]{3,2,1,0:T(8,128)(2,1)}, u32[]{:S(2)}) copy-start(bf16[16,2,32,1024]{3,2,1,0:T(8,128)(2,1)} %copy-done.21) | copy-start | bytes 6291460
  368.4 10.1 %copy-start.32 = (bf16[1024,64]{0,1:T(8,128)(2,1)S(1)}, bf16[1024,64]{0,1:T(8,128)(2,1)}, u32[]{:S(2)}) copy-start(bf16[1024,64]{0,1:T(8,128)(2,1)} %fusion.23) | copy-start | bytes 393220
  368.4 10.1 %copy-start.33 = (bf16[1024,64]{0,1:T(8,128)(2,1)S(1)}, bf16[1024,64]{0,1:T(8,128)(2,1)}, u32[]{:S(2)}) copy-start(bf16[1024,64]{0,1:T(8,128)(2,1)} %fusion.19) | copy-start | bytes 393220
  368.4 10.1 %copy-start.34 = (bf16[1024,64]{0,1:T(8,128)(2,1)S(1)}, bf16[1024,64]{0,1:T(8,128)(2,1)}, u32[]{:S(2)}) copy-start(bf16[1024,64]{0,1:T(8,128)(2,1)} %fusion.21) | copy-start | bytes 393220
  372.9 18.2 %all-to-all-start.7 = ((bf16[32,64,128]{2,1,0:T(8,128)(2,1)}), bf16[32,64,128]{2,1,0:T(8,128)(2,1)}, u32[]{:S(2)}, u32[]{:S(2)}) async-start(bf16[32,64,128]{2,1,0:T(8,128)(2,1)} %bitcast.63), calls=%async_computation.7 | async-start | bytes 1048576 | tf_op jit(solution)/shard_map/grad_context_in/all_to_all | solution.py:37
  378.5 13.6 %copy-start.27 = (bf16[1024,192]{0,1:T(8,128)(2,1)S(1)}, bf16[1024,192]{0,1:T(8,128)(2,1)}, u32[]{:S(2)}) copy-start(bf16[1024,192]{0,1:T(8,128)(2,1)} %copy-done.26) | copy-start | bytes 1179652
  379.9 20.2 %collective-permute-start.7 = (bf16[1040,192]{0,1:T(8,128)(2,1)S(1)}, bf16[1040,192]{0,1:T(8,128)(2,1)S(1)}, u32[]{:S(2)}, u32[]{:S(2)}) collective-permute-start(bf16[1040,192]{0,1:T(8,128)(2,1)S(1)} %fusion.36), channel_id=1, source_target_pairs={{0,64},{1,65},{2,66},{3,67},{4,68},{5,69},{6,70},{7,71},{8,72},{9,... | collective-permute-start | bytes 1198088 | tf_op jit(solution)/shard_map/swap_attend_grad/ppermute | solution.py:458
  401.1 23.0 %collective-permute-start.8 = (bf16[1040,192]{0,1:T(8,128)(2,1)}, bf16[1040,192]{0,1:T(8,128)(2,1)}, u32[]{:S(2)}, u32[]{:S(2)}) collective-permute-start(bf16[1040,192]{0,1:T(8,128)(2,1)} %get-tuple-element.119), channel_id=1, source_target_pairs={{64,0},{65,1},{66,2},{67,3},{68,4},{69,5},{70,6},{71,7},{72,8},{73... | collective-permute-start | bytes 1198088 | tf_op jit(solution)/shard_map/swap_attend_grad/ppermute | solution.py:477
  409.2 49.8 %all-to-all-start.8 = ((bf16[64,16,1024]{2,1,0:T(8,128)(2,1)}), bf16[64,16,1024]{2,1,0:T(8,128)(2,1)S(1)}, u32[]{:S(2)}, u32[]{:S(2)}) async-start(bf16[64,16,1024]{2,1,0:T(8,128)(2,1)} %bitcast.65), calls=%async_computation.8 | async-start | bytes 4194304 | tf_op jit(solution)/shard_map/sum_output_grad/all_to_all | solution.py:37
  428.4 20.7 %copy-start.37 = (bf16[1,256,1024]{2,1,0:T(8,128)(2,1)S(1)}, bf16[1,256,1024]{2,1,0:T(8,128)(2,1)}, u32[]{:S(2)}) copy-start(bf16[1,256,1024]{2,1,0:T(8,128)(2,1)} %param.16) | copy-start | bytes 1572868
  464.4 31.2 %all-to-all-start.9 = ((bf16[64,16,768]{2,1,0:T(8,128)(2,1)}), bf16[64,16,768]{2,1,0:T(8,128)(2,1)}, u32[]{:S(2)}, u32[]{:S(2)}) async-start(bf16[64,16,768]{2,1,0:T(8,128)(2,1)} %bitcast.266), calls=%async_computation.9 | async-start | bytes 3145728 | tf_op jit(solution)/shard_map/sum_attend_expand_grads/all_to_all | solution.py:37
  498.6 12.5 %all-to-all-start.10 = ((bf16[4,80,1024]{2,1,0:T(8,128)(2,1)}), bf16[4,80,1024]{2,1,0:T(8,128)(2,1)S(1)}, u32[]{:S(2)}, u32[]{:S(2)}) async-start(bf16[4,80,1024]{2,1,0:T(8,128)(2,1)} %pad_maximum_fusion.4), calls=%async_computation.10 | async-start | bytes 1310720 | tf_op jit(solution)/shard_map/sum_contract/all_to_all | solution.py:37
  502.1 46.0 %all-gather.13.cloned.1.call-start = ((), (), s32[]{:S(2)}) async-start(), calls=%async_computation.15 | async-start | bytes 1966080 | tf_op jit(solution)/shard_map/gather_weight_grads/all_gather | solution.py:542
  511.5 4.1 collective-permute-start.9
  517.3 23.6 %all-to-all-start.11 = ((bf16[32,32,384]{2,1,0:T(8,128)(2,1)}), bf16[32,32,384]{2,1,0:T(8,128)(2,1)S(1)}, u32[]{:S(2)}, u32[]{:S(2)}) async-start(bf16[32,32,384]{2,1,0:T(8,128)(2,1)} %bitcast.80), calls=%async_computation.11 | async-start | bytes 1572864 | tf_op jit(solution)/shard_map/grad_tokens_0/all_to_all | solution.py:37
  (36 other events, 110.3 us)
Sparse Core Ops, SparseCore 0:
  13.9 136.5 all-gather.14
  162.5 72.8 all-gather.6
  237.9 54.8 all-gather.8
  368.2 77.9 all-gather.10
  514.6 27.4 all-gather.12

commit v4 on v3

--- a/solution.py
+++ b/solution.py
@@ -68,19 +68,6 @@
     return exchange(sends, ALL).reshape(2, 2, 4, 2, 32, 2 * width)
 
 
-def as_rows(got):
-    return got.transpose(1, 3, 4, 0, 2, 5).reshape(128, 8 * got.shape[-1])
-
-
-def to_head(value, layer):
-    core = lax.axis_index("shard") % 2
-    sends = value.reshape(2, 64, 2, 4, 128).transpose(2, 0, 3, 1, 4)[:, :, :, None]
-    sends = jnp.broadcast_to(sends, (2, 2, 4, 2, 64, 128)).reshape(32, 64, 128)
-    got = exchange(sends, ALL)
-    got = got[16 * layer : 16 * layer + 16].reshape(1024, 128)
-    return jnp.where(core == 0, got[:, :HEAD_DIM], got[:, HEAD_DIM:])
-
-
 def masked_scores(queries, keys, seg):
     scores = times_transposed(queries, keys) * SCALE
     return jnp.where(seg[:, None] == seg[None, :], scores, NEGATIVE)
@@ -94,22 +81,6 @@
     totals = jnp.sum(exponent, -1, keepdims=True)
     context = matmul((exponent / totals).astype(LOW), values).astype(LOW)
     return context, highest + jnp.log(totals)
-
-
-def attend_back(packed, log_totals, seg, grad_context):
-    queries, keys, values = jnp.split(packed, 3, 1)
-    soft = jnp.exp(masked_scores(queries, keys, seg) - log_totals)
-    grad_soft = times_transposed(grad_context, values)
-    row_total = jnp.sum(soft * grad_soft, -1, keepdims=True)
-    grad_scores = (soft * (grad_soft - row_total)).astype(LOW)
-    return jnp.concatenate(
-        [
-            matmul(grad_scores, keys) * SCALE,
-            transposed_times(grad_scores, queries) * SCALE,
-            transposed_times(soft.astype(LOW), grad_context),
-        ],
-        1,
-    ).astype(LOW)
 
 
 def normed(value):
@@ -187,6 +158,7 @@
     first_low,
     inner,
     second,
+    context_rows,
     first,
     total,
     before,
@@ -195,7 +167,10 @@
 
     @pl.when(step == 0)
     def start():
-        attention = matmul(context[...], output_weight[...].reshape(1024, 1024))
+        pairs = [context[s, :, p].reshape(128, 128) for s in range(2) for p in range(4)]
+        rows = jnp.concatenate(pairs, 1)
+        context_rows[...] = rows
+        attention = matmul(rows, output_weight[...].reshape(1024, 1024))
         summed = tokens[...].astype(jnp.float32) + (attention + params[0:1])
         residual[...] = summed
         after = normed(summed)[0] * params[4:5] + params[1:2]
@@ -224,7 +199,7 @@
         grid=(PARTS + 1,),
         in_specs=[
             full(128, 1024),
-            full(128, 1024),
+            full(2, 2, 4, 2, 32, 128),
             *weight_specs(this_part, part_before),
             full(8, 1024),
             pl.BlockSpec((1, 1, WIDTH), lambda j: (this_part(j), 0, 0)),
@@ -234,6 +209,7 @@
             full(128, 1024),
             full(128, 1024),
             pl.BlockSpec((128, WIDTH), lambda j: (0, this_part(j))),
+            full(128, 1024),
             full(128, 1024),
         ],
         out_shape=[
@@ -242,6 +218,7 @@
             ROWS_LOW,
             jax.ShapeDtypeStruct((128, 4096), jnp.float32),
             ROWS_F32,
+            ROWS_LOW,
         ],
         scratch_shapes=[
             pltpu.VMEM((128, 1024), jnp.float32),
@@ -263,11 +240,11 @@
     residual,
     inner,
     second,
-    grad_mlp,
     grad_residual,
     grad_attn,
     grad_context,
     sums,
+    grad_mlp,
     grad_second,
     total,
     before,
@@ -299,9 +276,11 @@
         grad_residual[...] = by_value
         rounded = by_value.astype(LOW)
         grad_attn[...] = rounded
-        grad_context[...] = times_transposed(
-            rounded, output_weight[...].reshape(1024, 1024)
-        ).astype(LOW)
+        rows = times_transposed(rounded, output_weight[...].reshape(1024, 1024)).astype(LOW)
+        for s, m, p in ((s, m, p) for s in range(2) for m in range(2) for p in range(4)):
+            piece = rows[64 * m : 64 * m + 64, 128 * (4 * s + p) : 128 * (4 * s + p) + 128]
+            grad_context[s, m, p, 0] = piece
+            grad_context[s, m, p, 1] = piece
         sums[0:1] = by_gain
         sums[2:3] = jnp.sum(rounded.astype(jnp.float32), 0, keepdims=True)
         sums[3:4] = by_shift
@@ -309,7 +288,7 @@
 
 
 def block_back(grad, saved, gathered, params):
-    residual, unused, inner, second = saved
+    residual, first_low, inner, second, context_rows = saved
     return pl.pallas_call(
         backward_kernel,
         grid=(PARTS + 1,),
@@ -321,15 +300,20 @@
             pl.BlockSpec((128, WIDTH), lambda j: (0, part_before(j))),
             full(128, 1024),
         ],
-        out_specs=[full(128, 1024)] * 4 + [full(8, 1024)],
+        out_specs=[
+            full(128, 1024),
+            full(128, 1024),
+            full(2, 2, 4, 2, 64, 128),
+            full(8, 1024),
+        ],
         out_shape=[
-            ROWS_LOW,
             ROWS_F32,
             ROWS_LOW,
-            ROWS_LOW,
+            jax.ShapeDtypeStruct((2, 2, 4, 2, 64, 128), LOW),
             jax.ShapeDtypeStruct((8, 1024), jnp.float32),
         ],
         scratch_shapes=[
+            pltpu.VMEM((128, 1024), LOW),
             pltpu.VMEM((128, 1024), jnp.float32),
             pltpu.VMEM((128, 1024), jnp.float32),
             pltpu.VMEM((128, WIDTH), jnp.float32),
@@ -337,6 +321,113 @@
         compiler_params=BLOCK_PARAMS,
         cost_estimate=BLOCK_COST,
     )(grad, gathered, gathered, gathered, params, residual, inner, second)
+
+
+def grad_tokens_kernel(got, weight, grad_residual, result, rounded, total):
+    step = pl.program_id(0)
+    left = jnp.concatenate([got[0, :, p].reshape(128, 384) for p in range(2)], 1)
+    product = times_transposed(left, weight[...])
+
+    @pl.when(step == 0)
+    def start():
+        total[...] = grad_residual[...] + product
+
+    @pl.when(step > 0)
+    def proceed():
+        total[...] += product
+
+    @pl.when(step == 3)
+    def finish():
+        result[...] = total[...]
+        rounded[...] = total[...].astype(LOW)
+
+
+def grad_tokens(got, weight, grad_residual):
+    return pl.pallas_call(
+        grad_tokens_kernel,
+        grid=(4,),
+        in_specs=[
+            pl.BlockSpec((1, 2, 2, 2, 32, 384), lambda i: (i // 2, 0, i % 2, 0, 0, 0)),
+            pl.BlockSpec((1024, 768), lambda i: (0, i)),
+            full(128, 1024),
+        ],
+        out_specs=[full(128, 1024), full(128, 1024)],
+        out_shape=[ROWS_F32, ROWS_LOW],
+        scratch_shapes=[pltpu.VMEM((128, 1024), jnp.float32)],
+        compiler_params=BLOCK_PARAMS,
+        cost_estimate=pl.CostEstimate(
+            flops=2 * 128 * 3072 * 1024, bytes_accessed=8 * 1024 * 1024, transcendentals=0
+        ),
+    )(got, weight, grad_residual)
+
+
+def attend_back_kernel(
+    core,
+    packed,
+    log_totals,
+    seg_rows,
+    seg_columns,
+    got,
+    result,
+    queries,
+    keys,
+    values,
+    grads,
+    grad_keys,
+    grad_values,
+):
+    step = pl.program_id(0)
+
+    @pl.when(step == 0)
+    def start():
+        queries[...] = packed[:, :HEAD_DIM]
+        keys[...] = packed[:, HEAD_DIM : 2 * HEAD_DIM]
+        values[...] = packed[:, 2 * HEAD_DIM :]
+        pair = got[...].reshape(1024, 128)
+        grads[...] = jnp.where(core[0] == 0, pair[:, :HEAD_DIM], pair[:, HEAD_DIM:])
+        grad_keys[...] = jnp.zeros_like(grad_keys)
+        grad_values[...] = jnp.zeros_like(grad_values)
+
+    rows = pl.ds(pl.multiple_of(step * 256, 256), 256)
+    block_queries = queries[rows]
+    block_grads = grads[rows]
+    scores = times_transposed(block_queries, keys[...]) * SCALE
+    scores = jnp.where(seg_rows[rows] == seg_columns[...], scores, NEGATIVE)
+    soft = jnp.exp(scores - log_totals[rows])
+    grad_soft = times_transposed(block_grads, values[...])
+    row_total = jnp.sum(soft * grad_soft, -1, keepdims=True)
+    grad_scores = (soft * (grad_soft - row_total)).astype(LOW)
+    result[rows, :HEAD_DIM] = (matmul(grad_scores, keys[...]) * SCALE).astype(LOW)
+    grad_keys[...] += transposed_times(grad_scores, block_queries)
+    grad_values[...] += transposed_times(soft.astype(LOW), block_grads)
+
+    @pl.when(step == 3)
+    def finish():
+        result[:, HEAD_DIM : 2 * HEAD_DIM] = (grad_keys[...] * SCALE).astype(LOW)
+        result[:, 2 * HEAD_DIM :] = grad_values[...].astype(LOW)
+
+
+def attend_back(core, packed, log_totals, seg, got, layer):
+    return pl.pallas_call(
+        attend_back_kernel,
+        grid=(4,),
+        in_specs=[
+            pl.BlockSpec(memory_space=pltpu.SMEM),
+            full(1024, 192),
+            full(1024, 1),
+            full(1024, 1),
+            full(1, 1024),
+            pl.BlockSpec((16, 64, 128), lambda i: (layer, 0, 0)),
+        ],
+        out_specs=full(1024, 192),
+        out_shape=jax.ShapeDtypeStruct((1024, 192), LOW),
+        scratch_shapes=[pltpu.VMEM((1024, HEAD_DIM), LOW)] * 4
+        + [pltpu.VMEM((1024, HEAD_DIM), jnp.float32)] * 2,
+        compiler_params=BLOCK_PARAMS,
+        cost_estimate=pl.CostEstimate(
+            flops=10 * 1024 * 1024 * 64, bytes_accessed=2 * 1024 * 1024, transcendentals=1 << 20
+        ),
+    )(core, packed, log_totals, seg[:, None], seg[None, :], got)
 
 
 def with_sums(grad, sums):
@@ -413,15 +504,16 @@
             packed = (matmul(whole, head_weight[layer]) + head_bias[layer]).astype(LOW)
             context, log_totals = attend(packed, seg)
         with jax.named_scope("context_out"):
-            context = as_rows(send_tokens(context, 1))
+            context = send_tokens(context, 1)
         return context, (whole, packed, log_totals)
 
     def attention_back(layer, grad_context, kept):
         whole, packed, log_totals = kept
         with jax.named_scope("grad_context_in"):
-            grad_context = to_head(grad_context, layer)
+            got = exchange(grad_context.reshape(32, 64, 128), ALL)
         with jax.named_scope("attention_back"):
-            grad_packed = attend_back(packed, log_totals, seg, grad_context)
+            core = (shard % 2).astype(jnp.int32).reshape(1)
+            grad_packed = attend_back(core, packed, log_totals, seg, got, layer)
             grad_weight = transposed_times(whole, grad_packed)
             grad_sums = jnp.sum(grad_packed.astype(jnp.float32), 0)
         return grad_packed, grad_weight, grad_sums
@@ -449,7 +541,7 @@
 
     last_grad = cotangent.reshape(128, 1024)
     with jax.named_scope("block_back_1"):
-        unused, grad_residual, unused, grad_context, unused = block_back(
+        grad_residual, unused, grad_context, unused = block_back(
             last_grad, saved, gathered, params
         )
     grad_packed, grad_attend_1, grad_sums_1 = attention_back(1, grad_context, kept_1)
@@ -457,20 +549,24 @@
         part_1 = with_sums(grad_attend_1, grad_sums_1)
         take_1 = lax.ppermute(part_1, "section", [(0, 1)])
     with jax.named_scope("grad_tokens_1"):
-        grad_tokens_1 = grad_residual + times_transposed(as_rows(send_tokens(grad_packed, 3)), whole_attend)
+        grad_tokens_1, rounded = grad_tokens(
+            send_tokens(grad_packed, 3), whole_attend, grad_residual
+        )
     with jax.named_scope("to_previous_section"):
-        arrived = lax.ppermute(grad_tokens_1.astype(LOW), "section", [(1, 0)])
+        arrived = lax.ppermute(rounded, "section", [(1, 0)])
         own_grad = jnp.where(on_first, arrived, last_grad)
+    with jax.named_scope("gather_grad_mlp"):
+        grad_mlp = normed_back(own_grad.astype(jnp.float32), saved[3], params[5:6])[0].astype(LOW)
+        grad_mlp, own_grad = lax.optimization_barrier((grad_mlp, own_grad))
+        grad_mlp_all = lax.all_gather(grad_mlp, "shard", axis=0, tiled=True)
     with jax.named_scope("block_back_0"):
-        grad_mlp, grad_residual, grad_attn, grad_context, norm_sums = block_back(
+        grad_residual, grad_attn, grad_context, norm_sums = block_back(
             own_grad, saved, gathered, params
         )
-    with jax.named_scope("gather_grad_mlp"):
-        grad_mlp_all = lax.all_gather(grad_mlp, "shard", axis=0, tiled=True)
     grad_packed, grad_attend_0, grad_sums_0 = attention_back(0, grad_context, kept_0)
 
     with jax.named_scope("sum_output_grad"):
-        output_grad = transposed_times(own_context, grad_attn).astype(LOW)
+        output_grad = transposed_times(saved[4], grad_attn).astype(LOW)
         output_got = exchange(output_grad.reshape(64, 16, 1024), REST)
     with jax.named_scope("swap_attend_grad"):
         part_0 = with_sums(grad_attend_0, grad_sums_0)
@@ -489,6 +585,10 @@
         )
         vectors = jnp.broadcast_to(vectors[:, None], (16, 4, 16, 128)).reshape(1024, 128)
         vectors = vectors.astype(LOW)
+    with jax.named_scope("sum_attend_grad"):
+        parts = jnp.concatenate([attend_part, vectors], 1)
+        output_got, parts = lax.optimization_barrier((output_got, parts))
+        got = exchange(parts.reshape(64, 16, 512), REST)
     with jax.named_scope("block_weight_grads"):
         expand_part = lax.dynamic_slice(
             gathered, (0, 320 + shard // 4 * 64, shard % 4 * 256), (16, 64, 256)
@@ -513,21 +613,18 @@
         rows = jnp.concatenate(
             [contract_grad.reshape(4, 64, 1024), jnp.broadcast_to(extra, (4, 16, 1024))], 1
         )
-    output_got, attend_part, expand_grad, vectors, rows = lax.optimization_barrier(
-        (output_got, attend_part, expand_grad, vectors, rows)
-    )
-    with jax.named_scope("sum_attend_expand_grads"):
-        parts = jnp.concatenate([attend_part, expand_grad, vectors], 1)
-        got = exchange(parts.reshape(64, 16, 768), REST)
-        got, rows = lax.optimization_barrier((got, rows))
+    with jax.named_scope("sum_expand_grad"):
+        got, expand_grad, rows = lax.optimization_barrier((got, expand_grad, rows))
+        expand_got = exchange(expand_grad.reshape(64, 16, 256), REST)
+        expand_got, rows = lax.optimization_barrier((expand_got, rows))
     with jax.named_scope("sum_contract"):
         got_contract = exchange(rows, "replica").astype(jnp.float32).sum(0)
-    with jax.named_scope("sum_attend_expand_grads"):
+    with jax.named_scope("sum_attend_grad"):
         got_output = output_got.astype(jnp.float32).sum(0).astype(LOW)
         got_attend = got[:, :, :384].astype(jnp.float32).reshape(2, 8, 4, 16, 384).sum((0, 2))
-        got_expand = got[:, :, 384:640].astype(jnp.float32).reshape(16, 4, 16, 256).sum(1)
+        got_expand = expand_got.astype(jnp.float32).reshape(16, 4, 16, 256).sum(1)
         got_expand = got_expand.astype(LOW).transpose(1, 0, 2).reshape(16, 4096)
-        got_vectors = got[:, :7, 640:704].astype(jnp.float32).sum(0)
+        got_vectors = got[:, :7, 384:448].astype(jnp.float32).sum(0)
         got_attend, got_output = lax.optimization_barrier((got_attend.astype(LOW), got_output))
         got_attend = got_attend.reshape(8, 16, 2, 3, 64).transpose(1, 3, 2, 0, 4)
         got_attend = got_attend.reshape(16, 3072)
@@ -536,8 +633,9 @@
         owned = jnp.concatenate([got_attend, got_output, got_expand, *contract_rows], 1)
     with jax.named_scope("grad_tokens_0"):
         late_packed, owned = lax.optimization_barrier((grad_packed, owned))
-        packed_rows = as_rows(send_tokens(late_packed, 3))
-        grad_tokens_0 = grad_residual + times_transposed(packed_rows, whole_attend)
+        grad_tokens_0, unused = grad_tokens(
+            send_tokens(late_packed, 3), whole_attend, grad_residual
+        )
     with jax.named_scope("gather_weight_grads"):
         totals = lax.all_gather(owned, "replica", axis=0, tiled=True)
         contract_total = totals[:, 8192:].reshape(4, 16, 4, 1024).transpose(0, 2, 1, 3)

time: 572 us -> 525 us (0.918)
  blocking collectives: 70 us -> 41.7 us
  matrix products: 50.9 us -> 25.2 us
  Pallas kernels: 50.7 us -> 73.7 us
  local copies, waits for them, and re-layouts: 71.2 us -> 52.1 us
  starting transfers between devices: 72.4 us -> 83.5 us
  other arithmetic: 26.8 us -> 19.8 us
    all_to_all x3 -> x2, blocking collectives: 70 us -> 41.7 us  [exchange(): return lax.all_to_all(value, axes, 0, 0, tiled=True)]
    pallas_call x0 -> x4, Pallas kernels: none -> 22.4 us  [the longest x2 11.3 us: grad_tokens(): pl.pallas_call(grad_tokens_kernel, grid=(4,), in_specs=[pl.BlockSpec((1,...]
    dot_general x7 -> x3, matrix products: 25.2 us -> 6.93 us  [times_transposed(): lax.dot_general(left, right, (((1,), (1,)), ((), ())), preferred_element_...]
    all_gather x1, waiting for transfers between devices: 17.8 us -> 0.02 us  [on_device(): grad_mlp_all = lax.all_gather(grad_mlp, 'shard', axis=0, tiled=True)]
    ppermute x1, waiting for transfers between devices: 6.41 us -> 19.3 us  [on_device(): take_0 = lax.ppermute(part_0, 'section', [(1, 0)])]
    all_to_all x9 -> x11, starting transfers between devices: 57.3 us -> 68.1 us  [exchange(): return lax.all_to_all(value, axes, 0, 0, tiled=True)]
    concatenate x3 -> x1, other arithmetic: 5.88 us -> 0.07 us  [on_device(): parts = jnp.concatenate([attend_part, vectors], 1)]
    dot_general x9 -> x5, matrix products: 14.3 us -> 9.17 us  [transposed_times(): lax.dot_general(left, right, (((0,), (0,)), ((), ())), preferred_element_...]
  transfers between devices with their start and end apart: 24 -> 26, of which waited for: 19 -> 21; matrix products, arithmetic and copies ran while one was open for 20% -> 13% of each run, Pallas kernels for 7% -> 12%
where the time goes in v4:
time: 525 us; the launch traced here: 515 us
  waiting for transfers between devices  204 us (39%)
  starting transfers between devices  83.5 us (16%)
  Pallas kernels  73.7 us (14%)
  local copies, waits for them, and re-layouts  52.1 us (10%)
  blocking collectives  41.7 us (8%)
  matrix products  25.2 us (5%)
  other arithmetic  19.8 us (4%)
  between operations  15.5 us (3%)
    all_to_all x11, waiting for transfers between devices, exchange(): return lax.all_to_all(value, axes, 0, 0, tiled=True)  122 us
    all_to_all x11, starting transfers between devices, exchange(): return lax.all_to_all(value, axes, 0, 0, tiled=True)  68.1 us
    all_to_all x2, blocking collectives, exchange(): return lax.all_to_all(value, axes, 0, 0, tiled=True)  41.7 us
    all_gather x1, waiting for transfers between devices, on_device(): lax.all_gather(quarter, REST, axis=0, tiled=False).reshape(16, 576, 1024)  40.7 us
    pallas_call x2, Pallas kernels, block_back(): pl.pallas_call(backward_kernel, grid=(PARTS + 1,), in_specs=[full(128, 10...  28.3 us
    pallas_call x2, Pallas kernels, block_forward(): pl.pallas_call(forward_kernel, grid=(PARTS + 1,), in_specs=[full(128, 102...  23.1 us
    unnamed x102, local copies, waits for them, and re-layouts  19.9 us
    ppermute x1, waiting for transfers between devices, on_device(): take_0 = lax.ppermute(part_0, 'section', [(1, 0)])  19.3 us
  transfers between devices with their start and end apart: 26, of which 21 were waited for; matrix products, arithmetic and copies ran while one was open for 13% of the time, Pallas kernels for 12%

profile of v4, /device:TPU:1, one launch (start us, length us, event | category | flops | bytes accessed | tf_op | source)
XLA Modules:
  0.0 515.4 jit_solution(5873337984711512336)
XLA Ops:
  18.8 9.6 %all-to-all-start = ((bf16[32,80,192]{2,1,0:T(8,128)(2,1)}), bf16[32,80,192]{2,1,0:T(8,128)(2,1)S(1)}, u32[]{:S(2)}, u32[]{:S(2)}) async-start(bf16[32,80,192]{2,1,0:T(8,128)(2,1)} %bitcast.5), calls=%async_computation | async-start | bytes 2621440 | tf_op jit(solution)/shard_map/head_weights/all_to_all | solution.py:37
  30.0 20.3 %all-to-all-done = bf16[32,80,192]{2,1,0:T(8,128)(2,1)S(1)} async-done(((bf16[32,80,192]{2,1,0:T(8,128)(2,1)}), bf16[32,80,192]{2,1,0:T(8,128)(2,1)S(1)}, u32[]{:S(2)}, u32[]{:S(2)}) %all-to-all-start) | async-done | bytes 983072 | tf_op jit(solution)/shard_map/head_weights/all_to_all | solution.py:37
  51.4 4.7 all-to-all-start.1
  56.6 23.7 %all-to-all-done.1 = bf16[16,32,1024]{2,1,0:T(8,128)(2,1)S(1)} async-done(((bf16[16,32,1024]{2,1,0:T(8,128)(2,1)}), bf16[16,32,1024]{2,1,0:T(8,128)(2,1)S(1)}, u32[]{:S(2)}, u32[]{:S(2)}) %all-to-all-start.1) | async-done | bytes 1048608 | tf_op jit(solution)/shard_map/sequence_tokens/all_to_all | solution.py:37
  98.5 11.4 %all-to-all-done.2 = bf16[32,32,128]{2,1,0:T(8,128)(2,1)S(1)} async-done(((bf16[32,32,128]{2,1,0:T(8,128)(2,1)}), bf16[32,32,128]{2,1,0:T(8,128)(2,1)S(1)}, u32[]{:S(2)}, u32[]{:S(2)}) %all-to-all-start.2) | async-done | bytes 262176 | tf_op jit(solution)/shard_map/context_out/all_to_all | solution.py:37
  109.8 40.7 %all-gather.15.cloned.1.call-done = bf16[9216,1024]{1,0:T(8,128)(2,1)} async-done(((bf16[144,1024]{1,0:T(8,128)(2,1)}), bf16[9216,1024]{1,0:T(8,128)(2,1)}) %all-gather.15.cloned.1.call-update) | async-done | bytes 18874384 | tf_op jit(solution)/shard_map/gather_block_weights/all_gather | solution.py:462
  150.6 12.0 %block_0.1 = (bf16[128,1024]{1,0:T(8,128)(2,1)S(1)}, f32[128,1024]{1,0:T(8,128)}, bf16[128,1024]{1,0:T(8,128)(2,1)}, f32[128,4096]{1,0:T(8,128)}, f32[128,1024]{1,0:T(8,128)}, /*index=5*/bf16[128,1024]{1,0:T(8,128)(2,1)}) custom-call(bf16[128,1024]{1,0:T(8,128)(2,1)S(1)} %bitcast.245, bf16[2,2,4,2,32,128]{5,4,3,2,1,0:T(8,128)(2,1)S(1)} %bitcast.246, ...), custom_call_target="tpu_custom_call" | custom-call | flops 2415919104 | bytes 25165824 | tf_op jit(solution)/shard_map/block_0/pallas_call | solution.py:197
  164.8 5.5 %collective-permute-done.2 = bf16[128,1024]{1,0:T(8,128)(2,1)S(1)} collective-permute-done((bf16[128,1024]{1,0:T(8,128)(2,1)S(1)}, bf16[128,1024]{1,0:T(8,128)(2,1)S(1)}, u32[]{:S(2)}, u32[]{:S(2)}) %collective-permute-start.2) | collective-permute-done | bytes 262176 | tf_op jit(solution)/shard_map/to_next_section/ppermute | solution.py:527
  171.2 25.1 %all_to_all.65 = bf16[16,32,1024]{2,1,0:T(8,128)(2,1)S(1)} all-to-all(bf16[16,32,1024]{2,1,0:T(8,128)(2,1)S(1)} %bitcast.267), channel_id=1, replica_groups=mesh['section'=2,'shard'=16,'replica'=4] {'shard'}, dimensions={0} | all-to-all | bytes 2097152 | tf_op jit(solution)/shard_map/sequence_tokens/all_to_all | solution.py:37
  206.7 16.6 %all_to_all.66 = bf16[32,32,128]{2,1,0:T(8,128)(2,1)S(1)} all-to-all(bf16[32,32,128]{2,1,0:T(8,128)(2,1)S(1)} %bitcast.287), channel_id=1, replica_groups=mesh['section'=2,'shard'=16,'replica'=4] {'section','shard'}, dimensions={0} | all-to-all | bytes 524288 | tf_op jit(solution)/shard_map/context_out/all_to_all | solution.py:37
  223.3 11.1 %block_1.1 = (bf16[128,1024]{1,0:T(8,128)(2,1)}, f32[128,1024]{1,0:T(8,128)S(1)}, bf16[128,1024]{1,0:T(8,128)(2,1)S(1)}, f32[128,4096]{1,0:T(8,128)S(1)}, f32[12...) custom-call(bf16[128,1024]{1,0:T(8,128)(2,1)S(1)} %copy-done.5, ...), custom_call_target="tpu_custom_call" | custom-call | flops 2415919104 | bytes 25165824 | tf_op jit(solution)/shard_map/block_1/pallas_call | solution.py:197
  235.9 14.1 %block_back_1.1 = (f32[128,1024]{1,0:T(8,128)S(1)}, bf16[128,1024]{1,0:T(8,128)(2,1)}, bf16[2,2,4,2,64,128]{5,4,3,2,1,0:T(8,128)(2,1)S(1)}, f32[8,1024]{1,0:T(8,128)}) custom-call(bf16[128,1024]{1,0:T(8,128)(2,1)S(1)} %bitcast.248, bf16[16,576,1024]{2,1,0:T(8,128)(2,1)} %bitcast.256, bf16[16,576,1024]{2,1,0:T(8,128)(2,1)} %bitcast.257, ...), custom_call_target="tpu_custom_call" | custom-call | flops 2415919104 | bytes 25165824 | tf_op jit(solution)/shard_map/block_back_1/pallas_call | solution.py:292
  251.6 6.9 %all-to-all-start.5 = ((bf16[32,64,128]{2,1,0:T(8,128)(2,1)}), bf16[32,64,128]{2,1,0:T(8,128)(2,1)S(1)}, u32[]{:S(2)}, u32[]{:S(2)}) async-start(bf16[32,64,128]{2,1,0:T(8,128)(2,1)} %bitcast.249), calls=%async_computation.5 | async-start | bytes 1048576 | tf_op jit(solution)/shard_map/grad_context_in/all_to_all | solution.py:37
  260.1 9.8 %all-to-all-done.5.got = bf16[32,64,128]{2,1,0:T(8,128)(2,1)S(1)} async-done(((bf16[32,64,128]{2,1,0:T(8,128)(2,1)}), bf16[32,64,128]{2,1,0:T(8,128)(2,1)S(1)}, u32[]{:S(2)}, u32[]{:S(2)}) %all-to-all-start.5) | async-done | bytes 524320 | tf_op jit(solution)/shard_map/grad_context_in/all_to_all | solution.py:37
  273.9 5.5 %attention_back.2 = bf16[1024,192]{1,0:T(8,128)(2,1)S(1)} custom-call(s32[1]{0:T(128)} %bitcast.45.core, bf16[1024,192]{1,0:T(8,128)(2,1)S(1)} %copy-done.25, f32[1024,1]{1,0:T(8,128)S(1)} %copy-done.12, bf16[1024,1]{1,0:T(8,128)(2,1)S(1)} %select_n.386.seg_rows, bf16[1,1024]{1,0:T(2,128)(2,1)S(1)} %select_n.358.seg_columns, bf16[32,64,128]{2,1,0:T(8,128)(2,1)S(1)} %copy-done.10), custom_call_target="tpu_custom_call" | custom-call | flops 671088640 | bytes 2097152 | tf_op jit(solution)/shard_map/attention_back/pallas_call | solution.py:411
  290.7 14.2 %all-to-all-done.6 = bf16[32,32,384]{2,1,0:T(8,128)(2,1)} async-done(((bf16[32,32,384]{2,1,0:T(8,128)(2,1)}), bf16[32,32,384]{2,1,0:T(8,128)(2,1)}, u32[]{:S(2)}, u32[]{:S(2)}) %all-to-all-start.6) | async-done | bytes 786464 | tf_op jit(solution)/shard_map/grad_tokens_1/all_to_all | solution.py:37
  305.9 5.4 %grad_tokens_1.1 = (f32[128,1024]{1,0:T(8,128)S(1)}, bf16[128,1024]{1,0:T(8,128)(2,1)S(1)}) custom-call(bf16[2,2,4,2,32,384]{5,4,3,2,1,0:T(8,128)(2,1)} %bitcast.54.got, bf16[1024,3072]{1,0:T(8,128)(2,1)} %all-gather.7.cloned.1.call-done.weight, f32[128,1024]{1,0:T(8,128)S(1)} %copy-done.14), custom_call_target="tpu_custom_call" | custom-call | flops 805306368 | bytes 8388608 | tf_op jit(solution)/shard_map/grad_tokens_1/pallas_call | solution.py:346
  312.8 8.2 %collective-permute-done.6 = bf16[128,1024]{1,0:T(8,128)(2,1)S(1)} collective-permute-done((bf16[128,1024]{1,0:T(8,128)(2,1)S(1)}, bf16[128,1024]{1,0:T(8,128)(2,1)S(1)}, u32[]{:S(2)}, u32[]{:S(2)}) %collective-permute-start.6) | collective-permute-done | bytes 262176 | tf_op jit(solution)/shard_map/to_previous_section/ppermute | solution.py:556
  328.7 14.2 %block_back_0.1 = (f32[128,1024]{1,0:T(8,128)S(1)}, bf16[128,1024]{1,0:T(8,128)(2,1)S(1)}, bf16[2,2,4,2,64,128]{5,4,3,2,1,0:T(8,128)(2,1)}, f32[8,1024]{1,0:T(8,128)S(1)}) custom-call(bf16[128,1024]{1,0:T(8,128)(2,1)S(1)} %get-tuple-element.48.grad, bf16[16,576,1024]{2,1,0:T(8,128)(2,1)} %bitcast.260, bf16[16,576,1024]{2,1,0:T(8,128)(2,1)} %bitcast.261, ...), custom_call_target="tpu_custom_call" | custom-call | flops 2415919104 | bytes 25165824 | tf_op jit(solution)/shard_map/block_back_0/pallas_call | solution.py:292
  355.6 5.9 %all-to-all-done.7.got = bf16[32,64,128]{2,1,0:T(8,128)(2,1)S(1)} async-done(((bf16[32,64,128]{2,1,0:T(8,128)(2,1)}), bf16[32,64,128]{2,1,0:T(8,128)(2,1)S(1)}, u32[]{:S(2)}, u32[]{:S(2)}) %all-to-all-start.7) | async-done | bytes 524320 | tf_op jit(solution)/shard_map/grad_context_in/all_to_all | solution.py:37
  361.5 8.7 %all-to-all-start.8 = ((bf16[64,16,1024]{2,1,0:T(8,128)(2,1)}), bf16[64,16,1024]{2,1,0:T(8,128)(2,1)}, u32[]{:S(2)}, u32[]{:S(2)}) async-start(bf16[64,16,1024]{2,1,0:T(8,128)(2,1)} %bitcast.263), calls=%async_computation.8 | async-start | bytes 4194304 | tf_op jit(solution)/shard_map/sum_output_grad/all_to_all | solution.py:37
  370.2 5.5 %attention_back.3 = bf16[1024,192]{1,0:T(8,128)(2,1)S(1)} custom-call(s32[1]{0:T(128)} %bitcast.45.core, bf16[1024,192]{1,0:T(8,128)(2,1)S(1)} %copy-done.23, f32[1024,1]{1,0:T(8,128)S(1)} %copy-done.8, bf16[1024,1]{1,0:T(8,128)(2,1)S(1)} %copy-done.21, bf16[1,1024]{1,0:T(2,128)(2,1)S(1)} %select_n.358.seg_columns, bf16[32,64,128]{2,1,0:T(8,128)(2,1)S(1)} %all-to-all-done.7.got), custom_call_target="tpu_custom_call" | custom-call | flops 671088640 | bytes 2097152 | tf_op jit(solution)/shard_map/attention_back/pallas_call | solution.py:411
  378.2 5.0 convolution_add_fusion
  383.4 19.3 %collective-permute-done.8 = bf16[1040,192]{0,1:T(8,128)(2,1)S(1)} collective-permute-done((bf16[1040,192]{0,1:T(8,128)(2,1)S(1)}, bf16[1040,192]{0,1:T(8,128)(2,1)S(1)}, u32[]{:S(2)}, u32[]{:S(2)}) %collective-permute-start.8) | collective-permute-done | bytes 399392 | tf_op jit(solution)/shard_map/swap_attend_grad/ppermute | solution.py:573
  405.4 10.8 %all-to-all-start.9 = ((bf16[64,16,512]{2,1,0:T(8,128)(2,1)}), bf16[64,16,512]{2,1,0:T(8,128)(2,1)S(1)}, u32[]{:S(2)}, u32[]{:S(2)}) async-start(bf16[64,16,512]{2,1,0:T(8,128)(2,1)} %bitcast.62), calls=%async_computation.9 | async-start | bytes 2097152 | tf_op jit(solution)/shard_map/sum_attend_grad/all_to_all | solution.py:37
  419.2 5.4 %fusion.50 = (bf16[256]{0:T(256)(128)(2,1)S(1)}, bf16[2048,256]{1,0:T(8,128)(2,1)S(1)}) fusion(f32[2048,256]{1,0:T(8,128)} %convolution_add_fusion, bf16[2048,1024]{1,0:T(8,128)(2,1)} %all-gather.11.cloned.1.call-done, bf16[1,256,1024]{2,1,0:T(8,128)(2,1)S(1)} %copy-done.34), kind=kOutput, calls=%fused_computation.163 | convolution fusion | flops 1079508736 | bytes 7864832 | tf_op jit(solution)/shard_map/block_weight_grads/dot_general | solution.py:25
  429.1 5.7 %all-to-all-done.9 = bf16[64,16,512]{2,1,0:T(8,128)(2,1)S(1)} async-done(((bf16[64,16,512]{2,1,0:T(8,128)(2,1)}), bf16[64,16,512]{2,1,0:T(8,128)(2,1)S(1)}, u32[]{:S(2)}, u32[]{:S(2)}) %all-to-all-start.9) | async-done | bytes 1048608 | tf_op jit(solution)/shard_map/sum_attend_grad/all_to_all | solution.py:37
  434.8 6.9 %all-to-all-start.10 = ((bf16[64,16,256]{2,1,0:T(8,128)(2,1)}), bf16[64,16,256]{2,1,0:T(8,128)(2,1)}, u32[]{:S(2)}, u32[]{:S(2)}) async-start(bf16[64,16,256]{2,1,0:T(8,128)(2,1)} %bitcast.68), calls=%async_computation.10 | async-start | bytes 1048576 | tf_op jit(solution)/shard_map/sum_expand_grad/all_to_all | solution.py:37
  444.5 10.5 %all-to-all-done.10 = bf16[64,16,256]{2,1,0:T(8,128)(2,1)} async-done(((bf16[64,16,256]{2,1,0:T(8,128)(2,1)}), bf16[64,16,256]{2,1,0:T(8,128)(2,1)}, u32[]{:S(2)}, u32[]{:S(2)}) %all-to-all-start.10) | async-done | bytes 524320 | tf_op jit(solution)/shard_map/sum_expand_grad/all_to_all | solution.py:37
  460.4 7.7 %all-to-all-done.11 = bf16[4,80,1024]{2,1,0:T(8,128)(2,1)S(1)} async-done(((bf16[4,80,1024]{2,1,0:T(8,128)(2,1)}), bf16[4,80,1024]{2,1,0:T(8,128)(2,1)S(1)}, u32[]{:S(2)}, u32[]{:S(2)}) %all-to-all-start.11) | async-done | bytes 655392 | tf_op jit(solution)/shard_map/sum_contract/all_to_all | solution.py:37
  481.6 12.5 %all-to-all-done.12 = bf16[32,32,384]{2,1,0:T(8,128)(2,1)S(1)} async-done(((bf16[32,32,384]{2,1,0:T(8,128)(2,1)}), bf16[32,32,384]{2,1,0:T(8,128)(2,1)S(1)}, u32[]{:S(2)}, u32[]{:S(2)}) %all-to-all-start.12) | async-done | bytes 786464 | tf_op jit(solution)/shard_map/grad_tokens_0/all_to_all | solution.py:37
  494.1 5.9 %grad_tokens_0.1 = (f32[128,1024]{1,0:T(8,128)S(1)}, bf16[128,1024]{1,0:T(8,128)(2,1)}) custom-call(bf16[2,2,4,2,32,384]{5,4,3,2,1,0:T(8,128)(2,1)S(1)} %bitcast.243, bf16[1024,3072]{1,0:T(8,128)(2,1)} %all-gather.7.cloned.1.call-done.weight, f32[128,1024]{1,0:T(8,128)S(1)} %get-tuple-element.65.grad_residual), custom_call_target="tpu_custom_call" | custom-call | flops 805306368 | bytes 8388608 | tf_op jit(solution)/shard_map/grad_tokens_0/pallas_call | solution.py:346
  (317 shorter events, 131.1 us)
Async XLA Ops:
  7.2 143.3 %all-gather.15.cloned.1.call-start = ((), (), s32[]{:S(2)}) async-start(), calls=%async_computation.17 | async-start | bytes 19169280 | tf_op jit(solution)/shard_map/gather_block_weights/all_gather | solution.py:462
  18.8 31.5 %copy-start = (bf16[2,1,64,1024]{3,2,1,0:T(8,128)(2,1)S(1)}, bf16[2,1,64,1024]{3,2,1,0:T(8,128)(2,1)}, u32[]{:S(2)}) copy-start(bf16[2,1,64,1024]{3,2,1,0:T(8,128)(2,1)} %param.10) | copy-start | bytes 786436
  18.8 31.5 %all-to-all-start = ((bf16[32,80,192]{2,1,0:T(8,128)(2,1)}), bf16[32,80,192]{2,1,0:T(8,128)(2,1)S(1)}, u32[]{:S(2)}, u32[]{:S(2)}) async-start(bf16[32,80,192]{2,1,0:T(8,128)(2,1)} %bitcast.5), calls=%async_computation | async-start | bytes 2621440 | tf_op jit(solution)/shard_map/head_weights/all_to_all | solution.py:37
  51.4 28.9 %all-to-all-start.1 = ((bf16[16,32,1024]{2,1,0:T(8,128)(2,1)}), bf16[16,32,1024]{2,1,0:T(8,128)(2,1)S(1)}, u32[]{:S(2)}, u32[]{:S(2)}) async-start(bf16[16,32,1024]{2,1,0:T(8,128)(2,1)} %bitcast.266), calls=%async_computation.1 | async-start | bytes 2097152 | tf_op jit(solution)/shard_map/sequence_tokens/all_to_all | solution.py:37
  80.3 4.3 collective-permute-start
  91.6 1.4 collective-permute-start.1
  93.9 16.0 %all-to-all-start.2 = ((bf16[32,32,128]{2,1,0:T(8,128)(2,1)}), bf16[32,32,128]{2,1,0:T(8,128)(2,1)S(1)}, u32[]{:S(2)}, u32[]{:S(2)}) async-start(bf16[32,32,128]{2,1,0:T(8,128)(2,1)} %bitcast.22), calls=%async_computation.2 | async-start | bytes 524288 | tf_op jit(solution)/shard_map/context_out/all_to_all | solution.py:37
  97.8 207.1 %all-gather.7.cloned.1.call-start = ((), (), s32[]{:S(2)}) async-start(), calls=%async_computation.13 | async-start | bytes 6684672 | tf_op jit(solution)/shard_map/gather_attend_weight/all_gather | solution.py:532
  162.5 215.6 %all-gather.9.cloned.1.call-start = ((), (), s32[]{:S(2)}) async-start(), calls=%async_computation.14 | async-start | bytes 4456448 | tf_op jit(solution)/shard_map/gather_first/all_gather | solution.py:540
  162.6 7.7 %collective-permute-start.2 = (bf16[128,1024]{1,0:T(8,128)(2,1)S(1)}, bf16[128,1024]{1,0:T(8,128)(2,1)S(1)}, u32[]{:S(2)}, u32[]{:S(2)}) collective-permute-start(bf16[128,1024]{1,0:T(8,128)(2,1)S(1)} %get-tuple-element.39), channel_id=1, source_target_pairs={{0,64},{1,65},{2,66},{3,67},{4,68},{5,69},{6,70},{7,71},{8,72},{9,... | collective-permute-start | bytes 786440 | tf_op jit(solution)/shard_map/to_next_section/ppermute | solution.py:527
  196.3 2.7 collective-permute-start.3
  205.0 18.3 %copy-start.5 = (bf16[128,1024]{1,0:T(8,128)(2,1)S(1)}, bf16[128,1024]{1,0:T(8,128)(2,1)}, u32[]{:S(2)}) copy-start(bf16[128,1024]{1,0:T(8,128)(2,1)} %get-tuple-element.117.tokens) | copy-start | bytes 786436
  205.1 1.4 collective-permute-start.4
  235.9 14.1 %copy-start.1 = (f32[128,1024]{1,0:T(8,128)}, f32[128,1024]{1,0:T(8,128)S(1)}, u32[]{:S(2)}) copy-start(f32[128,1024]{1,0:T(8,128)S(1)} %get-tuple-element.42.residual) | copy-start | bytes 1572868
  251.6 18.3 %all-to-all-start.5 = ((bf16[32,64,128]{2,1,0:T(8,128)(2,1)}), bf16[32,64,128]{2,1,0:T(8,128)(2,1)S(1)}, u32[]{:S(2)}, u32[]{:S(2)}) async-start(bf16[32,64,128]{2,1,0:T(8,128)(2,1)} %bitcast.249), calls=%async_computation.5 | async-start | bytes 1048576 | tf_op jit(solution)/shard_map/grad_context_in/all_to_all | solution.py:37
  259.0 22.1 %copy-start.20 = (bf16[1024,1]{1,0:T(8,128)(2,1)}, bf16[1024,1]{1,0:T(8,128)(2,1)S(1)}, u32[]{:S(2)}) copy-start(bf16[1024,1]{1,0:T(8,128)(2,1)S(1)} %select_n.386.seg_rows) | copy-start | bytes 6148
  279.4 1.6 collective-permute-start.5
  285.9 19.0 %all-to-all-start.6 = ((bf16[32,32,384]{2,1,0:T(8,128)(2,1)}), bf16[32,32,384]{2,1,0:T(8,128)(2,1)}, u32[]{:S(2)}, u32[]{:S(2)}) async-start(bf16[32,32,384]{2,1,0:T(8,128)(2,1)} %bitcast.269), calls=%async_computation.6 | async-start | bytes 1572864 | tf_op jit(solution)/shard_map/grad_tokens_1/all_to_all | solution.py:37
  290.4 125.9 %all-gather.11.cloned.1.call-start = ((), (), s32[]{:S(2)}) async-start(), calls=%async_computation.15 | async-start | bytes 4456448 | tf_op jit(solution)/shard_map/gather_grad_mlp/all_gather | solution.py:561
  305.9 15.1 %copy-start.4 = (bf16[2,1,64,1024]{3,2,1,0:T(8,128)(2,1)S(1)}, bf16[2,1,64,1024]{3,2,1,0:T(8,128)(2,1)}, u32[]{:S(2)}) copy-start(bf16[2,1,64,1024]{3,2,1,0:T(8,128)(2,1)} %param.12) | copy-start | bytes 786436
  311.3 9.7 %collective-permute-start.6 = (bf16[128,1024]{1,0:T(8,128)(2,1)S(1)}, bf16[128,1024]{1,0:T(8,128)(2,1)S(1)}, u32[]{:S(2)}, u32[]{:S(2)}) collective-permute-start(bf16[128,1024]{1,0:T(8,128)(2,1)S(1)} %get-tuple-element.47), channel_id=1, source_target_pairs={{64,0},{65,1},{66,2},{67,3},{68,4},{69,5},{70,6},{71,7},{72,8},{73... | collective-permute-start | bytes 786440 | tf_op jit(solution)/shard_map/to_previous_section/ppermute | solution.py:556
  343.7 17.9 %all-to-all-start.7 = ((bf16[32,64,128]{2,1,0:T(8,128)(2,1)}), bf16[32,64,128]{2,1,0:T(8,128)(2,1)S(1)}, u32[]{:S(2)}, u32[]{:S(2)}) async-start(bf16[32,64,128]{2,1,0:T(8,128)(2,1)} %bitcast.57), calls=%async_computation.7 | async-start | bytes 1048576 | tf_op jit(solution)/shard_map/grad_context_in/all_to_all | solution.py:37
  349.3 27.4 %collective-permute-start.7 = (bf16[1040,192]{0,1:T(8,128)(2,1)S(1)}, bf16[1040,192]{0,1:T(8,128)(2,1)}, u32[]{:S(2)}, u32[]{:S(2)}) collective-permute-start(bf16[1040,192]{0,1:T(8,128)(2,1)S(1)} %fusion.25), channel_id=1, source_target_pairs={{0,64},{1,65},{2,66},{3,67},{4,68},{5,69},{6,70},{7,71},{8,72},{9,... | collective-permute-start | bytes 1198088 | tf_op jit(solution)/shard_map/swap_attend_grad/ppermute | solution.py:550
  361.5 42.6 %all-to-all-start.8 = ((bf16[64,16,1024]{2,1,0:T(8,128)(2,1)}), bf16[64,16,1024]{2,1,0:T(8,128)(2,1)}, u32[]{:S(2)}, u32[]{:S(2)}) async-start(bf16[64,16,1024]{2,1,0:T(8,128)(2,1)} %bitcast.263), calls=%async_computation.8 | async-start | bytes 4194304 | tf_op jit(solution)/shard_map/sum_output_grad/all_to_all | solution.py:37
  376.8 25.9 %collective-permute-start.8 = (bf16[1040,192]{0,1:T(8,128)(2,1)S(1)}, bf16[1040,192]{0,1:T(8,128)(2,1)S(1)}, u32[]{:S(2)}, u32[]{:S(2)}) collective-permute-start(bf16[1040,192]{0,1:T(8,128)(2,1)S(1)} %get-tuple-element.130), channel_id=1, source_target_pairs={{64,0},{65,1},{66,2},{67,3},{68,4},{69,5},{70,6},{71,7},{72,8},{73... | collective-permute-start | bytes 1198088 | tf_op jit(solution)/shard_map/swap_attend_grad/ppermute | solution.py:573
  378.2 24.6 %copy-start.30 = (bf16[1024,192]{0,1:T(8,128)(2,1)S(1)}, bf16[1024,192]{0,1:T(8,128)(2,1)}, u32[]{:S(2)}) copy-start(bf16[1024,192]{0,1:T(8,128)(2,1)} %convolution_convert_fusion.3) | copy-start | bytes 1179652
  405.4 29.4 %all-to-all-start.9 = ((bf16[64,16,512]{2,1,0:T(8,128)(2,1)}), bf16[64,16,512]{2,1,0:T(8,128)(2,1)S(1)}, u32[]{:S(2)}, u32[]{:S(2)}) async-start(bf16[64,16,512]{2,1,0:T(8,128)(2,1)} %bitcast.62), calls=%async_computation.9 | async-start | bytes 2097152 | tf_op jit(solution)/shard_map/sum_attend_grad/all_to_all | solution.py:37
  434.8 20.2 %all-to-all-start.10 = ((bf16[64,16,256]{2,1,0:T(8,128)(2,1)}), bf16[64,16,256]{2,1,0:T(8,128)(2,1)}, u32[]{:S(2)}, u32[]{:S(2)}) async-start(bf16[64,16,256]{2,1,0:T(8,128)(2,1)} %bitcast.68), calls=%async_computation.10 | async-start | bytes 1048576 | tf_op jit(solution)/shard_map/sum_expand_grad/all_to_all | solution.py:37
  454.9 13.2 %all-to-all-start.11 = ((bf16[4,80,1024]{2,1,0:T(8,128)(2,1)}), bf16[4,80,1024]{2,1,0:T(8,128)(2,1)S(1)}, u32[]{:S(2)}, u32[]{:S(2)}) async-start(bf16[4,80,1024]{2,1,0:T(8,128)(2,1)} %pad_maximum_fusion.3), calls=%async_computation.11 | async-start | bytes 1310720 | tf_op jit(solution)/shard_map/sum_contract/all_to_all | solution.py:37
  458.4 42.5 %all-gather.13.cloned.1.call-start = ((), (), s32[]{:S(2)}) async-start(), calls=%async_computation.16 | async-start | bytes 1966080 | tf_op jit(solution)/shard_map/gather_weight_grads/all_gather | solution.py:640
  470.8 3.4 collective-permute-start.9
  475.8 18.3 %all-to-all-start.12 = ((bf16[32,32,384]{2,1,0:T(8,128)(2,1)}), bf16[32,32,384]{2,1,0:T(8,128)(2,1)S(1)}, u32[]{:S(2)}, u32[]{:S(2)}) async-start(bf16[32,32,384]{2,1,0:T(8,128)(2,1)} %bitcast.77), calls=%async_computation.12 | async-start | bytes 1572864 | tf_op jit(solution)/shard_map/grad_tokens_0/all_to_all | solution.py:37
  (36 other events, 153.4 us)
Sparse Core Ops, SparseCore 0:
  13.9 136.6 all-gather.14
  162.7 72.7 all-gather.6
  237.9 54.6 all-gather.8
  322.4 77.0 all-gather.10
  470.8 23.7 all-gather.12

commit v5 on v4

--- a/solution.py
+++ b/solution.py
@@ -326,7 +326,7 @@
 def grad_tokens_kernel(got, weight, grad_residual, result, rounded, total):
     step = pl.program_id(0)
     left = jnp.concatenate([got[0, :, p].reshape(128, 384) for p in range(2)], 1)
-    product = times_transposed(left, weight[...])
+    product = times_transposed(left, weight[...].reshape(1024, 768))
 
     @pl.when(step == 0)
     def start():
@@ -342,13 +342,13 @@
         rounded[...] = total[...].astype(LOW)
 
 
-def grad_tokens(got, weight, grad_residual):
+def grad_tokens(layer, got, weight, grad_residual):
     return pl.pallas_call(
         grad_tokens_kernel,
         grid=(4,),
         in_specs=[
             pl.BlockSpec((1, 2, 2, 2, 32, 384), lambda i: (i // 2, 0, i % 2, 0, 0, 0)),
-            pl.BlockSpec((1024, 768), lambda i: (0, i)),
+            pl.BlockSpec((16, 64, 768), lambda i: (0, layer, i)),
             full(128, 1024),
         ],
         out_specs=[full(128, 1024), full(128, 1024)],
@@ -508,15 +508,17 @@
         return context, (whole, packed, log_totals)
 
     def attention_back(layer, grad_context, kept):
-        whole, packed, log_totals = kept
+        unused, packed, log_totals = kept
         with jax.named_scope("grad_context_in"):
             got = exchange(grad_context.reshape(32, 64, 128), ALL)
         with jax.named_scope("attention_back"):
             core = (shard % 2).astype(jnp.int32).reshape(1)
             grad_packed = attend_back(core, packed, log_totals, seg, got, layer)
-            grad_weight = transposed_times(whole, grad_packed)
-            grad_sums = jnp.sum(grad_packed.astype(jnp.float32), 0)
-        return grad_packed, grad_weight, grad_sums
+        return grad_packed
+
+    def attend_part(tokens, grad_packed):
+        grad_weight = transposed_times(tokens, grad_packed)
+        return with_sums(grad_weight, jnp.sum(grad_packed.astype(jnp.float32), 0))
 
     context_0, kept_0 = attention(0, inputs)
     tokens_0 = inputs.reshape(128, 1024)
@@ -527,9 +529,17 @@
             on_first, output, lax.ppermute(output, "section", [(0, 1)])
         )
     with jax.named_scope("gather_attend_weight"):
-        by_pair = attend_weight[0].reshape(64, 3, 8, 128).transpose(0, 2, 1, 3).reshape(64, 3072)
-        late_weight, unused = lax.optimization_barrier((by_pair, output))
-        whole_attend = lax.all_gather(late_weight, "shard", axis=0, tiled=True)
+        own_pairs = attend_weight[0].reshape(64, 3, 8, 128).transpose(0, 2, 1, 3).reshape(64, 3072)
+        other_pairs = lax.ppermute(own_pairs, "section", [(0, 1), (1, 0)])
+        both_pairs = jnp.concatenate(
+            [
+                jnp.where(on_first, own_pairs, other_pairs),
+                jnp.where(on_first, other_pairs, own_pairs),
+            ],
+            0,
+        )
+        both_pairs, output = lax.optimization_barrier((both_pairs, output))
+        whole_attend = lax.all_gather(both_pairs, "shard", axis=0, tiled=False)
     context_1, kept_1 = attention(1, tokens_1.reshape(2, 64, 1024))
     own_tokens = jnp.where(on_first, tokens_0, tokens_1)
     own_context = jnp.where(on_first, context_0, context_1)
@@ -544,17 +554,15 @@
         grad_residual, unused, grad_context, unused = block_back(
             last_grad, saved, gathered, params
         )
-    grad_packed, grad_attend_1, grad_sums_1 = attention_back(1, grad_context, kept_1)
-    with jax.named_scope("swap_attend_grad"):
-        part_1 = with_sums(grad_attend_1, grad_sums_1)
-        take_1 = lax.ppermute(part_1, "section", [(0, 1)])
+    with jax.named_scope("residual_to_previous_section"):
+        arrived = lax.ppermute(grad_residual, "section", [(1, 0)])
+        grad_residual = jnp.where(on_first, arrived, grad_residual)
+    grad_packed_1 = attention_back(1, grad_context, kept_1)
     with jax.named_scope("grad_tokens_1"):
         grad_tokens_1, rounded = grad_tokens(
-            send_tokens(grad_packed, 3), whole_attend, grad_residual
-        )
-    with jax.named_scope("to_previous_section"):
-        arrived = lax.ppermute(rounded, "section", [(1, 0)])
-        own_grad = jnp.where(on_first, arrived, last_grad)
+            1, send_tokens(grad_packed_1, 3), whole_attend, grad_residual
+        )
+    own_grad = jnp.where(on_first, rounded, last_grad)
     with jax.named_scope("gather_grad_mlp"):
         grad_mlp = normed_back(own_grad.astype(jnp.float32), saved[3], params[5:6])[0].astype(LOW)
         grad_mlp, own_grad = lax.optimization_barrier((grad_mlp, own_grad))
@@ -563,17 +571,28 @@
         grad_residual, grad_attn, grad_context, norm_sums = block_back(
             own_grad, saved, gathered, params
         )
-    grad_packed, grad_attend_0, grad_sums_0 = attention_back(0, grad_context, kept_0)
+    late_tokens, late_packed, late_gathered, grad_context = lax.optimization_barrier(
+        (kept_1[0], grad_packed_1, gathered, grad_context)
+    )
+    with jax.named_scope("swap_attend_grad"):
+        part_1 = attend_part(late_tokens, late_packed)
+        take_1 = lax.ppermute(part_1, "section", [(0, 1)])
+    grad_packed = attention_back(0, grad_context, kept_0)
 
     with jax.named_scope("sum_output_grad"):
-        output_grad = transposed_times(saved[4], grad_attn).astype(LOW)
-        output_got = exchange(output_grad.reshape(64, 16, 1024), REST)
+        output_grad = transposed_times(saved[4], grad_attn)
+        halves = [output_grad[:, :512], output_grad[:, 512:]]
+        core = shard % 2
+        keep = jnp.where(core == 0, halves[0], halves[1])
+        give = jnp.where(core == 0, halves[1], halves[0]).astype(LOW)
+        output_grad = (keep + swap_cores(give).astype(jnp.float32)).astype(LOW)
+        output_got = exchange(output_grad.reshape(64, 16, 512), REST)
     with jax.named_scope("swap_attend_grad"):
-        part_0 = with_sums(grad_attend_0, grad_sums_0)
+        part_0 = attend_part(kept_0[0], grad_packed)
         take_0 = lax.ppermute(part_0, "section", [(1, 0)])
         lower = jnp.where(on_first, part_0, take_1)
         upper = jnp.where(on_first, take_0, part_1)
-        attend_part = jnp.concatenate([lower[:1024], upper[:1024]], 1)
+        attend_grad = jnp.concatenate([lower[:1024], upper[:1024]], 1)
         sums = jnp.stack([lower[1024], upper[1024]]).reshape(2, 3, HEAD_DIM)
         norm_rows = norm_sums[:5].reshape(5, 16, 64).transpose(1, 0, 2)
         mine = jnp.arange(8) == shard % 8
@@ -585,13 +604,9 @@
         )
         vectors = jnp.broadcast_to(vectors[:, None], (16, 4, 16, 128)).reshape(1024, 128)
         vectors = vectors.astype(LOW)
-    with jax.named_scope("sum_attend_grad"):
-        parts = jnp.concatenate([attend_part, vectors], 1)
-        output_got, parts = lax.optimization_barrier((output_got, parts))
-        got = exchange(parts.reshape(64, 16, 512), REST)
     with jax.named_scope("block_weight_grads"):
         expand_part = lax.dynamic_slice(
-            gathered, (0, 320 + shard // 4 * 64, shard % 4 * 256), (16, 64, 256)
+            late_gathered, (0, 320 + shard // 4 * 64, shard % 4 * 256), (16, 64, 256)
         ).reshape(1024, 256)
         hidden_part = lax.dynamic_slice_in_dim(own_hidden.reshape(4096), shard * 256, 256, 0)
         inner = matmul(first_all, expand_part) + hidden_part
@@ -613,18 +628,20 @@
         rows = jnp.concatenate(
             [contract_grad.reshape(4, 64, 1024), jnp.broadcast_to(extra, (4, 16, 1024))], 1
         )
-    with jax.named_scope("sum_expand_grad"):
-        got, expand_grad, rows = lax.optimization_barrier((got, expand_grad, rows))
-        expand_got = exchange(expand_grad.reshape(64, 16, 256), REST)
-        expand_got, rows = lax.optimization_barrier((expand_got, rows))
+    with jax.named_scope("sum_attend_expand_grads"):
+        parts = jnp.concatenate([attend_grad, expand_grad, vectors], 1)
+        parts, rows, output_got = lax.optimization_barrier((parts, rows, output_got))
+        got = exchange(parts.reshape(64, 16, 768), REST)
+        got, rows = lax.optimization_barrier((got, rows))
     with jax.named_scope("sum_contract"):
         got_contract = exchange(rows, "replica").astype(jnp.float32).sum(0)
     with jax.named_scope("sum_attend_grad"):
-        got_output = output_got.astype(jnp.float32).sum(0).astype(LOW)
+        got_output = output_got.astype(jnp.float32).reshape(8, 2, 4, 16, 512).sum((0, 2))
+        got_output = jnp.concatenate([got_output[0], got_output[1]], 1).astype(LOW)
         got_attend = got[:, :, :384].astype(jnp.float32).reshape(2, 8, 4, 16, 384).sum((0, 2))
-        got_expand = expand_got.astype(jnp.float32).reshape(16, 4, 16, 256).sum(1)
+        got_expand = got[:, :, 384:640].astype(jnp.float32).reshape(16, 4, 16, 256).sum(1)
         got_expand = got_expand.astype(LOW).transpose(1, 0, 2).reshape(16, 4096)
-        got_vectors = got[:, :7, 384:448].astype(jnp.float32).sum(0)
+        got_vectors = got[:, :7, 640:704].astype(jnp.float32).sum(0)
         got_attend, got_output = lax.optimization_barrier((got_attend.astype(LOW), got_output))
         got_attend = got_attend.reshape(8, 16, 2, 3, 64).transpose(1, 3, 2, 0, 4)
         got_attend = got_attend.reshape(16, 3072)
@@ -634,7 +651,7 @@
     with jax.named_scope("grad_tokens_0"):
         late_packed, owned = lax.optimization_barrier((grad_packed, owned))
         grad_tokens_0, unused = grad_tokens(
-            send_tokens(late_packed, 3), whole_attend, grad_residual
+            0, send_tokens(late_packed, 3), whole_attend, grad_residual
         )
     with jax.named_scope("gather_weight_grads"):
         totals = lax.all_gather(owned, "replica", axis=0, tiled=True)

time: 525 us -> 544 us (1.036)
  starting transfers between devices: 83.5 us -> 99.1 us
  waiting for transfers between devices: 204 us -> 190 us
  other arithmetic: 19.8 us -> 27.8 us
    ppermute x1, waiting for transfers between devices: 19.3 us -> 5.79 us  [on_device(): take_0 = lax.ppermute(part_0, 'section', [(1, 0)])]
    all_to_all x11 -> x10, starting transfers between devices: 68.1 us -> 81.6 us  [exchange(): return lax.all_to_all(value, axes, 0, 0, tiled=True)]
    ppermute x1, waiting for transfers between devices: 0.01 us -> 5.67 us  [on_device(): take_1 = lax.ppermute(part_1, 'section', [(0, 1)])]
    unnamed x102 -> x114, local copies, waits for them, and re-layouts: 19.9 us -> 23.3 us
    all_to_all x11 -> x10, waiting for transfers between devices: 122 us -> 119 us  [exchange(): return lax.all_to_all(value, axes, 0, 0, tiled=True)]
  transfers between devices with their start and end apart: 26 -> 27, of which waited for: 21 -> 20; matrix products, arithmetic and copies ran while one was open for 13% -> 14% of each run, Pallas kernels for 12% -> 11%
where the time goes in v5:
time: 544 us; the launch traced here: 534 us
  waiting for transfers between devices  190 us (35%)
  starting transfers between devices  99.1 us (18%)
  Pallas kernels  72.9 us (13%)
  local copies, waits for them, and re-layouts  56.5 us (10%)
  blocking collectives  45.6 us (8%)
  other arithmetic  27.8 us (5%)
  matrix products  27.2 us (5%)
  between operations  15.5 us (3%)
    all_to_all x10, waiting for transfers between devices, exchange(): return lax.all_to_all(value, axes, 0, 0, tiled=True)  119 us
    all_to_all x10, starting transfers between devices, exchange(): return lax.all_to_all(value, axes, 0, 0, tiled=True)  81.6 us
    all_to_all x2, blocking collectives, exchange(): return lax.all_to_all(value, axes, 0, 0, tiled=True)  45.6 us
    all_gather x1, waiting for transfers between devices, on_device(): lax.all_gather(quarter, REST, axis=0, tiled=False).reshape(16, 576, 1024)  40.1 us
    pallas_call x2, Pallas kernels, block_back(): pl.pallas_call(backward_kernel, grid=(PARTS + 1,), in_specs=[full(128, 10...  27.5 us
    unnamed x114, local copies, waits for them, and re-layouts  23.3 us
    pallas_call x2, Pallas kernels, block_forward(): pl.pallas_call(forward_kernel, grid=(PARTS + 1,), in_specs=[full(128, 102...  23 us
    pallas_call x2, Pallas kernels, grad_tokens(): pl.pallas_call(grad_tokens_kernel, grid=(4,), in_specs=[pl.BlockSpec((1,...  11.4 us
  transfers between devices with their start and end apart: 27, of which 20 were waited for; matrix products, arithmetic and copies ran while one was open for 14% of the time, Pallas kernels for 11%

profile of v5, /device:TPU:1, one launch (start us, length us, event | category | flops | bytes accessed | tf_op | source)
XLA Modules:
  0.0 534.4 jit_solution(3988387549684699750)
XLA Ops:
  21.5 8.6 %all-to-all-start = ((bf16[32,80,192]{2,1,0:T(8,128)(2,1)}), bf16[32,80,192]{2,1,0:T(8,128)(2,1)S(1)}, u32[]{:S(2)}, u32[]{:S(2)}) async-start(bf16[32,80,192]{2,1,0:T(8,128)(2,1)} %bitcast.5), calls=%async_computation | async-start | bytes 2621440 | tf_op jit(solution)/shard_map/head_weights/all_to_all | solution.py:37
  31.4 19.0 %all-to-all-done = bf16[32,80,192]{2,1,0:T(8,128)(2,1)S(1)} async-done(((bf16[32,80,192]{2,1,0:T(8,128)(2,1)}), bf16[32,80,192]{2,1,0:T(8,128)(2,1)S(1)}, u32[]{:S(2)}, u32[]{:S(2)}) %all-to-all-start) | async-done | bytes 983072 | tf_op jit(solution)/shard_map/head_weights/all_to_all | solution.py:37
  51.4 5.5 %all-to-all-start.1 = ((bf16[16,32,1024]{2,1,0:T(8,128)(2,1)}), bf16[16,32,1024]{2,1,0:T(8,128)(2,1)S(1)}, u32[]{:S(2)}, u32[]{:S(2)}) async-start(bf16[16,32,1024]{2,1,0:T(8,128)(2,1)} %bitcast.273), calls=%async_computation.1 | async-start | bytes 2097152 | tf_op jit(solution)/shard_map/sequence_tokens/all_to_all | solution.py:37
  57.3 24.4 %all-to-all-done.1 = bf16[16,32,1024]{2,1,0:T(8,128)(2,1)S(1)} async-done(((bf16[16,32,1024]{2,1,0:T(8,128)(2,1)}), bf16[16,32,1024]{2,1,0:T(8,128)(2,1)S(1)}, u32[]{:S(2)}, u32[]{:S(2)}) %all-to-all-start.1) | async-done | bytes 1048608 | tf_op jit(solution)/shard_map/sequence_tokens/all_to_all | solution.py:37
  99.8 11.4 %all-to-all-done.2 = bf16[32,32,128]{2,1,0:T(8,128)(2,1)S(1)} async-done(((bf16[32,32,128]{2,1,0:T(8,128)(2,1)}), bf16[32,32,128]{2,1,0:T(8,128)(2,1)S(1)}, u32[]{:S(2)}, u32[]{:S(2)}) %all-to-all-start.2) | async-done | bytes 262176 | tf_op jit(solution)/shard_map/context_out/all_to_all | solution.py:37
  111.2 40.1 %all-gather.14.cloned.1.call-done = bf16[9216,1024]{1,0:T(8,128)(2,1)} async-done(((bf16[144,1024]{1,0:T(8,128)(2,1)}), bf16[9216,1024]{1,0:T(8,128)(2,1)}) %all-gather.14.cloned.1.call-update) | async-done | bytes 18874384 | tf_op jit(solution)/shard_map/gather_block_weights/all_gather | solution.py:462
  151.3 12.0 %block_0.1 = (bf16[128,1024]{1,0:T(8,128)(2,1)S(1)}, f32[128,1024]{1,0:T(8,128)}, bf16[128,1024]{1,0:T(8,128)(2,1)}, f32[128,4096]{1,0:T(8,128)}, f32[128,1024]{1,0:T(8,128)}, /*index=5*/bf16[128,1024]{1,0:T(8,128)(2,1)}) custom-call(bf16[128,1024]{1,0:T(8,128)(2,1)S(1)} %bitcast.250, bf16[2,2,4,2,32,128]{5,4,3,2,1,0:T(8,128)(2,1)S(1)} %bitcast.251, ...), custom_call_target="tpu_custom_call" | custom-call | flops 2415919104 | bytes 25165824 | tf_op jit(solution)/shard_map/block_0/pallas_call | solution.py:197
  165.6 5.5 %collective-permute-done.2 = bf16[128,1024]{1,0:T(8,128)(2,1)S(1)} collective-permute-done((bf16[128,1024]{1,0:T(8,128)(2,1)S(1)}, bf16[128,1024]{1,0:T(8,128)(2,1)S(1)}, u32[]{:S(2)}, u32[]{:S(2)}) %collective-permute-start.2) | collective-permute-done | bytes 262176 | tf_op jit(solution)/shard_map/to_next_section/ppermute | solution.py:529
  171.9 27.4 %all_to_all.60 = bf16[16,32,1024]{2,1,0:T(8,128)(2,1)S(1)} all-to-all(bf16[16,32,1024]{2,1,0:T(8,128)(2,1)S(1)} %bitcast.274), channel_id=1, replica_groups=mesh['section'=2,'shard'=16,'replica'=4] {'shard'}, dimensions={0} | all-to-all | bytes 2097152 | tf_op jit(solution)/shard_map/sequence_tokens/all_to_all | solution.py:37
  209.8 18.2 %all_to_all.61 = bf16[32,32,128]{2,1,0:T(8,128)(2,1)S(1)} all-to-all(bf16[32,32,128]{2,1,0:T(8,128)(2,1)S(1)} %bitcast.296), channel_id=1, replica_groups=mesh['section'=2,'shard'=16,'replica'=4] {'section','shard'}, dimensions={0} | all-to-all | bytes 524288 | tf_op jit(solution)/shard_map/context_out/all_to_all | solution.py:37
  228.0 11.0 %block_1.1 = (bf16[128,1024]{1,0:T(8,128)(2,1)}, f32[128,1024]{1,0:T(8,128)S(1)}, bf16[128,1024]{1,0:T(8,128)(2,1)S(1)}, f32[128,4096]{1,0:T(8,128)S(1)}, f32[12...) custom-call(bf16[128,1024]{1,0:T(8,128)(2,1)S(1)} %copy-done.6, ...), custom_call_target="tpu_custom_call" | custom-call | flops 2415919104 | bytes 25165824 | tf_op jit(solution)/shard_map/block_1/pallas_call | solution.py:197
  240.5 14.1 %block_back_1.1 = (f32[128,1024]{1,0:T(8,128)S(1)}, bf16[128,1024]{1,0:T(8,128)(2,1)}, bf16[2,2,4,2,64,128]{5,4,3,2,1,0:T(8,128)(2,1)S(1)}, f32[8,1024]{1,0:T(8,128)}) custom-call(bf16[128,1024]{1,0:T(8,128)(2,1)S(1)} %bitcast.253, bf16[16,576,1024]{2,1,0:T(8,128)(2,1)} %bitcast.262, bf16[16,576,1024]{2,1,0:T(8,128)(2,1)} %bitcast.263, ...), custom_call_target="tpu_custom_call" | custom-call | flops 2415919104 | bytes 25165824 | tf_op jit(solution)/shard_map/block_back_1/pallas_call | solution.py:292
  256.2 25.9 %all-to-all-start.5 = ((bf16[32,64,128]{2,1,0:T(8,128)(2,1)}), bf16[32,64,128]{2,1,0:T(8,128)(2,1)S(1)}, u32[]{:S(2)}, u32[]{:S(2)}) async-start(bf16[32,64,128]{2,1,0:T(8,128)(2,1)} %bitcast.255), calls=%async_computation.5 | async-start | bytes 1048576 | tf_op jit(solution)/shard_map/grad_context_in/all_to_all | solution.py:37
  283.7 9.8 %all-to-all-done.5.got = bf16[32,64,128]{2,1,0:T(8,128)(2,1)S(1)} async-done(((bf16[32,64,128]{2,1,0:T(8,128)(2,1)}), bf16[32,64,128]{2,1,0:T(8,128)(2,1)S(1)}, u32[]{:S(2)}, u32[]{:S(2)}) %all-to-all-start.5) | async-done | bytes 524320 | tf_op jit(solution)/shard_map/grad_context_in/all_to_all | solution.py:37
  297.4 5.5 %attention_back.2 = bf16[1024,192]{1,0:T(8,128)(2,1)S(1)} custom-call(s32[1]{0:T(128)} %bitcast.45.core, bf16[1024,192]{1,0:T(8,128)(2,1)S(1)} %copy-done.28, f32[1024,1]{1,0:T(8,128)S(1)} %copy-done.15, bf16[1024,1]{1,0:T(8,128)(2,1)S(1)} %select_n.423.seg_rows, bf16[1,1024]{1,0:T(2,128)(2,1)S(1)} %select_n.388.seg_columns, bf16[32,64,128]{2,1,0:T(8,128)(2,1)S(1)} %copy-done.13), custom_call_target="tpu_custom_call" | custom-call | flops 671088640 | bytes 2097152 | tf_op jit(solution)/shard_map/attention_back/pallas_call | solution.py:411
  311.5 6.0 %all-to-all-start.6 = ((bf16[32,32,384]{2,1,0:T(8,128)(2,1)}), bf16[32,32,384]{2,1,0:T(8,128)(2,1)}, u32[]{:S(2)}, u32[]{:S(2)}) async-start(bf16[32,32,384]{2,1,0:T(8,128)(2,1)} %bitcast.278), calls=%async_computation.6 | async-start | bytes 1572864 | tf_op jit(solution)/shard_map/grad_tokens_1/all_to_all | solution.py:37
  317.8 5.4 %collective-permute-done.7 = f32[128,1024]{1,0:T(8,128)} collective-permute-done((f32[128,1024]{1,0:T(8,128)}, f32[128,1024]{1,0:T(8,128)}, u32[]{:S(2)}, u32[]{:S(2)}) %collective-permute-start.7) | collective-permute-done | bytes 524320 | tf_op jit(solution)/shard_map/residual_to_previous_section/ppermute | solution.py:558
  325.2 8.3 %all-to-all-done.6 = bf16[32,32,384]{2,1,0:T(8,128)(2,1)} async-done(((bf16[32,32,384]{2,1,0:T(8,128)(2,1)}), bf16[32,32,384]{2,1,0:T(8,128)(2,1)}, u32[]{:S(2)}, u32[]{:S(2)}) %all-to-all-start.6) | async-done | bytes 786464 | tf_op jit(solution)/shard_map/grad_tokens_1/all_to_all | solution.py:37
  334.5 5.4 %grad_tokens_1.1 = (f32[128,1024]{1,0:T(8,128)S(1)}, bf16[128,1024]{1,0:T(8,128)(2,1)S(1)}) custom-call(bf16[2,2,4,2,32,384]{5,4,3,2,1,0:T(8,128)(2,1)} %bitcast.54.got, bf16[16,128,3072]{2,1,0:T(8,128)(2,1)} %bitcast.269, f32[128,1024]{1,0:T(8,128)S(1)} %copy-done.3), custom_call_target="tpu_custom_call" | custom-call | flops 805306368 | bytes 8388608 | tf_op jit(solution)/shard_map/grad_tokens_1/pallas_call | solution.py:346
  344.1 13.4 %block_back_0.1 = (f32[128,1024]{1,0:T(8,128)S(1)}, bf16[128,1024]{1,0:T(8,128)(2,1)S(1)}, bf16[2,2,4,2,64,128]{5,4,3,2,1,0:T(8,128)(2,1)S(1)}, f32[8,1024]{1,0:T(8,128)S(1)}) custom-call(bf16[128,1024]{1,0:T(8,128)(2,1)S(1)} %get-tuple-element.50.grad, bf16[16,576,1024]{2,1,0:T(8,128)(2,1)} %bitcast.265, bf16[16,576,1024]{2,1,0:T(8,128)(2,1)} %bitcast.266, ...), custom_call_target="tpu_custom_call" | custom-call | flops 2415919104 | bytes 25165824 | tf_op jit(solution)/shard_map/block_back_0/pallas_call | solution.py:292
  359.8 5.4 %all-to-all-start.7 = ((bf16[32,64,128]{2,1,0:T(8,128)(2,1)}), bf16[32,64,128]{2,1,0:T(8,128)(2,1)S(1)}, u32[]{:S(2)}, u32[]{:S(2)}) async-start(bf16[32,64,128]{2,1,0:T(8,128)(2,1)} %bitcast.254), calls=%async_computation.7 | async-start | bytes 1048576 | tf_op jit(solution)/shard_map/grad_context_in/all_to_all | solution.py:37
  376.7 5.5 %attention_back.3 = bf16[1024,192]{1,0:T(8,128)(2,1)S(1)} custom-call(s32[1]{0:T(128)} %bitcast.45.core, bf16[1024,192]{1,0:T(8,128)(2,1)S(1)} %copy-done.26, f32[1024,1]{1,0:T(8,128)S(1)} %copy-done.10, bf16[1024,1]{1,0:T(8,128)(2,1)S(1)} %copy-done.24, bf16[1,1024]{1,0:T(2,128)(2,1)S(1)} %select_n.388.seg_columns, bf16[32,64,128]{2,1,0:T(8,128)(2,1)S(1)} %all-to-all-done.7.got), custom_call_target="tpu_custom_call" | custom-call | flops 671088640 | bytes 2097152 | tf_op jit(solution)/shard_map/attention_back/pallas_call | solution.py:411
  384.7 5.7 %collective-permute-done.8 = bf16[1040,192]{0,1:T(8,128)(2,1)S(1)} collective-permute-done((bf16[1040,192]{0,1:T(8,128)(2,1)}, bf16[1040,192]{0,1:T(8,128)(2,1)S(1)}, u32[]{:S(2)}, u32[]{:S(2)}) %collective-permute-start.8) | collective-permute-done | bytes 399392 | tf_op jit(solution)/shard_map/swap_attend_grad/ppermute | solution.py:579
  391.8 4.9 convolution_add_fusion
  396.9 5.8 %collective-permute-done.9 = bf16[1040,192]{0,1:T(8,128)(2,1)S(1)} collective-permute-done((bf16[1040,192]{0,1:T(8,128)(2,1)S(1)}, bf16[1040,192]{0,1:T(8,128)(2,1)S(1)}, u32[]{:S(2)}, u32[]{:S(2)}) %collective-permute-start.9) | collective-permute-done | bytes 399392 | tf_op jit(solution)/shard_map/swap_attend_grad/ppermute | solution.py:592
  409.1 10.5 %all-to-all-start.8 = ((bf16[64,16,512]{2,1,0:T(8,128)(2,1)}), bf16[64,16,512]{2,1,0:T(8,128)(2,1)S(1)}, u32[]{:S(2)}, u32[]{:S(2)}) async-start(bf16[64,16,512]{2,1,0:T(8,128)(2,1)} %bitcast.65), calls=%async_computation.8 | async-start | bytes 2097152 | tf_op jit(solution)/shard_map/sum_output_grad/all_to_all | solution.py:37
  419.6 6.2 %fusion.50 = (bf16[256]{0:T(256)(128)(2,1)S(1)}, bf16[2048,256]{1,0:T(8,128)(2,1)}) fusion(f32[2048,256]{1,0:T(8,128)} %convolution_add_fusion, bf16[2048,1024]{1,0:T(8,128)(2,1)} %all-gather.10.cloned.1.call-done, bf16[1,256,1024]{2,1,0:T(8,128)(2,1)S(1)} %copy-done.40), kind=kOutput, calls=%fused_computation.171 | convolution fusion | flops 1079508736 | bytes 7864832 | tf_op jit(solution)/shard_map/block_weight_grads/dot_general | solution.py:25
  439.7 7.7 %all-to-all-start.9 = ((bf16[64,16,768]{2,1,0:T(8,128)(2,1)}), bf16[64,16,768]{2,1,0:T(8,128)(2,1)S(1)}, u32[]{:S(2)}, u32[]{:S(2)}) async-start(bf16[64,16,768]{2,1,0:T(8,128)(2,1)} %bitcast.66), calls=%async_computation.9 | async-start | bytes 3145728 | tf_op jit(solution)/shard_map/sum_attend_expand_grads/all_to_all | solution.py:37
  448.8 22.3 %all-to-all-done.9 = bf16[64,16,768]{2,1,0:T(8,128)(2,1)S(1)} async-done(((bf16[64,16,768]{2,1,0:T(8,128)(2,1)}), bf16[64,16,768]{2,1,0:T(8,128)(2,1)S(1)}, u32[]{:S(2)}, u32[]{:S(2)}) %all-to-all-start.9) | async-done | bytes 1572896 | tf_op jit(solution)/shard_map/sum_attend_expand_grads/all_to_all | solution.py:37
  476.3 8.1 %all-to-all-done.10 = bf16[4,80,1024]{2,1,0:T(8,128)(2,1)S(1)} async-done(((bf16[4,80,1024]{2,1,0:T(8,128)(2,1)}), bf16[4,80,1024]{2,1,0:T(8,128)(2,1)S(1)}, u32[]{:S(2)}, u32[]{:S(2)}) %all-to-all-start.10) | async-done | bytes 655392 | tf_op jit(solution)/shard_map/sum_contract/all_to_all | solution.py:37
  500.7 12.4 %all-to-all-done.11 = bf16[32,32,384]{2,1,0:T(8,128)(2,1)S(1)} async-done(((bf16[32,32,384]{2,1,0:T(8,128)(2,1)}), bf16[32,32,384]{2,1,0:T(8,128)(2,1)S(1)}, u32[]{:S(2)}, u32[]{:S(2)}) %all-to-all-start.11) | async-done | bytes 786464 | tf_op jit(solution)/shard_map/grad_tokens_0/all_to_all | solution.py:37
  513.1 6.0 %grad_tokens_0.1 = (f32[128,1024]{1,0:T(8,128)S(1)}, bf16[128,1024]{1,0:T(8,128)(2,1)}) custom-call(bf16[2,2,4,2,32,384]{5,4,3,2,1,0:T(8,128)(2,1)S(1)} %bitcast.248, bf16[16,128,3072]{2,1,0:T(8,128)(2,1)} %bitcast.270, f32[128,1024]{1,0:T(8,128)S(1)} %copy-done.17), custom_call_target="tpu_custom_call" | custom-call | flops 805306368 | bytes 8388608 | tf_op jit(solution)/shard_map/grad_tokens_0/pallas_call | solution.py:346
  (338 shorter events, 141.8 us)
Async XLA Ops:
  7.2 144.1 %all-gather.14.cloned.1.call-start = ((), (), s32[]{:S(2)}) async-start(), calls=%async_computation.15 | async-start | bytes 19169280 | tf_op jit(solution)/shard_map/gather_block_weights/all_gather | solution.py:462
  14.4 16.0 %collective-permute-start.6 = (bf16[64,3072]{1,0:T(8,128)(2,1)S(1)}, bf16[64,3072]{1,0:T(8,128)(2,1)S(1)}, u32[]{:S(2)}, u32[]{:S(2)}) collective-permute-start(bf16[64,3072]{1,0:T(8,128)(2,1)S(1)} %reshape.434), channel_id=1, source_target_pairs={{0,64},{64,0},{1,65},{65,1},{2,66},{66,2},{3,67},{67,3},{4,68},{68... | collective-permute-start | bytes 1179656 | tf_op jit(solution)/shard_map/gather_attend_weight/ppermute | solution.py:533
  21.5 28.8 %all-to-all-start = ((bf16[32,80,192]{2,1,0:T(8,128)(2,1)}), bf16[32,80,192]{2,1,0:T(8,128)(2,1)S(1)}, u32[]{:S(2)}, u32[]{:S(2)}) async-start(bf16[32,80,192]{2,1,0:T(8,128)(2,1)} %bitcast.5), calls=%async_computation | async-start | bytes 2621440 | tf_op jit(solution)/shard_map/head_weights/all_to_all | solution.py:37
  30.1 20.2 %copy-start = (bf16[2,1,64,1024]{3,2,1,0:T(8,128)(2,1)S(1)}, bf16[2,1,64,1024]{3,2,1,0:T(8,128)(2,1)}, u32[]{:S(2)}) copy-start(bf16[2,1,64,1024]{3,2,1,0:T(8,128)(2,1)} %param.10) | copy-start | bytes 786436
  51.4 30.2 %all-to-all-start.1 = ((bf16[16,32,1024]{2,1,0:T(8,128)(2,1)}), bf16[16,32,1024]{2,1,0:T(8,128)(2,1)S(1)}, u32[]{:S(2)}, u32[]{:S(2)}) async-start(bf16[16,32,1024]{2,1,0:T(8,128)(2,1)} %bitcast.273), calls=%async_computation.1 | async-start | bytes 2097152 | tf_op jit(solution)/shard_map/sequence_tokens/all_to_all | solution.py:37
  81.6 4.2 collective-permute-start
  92.9 1.4 collective-permute-start.1
  95.2 16.0 %all-to-all-start.2 = ((bf16[32,32,128]{2,1,0:T(8,128)(2,1)}), bf16[32,32,128]{2,1,0:T(8,128)(2,1)S(1)}, u32[]{:S(2)}, u32[]{:S(2)}) async-start(bf16[32,32,128]{2,1,0:T(8,128)(2,1)} %bitcast.22), calls=%async_computation.2 | async-start | bytes 524288 | tf_op jit(solution)/shard_map/context_out/all_to_all | solution.py:37
  99.1 234.4 %all-gather.16.cloned.1.call-start = ((), (), s32[]{:S(2)}) async-start(), calls=%async_computation.16 | async-start | bytes 13369344 | tf_op jit(solution)/shard_map/gather_attend_weight/all_gather | solution.py:542
  163.3 228.6 %all-gather.8.cloned.1.call-start = ((), (), s32[]{:S(2)}) async-start(), calls=%async_computation.12 | async-start | bytes 4456448 | tf_op jit(solution)/shard_map/gather_first/all_gather | solution.py:550
  163.3 7.7 %collective-permute-start.2 = (bf16[128,1024]{1,0:T(8,128)(2,1)S(1)}, bf16[128,1024]{1,0:T(8,128)(2,1)S(1)}, u32[]{:S(2)}, u32[]{:S(2)}) collective-permute-start(bf16[128,1024]{1,0:T(8,128)(2,1)S(1)} %get-tuple-element.41), channel_id=1, source_target_pairs={{0,64},{1,65},{2,66},{3,67},{4,68},{5,69},{6,70},{7,71},{8,72},{9,... | collective-permute-start | bytes 786440 | tf_op jit(solution)/shard_map/to_next_section/ppermute | solution.py:529
  199.3 2.7 collective-permute-start.3
  207.9 20.1 %copy-start.6 = (bf16[128,1024]{1,0:T(8,128)(2,1)S(1)}, bf16[128,1024]{1,0:T(8,128)(2,1)}, u32[]{:S(2)}) copy-start(bf16[128,1024]{1,0:T(8,128)(2,1)} %get-tuple-element.121.tokens) | copy-start | bytes 786436
  208.0 1.6 collective-permute-start.4
  240.5 14.2 %copy-start.1 = (f32[128,1024]{1,0:T(8,128)}, f32[128,1024]{1,0:T(8,128)S(1)}, u32[]{:S(2)}) copy-start(f32[128,1024]{1,0:T(8,128)S(1)} %get-tuple-element.43.residual) | copy-start | bytes 1572868
  256.2 37.3 %all-to-all-start.5 = ((bf16[32,64,128]{2,1,0:T(8,128)(2,1)}), bf16[32,64,128]{2,1,0:T(8,128)(2,1)S(1)}, u32[]{:S(2)}, u32[]{:S(2)}) async-start(bf16[32,64,128]{2,1,0:T(8,128)(2,1)} %bitcast.255), calls=%async_computation.5 | async-start | bytes 1048576 | tf_op jit(solution)/shard_map/grad_context_in/all_to_all | solution.py:37
  282.6 21.6 %copy-start.23 = (bf16[1024,1]{1,0:T(8,128)(2,1)}, bf16[1024,1]{1,0:T(8,128)(2,1)S(1)}, u32[]{:S(2)}) copy-start(bf16[1024,1]{1,0:T(8,128)(2,1)S(1)} %select_n.423.seg_rows) | copy-start | bytes 6148
  303.7 1.9 collective-permute-start.5
  304.3 19.0 %collective-permute-start.7 = (f32[128,1024]{1,0:T(8,128)}, f32[128,1024]{1,0:T(8,128)}, u32[]{:S(2)}, u32[]{:S(2)}) collective-permute-start(f32[128,1024]{1,0:T(8,128)} %copy-done.9), channel_id=1, source_target_pairs={{64,0},{65,1},{66,2},{67,3},{68,4},{69,5},{70,6},{71,7},{72,8},{73... | collective-permute-start | bytes 1572872 | tf_op jit(solution)/shard_map/residual_to_previous_section/ppermute | solution.py:558
  311.5 22.0 %all-to-all-start.6 = ((bf16[32,32,384]{2,1,0:T(8,128)(2,1)}), bf16[32,32,384]{2,1,0:T(8,128)(2,1)}, u32[]{:S(2)}, u32[]{:S(2)}) async-start(bf16[32,32,384]{2,1,0:T(8,128)(2,1)} %bitcast.278), calls=%async_computation.6 | async-start | bytes 1572864 | tf_op jit(solution)/shard_map/grad_tokens_1/all_to_all | solution.py:37
  317.5 102.0 %all-gather.10.cloned.1.call-start = ((), (), s32[]{:S(2)}) async-start(), calls=%async_computation.13 | async-start | bytes 4456448 | tf_op jit(solution)/shard_map/gather_grad_mlp/all_gather | solution.py:569
  359.8 16.9 %all-to-all-start.7 = ((bf16[32,64,128]{2,1,0:T(8,128)(2,1)}), bf16[32,64,128]{2,1,0:T(8,128)(2,1)S(1)}, u32[]{:S(2)}, u32[]{:S(2)}) async-start(bf16[32,64,128]{2,1,0:T(8,128)(2,1)} %bitcast.254), calls=%async_computation.7 | async-start | bytes 1048576 | tf_op jit(solution)/shard_map/grad_context_in/all_to_all | solution.py:37
  368.6 21.7 %collective-permute-start.8 = (bf16[1040,192]{0,1:T(8,128)(2,1)}, bf16[1040,192]{0,1:T(8,128)(2,1)S(1)}, u32[]{:S(2)}, u32[]{:S(2)}) collective-permute-start(bf16[1040,192]{0,1:T(8,128)(2,1)} %fusion.25), channel_id=1, source_target_pairs={{0,64},{1,65},{2,66},{3,67},{4,68},{5,69},{6,70},{7,71},{8,72},{9,... | collective-permute-start | bytes 1198088 | tf_op jit(solution)/shard_map/swap_attend_grad/ppermute | solution.py:579
  373.9 31.0 %collective-permute-start.10 = (bf16[1024,512]{1,0:T(8,128)(2,1)}, bf16[1024,512]{1,0:T(8,128)(2,1)}, u32[]{:S(2)}, u32[]{:S(2)}) collective-permute-start(bf16[1024,512]{1,0:T(8,128)(2,1)} %select_convert_fusion), channel_id=1, source_target_pairs={{0,4},{4,0},{8,12},{12,8},{16,20},{20,16},{24,28},{28,24},{32,36},... | collective-permute-start | bytes 3145736 | tf_op jit(solution)/shard_map/sum_output_grad/ppermute | solution.py:41
  390.5 12.2 %collective-permute-start.9 = (bf16[1040,192]{0,1:T(8,128)(2,1)S(1)}, bf16[1040,192]{0,1:T(8,128)(2,1)S(1)}, u32[]{:S(2)}, u32[]{:S(2)}) collective-permute-start(bf16[1040,192]{0,1:T(8,128)(2,1)S(1)} %get-tuple-element.136), channel_id=1, source_target_pairs={{64,0},{65,1},{66,2},{67,3},{68,4},{69,5},{70,6},{71,7},{72,8},{73... | collective-permute-start | bytes 1198088 | tf_op jit(solution)/shard_map/swap_attend_grad/ppermute | solution.py:592
  409.1 29.0 %all-to-all-start.8 = ((bf16[64,16,512]{2,1,0:T(8,128)(2,1)}), bf16[64,16,512]{2,1,0:T(8,128)(2,1)S(1)}, u32[]{:S(2)}, u32[]{:S(2)}) async-start(bf16[64,16,512]{2,1,0:T(8,128)(2,1)} %bitcast.65), calls=%async_computation.8 | async-start | bytes 2097152 | tf_op jit(solution)/shard_map/sum_output_grad/all_to_all | solution.py:37
  439.7 31.4 %all-to-all-start.9 = ((bf16[64,16,768]{2,1,0:T(8,128)(2,1)}), bf16[64,16,768]{2,1,0:T(8,128)(2,1)S(1)}, u32[]{:S(2)}, u32[]{:S(2)}) async-start(bf16[64,16,768]{2,1,0:T(8,128)(2,1)} %bitcast.66), calls=%async_computation.9 | async-start | bytes 3145728 | tf_op jit(solution)/shard_map/sum_attend_expand_grads/all_to_all | solution.py:37
  471.9 12.5 %all-to-all-start.10 = ((bf16[4,80,1024]{2,1,0:T(8,128)(2,1)}), bf16[4,80,1024]{2,1,0:T(8,128)(2,1)S(1)}, u32[]{:S(2)}, u32[]{:S(2)}) async-start(bf16[4,80,1024]{2,1,0:T(8,128)(2,1)} %pad_maximum_fusion.4), calls=%async_computation.10 | async-start | bytes 1310720 | tf_op jit(solution)/shard_map/sum_contract/all_to_all | solution.py:37
  475.4 44.5 %all-gather.12.cloned.1.call-start = ((), (), s32[]{:S(2)}) async-start(), calls=%async_computation.14 | async-start | bytes 1966080 | tf_op jit(solution)/shard_map/gather_weight_grads/all_gather | solution.py:657
  487.1 4.1 collective-permute-start.11
  492.0 21.1 %copy-start.17 = (f32[128,1024]{1,0:T(8,128)S(1)}, f32[128,1024]{1,0:T(8,128)}, u32[]{:S(2)}) copy-start(f32[128,1024]{1,0:T(8,128)} %copy-done.16) | copy-start | bytes 1572868
  494.2 18.9 %all-to-all-start.11 = ((bf16[32,32,384]{2,1,0:T(8,128)(2,1)}), bf16[32,32,384]{2,1,0:T(8,128)(2,1)S(1)}, u32[]{:S(2)}, u32[]{:S(2)}) async-start(bf16[32,32,384]{2,1,0:T(8,128)(2,1)} %bitcast.277), calls=%async_computation.11 | async-start | bytes 1572864 | tf_op jit(solution)/shard_map/grad_tokens_0/all_to_all | solution.py:37
  (43 other events, 151.2 us)
Sparse Core Ops, SparseCore 0:
  13.9 137.3 all-gather.13
  163.4 100.0 all-gather.15
  266.0 56.4 all-gather.7
  341.9 63.4 all-gather.9
  487.2 25.3 all-gather.11

commit v6 on v5

--- a/solution.py
+++ b/solution.py
@@ -326,7 +326,7 @@
 def grad_tokens_kernel(got, weight, grad_residual, result, rounded, total):
     step = pl.program_id(0)
     left = jnp.concatenate([got[0, :, p].reshape(128, 384) for p in range(2)], 1)
-    product = times_transposed(left, weight[...].reshape(1024, 768))
+    product = times_transposed(left, weight[...])
 
     @pl.when(step == 0)
     def start():
@@ -342,13 +342,13 @@
         rounded[...] = total[...].astype(LOW)
 
 
-def grad_tokens(layer, got, weight, grad_residual):
+def grad_tokens(got, weight, grad_residual):
     return pl.pallas_call(
         grad_tokens_kernel,
         grid=(4,),
         in_specs=[
             pl.BlockSpec((1, 2, 2, 2, 32, 384), lambda i: (i // 2, 0, i % 2, 0, 0, 0)),
-            pl.BlockSpec((16, 64, 768), lambda i: (0, layer, i)),
+            pl.BlockSpec((1024, 768), lambda i: (0, i)),
             full(128, 1024),
         ],
         out_specs=[full(128, 1024), full(128, 1024)],
@@ -507,14 +507,15 @@
             context = send_tokens(context, 1)
         return context, (whole, packed, log_totals)
 
-    def attention_back(layer, grad_context, kept):
+    def attention_back(layer, grad_context, kept, beside):
         unused, packed, log_totals = kept
         with jax.named_scope("grad_context_in"):
             got = exchange(grad_context.reshape(32, 64, 128), ALL)
+            got, beside = lax.optimization_barrier((got, beside))
         with jax.named_scope("attention_back"):
             core = (shard % 2).astype(jnp.int32).reshape(1)
             grad_packed = attend_back(core, packed, log_totals, seg, got, layer)
-        return grad_packed
+        return grad_packed, beside
 
     def attend_part(tokens, grad_packed):
         grad_weight = transposed_times(tokens, grad_packed)
@@ -531,15 +532,8 @@
     with jax.named_scope("gather_attend_weight"):
         own_pairs = attend_weight[0].reshape(64, 3, 8, 128).transpose(0, 2, 1, 3).reshape(64, 3072)
         other_pairs = lax.ppermute(own_pairs, "section", [(0, 1), (1, 0)])
-        both_pairs = jnp.concatenate(
-            [
-                jnp.where(on_first, own_pairs, other_pairs),
-                jnp.where(on_first, other_pairs, own_pairs),
-            ],
-            0,
-        )
-        both_pairs, output = lax.optimization_barrier((both_pairs, output))
-        whole_attend = lax.all_gather(both_pairs, "shard", axis=0, tiled=False)
+        other_pairs, output = lax.optimization_barrier((other_pairs, output))
+        other_attend = lax.all_gather(other_pairs, "shard", axis=0, tiled=True)
     context_1, kept_1 = attention(1, tokens_1.reshape(2, 64, 1024))
     own_tokens = jnp.where(on_first, tokens_0, tokens_1)
     own_context = jnp.where(on_first, context_0, context_1)
@@ -554,14 +548,12 @@
         grad_residual, unused, grad_context, unused = block_back(
             last_grad, saved, gathered, params
         )
-    with jax.named_scope("residual_to_previous_section"):
-        arrived = lax.ppermute(grad_residual, "section", [(1, 0)])
-        grad_residual = jnp.where(on_first, arrived, grad_residual)
-    grad_packed_1 = attention_back(1, grad_context, kept_1)
+    with jax.named_scope("residual_to_other_section"):
+        arrived_1 = lax.ppermute(grad_residual, "section", [(1, 0)])
+    grad_packed_1, arrived_1 = attention_back(1, grad_context, kept_1, arrived_1)
     with jax.named_scope("grad_tokens_1"):
-        grad_tokens_1, rounded = grad_tokens(
-            1, send_tokens(grad_packed_1, 3), whole_attend, grad_residual
-        )
+        result_1, rounded = grad_tokens(send_tokens(grad_packed_1, 3), other_attend, arrived_1)
+        grad_tokens_1 = lax.ppermute(result_1, "section", [(0, 1)])
     own_grad = jnp.where(on_first, rounded, last_grad)
     with jax.named_scope("gather_grad_mlp"):
         grad_mlp = normed_back(own_grad.astype(jnp.float32), saved[3], params[5:6])[0].astype(LOW)
@@ -571,14 +563,14 @@
         grad_residual, grad_attn, grad_context, norm_sums = block_back(
             own_grad, saved, gathered, params
         )
+    with jax.named_scope("residual_to_other_section"):
+        arrived_0 = lax.ppermute(grad_residual, "section", [(0, 1)])
     late_tokens, late_packed, late_gathered, grad_context = lax.optimization_barrier(
         (kept_1[0], grad_packed_1, gathered, grad_context)
     )
     with jax.named_scope("swap_attend_grad"):
         part_1 = attend_part(late_tokens, late_packed)
         take_1 = lax.ppermute(part_1, "section", [(0, 1)])
-    grad_packed = attention_back(0, grad_context, kept_0)
-
     with jax.named_scope("sum_output_grad"):
         output_grad = transposed_times(saved[4], grad_attn)
         halves = [output_grad[:, :512], output_grad[:, 512:]]
@@ -586,6 +578,9 @@
         keep = jnp.where(core == 0, halves[0], halves[1])
         give = jnp.where(core == 0, halves[1], halves[0]).astype(LOW)
         output_grad = (keep + swap_cores(give).astype(jnp.float32)).astype(LOW)
+    grad_packed, output_grad = attention_back(0, grad_context, kept_0, output_grad)
+
+    with jax.named_scope("sum_output_grad"):
         output_got = exchange(output_grad.reshape(64, 16, 512), REST)
     with jax.named_scope("swap_attend_grad"):
         part_0 = attend_part(kept_0[0], grad_packed)
@@ -604,6 +599,10 @@
         )
         vectors = jnp.broadcast_to(vectors[:, None], (16, 4, 16, 128)).reshape(1024, 128)
         vectors = vectors.astype(LOW)
+    with jax.named_scope("sum_attend_grad"):
+        parts = jnp.concatenate([attend_grad, vectors], 1)
+        output_got, parts = lax.optimization_barrier((output_got, parts))
+        got = exchange(parts.reshape(64, 16, 512), REST)
     with jax.named_scope("block_weight_grads"):
         expand_part = lax.dynamic_slice(
             late_gathered, (0, 320 + shard // 4 * 64, shard % 4 * 256), (16, 64, 256)
@@ -628,20 +627,19 @@
         rows = jnp.concatenate(
             [contract_grad.reshape(4, 64, 1024), jnp.broadcast_to(extra, (4, 16, 1024))], 1
         )
-    with jax.named_scope("sum_attend_expand_grads"):
-        parts = jnp.concatenate([attend_grad, expand_grad, vectors], 1)
-        parts, rows, output_got = lax.optimization_barrier((parts, rows, output_got))
-        got = exchange(parts.reshape(64, 16, 768), REST)
-        got, rows = lax.optimization_barrier((got, rows))
+    with jax.named_scope("sum_expand_grad"):
+        got, expand_grad, rows = lax.optimization_barrier((got, expand_grad, rows))
+        expand_got = exchange(expand_grad.reshape(64, 16, 256), REST)
+        expand_got, rows = lax.optimization_barrier((expand_got, rows))
     with jax.named_scope("sum_contract"):
         got_contract = exchange(rows, "replica").astype(jnp.float32).sum(0)
     with jax.named_scope("sum_attend_grad"):
         got_output = output_got.astype(jnp.float32).reshape(8, 2, 4, 16, 512).sum((0, 2))
         got_output = jnp.concatenate([got_output[0], got_output[1]], 1).astype(LOW)
         got_attend = got[:, :, :384].astype(jnp.float32).reshape(2, 8, 4, 16, 384).sum((0, 2))
-        got_expand = got[:, :, 384:640].astype(jnp.float32).reshape(16, 4, 16, 256).sum(1)
+        got_expand = expand_got.astype(jnp.float32).reshape(16, 4, 16, 256).sum(1)
         got_expand = got_expand.astype(LOW).transpose(1, 0, 2).reshape(16, 4096)
-        got_vectors = got[:, :7, 640:704].astype(jnp.float32).sum(0)
+        got_vectors = got[:, :7, 384:448].astype(jnp.float32).sum(0)
         got_attend, got_output = lax.optimization_barrier((got_attend.astype(LOW), got_output))
         got_attend = got_attend.reshape(8, 16, 2, 3, 64).transpose(1, 3, 2, 0, 4)
         got_attend = got_attend.reshape(16, 3072)
@@ -650,9 +648,8 @@
         owned = jnp.concatenate([got_attend, got_output, got_expand, *contract_rows], 1)
     with jax.named_scope("grad_tokens_0"):
         late_packed, owned = lax.optimization_barrier((grad_packed, owned))
-        grad_tokens_0, unused = grad_tokens(
-            0, send_tokens(late_packed, 3), whole_attend, grad_residual
-        )
+        result_0, unused = grad_tokens(send_tokens(late_packed, 3), other_attend, arrived_0)
+        grad_tokens_0 = lax.ppermute(result_0, "section", [(1, 0)])
     with jax.named_scope("gather_weight_grads"):
         totals = lax.all_gather(owned, "replica", axis=0, tiled=True)
         contract_total = totals[:, 8192:].reshape(4, 16, 4, 1024).transpose(0, 2, 1, 3)

time: 544 us -> 540 us (level)
  waiting for transfers between devices: 190 us -> 202 us
  local copies, waits for them, and re-layouts: 56.5 us -> 48.6 us
    ppermute x1 -> x4, waiting for transfers between devices: 5.43 us -> 24.5 us  [the longest x1 14.5 us: on_device(): arrived_0 = lax.ppermute(grad_residual, 'section', [(0, 1)])]
    all_to_all x10 -> x11, starting transfers between devices: 81.6 us -> 70.4 us  [exchange(): return lax.all_to_all(value, axes, 0, 0, tiled=True)]
    ppermute x1 -> x4, starting transfers between devices: 1.29 us -> 7.98 us  [the longest x1 3.33 us: on_device(): arrived_0 = lax.ppermute(grad_residual, 'section', [(0, 1)])]
    unnamed x114 -> x96, local copies, waits for them, and re-layouts: 23.3 us -> 17.2 us
    ppermute x1, waiting for transfers between devices: 5.79 us -> 0.01 us  [on_device(): take_0 = lax.ppermute(part_0, 'section', [(1, 0)])]
    all_to_all x10 -> x11, waiting for transfers between devices: 119 us -> 117 us  [exchange(): return lax.all_to_all(value, axes, 0, 0, tiled=True)]
  transfers between devices with their start and end apart: 27 -> 31, of which waited for: 20 -> 21; matrix products, arithmetic and copies ran while one was open for 14% -> 14% of each run, Pallas kernels for 11% -> 14%
where the time goes in v6:
time: 540 us; the launch traced here: 529 us
  waiting for transfers between devices  202 us (37%)
  starting transfers between devices  95.4 us (18%)
  Pallas kernels  73.1 us (14%)
  local copies, waits for them, and re-layouts  48.6 us (9%)
  blocking collectives  41.7 us (8%)
  matrix products  28 us (5%)
  other arithmetic  25 us (5%)
  between operations  15.5 us (3%)
    all_to_all x11, waiting for transfers between devices, exchange(): return lax.all_to_all(value, axes, 0, 0, tiled=True)  117 us
    all_to_all x11, starting transfers between devices, exchange(): return lax.all_to_all(value, axes, 0, 0, tiled=True)  70.4 us
    all_to_all x2, blocking collectives, exchange(): return lax.all_to_all(value, axes, 0, 0, tiled=True)  41.7 us
    all_gather x1, waiting for transfers between devices, on_device(): lax.all_gather(quarter, REST, axis=0, tiled=False).reshape(16, 576, 1024)  40.7 us
    pallas_call x2, Pallas kernels, block_back(): pl.pallas_call(backward_kernel, grid=(PARTS + 1,), in_specs=[full(128, 10...  27.6 us
    pallas_call x2, Pallas kernels, block_forward(): pl.pallas_call(forward_kernel, grid=(PARTS + 1,), in_specs=[full(128, 102...  23.1 us
    unnamed x96, local copies, waits for them, and re-layouts  17.2 us
    ppermute x1, waiting for transfers between devices, on_device(): arrived_0 = lax.ppermute(grad_residual, 'section', [(0, 1)])  14.5 us
  transfers between devices with their start and end apart: 31, of which 21 were waited for; matrix products, arithmetic and copies ran while one was open for 14% of the time, Pallas kernels for 14%

profile of v6, /device:TPU:1, one launch (start us, length us, event | category | flops | bytes accessed | tf_op | source)
XLA Modules:
  0.0 529.3 jit_solution(5711535326148098804)
XLA Ops:
  18.9 9.6 %all-to-all-start = ((bf16[32,80,192]{2,1,0:T(8,128)(2,1)}), bf16[32,80,192]{2,1,0:T(8,128)(2,1)S(1)}, u32[]{:S(2)}, u32[]{:S(2)}) async-start(bf16[32,80,192]{2,1,0:T(8,128)(2,1)} %bitcast.5), calls=%async_computation | async-start | bytes 2621440 | tf_op jit(solution)/shard_map/head_weights/all_to_all | solution.py:37
  31.3 19.0 %all-to-all-done = bf16[32,80,192]{2,1,0:T(8,128)(2,1)S(1)} async-done(((bf16[32,80,192]{2,1,0:T(8,128)(2,1)}), bf16[32,80,192]{2,1,0:T(8,128)(2,1)S(1)}, u32[]{:S(2)}, u32[]{:S(2)}) %all-to-all-start) | async-done | bytes 983072 | tf_op jit(solution)/shard_map/head_weights/all_to_all | solution.py:37
  56.5 23.7 %all-to-all-done.1 = bf16[16,32,1024]{2,1,0:T(8,128)(2,1)S(1)} async-done(((bf16[16,32,1024]{2,1,0:T(8,128)(2,1)}), bf16[16,32,1024]{2,1,0:T(8,128)(2,1)S(1)}, u32[]{:S(2)}, u32[]{:S(2)}) %all-to-all-start.1) | async-done | bytes 1048608 | tf_op jit(solution)/shard_map/sequence_tokens/all_to_all | solution.py:37
  98.4 11.4 %all-to-all-done.2 = bf16[32,32,128]{2,1,0:T(8,128)(2,1)S(1)} async-done(((bf16[32,32,128]{2,1,0:T(8,128)(2,1)}), bf16[32,32,128]{2,1,0:T(8,128)(2,1)S(1)}, u32[]{:S(2)}, u32[]{:S(2)}) %all-to-all-start.2) | async-done | bytes 262176 | tf_op jit(solution)/shard_map/context_out/all_to_all | solution.py:37
  109.8 40.7 %all-gather.15.cloned.1.call-done = bf16[9216,1024]{1,0:T(8,128)(2,1)} async-done(((bf16[144,1024]{1,0:T(8,128)(2,1)}), bf16[9216,1024]{1,0:T(8,128)(2,1)}) %all-gather.15.cloned.1.call-update) | async-done | bytes 18874384 | tf_op jit(solution)/shard_map/gather_block_weights/all_gather | solution.py:462
  150.5 12.0 %block_0.1 = (bf16[128,1024]{1,0:T(8,128)(2,1)S(1)}, f32[128,1024]{1,0:T(8,128)}, bf16[128,1024]{1,0:T(8,128)(2,1)}, f32[128,4096]{1,0:T(8,128)}, f32[128,1024]{1,0:T(8,128)}, /*index=5*/bf16[128,1024]{1,0:T(8,128)(2,1)}) custom-call(bf16[128,1024]{1,0:T(8,128)(2,1)S(1)} %bitcast.250, bf16[2,2,4,2,32,128]{5,4,3,2,1,0:T(8,128)(2,1)S(1)} %bitcast.251, ...), custom_call_target="tpu_custom_call" | custom-call | flops 2415919104 | bytes 25165824 | tf_op jit(solution)/shard_map/block_0/pallas_call | solution.py:197
  164.8 5.5 %collective-permute-done.2 = bf16[128,1024]{1,0:T(8,128)(2,1)S(1)} collective-permute-done((bf16[128,1024]{1,0:T(8,128)(2,1)S(1)}, bf16[128,1024]{1,0:T(8,128)(2,1)S(1)}, u32[]{:S(2)}, u32[]{:S(2)}) %collective-permute-start.2) | collective-permute-done | bytes 262176 | tf_op jit(solution)/shard_map/to_next_section/ppermute | solution.py:530
  171.2 25.1 %all_to_all.65 = bf16[16,32,1024]{2,1,0:T(8,128)(2,1)S(1)} all-to-all(bf16[16,32,1024]{2,1,0:T(8,128)(2,1)S(1)} %bitcast.272), channel_id=1, replica_groups=mesh['section'=2,'shard'=16,'replica'=4] {'shard'}, dimensions={0} | all-to-all | bytes 2097152 | tf_op jit(solution)/shard_map/sequence_tokens/all_to_all | solution.py:37
  206.6 16.6 %all_to_all.66 = bf16[32,32,128]{2,1,0:T(8,128)(2,1)S(1)} all-to-all(bf16[32,32,128]{2,1,0:T(8,128)(2,1)S(1)} %bitcast.294), channel_id=1, replica_groups=mesh['section'=2,'shard'=16,'replica'=4] {'section','shard'}, dimensions={0} | all-to-all | bytes 524288 | tf_op jit(solution)/shard_map/context_out/all_to_all | solution.py:37
  223.3 11.1 %block_1.1 = (bf16[128,1024]{1,0:T(8,128)(2,1)}, f32[128,1024]{1,0:T(8,128)S(1)}, bf16[128,1024]{1,0:T(8,128)(2,1)S(1)}, f32[128,4096]{1,0:T(8,128)S(1)}, f32[12...) custom-call(bf16[128,1024]{1,0:T(8,128)(2,1)S(1)} %copy-done.5, ...), custom_call_target="tpu_custom_call" | custom-call | flops 2415919104 | bytes 25165824 | tf_op jit(solution)/shard_map/block_1/pallas_call | solution.py:197
  235.8 14.3 %block_back_1.1 = (f32[128,1024]{1,0:T(8,128)}, bf16[128,1024]{1,0:T(8,128)(2,1)}, bf16[2,2,4,2,64,128]{5,4,3,2,1,0:T(8,128)(2,1)S(1)}, f32[8,1024]{1,0:T(8,128)}) custom-call(bf16[128,1024]{1,0:T(8,128)(2,1)S(1)} %bitcast.253, bf16[16,576,1024]{2,1,0:T(8,128)(2,1)} %bitcast.262, bf16[16,576,1024]{2,1,0:T(8,128)(2,1)} %bitcast.263, ...), custom_call_target="tpu_custom_call" | custom-call | flops 2415919104 | bytes 25165824 | tf_op jit(solution)/shard_map/block_back_1/pallas_call | solution.py:292
  252.2 8.9 %all-to-all-start.5 = ((bf16[32,64,128]{2,1,0:T(8,128)(2,1)}), bf16[32,64,128]{2,1,0:T(8,128)(2,1)S(1)}, u32[]{:S(2)}, u32[]{:S(2)}) async-start(bf16[32,64,128]{2,1,0:T(8,128)(2,1)} %bitcast.255), calls=%async_computation.5 | async-start | bytes 1048576 | tf_op jit(solution)/shard_map/grad_context_in/all_to_all | solution.py:37
  262.7 10.5 %all-to-all-done.5.got = bf16[32,64,128]{2,1,0:T(8,128)(2,1)S(1)} async-done(((bf16[32,64,128]{2,1,0:T(8,128)(2,1)}), bf16[32,64,128]{2,1,0:T(8,128)(2,1)S(1)}, u32[]{:S(2)}, u32[]{:S(2)}) %all-to-all-start.5) | async-done | bytes 524320 | tf_op jit(solution)/shard_map/grad_context_in/all_to_all | solution.py:37
  277.2 5.5 %attention_back.2 = bf16[1024,192]{1,0:T(8,128)(2,1)S(1)} custom-call(s32[1]{0:T(128)} %bitcast.45.core, bf16[1024,192]{1,0:T(8,128)(2,1)S(1)} %copy-done.23, f32[1024,1]{1,0:T(8,128)S(1)} %copy-done.10, bf16[1024,1]{1,0:T(8,128)(2,1)S(1)} %select_n.403.seg_rows, bf16[1,1024]{1,0:T(2,128)(2,1)S(1)} %select_n.372.seg_columns, bf16[32,64,128]{2,1,0:T(8,128)(2,1)S(1)} %copy-done.8), custom_call_target="tpu_custom_call" | custom-call | flops 671088640 | bytes 2097152 | tf_op jit(solution)/shard_map/attention_back/pallas_call | solution.py:411
  290.3 5.1 all-to-all-start.6
  295.9 13.8 %all-to-all-done.6 = bf16[32,32,384]{2,1,0:T(8,128)(2,1)} async-done(((bf16[32,32,384]{2,1,0:T(8,128)(2,1)}), bf16[32,32,384]{2,1,0:T(8,128)(2,1)}, u32[]{:S(2)}, u32[]{:S(2)}) %all-to-all-start.6) | async-done | bytes 786464 | tf_op jit(solution)/shard_map/grad_tokens_1/all_to_all | solution.py:37
  309.8 5.5 %grad_tokens_1.1 = (f32[128,1024]{1,0:T(8,128)S(1)}, bf16[128,1024]{1,0:T(8,128)(2,1)S(1)}) custom-call(bf16[2,2,4,2,32,384]{5,4,3,2,1,0:T(8,128)(2,1)} %bitcast.54.got, bf16[1024,3072]{1,0:T(8,128)(2,1)} %all-gather.7.cloned.1.call-done.weight, f32[128,1024]{1,0:T(8,128)} %collective-permute-done.5.grad_residual), custom_call_target="tpu_custom_call" | custom-call | flops 805306368 | bytes 8388608 | tf_op jit(solution)/shard_map/grad_tokens_1/pallas_call | solution.py:346
  318.4 13.3 %block_back_0.1 = (f32[128,1024]{1,0:T(8,128)S(1)}, bf16[128,1024]{1,0:T(8,128)(2,1)S(1)}, bf16[2,2,4,2,64,128]{5,4,3,2,1,0:T(8,128)(2,1)S(1)}, f32[8,1024]{1,0:T(8,128)S(1)}) custom-call(bf16[128,1024]{1,0:T(8,128)(2,1)S(1)} %get-tuple-element.58.grad, bf16[16,576,1024]{2,1,0:T(8,128)(2,1)} %bitcast.265, bf16[16,576,1024]{2,1,0:T(8,128)(2,1)} %bitcast.266, ...), custom_call_target="tpu_custom_call" | custom-call | flops 2415919104 | bytes 25165824 | tf_op jit(solution)/shard_map/block_back_0/pallas_call | solution.py:292
  352.2 5.5 %attention_back.3 = bf16[1024,192]{1,0:T(8,128)(2,1)S(1)} custom-call(s32[1]{0:T(128)} %bitcast.45.core, bf16[1024,192]{1,0:T(8,128)(2,1)S(1)} %copy-done.21, f32[1024,1]{1,0:T(8,128)S(1)} %copy.180.log_totals, bf16[1024,1]{1,0:T(8,128)(2,1)S(1)} %copy-done.15, bf16[1,1024]{1,0:T(2,128)(2,1)S(1)} %select_n.372.seg_columns, ...), custom_call_target="tpu_custom_call" | custom-call | flops 671088640 | bytes 2097152 | tf_op jit(solution)/shard_map/attention_back/pallas_call | solution.py:411
  360.2 5.0 collective-permute-done.9
  367.4 4.8 convolution_add_fusion
  372.3 9.8 %all-to-all-start.8 = ((bf16[64,16,512]{2,1,0:T(8,128)(2,1)}), bf16[64,16,512]{2,1,0:T(8,128)(2,1)S(1)}, u32[]{:S(2)}, u32[]{:S(2)}) async-start(bf16[64,16,512]{2,1,0:T(8,128)(2,1)} %bitcast.58), calls=%async_computation.8 | async-start | bytes 2097152 | tf_op jit(solution)/shard_map/sum_output_grad/all_to_all | solution.py:37
  385.6 15.0 %all-to-all-done.8 = bf16[64,16,512]{2,1,0:T(8,128)(2,1)S(1)} async-done(((bf16[64,16,512]{2,1,0:T(8,128)(2,1)}), bf16[64,16,512]{2,1,0:T(8,128)(2,1)S(1)}, u32[]{:S(2)}, u32[]{:S(2)}) %all-to-all-start.8) | async-done | bytes 1048608 | tf_op jit(solution)/shard_map/sum_output_grad/all_to_all | solution.py:37
  401.9 6.2 %all-to-all-start.9 = ((bf16[64,16,512]{2,1,0:T(8,128)(2,1)}), bf16[64,16,512]{2,1,0:T(8,128)(2,1)S(1)}, u32[]{:S(2)}, u32[]{:S(2)}) async-start(bf16[64,16,512]{2,1,0:T(8,128)(2,1)} %bitcast.62), calls=%async_computation.9 | async-start | bytes 2097152 | tf_op jit(solution)/shard_map/sum_attend_grad/all_to_all | solution.py:37
  408.4 6.0 %fusion.50 = (bf16[256]{0:T(256)(128)(2,1)S(1)}, bf16[2048,256]{1,0:T(8,128)(2,1)}) fusion(f32[2048,256]{1,0:T(8,128)} %convolution_add_fusion, bf16[2048,1024]{1,0:T(8,128)(2,1)} %all-gather.11.cloned.1.call-done, bf16[1,256,1024]{2,1,0:T(8,128)(2,1)S(1)} %copy-done.32), kind=kOutput, calls=%fused_computation.167 | convolution fusion | flops 1079508736 | bytes 7864832 | tf_op jit(solution)/shard_map/block_weight_grads/dot_general | solution.py:25
  426.7 8.4 %all-to-all-start.10 = ((bf16[64,16,256]{2,1,0:T(8,128)(2,1)}), bf16[64,16,256]{2,1,0:T(8,128)(2,1)S(1)}, u32[]{:S(2)}, u32[]{:S(2)}) async-start(bf16[64,16,256]{2,1,0:T(8,128)(2,1)} %bitcast.71), calls=%async_computation.10 | async-start | bytes 1048576 | tf_op jit(solution)/shard_map/sum_expand_grad/all_to_all | solution.py:37
  435.9 12.6 %all-to-all-done.10 = bf16[64,16,256]{2,1,0:T(8,128)(2,1)S(1)} async-done(((bf16[64,16,256]{2,1,0:T(8,128)(2,1)}), bf16[64,16,256]{2,1,0:T(8,128)(2,1)S(1)}, u32[]{:S(2)}, u32[]{:S(2)}) %all-to-all-start.10) | async-done | bytes 524320 | tf_op jit(solution)/shard_map/sum_expand_grad/all_to_all | solution.py:37
  452.2 9.5 %all-to-all-done.11 = bf16[4,80,1024]{2,1,0:T(8,128)(2,1)S(1)} async-done(((bf16[4,80,1024]{2,1,0:T(8,128)(2,1)}), bf16[4,80,1024]{2,1,0:T(8,128)(2,1)S(1)}, u32[]{:S(2)}, u32[]{:S(2)}) %all-to-all-start.11) | async-done | bytes 655392 | tf_op jit(solution)/shard_map/sum_contract/all_to_all | solution.py:37
  467.0 6.5 %all-to-all-start.12 = ((bf16[32,32,384]{2,1,0:T(8,128)(2,1)}), bf16[32,32,384]{2,1,0:T(8,128)(2,1)S(1)}, u32[]{:S(2)}, u32[]{:S(2)}) async-start(bf16[32,32,384]{2,1,0:T(8,128)(2,1)} %bitcast.275), calls=%async_computation.12 | async-start | bytes 1572864 | tf_op jit(solution)/shard_map/grad_tokens_0/all_to_all | solution.py:37
  478.9 14.5 %collective-permute-done.12.grad_residual = f32[128,1024]{1,0:T(8,128)S(1)} collective-permute-done((f32[128,1024]{1,0:T(8,128)S(1)}, f32[128,1024]{1,0:T(8,128)S(1)}, u32[]{:S(2)}, u32[]{:S(2)}) %collective-permute-start.12) | collective-permute-done | bytes 524320 | tf_op jit(solution)/shard_map/residual_to_other_section/ppermute | solution.py:567
  493.5 5.9 %grad_tokens_0.1 = (f32[128,1024]{1,0:T(8,128)S(1)}, bf16[128,1024]{1,0:T(8,128)(2,1)}) custom-call(bf16[2,2,4,2,32,384]{5,4,3,2,1,0:T(8,128)(2,1)S(1)} %bitcast.248, bf16[1024,3072]{1,0:T(8,128)(2,1)} %all-gather.7.cloned.1.call-done.weight, f32[128,1024]{1,0:T(8,128)S(1)} %collective-permute-done.12.grad_residual), custom_call_target="tpu_custom_call" | custom-call | flops 805306368 | bytes 8388608 | tf_op jit(solution)/shard_map/grad_tokens_0/pallas_call | solution.py:346
  504.7 9.3 %collective-permute-done.13 = f32[128,1024]{1,0:T(8,128)S(1)} collective-permute-done((f32[128,1024]{1,0:T(8,128)S(1)}, f32[128,1024]{1,0:T(8,128)S(1)}, u32[]{:S(2)}, u32[]{:S(2)}) %collective-permute-start.13) | collective-permute-done | bytes 524320 | tf_op jit(solution)/shard_map/grad_tokens_0/ppermute | solution.py:652
  (325 shorter events, 143.2 us)
Async XLA Ops:
  7.2 143.4 %all-gather.15.cloned.1.call-start = ((), (), s32[]{:S(2)}) async-start(), calls=%async_computation.17 | async-start | bytes 19169280 | tf_op jit(solution)/shard_map/gather_block_weights/all_gather | solution.py:462
  18.8 31.5 %copy-start = (bf16[2,1,64,1024]{3,2,1,0:T(8,128)(2,1)S(1)}, bf16[2,1,64,1024]{3,2,1,0:T(8,128)(2,1)}, u32[]{:S(2)}) copy-start(bf16[2,1,64,1024]{3,2,1,0:T(8,128)(2,1)} %param.10) | copy-start | bytes 786436
  18.9 31.5 %all-to-all-start = ((bf16[32,80,192]{2,1,0:T(8,128)(2,1)}), bf16[32,80,192]{2,1,0:T(8,128)(2,1)S(1)}, u32[]{:S(2)}, u32[]{:S(2)}) async-start(bf16[32,80,192]{2,1,0:T(8,128)(2,1)} %bitcast.5), calls=%async_computation | async-start | bytes 2621440 | tf_op jit(solution)/shard_map/head_weights/all_to_all | solution.py:37
  29.8 132.7 %collective-permute-start.7 = (bf16[64,3072]{1,0:T(8,128)(2,1)}, bf16[64,3072]{1,0:T(8,128)(2,1)}, u32[]{:S(2)}, u32[]{:S(2)}) collective-permute-start(bf16[64,3072]{1,0:T(8,128)(2,1)} %reshape.437), channel_id=1, source_target_pairs={{0,64},{64,0},{1,65},{65,1},{2,66},{66,2},{3,67},{67,3},{4,68},{68... | collective-permute-start | bytes 1179656 | tf_op jit(solution)/shard_map/gather_attend_weight/ppermute | solution.py:534
  51.4 28.8 %all-to-all-start.1 = ((bf16[16,32,1024]{2,1,0:T(8,128)(2,1)}), bf16[16,32,1024]{2,1,0:T(8,128)(2,1)S(1)}, u32[]{:S(2)}, u32[]{:S(2)}) async-start(bf16[16,32,1024]{2,1,0:T(8,128)(2,1)} %bitcast.271), calls=%async_computation.1 | async-start | bytes 2097152 | tf_op jit(solution)/shard_map/sequence_tokens/all_to_all | solution.py:37
  80.2 4.3 collective-permute-start
  91.5 1.4 collective-permute-start.1
  93.8 16.0 %all-to-all-start.2 = ((bf16[32,32,128]{2,1,0:T(8,128)(2,1)}), bf16[32,32,128]{2,1,0:T(8,128)(2,1)S(1)}, u32[]{:S(2)}, u32[]{:S(2)}) async-start(bf16[32,32,128]{2,1,0:T(8,128)(2,1)} %bitcast.22), calls=%async_computation.2 | async-start | bytes 524288 | tf_op jit(solution)/shard_map/context_out/all_to_all | solution.py:37
  97.7 212.1 %all-gather.7.cloned.1.call-start = ((), (), s32[]{:S(2)}) async-start(), calls=%async_computation.13 | async-start | bytes 6684672 | tf_op jit(solution)/shard_map/gather_attend_weight/all_gather | solution.py:536
  162.5 204.8 %all-gather.9.cloned.1.call-start = ((), (), s32[]{:S(2)}) async-start(), calls=%async_computation.14 | async-start | bytes 4456448 | tf_op jit(solution)/shard_map/gather_first/all_gather | solution.py:544
  162.6 7.7 %collective-permute-start.2 = (bf16[128,1024]{1,0:T(8,128)(2,1)S(1)}, bf16[128,1024]{1,0:T(8,128)(2,1)S(1)}, u32[]{:S(2)}, u32[]{:S(2)}) collective-permute-start(bf16[128,1024]{1,0:T(8,128)(2,1)S(1)} %get-tuple-element.47), channel_id=1, source_target_pairs={{0,64},{1,65},{2,66},{3,67},{4,68},{5,69},{6,70},{7,71},{8,72},{9,... | collective-permute-start | bytes 786440 | tf_op jit(solution)/shard_map/to_next_section/ppermute | solution.py:530
  196.3 2.7 collective-permute-start.3
  205.0 1.4 collective-permute-start.4
  250.9 23.1 %collective-permute-start.5 = (f32[128,1024]{1,0:T(8,128)}, f32[128,1024]{1,0:T(8,128)}, u32[]{:S(2)}, u32[]{:S(2)}) collective-permute-start(f32[128,1024]{1,0:T(8,128)} %get-tuple-element.53), channel_id=1, source_target_pairs={{64,0},{65,1},{66,2},{67,3},{68,4},{69,5},{70,6},{71,7},{72,8},{73... | collective-permute-start | bytes 1572872 | tf_op jit(solution)/shard_map/residual_to_other_section/ppermute | solution.py:552
  252.2 21.1 %all-to-all-start.5 = ((bf16[32,64,128]{2,1,0:T(8,128)(2,1)}), bf16[32,64,128]{2,1,0:T(8,128)(2,1)S(1)}, u32[]{:S(2)}, u32[]{:S(2)}) async-start(bf16[32,64,128]{2,1,0:T(8,128)(2,1)} %bitcast.255), calls=%async_computation.5 | async-start | bytes 1048576 | tf_op jit(solution)/shard_map/grad_context_in/all_to_all | solution.py:37
  282.7 2.7 collective-permute-start.6
  290.3 19.5 %all-to-all-start.6 = ((bf16[32,32,384]{2,1,0:T(8,128)(2,1)}), bf16[32,32,384]{2,1,0:T(8,128)(2,1)}, u32[]{:S(2)}, u32[]{:S(2)}) async-start(bf16[32,32,384]{2,1,0:T(8,128)(2,1)} %bitcast.276), calls=%async_computation.6 | async-start | bytes 1572864 | tf_op jit(solution)/shard_map/grad_tokens_1/all_to_all | solution.py:37
  295.5 112.9 %all-gather.11.cloned.1.call-start = ((), (), s32[]{:S(2)}) async-start(), calls=%async_computation.15 | async-start | bytes 4456448 | tf_op jit(solution)/shard_map/gather_grad_mlp/all_gather | solution.py:561
  333.9 14.0 %collective-permute-start.8 = (bf16[1024,512]{1,0:T(8,128)(2,1)}, bf16[1024,512]{1,0:T(8,128)(2,1)}, u32[]{:S(2)}, u32[]{:S(2)}) collective-permute-start(bf16[1024,512]{1,0:T(8,128)(2,1)} %select_convert_fusion), channel_id=1, source_target_pairs={{0,4},{4,0},{8,12},{12,8},{16,20},{20,16},{24,28},{28,24},{32,36},... | collective-permute-start | bytes 3145736 | tf_op jit(solution)/shard_map/sum_output_grad/ppermute | solution.py:41
  335.2 16.9 %all-to-all-start.7 = ((bf16[32,64,128]{2,1,0:T(8,128)(2,1)}), bf16[32,64,128]{2,1,0:T(8,128)(2,1)S(1)}, u32[]{:S(2)}, u32[]{:S(2)}) async-start(bf16[32,64,128]{2,1,0:T(8,128)(2,1)} %bitcast.254), calls=%async_computation.7 | async-start | bytes 1048576 | tf_op jit(solution)/shard_map/grad_context_in/all_to_all | solution.py:37
  342.4 22.7 %collective-permute-start.9 = (bf16[1040,192]{0,1:T(8,128)(2,1)}, bf16[1040,192]{0,1:T(8,128)(2,1)}, u32[]{:S(2)}, u32[]{:S(2)}) collective-permute-start(bf16[1040,192]{0,1:T(8,128)(2,1)} %fusion.25), channel_id=1, source_target_pairs={{0,64},{1,65},{2,66},{3,67},{4,68},{5,69},{6,70},{7,71},{8,72},{9,... | collective-permute-start | bytes 1198088 | tf_op jit(solution)/shard_map/swap_attend_grad/ppermute | solution.py:573
  366.1 16.0 %collective-permute-start.10 = (bf16[1040,192]{0,1:T(8,128)(2,1)}, bf16[1040,192]{0,1:T(8,128)(2,1)}, u32[]{:S(2)}, u32[]{:S(2)}) collective-permute-start(bf16[1040,192]{0,1:T(8,128)(2,1)} %get-tuple-element.146), channel_id=1, source_target_pairs={{64,0},{65,1},{66,2},{67,3},{68,4},{69,5},{70,6},{71,7},{72,8},{73... | collective-permute-start | bytes 1198088 | tf_op jit(solution)/shard_map/swap_attend_grad/ppermute | solution.py:587
  372.3 28.3 %all-to-all-start.8 = ((bf16[64,16,512]{2,1,0:T(8,128)(2,1)}), bf16[64,16,512]{2,1,0:T(8,128)(2,1)S(1)}, u32[]{:S(2)}, u32[]{:S(2)}) async-start(bf16[64,16,512]{2,1,0:T(8,128)(2,1)} %bitcast.58), calls=%async_computation.8 | async-start | bytes 2097152 | tf_op jit(solution)/shard_map/sum_output_grad/all_to_all | solution.py:37
  401.9 24.7 %all-to-all-start.9 = ((bf16[64,16,512]{2,1,0:T(8,128)(2,1)}), bf16[64,16,512]{2,1,0:T(8,128)(2,1)S(1)}, u32[]{:S(2)}, u32[]{:S(2)}) async-start(bf16[64,16,512]{2,1,0:T(8,128)(2,1)} %bitcast.62), calls=%async_computation.9 | async-start | bytes 2097152 | tf_op jit(solution)/shard_map/sum_attend_grad/all_to_all | solution.py:37
  426.7 21.9 %all-to-all-start.10 = ((bf16[64,16,256]{2,1,0:T(8,128)(2,1)}), bf16[64,16,256]{2,1,0:T(8,128)(2,1)S(1)}, u32[]{:S(2)}, u32[]{:S(2)}) async-start(bf16[64,16,256]{2,1,0:T(8,128)(2,1)} %bitcast.71), calls=%async_computation.10 | async-start | bytes 1048576 | tf_op jit(solution)/shard_map/sum_expand_grad/all_to_all | solution.py:37
  448.5 13.2 %all-to-all-start.11 = ((bf16[4,80,1024]{2,1,0:T(8,128)(2,1)}), bf16[4,80,1024]{2,1,0:T(8,128)(2,1)S(1)}, u32[]{:S(2)}, u32[]{:S(2)}) async-start(bf16[4,80,1024]{2,1,0:T(8,128)(2,1)} %pad_maximum_fusion.3), calls=%async_computation.11 | async-start | bytes 1310720 | tf_op jit(solution)/shard_map/sum_contract/all_to_all | solution.py:37
  452.0 62.8 %all-gather.13.cloned.1.call-start = ((), (), s32[]{:S(2)}) async-start(), calls=%async_computation.16 | async-start | bytes 1966080 | tf_op jit(solution)/shard_map/gather_weight_grads/all_gather | solution.py:654
  461.9 3.4 collective-permute-start.11
  467.0 26.5 %all-to-all-start.12 = ((bf16[32,32,384]{2,1,0:T(8,128)(2,1)}), bf16[32,32,384]{2,1,0:T(8,128)(2,1)S(1)}, u32[]{:S(2)}, u32[]{:S(2)}) async-start(bf16[32,32,384]{2,1,0:T(8,128)(2,1)} %bitcast.275), calls=%async_computation.12 | async-start | bytes 1572864 | tf_op jit(solution)/shard_map/grad_tokens_0/all_to_all | solution.py:37
  473.5 20.0 %collective-permute-start.12 = (f32[128,1024]{1,0:T(8,128)S(1)}, f32[128,1024]{1,0:T(8,128)S(1)}, u32[]{:S(2)}, u32[]{:S(2)}) collective-permute-start(f32[128,1024]{1,0:T(8,128)S(1)} %copy-done.19), channel_id=1, source_target_pairs={{0,64},{1,65},{2,66},{3,67},{4,68},{5,69},{6,70},{7,71},{8,72},{9,... | collective-permute-start | bytes 1572872 | tf_op jit(solution)/shard_map/residual_to_other_section/ppermute | solution.py:567
  476.8 27.9 %collective-permute-start.14 = (f32[128,1024]{1,0:T(8,128)S(1)}, f32[128,1024]{1,0:T(8,128)}, u32[]{:S(2)}, u32[]{:S(2)}) collective-permute-start(f32[128,1024]{1,0:T(8,128)S(1)} %copy-done.17), channel_id=1, source_target_pairs={{0,64},{1,65},{2,66},{3,67},{4,68},{5,69},{6,70},{7,71},{8,72},{9,... | collective-permute-start | bytes 1572872 | tf_op jit(solution)/shard_map/grad_tokens_1/ppermute | solution.py:556
  499.3 14.6 %collective-permute-start.13 = (f32[128,1024]{1,0:T(8,128)S(1)}, f32[128,1024]{1,0:T(8,128)S(1)}, u32[]{:S(2)}, u32[]{:S(2)}) collective-permute-start(f32[128,1024]{1,0:T(8,128)S(1)} %get-tuple-element.82), channel_id=1, source_target_pairs={{64,0},{65,1},{66,2},{67,3},{68,4},{69,5},{70,6},{71,7},{72,8},{73... | collective-permute-start | bytes 1572872 | tf_op jit(solution)/shard_map/grad_tokens_0/ppermute | solution.py:652
  (38 other events, 200.4 us)
Sparse Core Ops, SparseCore 0:
  13.9 136.5 all-gather.14
  162.7 72.8 all-gather.6
  238.0 54.5 all-gather.8
  317.2 61.9 all-gather.10
  464.3 25.0 all-gather.12

commit v7 on v6

--- a/solution.py
+++ b/solution.py
@@ -578,10 +578,13 @@
         keep = jnp.where(core == 0, halves[0], halves[1])
         give = jnp.where(core == 0, halves[1], halves[0]).astype(LOW)
         output_grad = (keep + swap_cores(give).astype(jnp.float32)).astype(LOW)
-    grad_packed, output_grad = attention_back(0, grad_context, kept_0, output_grad)
+    grad_packed, (output_grad, arrived_0, grad_tokens_1) = attention_back(
+        0, grad_context, kept_0, (output_grad, arrived_0, grad_tokens_1)
+    )
 
     with jax.named_scope("sum_output_grad"):
         output_got = exchange(output_grad.reshape(64, 16, 512), REST)
+        output_got, grad_packed = lax.optimization_barrier((output_got, grad_packed))
     with jax.named_scope("swap_attend_grad"):
         part_0 = attend_part(kept_0[0], grad_packed)
         take_0 = lax.ppermute(part_0, "section", [(1, 0)])
@@ -599,10 +602,6 @@
         )
         vectors = jnp.broadcast_to(vectors[:, None], (16, 4, 16, 128)).reshape(1024, 128)
         vectors = vectors.astype(LOW)
-    with jax.named_scope("sum_attend_grad"):
-        parts = jnp.concatenate([attend_grad, vectors], 1)
-        output_got, parts = lax.optimization_barrier((output_got, parts))
-        got = exchange(parts.reshape(64, 16, 512), REST)
     with jax.named_scope("block_weight_grads"):
         expand_part = lax.dynamic_slice(
             late_gathered, (0, 320 + shard // 4 * 64, shard % 4 * 256), (16, 64, 256)
@@ -627,19 +626,22 @@
         rows = jnp.concatenate(
             [contract_grad.reshape(4, 64, 1024), jnp.broadcast_to(extra, (4, 16, 1024))], 1
         )
-    with jax.named_scope("sum_expand_grad"):
-        got, expand_grad, rows = lax.optimization_barrier((got, expand_grad, rows))
-        expand_got = exchange(expand_grad.reshape(64, 16, 256), REST)
-        expand_got, rows = lax.optimization_barrier((expand_got, rows))
+    with jax.named_scope("sum_attend_expand_grads"):
+        attend_grad, expand_grad, vectors, rows = lax.optimization_barrier(
+            (attend_grad, expand_grad, vectors, rows)
+        )
+        parts = jnp.concatenate([attend_grad, expand_grad, vectors], 1)
+        got = exchange(parts.reshape(64, 16, 768), REST)
+        got, rows = lax.optimization_barrier((got, rows))
     with jax.named_scope("sum_contract"):
         got_contract = exchange(rows, "replica").astype(jnp.float32).sum(0)
     with jax.named_scope("sum_attend_grad"):
         got_output = output_got.astype(jnp.float32).reshape(8, 2, 4, 16, 512).sum((0, 2))
         got_output = jnp.concatenate([got_output[0], got_output[1]], 1).astype(LOW)
         got_attend = got[:, :, :384].astype(jnp.float32).reshape(2, 8, 4, 16, 384).sum((0, 2))
-        got_expand = expand_got.astype(jnp.float32).reshape(16, 4, 16, 256).sum(1)
+        got_expand = got[:, :, 384:640].astype(jnp.float32).reshape(16, 4, 16, 256).sum(1)
         got_expand = got_expand.astype(LOW).transpose(1, 0, 2).reshape(16, 4096)
-        got_vectors = got[:, :7, 384:448].astype(jnp.float32).sum(0)
+        got_vectors = got[:, :7, 640:704].astype(jnp.float32).sum(0)
         got_attend, got_output = lax.optimization_barrier((got_attend.astype(LOW), got_output))
         got_attend = got_attend.reshape(8, 16, 2, 3, 64).transpose(1, 3, 2, 0, 4)
         got_attend = got_attend.reshape(16, 3072)
@@ -655,6 +657,14 @@
         contract_total = totals[:, 8192:].reshape(4, 16, 4, 1024).transpose(0, 2, 1, 3)
         contract_total = contract_total.reshape(1, 256, 1024).astype(jnp.float32)
         totals = totals[None, :, :8192].astype(jnp.float32)
+    attend_total = totals[:, :, :3072]
+    output_total = totals[:, :, 3072:4096]
+    expand_total = totals[:, :, 4096:]
+    grad_tokens_0, attend_total, output_total, expand_total, contract_total = (
+        lax.optimization_barrier(
+            (grad_tokens_0, attend_total, output_total, expand_total, contract_total)
+        )
+    )
     input_grad = jnp.where(on_first, grad_tokens_0, grad_tokens_1).reshape(1, 2, 1, 64, 1024)
     mlp_own = lax.dynamic_slice_in_dim(got_contract[65], shard * 64, 64, 0)
     biases_grad = jnp.stack(
@@ -670,9 +680,9 @@
     return (
         layer_output,
         input_grad,
-        totals[:, :, :3072],
-        totals[:, :, 3072:4096],
-        totals[:, :, 4096:],
+        attend_total,
+        output_total,
+        expand_total,
         contract_total,
         biases_grad[None],
         got_contract[None, 64, :256],

time: 540 us -> 557 us (1.031)
  waiting for transfers between devices: 202 us -> 218 us
    all_to_all x11 -> x10, waiting for transfers between devices: 117 us -> 137 us  [exchange(): return lax.all_to_all(value, axes, 0, 0, tiled=True)]
    ppermute x1, waiting for transfers between devices: 14.5 us -> 0.01 us  [on_device(): arrived_0 = lax.ppermute(grad_residual, 'section', [(0, 1)])]
    ppermute x1, waiting for transfers between devices: 0.72 us -> 12.9 us  [on_device(): grad_tokens_1 = lax.ppermute(result_1, 'section', [(0, 1)])]
    ppermute x1, waiting for transfers between devices: 0.01 us -> 6.86 us  [on_device(): take_0 = lax.ppermute(part_0, 'section', [(1, 0)])]
    all_to_all x11 -> x10, starting transfers between devices: 70.4 us -> 64.5 us  [exchange(): return lax.all_to_all(value, axes, 0, 0, tiled=True)]
    unnamed x96 -> x94, local copies, waits for them, and re-layouts: 17.2 us -> 19.3 us
  transfers between devices with their start and end apart: 31 -> 30, of which waited for: 21 -> 21; matrix products, arithmetic and copies ran while one was open for 14% -> 12% of each run, Pallas kernels for 14% -> 13%
where the time goes in v7:
time: 557 us; the launch traced here: 547 us
  waiting for transfers between devices  218 us (39%)
  starting transfers between devices  91.7 us (16%)
  Pallas kernels  73.1 us (13%)
  local copies, waits for them, and re-layouts  51.7 us (9%)
  blocking collectives  41.7 us (7%)
  other arithmetic  27.9 us (5%)
  matrix products  27.4 us (5%)
  between operations  15.5 us (3%)
    all_to_all x10, waiting for transfers between devices, exchange(): return lax.all_to_all(value, axes, 0, 0, tiled=True)  137 us
    all_to_all x10, starting transfers between devices, exchange(): return lax.all_to_all(value, axes, 0, 0, tiled=True)  64.5 us
    all_to_all x2, blocking collectives, exchange(): return lax.all_to_all(value, axes, 0, 0, tiled=True)  41.7 us
    all_gather x1, waiting for transfers between devices, on_device(): lax.all_gather(quarter, REST, axis=0, tiled=False).reshape(16, 576, 1024)  40.8 us
    pallas_call x2, Pallas kernels, block_back(): pl.pallas_call(backward_kernel, grid=(PARTS + 1,), in_specs=[full(128, 10...  27.5 us
    pallas_call x2, Pallas kernels, block_forward(): pl.pallas_call(forward_kernel, grid=(PARTS + 1,), in_specs=[full(128, 102...  23.1 us
    unnamed x94, local copies, waits for them, and re-layouts  19.3 us
    ppermute x1, waiting for transfers between devices, on_device(): grad_tokens_1 = lax.ppermute(result_1, 'section', [(0, 1)])  12.9 us
  transfers between devices with their start and end apart: 30, of which 21 were waited for; matrix products, arithmetic and copies ran while one was open for 12% of the time, Pallas kernels for 13%

profile of v7, /device:TPU:1, one launch (start us, length us, event | category | flops | bytes accessed | tf_op | source)
XLA Modules:
  0.0 546.7 jit_solution(15666842905525898353)
XLA Ops:
  18.8 9.6 %all-to-all-start = ((bf16[32,80,192]{2,1,0:T(8,128)(2,1)}), bf16[32,80,192]{2,1,0:T(8,128)(2,1)S(1)}, u32[]{:S(2)}, u32[]{:S(2)}) async-start(bf16[32,80,192]{2,1,0:T(8,128)(2,1)} %bitcast.5), calls=%async_computation | async-start | bytes 2621440 | tf_op jit(solution)/shard_map/head_weights/all_to_all | solution.py:37
  31.4 19.0 %all-to-all-done = bf16[32,80,192]{2,1,0:T(8,128)(2,1)S(1)} async-done(((bf16[32,80,192]{2,1,0:T(8,128)(2,1)}), bf16[32,80,192]{2,1,0:T(8,128)(2,1)S(1)}, u32[]{:S(2)}, u32[]{:S(2)}) %all-to-all-start) | async-done | bytes 983072 | tf_op jit(solution)/shard_map/head_weights/all_to_all | solution.py:37
  51.4 4.7 all-to-all-start.1
  56.5 23.7 %all-to-all-done.1 = bf16[16,32,1024]{2,1,0:T(8,128)(2,1)S(1)} async-done(((bf16[16,32,1024]{2,1,0:T(8,128)(2,1)}), bf16[16,32,1024]{2,1,0:T(8,128)(2,1)S(1)}, u32[]{:S(2)}, u32[]{:S(2)}) %all-to-all-start.1) | async-done | bytes 1048608 | tf_op jit(solution)/shard_map/sequence_tokens/all_to_all | solution.py:37
  98.4 11.4 %all-to-all-done.2 = bf16[32,32,128]{2,1,0:T(8,128)(2,1)S(1)} async-done(((bf16[32,32,128]{2,1,0:T(8,128)(2,1)}), bf16[32,32,128]{2,1,0:T(8,128)(2,1)S(1)}, u32[]{:S(2)}, u32[]{:S(2)}) %all-to-all-start.2) | async-done | bytes 262176 | tf_op jit(solution)/shard_map/context_out/all_to_all | solution.py:37
  109.8 40.8 %all-gather.15.cloned.1.call-done = bf16[9216,1024]{1,0:T(8,128)(2,1)} async-done(((bf16[144,1024]{1,0:T(8,128)(2,1)}), bf16[9216,1024]{1,0:T(8,128)(2,1)}) %all-gather.15.cloned.1.call-update) | async-done | bytes 18874384 | tf_op jit(solution)/shard_map/gather_block_weights/all_gather | solution.py:462
  150.5 12.0 %block_0.1 = (bf16[128,1024]{1,0:T(8,128)(2,1)S(1)}, f32[128,1024]{1,0:T(8,128)}, bf16[128,1024]{1,0:T(8,128)(2,1)}, f32[128,4096]{1,0:T(8,128)}, f32[128,1024]{1,0:T(8,128)}, /*index=5*/bf16[128,1024]{1,0:T(8,128)(2,1)}) custom-call(bf16[128,1024]{1,0:T(8,128)(2,1)S(1)} %bitcast.249, bf16[2,2,4,2,32,128]{5,4,3,2,1,0:T(8,128)(2,1)S(1)} %bitcast.250, ...), custom_call_target="tpu_custom_call" | custom-call | flops 2415919104 | bytes 25165824 | tf_op jit(solution)/shard_map/block_0/pallas_call | solution.py:197
  164.8 5.5 collective-permute-done.2
  171.2 25.1 %all_to_all.60 = bf16[16,32,1024]{2,1,0:T(8,128)(2,1)S(1)} all-to-all(bf16[16,32,1024]{2,1,0:T(8,128)(2,1)S(1)} %bitcast.272), channel_id=1, replica_groups=mesh['section'=2,'shard'=16,'replica'=4] {'shard'}, dimensions={0} | all-to-all | bytes 2097152 | tf_op jit(solution)/shard_map/sequence_tokens/all_to_all | solution.py:37
  206.7 16.6 %all_to_all.61 = bf16[32,32,128]{2,1,0:T(8,128)(2,1)S(1)} all-to-all(bf16[32,32,128]{2,1,0:T(8,128)(2,1)S(1)} %bitcast.292), channel_id=1, replica_groups=mesh['section'=2,'shard'=16,'replica'=4] {'section','shard'}, dimensions={0} | all-to-all | bytes 524288 | tf_op jit(solution)/shard_map/context_out/all_to_all | solution.py:37
  223.3 11.1 %block_1.1 = (bf16[128,1024]{1,0:T(8,128)(2,1)}, f32[128,1024]{1,0:T(8,128)S(1)}, bf16[128,1024]{1,0:T(8,128)(2,1)S(1)}, f32[128,4096]{1,0:T(8,128)S(1)}, f32[12...) custom-call(bf16[128,1024]{1,0:T(8,128)(2,1)S(1)} %copy-done.5, ...), custom_call_target="tpu_custom_call" | custom-call | flops 2415919104 | bytes 25165824 | tf_op jit(solution)/shard_map/block_1/pallas_call | solution.py:197
  235.9 14.2 %block_back_1.1 = (f32[128,1024]{1,0:T(8,128)}, bf16[128,1024]{1,0:T(8,128)(2,1)}, bf16[2,2,4,2,64,128]{5,4,3,2,1,0:T(8,128)(2,1)S(1)}, f32[8,1024]{1,0:T(8,128)}) custom-call(bf16[128,1024]{1,0:T(8,128)(2,1)S(1)} %bitcast.252, bf16[16,576,1024]{2,1,0:T(8,128)(2,1)} %bitcast.261, bf16[16,576,1024]{2,1,0:T(8,128)(2,1)} %bitcast.262, ...), custom_call_target="tpu_custom_call" | custom-call | flops 2415919104 | bytes 25165824 | tf_op jit(solution)/shard_map/block_back_1/pallas_call | solution.py:292
  252.2 8.9 %all-to-all-start.5 = ((bf16[32,64,128]{2,1,0:T(8,128)(2,1)}), bf16[32,64,128]{2,1,0:T(8,128)(2,1)S(1)}, u32[]{:S(2)}, u32[]{:S(2)}) async-start(bf16[32,64,128]{2,1,0:T(8,128)(2,1)} %bitcast.254), calls=%async_computation.5 | async-start | bytes 1048576 | tf_op jit(solution)/shard_map/grad_context_in/all_to_all | solution.py:37
  262.8 10.6 %all-to-all-done.5.got = bf16[32,64,128]{2,1,0:T(8,128)(2,1)S(1)} async-done(((bf16[32,64,128]{2,1,0:T(8,128)(2,1)}), bf16[32,64,128]{2,1,0:T(8,128)(2,1)S(1)}, u32[]{:S(2)}, u32[]{:S(2)}) %all-to-all-start.5) | async-done | bytes 524320 | tf_op jit(solution)/shard_map/grad_context_in/all_to_all | solution.py:37
  277.3 5.5 %attention_back.2 = bf16[1024,192]{1,0:T(8,128)(2,1)S(1)} custom-call(s32[1]{0:T(128)} %bitcast.45.core, bf16[1024,192]{1,0:T(8,128)(2,1)S(1)} %copy-done.22, f32[1024,1]{1,0:T(8,128)S(1)} %copy-done.10, bf16[1024,1]{1,0:T(8,128)(2,1)S(1)} %select_n.403.seg_rows, bf16[1,1024]{1,0:T(2,128)(2,1)S(1)} %select_n.372.seg_columns, bf16[32,64,128]{2,1,0:T(8,128)(2,1)S(1)} %copy-done.8), custom_call_target="tpu_custom_call" | custom-call | flops 671088640 | bytes 2097152 | tf_op jit(solution)/shard_map/attention_back/pallas_call | solution.py:411
  290.4 5.6 %all-to-all-start.6 = ((bf16[32,32,384]{2,1,0:T(8,128)(2,1)}), bf16[32,32,384]{2,1,0:T(8,128)(2,1)}, u32[]{:S(2)}, u32[]{:S(2)}) async-start(bf16[32,32,384]{2,1,0:T(8,128)(2,1)} %bitcast.274), calls=%async_computation.6 | async-start | bytes 1572864 | tf_op jit(solution)/shard_map/grad_tokens_1/all_to_all | solution.py:37
  296.4 13.8 %all-to-all-done.6 = bf16[32,32,384]{2,1,0:T(8,128)(2,1)} async-done(((bf16[32,32,384]{2,1,0:T(8,128)(2,1)}), bf16[32,32,384]{2,1,0:T(8,128)(2,1)}, u32[]{:S(2)}, u32[]{:S(2)}) %all-to-all-start.6) | async-done | bytes 786464 | tf_op jit(solution)/shard_map/grad_tokens_1/all_to_all | solution.py:37
  310.3 5.5 %grad_tokens_1.1 = (f32[128,1024]{1,0:T(8,128)S(1)}, bf16[128,1024]{1,0:T(8,128)(2,1)S(1)}) custom-call(bf16[2,2,4,2,32,384]{5,4,3,2,1,0:T(8,128)(2,1)} %bitcast.53.got, bf16[1024,3072]{1,0:T(8,128)(2,1)} %all-gather.7.cloned.1.call-done.weight, f32[128,1024]{1,0:T(8,128)} %collective-permute-done.5.grad_residual), custom_call_target="tpu_custom_call" | custom-call | flops 805306368 | bytes 8388608 | tf_op jit(solution)/shard_map/grad_tokens_1/pallas_call | solution.py:346
  318.6 13.3 %block_back_0.1 = (f32[128,1024]{1,0:T(8,128)S(1)}, bf16[128,1024]{1,0:T(8,128)(2,1)S(1)}, bf16[2,2,4,2,64,128]{5,4,3,2,1,0:T(8,128)(2,1)S(1)}, f32[8,1024]{1,0:T(8,128)S(1)}) custom-call(bf16[128,1024]{1,0:T(8,128)(2,1)S(1)} %get-tuple-element.66.grad, bf16[16,576,1024]{2,1,0:T(8,128)(2,1)} %bitcast.264, bf16[16,576,1024]{2,1,0:T(8,128)(2,1)} %bitcast.265, ...), custom_call_target="tpu_custom_call" | custom-call | flops 2415919104 | bytes 25165824 | tf_op jit(solution)/shard_map/block_back_0/pallas_call | solution.py:292
  350.4 14.3 %all-to-all-done.7.got = bf16[32,64,128]{2,1,0:T(8,128)(2,1)S(1)} async-done(((bf16[32,64,128]{2,1,0:T(8,128)(2,1)}), bf16[32,64,128]{2,1,0:T(8,128)(2,1)S(1)}, u32[]{:S(2)}, u32[]{:S(2)}) %all-to-all-start.7) | async-done | bytes 524320 | tf_op jit(solution)/shard_map/grad_context_in/all_to_all | solution.py:37
  364.7 12.9 %collective-permute-done.10 = f32[128,1024]{1,0:T(8,128)} collective-permute-done((f32[128,1024]{1,0:T(8,128)S(1)}, f32[128,1024]{1,0:T(8,128)}, u32[]{:S(2)}, u32[]{:S(2)}) %collective-permute-start.10) | collective-permute-done | bytes 524320 | tf_op jit(solution)/shard_map/grad_tokens_1/ppermute | solution.py:556
  377.6 7.1 %all-to-all-start.8 = ((bf16[64,16,512]{2,1,0:T(8,128)(2,1)}), bf16[64,16,512]{2,1,0:T(8,128)(2,1)}, u32[]{:S(2)}, u32[]{:S(2)}) async-start(bf16[64,16,512]{2,1,0:T(8,128)(2,1)} %bitcast.57), calls=%async_computation.8 | async-start | bytes 2097152 | tf_op jit(solution)/shard_map/sum_output_grad/all_to_all | solution.py:37
  395.7 5.5 %attention_back.3 = bf16[1024,192]{1,0:T(8,128)(2,1)S(1)} custom-call(s32[1]{0:T(128)} %bitcast.45.core, bf16[1024,192]{1,0:T(8,128)(2,1)S(1)} %copy-done.20, f32[1024,1]{1,0:T(8,128)S(1)} %copy.184.log_totals, bf16[1024,1]{1,0:T(8,128)(2,1)S(1)} %copy-done.15, bf16[1,1024]{1,0:T(2,128)(2,1)S(1)} %select_n.372.seg_columns, ...), custom_call_target="tpu_custom_call" | custom-call | flops 671088640 | bytes 2097152 | tf_op jit(solution)/shard_map/attention_back/pallas_call | solution.py:411
  407.9 4.8 convolution_add_fusion
  412.9 6.9 %collective-permute-done.12 = bf16[1040,192]{0,1:T(8,128)(2,1)} collective-permute-done((bf16[1040,192]{0,1:T(8,128)(2,1)}, bf16[1040,192]{0,1:T(8,128)(2,1)}, u32[]{:S(2)}, u32[]{:S(2)}) %collective-permute-start.12) | collective-permute-done | bytes 399392 | tf_op jit(solution)/shard_map/swap_attend_grad/ppermute | solution.py:590
  421.5 6.0 %fusion.50 = (bf16[256]{0:T(256)(128)(2,1)S(1)}, bf16[2048,256]{1,0:T(8,128)(2,1)}) fusion(f32[2048,256]{1,0:T(8,128)} %convolution_add_fusion, bf16[2048,1024]{1,0:T(8,128)(2,1)} %all-gather.11.cloned.1.call-done, bf16[1,256,1024]{2,1,0:T(8,128)(2,1)S(1)} %copy-done.31), kind=kOutput, calls=%fused_computation.168 | convolution fusion | flops 1079508736 | bytes 7864832 | tf_op jit(solution)/shard_map/block_weight_grads/dot_general | solution.py:25
  441.0 12.4 %all-to-all-start.9 = ((bf16[64,16,768]{2,1,0:T(8,128)(2,1)}), bf16[64,16,768]{2,1,0:T(8,128)(2,1)}, u32[]{:S(2)}, u32[]{:S(2)}) async-start(bf16[64,16,768]{2,1,0:T(8,128)(2,1)} %bitcast.268), calls=%async_computation.9 | async-start | bytes 3145728 | tf_op jit(solution)/shard_map/sum_attend_expand_grads/all_to_all | solution.py:37
  454.8 22.3 %all-to-all-done.9 = bf16[64,16,768]{2,1,0:T(8,128)(2,1)} async-done(((bf16[64,16,768]{2,1,0:T(8,128)(2,1)}), bf16[64,16,768]{2,1,0:T(8,128)(2,1)}, u32[]{:S(2)}, u32[]{:S(2)}) %all-to-all-start.9) | async-done | bytes 1572896 | tf_op jit(solution)/shard_map/sum_attend_expand_grads/all_to_all | solution.py:37
  483.7 8.2 %all-to-all-done.10 = bf16[4,80,1024]{2,1,0:T(8,128)(2,1)S(1)} async-done(((bf16[4,80,1024]{2,1,0:T(8,128)(2,1)}), bf16[4,80,1024]{2,1,0:T(8,128)(2,1)S(1)}, u32[]{:S(2)}, u32[]{:S(2)}) %all-to-all-start.10) | async-done | bytes 655392 | tf_op jit(solution)/shard_map/sum_contract/all_to_all | solution.py:37
  506.3 11.5 %all-to-all-done.11 = bf16[32,32,384]{2,1,0:T(8,128)(2,1)S(1)} async-done(((bf16[32,32,384]{2,1,0:T(8,128)(2,1)}), bf16[32,32,384]{2,1,0:T(8,128)(2,1)S(1)}, u32[]{:S(2)}, u32[]{:S(2)}) %all-to-all-start.11) | async-done | bytes 786464 | tf_op jit(solution)/shard_map/grad_tokens_0/all_to_all | solution.py:37
  517.8 5.9 %grad_tokens_0.1 = (f32[128,1024]{1,0:T(8,128)S(1)}, bf16[128,1024]{1,0:T(8,128)(2,1)}) custom-call(bf16[2,2,4,2,32,384]{5,4,3,2,1,0:T(8,128)(2,1)S(1)} %bitcast.247, bf16[1024,3072]{1,0:T(8,128)(2,1)} %all-gather.7.cloned.1.call-done.weight, f32[128,1024]{1,0:T(8,128)S(1)} %collective-permute-done.9.grad_residual), custom_call_target="tpu_custom_call" | custom-call | flops 805306368 | bytes 8388608 | tf_op jit(solution)/shard_map/grad_tokens_0/pallas_call | solution.py:346
  532.5 6.4 %collective-permute-done.14 = f32[128,1024]{1,0:T(8,128)S(1)} collective-permute-done((f32[128,1024]{1,0:T(8,128)S(1)}, f32[128,1024]{1,0:T(8,128)S(1)}, u32[]{:S(2)}, u32[]{:S(2)}) %collective-permute-start.14) | collective-permute-done | bytes 524320 | tf_op jit(solution)/shard_map/grad_tokens_0/ppermute | solution.py:654
  (322 shorter events, 150.3 us)
Async XLA Ops:
  7.2 143.3 %all-gather.15.cloned.1.call-start = ((), (), s32[]{:S(2)}) async-start(), calls=%async_computation.16 | async-start | bytes 19169280 | tf_op jit(solution)/shard_map/gather_block_weights/all_gather | solution.py:462
  18.8 31.5 %copy-start = (bf16[2,1,64,1024]{3,2,1,0:T(8,128)(2,1)S(1)}, bf16[2,1,64,1024]{3,2,1,0:T(8,128)(2,1)}, u32[]{:S(2)}) copy-start(bf16[2,1,64,1024]{3,2,1,0:T(8,128)(2,1)} %param.10) | copy-start | bytes 786436
  18.8 31.5 %all-to-all-start = ((bf16[32,80,192]{2,1,0:T(8,128)(2,1)}), bf16[32,80,192]{2,1,0:T(8,128)(2,1)S(1)}, u32[]{:S(2)}, u32[]{:S(2)}) async-start(bf16[32,80,192]{2,1,0:T(8,128)(2,1)} %bitcast.5), calls=%async_computation | async-start | bytes 2621440 | tf_op jit(solution)/shard_map/head_weights/all_to_all | solution.py:37
  29.8 132.7 %collective-permute-start.7 = (bf16[64,3072]{1,0:T(8,128)(2,1)}, bf16[64,3072]{1,0:T(8,128)(2,1)}, u32[]{:S(2)}, u32[]{:S(2)}) collective-permute-start(bf16[64,3072]{1,0:T(8,128)(2,1)} %reshape.434), channel_id=1, source_target_pairs={{0,64},{64,0},{1,65},{65,1},{2,66},{66,2},{3,67},{67,3},{4,68},{68... | collective-permute-start | bytes 1179656 | tf_op jit(solution)/shard_map/gather_attend_weight/ppermute | solution.py:534
  51.4 28.8 %all-to-all-start.1 = ((bf16[16,32,1024]{2,1,0:T(8,128)(2,1)}), bf16[16,32,1024]{2,1,0:T(8,128)(2,1)S(1)}, u32[]{:S(2)}, u32[]{:S(2)}) async-start(bf16[16,32,1024]{2,1,0:T(8,128)(2,1)} %bitcast.271), calls=%async_computation.1 | async-start | bytes 2097152 | tf_op jit(solution)/shard_map/sequence_tokens/all_to_all | solution.py:37
  80.2 4.3 collective-permute-start
  91.5 1.4 collective-permute-start.1
  93.8 16.0 %all-to-all-start.2 = ((bf16[32,32,128]{2,1,0:T(8,128)(2,1)}), bf16[32,32,128]{2,1,0:T(8,128)(2,1)S(1)}, u32[]{:S(2)}, u32[]{:S(2)}) async-start(bf16[32,32,128]{2,1,0:T(8,128)(2,1)} %bitcast.22), calls=%async_computation.2 | async-start | bytes 524288 | tf_op jit(solution)/shard_map/context_out/all_to_all | solution.py:37
  97.7 212.6 %all-gather.7.cloned.1.call-start = ((), (), s32[]{:S(2)}) async-start(), calls=%async_computation.12 | async-start | bytes 6684672 | tf_op jit(solution)/shard_map/gather_attend_weight/all_gather | solution.py:536
  162.5 245.4 %all-gather.9.cloned.1.call-start = ((), (), s32[]{:S(2)}) async-start(), calls=%async_computation.13 | async-start | bytes 4456448 | tf_op jit(solution)/shard_map/gather_first/all_gather | solution.py:544
  162.6 7.7 %collective-permute-start.2 = (bf16[128,1024]{1,0:T(8,128)(2,1)S(1)}, bf16[128,1024]{1,0:T(8,128)(2,1)S(1)}, u32[]{:S(2)}, u32[]{:S(2)}) collective-permute-start(bf16[128,1024]{1,0:T(8,128)(2,1)S(1)} %get-tuple-element.55), channel_id=1, source_target_pairs={{0,64},{1,65},{2,66},{3,67},{4,68},{5,69},{6,70},{7,71},{8,72},{9,... | collective-permute-start | bytes 786440 | tf_op jit(solution)/shard_map/to_next_section/ppermute | solution.py:530
  196.3 2.7 collective-permute-start.3
  205.0 1.4 collective-permute-start.4
  250.9 23.2 %collective-permute-start.5 = (f32[128,1024]{1,0:T(8,128)}, f32[128,1024]{1,0:T(8,128)}, u32[]{:S(2)}, u32[]{:S(2)}) collective-permute-start(f32[128,1024]{1,0:T(8,128)} %get-tuple-element.61), channel_id=1, source_target_pairs={{64,0},{65,1},{66,2},{67,3},{68,4},{69,5},{70,6},{71,7},{72,8},{73... | collective-permute-start | bytes 1572872 | tf_op jit(solution)/shard_map/residual_to_other_section/ppermute | solution.py:552
  252.2 21.1 %all-to-all-start.5 = ((bf16[32,64,128]{2,1,0:T(8,128)(2,1)}), bf16[32,64,128]{2,1,0:T(8,128)(2,1)S(1)}, u32[]{:S(2)}, u32[]{:S(2)}) async-start(bf16[32,64,128]{2,1,0:T(8,128)(2,1)} %bitcast.254), calls=%async_computation.5 | async-start | bytes 1048576 | tf_op jit(solution)/shard_map/grad_context_in/all_to_all | solution.py:37
  261.6 23.9 %copy-start.14 = (bf16[1024,1]{1,0:T(8,128)(2,1)}, bf16[1024,1]{1,0:T(8,128)(2,1)S(1)}, u32[]{:S(2)}) copy-start(bf16[1024,1]{1,0:T(8,128)(2,1)S(1)} %select_n.403.seg_rows) | copy-start | bytes 6148
  282.8 2.7 collective-permute-start.6
  290.4 19.9 %all-to-all-start.6 = ((bf16[32,32,384]{2,1,0:T(8,128)(2,1)}), bf16[32,32,384]{2,1,0:T(8,128)(2,1)}, u32[]{:S(2)}, u32[]{:S(2)}) async-start(bf16[32,32,384]{2,1,0:T(8,128)(2,1)} %bitcast.274), calls=%async_computation.6 | async-start | bytes 1572864 | tf_op jit(solution)/shard_map/grad_tokens_1/all_to_all | solution.py:37
  295.9 125.5 %all-gather.11.cloned.1.call-start = ((), (), s32[]{:S(2)}) async-start(), calls=%async_computation.14 | async-start | bytes 4456448 | tf_op jit(solution)/shard_map/gather_grad_mlp/all_gather | solution.py:561
  335.3 11.3 %collective-permute-start.8 = (bf16[1024,512]{1,0:T(8,128)(2,1)}, bf16[1024,512]{1,0:T(8,128)(2,1)S(1)}, u32[]{:S(2)}, u32[]{:S(2)}) collective-permute-start(bf16[1024,512]{1,0:T(8,128)(2,1)} %select_convert_fusion), channel_id=1, source_target_pairs={{0,4},{4,0},{8,12},{12,8},{16,20},{20,16},{24,28},{28,24},{32,36},... | collective-permute-start | bytes 3145736 | tf_op jit(solution)/shard_map/sum_output_grad/ppermute | solution.py:41
  335.7 29.0 %collective-permute-start.9 = (f32[128,1024]{1,0:T(8,128)}, f32[128,1024]{1,0:T(8,128)S(1)}, u32[]{:S(2)}, u32[]{:S(2)}) collective-permute-start(f32[128,1024]{1,0:T(8,128)} %copy-done.18), channel_id=1, source_target_pairs={{0,64},{1,65},{2,66},{3,67},{4,68},{5,69},{6,70},{7,71},{8,72},{9,... | collective-permute-start | bytes 1572872 | tf_op jit(solution)/shard_map/residual_to_other_section/ppermute | solution.py:567
  338.1 26.6 %all-to-all-start.7 = ((bf16[32,64,128]{2,1,0:T(8,128)(2,1)}), bf16[32,64,128]{2,1,0:T(8,128)(2,1)S(1)}, u32[]{:S(2)}, u32[]{:S(2)}) async-start(bf16[32,64,128]{2,1,0:T(8,128)(2,1)} %bitcast.253), calls=%async_computation.7 | async-start | bytes 1048576 | tf_op jit(solution)/shard_map/grad_context_in/all_to_all | solution.py:37
  342.4 35.2 %collective-permute-start.10 = (f32[128,1024]{1,0:T(8,128)S(1)}, f32[128,1024]{1,0:T(8,128)}, u32[]{:S(2)}, u32[]{:S(2)}) collective-permute-start(f32[128,1024]{1,0:T(8,128)S(1)} %copy-done.17), channel_id=1, source_target_pairs={{0,64},{1,65},{2,66},{3,67},{4,68},{5,69},{6,70},{7,71},{8,72},{9,... | collective-permute-start | bytes 1572872 | tf_op jit(solution)/shard_map/grad_tokens_1/ppermute | solution.py:556
  377.6 25.5 %all-to-all-start.8 = ((bf16[64,16,512]{2,1,0:T(8,128)(2,1)}), bf16[64,16,512]{2,1,0:T(8,128)(2,1)}, u32[]{:S(2)}, u32[]{:S(2)}) async-start(bf16[64,16,512]{2,1,0:T(8,128)(2,1)} %bitcast.57), calls=%async_computation.8 | async-start | bytes 2097152 | tf_op jit(solution)/shard_map/sum_output_grad/all_to_all | solution.py:37
  389.1 16.6 %collective-permute-start.11 = (bf16[1040,192]{0,1:T(8,128)(2,1)}, bf16[1040,192]{0,1:T(8,128)(2,1)}, u32[]{:S(2)}, u32[]{:S(2)}) collective-permute-start(bf16[1040,192]{0,1:T(8,128)(2,1)} %fusion.25), channel_id=1, source_target_pairs={{0,64},{1,65},{2,66},{3,67},{4,68},{5,69},{6,70},{7,71},{8,72},{9,... | collective-permute-start | bytes 1198088 | tf_op jit(solution)/shard_map/swap_attend_grad/ppermute | solution.py:573
  406.6 13.2 %collective-permute-start.12 = (bf16[1040,192]{0,1:T(8,128)(2,1)}, bf16[1040,192]{0,1:T(8,128)(2,1)}, u32[]{:S(2)}, u32[]{:S(2)}) collective-permute-start(bf16[1040,192]{0,1:T(8,128)(2,1)} %get-tuple-element.162), channel_id=1, source_target_pairs={{64,0},{65,1},{66,2},{67,3},{68,4},{69,5},{70,6},{71,7},{72,8},{73... | collective-permute-start | bytes 1198088 | tf_op jit(solution)/shard_map/swap_attend_grad/ppermute | solution.py:590
  441.0 36.1 %all-to-all-start.9 = ((bf16[64,16,768]{2,1,0:T(8,128)(2,1)}), bf16[64,16,768]{2,1,0:T(8,128)(2,1)}, u32[]{:S(2)}, u32[]{:S(2)}) async-start(bf16[64,16,768]{2,1,0:T(8,128)(2,1)} %bitcast.268), calls=%async_computation.9 | async-start | bytes 3145728 | tf_op jit(solution)/shard_map/sum_attend_expand_grads/all_to_all | solution.py:37
  479.5 12.5 %all-to-all-start.10 = ((bf16[4,80,1024]{2,1,0:T(8,128)(2,1)}), bf16[4,80,1024]{2,1,0:T(8,128)(2,1)S(1)}, u32[]{:S(2)}, u32[]{:S(2)}) async-start(bf16[4,80,1024]{2,1,0:T(8,128)(2,1)} %pad_maximum_fusion.4), calls=%async_computation.10 | async-start | bytes 1310720 | tf_op jit(solution)/shard_map/sum_contract/all_to_all | solution.py:37
  483.0 42.0 %all-gather.13.cloned.1.call-start = ((), (), s32[]{:S(2)}) async-start(), calls=%async_computation.15 | async-start | bytes 1966080 | tf_op jit(solution)/shard_map/gather_weight_grads/all_gather | solution.py:656
  492.9 4.3 collective-permute-start.13
  498.9 18.9 %all-to-all-start.11 = ((bf16[32,32,384]{2,1,0:T(8,128)(2,1)}), bf16[32,32,384]{2,1,0:T(8,128)(2,1)S(1)}, u32[]{:S(2)}, u32[]{:S(2)}) async-start(bf16[32,32,384]{2,1,0:T(8,128)(2,1)} %bitcast.79), calls=%async_computation.11 | async-start | bytes 1572864 | tf_op jit(solution)/shard_map/grad_tokens_0/all_to_all | solution.py:37
  523.7 15.2 %collective-permute-start.14 = (f32[128,1024]{1,0:T(8,128)S(1)}, f32[128,1024]{1,0:T(8,128)S(1)}, u32[]{:S(2)}, u32[]{:S(2)}) collective-permute-start(f32[128,1024]{1,0:T(8,128)S(1)} %get-tuple-element.93), channel_id=1, source_target_pairs={{64,0},{65,1},{66,2},{67,3},{68,4},{69,5},{70,6},{71,7},{72,8},{73... | collective-permute-start | bytes 1572872 | tf_op jit(solution)/shard_map/grad_tokens_0/ppermute | solution.py:654
  (36 other events, 172.8 us)
Sparse Core Ops, SparseCore 0:
  13.9 136.5 all-gather.14
  162.7 72.8 all-gather.6
  238.0 54.5 all-gather.8
  317.7 64.0 all-gather.10
  493.0 25.3 all-gather.12

commit v8 on v6

--- a/solution.py
+++ b/solution.py
@@ -323,7 +323,7 @@
     )(grad, gathered, gathered, gathered, params, residual, inner, second)
 
 
-def grad_tokens_kernel(got, weight, grad_residual, result, rounded, total):
+def grad_tokens_kernel(got, weight, grad_residual, rounded, total):
     step = pl.program_id(0)
     left = jnp.concatenate([got[0, :, p].reshape(128, 384) for p in range(2)], 1)
     product = times_transposed(left, weight[...])
@@ -338,7 +338,6 @@
 
     @pl.when(step == 3)
     def finish():
-        result[...] = total[...]
         rounded[...] = total[...].astype(LOW)
 
 
@@ -351,8 +350,8 @@
             pl.BlockSpec((1024, 768), lambda i: (0, i)),
             full(128, 1024),
         ],
-        out_specs=[full(128, 1024), full(128, 1024)],
-        out_shape=[ROWS_F32, ROWS_LOW],
+        out_specs=full(128, 1024),
+        out_shape=ROWS_LOW,
         scratch_shapes=[pltpu.VMEM((128, 1024), jnp.float32)],
         compiler_params=BLOCK_PARAMS,
         cost_estimate=pl.CostEstimate(
@@ -552,8 +551,8 @@
         arrived_1 = lax.ppermute(grad_residual, "section", [(1, 0)])
     grad_packed_1, arrived_1 = attention_back(1, grad_context, kept_1, arrived_1)
     with jax.named_scope("grad_tokens_1"):
-        result_1, rounded = grad_tokens(send_tokens(grad_packed_1, 3), other_attend, arrived_1)
-        grad_tokens_1 = lax.ppermute(result_1, "section", [(0, 1)])
+        rounded = grad_tokens(send_tokens(grad_packed_1, 3), other_attend, arrived_1)
+        grad_tokens_1 = lax.ppermute(rounded, "section", [(0, 1)])
     own_grad = jnp.where(on_first, rounded, last_grad)
     with jax.named_scope("gather_grad_mlp"):
         grad_mlp = normed_back(own_grad.astype(jnp.float32), saved[3], params[5:6])[0].astype(LOW)
@@ -564,7 +563,7 @@
             own_grad, saved, gathered, params
         )
     with jax.named_scope("residual_to_other_section"):
-        arrived_0 = lax.ppermute(grad_residual, "section", [(0, 1)])
+        arrived_0 = lax.ppermute(grad_attn, "section", [(0, 1)])
     late_tokens, late_packed, late_gathered, grad_context = lax.optimization_barrier(
         (kept_1[0], grad_packed_1, gathered, grad_context)
     )
@@ -582,6 +581,7 @@
 
     with jax.named_scope("sum_output_grad"):
         output_got = exchange(output_grad.reshape(64, 16, 512), REST)
+        output_got, grad_packed = lax.optimization_barrier((output_got, grad_packed))
     with jax.named_scope("swap_attend_grad"):
         part_0 = attend_part(kept_0[0], grad_packed)
         take_0 = lax.ppermute(part_0, "section", [(1, 0)])
@@ -601,7 +601,6 @@
         vectors = vectors.astype(LOW)
     with jax.named_scope("sum_attend_grad"):
         parts = jnp.concatenate([attend_grad, vectors], 1)
-        output_got, parts = lax.optimization_barrier((output_got, parts))
         got = exchange(parts.reshape(64, 16, 512), REST)
     with jax.named_scope("block_weight_grads"):
         expand_part = lax.dynamic_slice(
@@ -628,7 +627,9 @@
             [contract_grad.reshape(4, 64, 1024), jnp.broadcast_to(extra, (4, 16, 1024))], 1
         )
     with jax.named_scope("sum_expand_grad"):
-        got, expand_grad, rows = lax.optimization_barrier((got, expand_grad, rows))
+        got, expand_grad, rows, arrived_0, grad_tokens_1 = lax.optimization_barrier(
+            (got, expand_grad, rows, arrived_0, grad_tokens_1)
+        )
         expand_got = exchange(expand_grad.reshape(64, 16, 256), REST)
         expand_got, rows = lax.optimization_barrier((expand_got, rows))
     with jax.named_scope("sum_contract"):
@@ -648,14 +649,25 @@
         owned = jnp.concatenate([got_attend, got_output, got_expand, *contract_rows], 1)
     with jax.named_scope("grad_tokens_0"):
         late_packed, owned = lax.optimization_barrier((grad_packed, owned))
-        result_0, unused = grad_tokens(send_tokens(late_packed, 3), other_attend, arrived_0)
-        grad_tokens_0 = lax.ppermute(result_0, "section", [(1, 0)])
+        rounded = grad_tokens(
+            send_tokens(late_packed, 3), other_attend, arrived_0.astype(jnp.float32)
+        )
+        grad_tokens_0 = lax.ppermute(rounded, "section", [(1, 0)])
     with jax.named_scope("gather_weight_grads"):
         totals = lax.all_gather(owned, "replica", axis=0, tiled=True)
         contract_total = totals[:, 8192:].reshape(4, 16, 4, 1024).transpose(0, 2, 1, 3)
         contract_total = contract_total.reshape(1, 256, 1024).astype(jnp.float32)
         totals = totals[None, :, :8192].astype(jnp.float32)
-    input_grad = jnp.where(on_first, grad_tokens_0, grad_tokens_1).reshape(1, 2, 1, 64, 1024)
+    attend_total = totals[:, :, :3072]
+    output_total = totals[:, :, 3072:4096]
+    expand_total = totals[:, :, 4096:]
+    grad_tokens_0, attend_total, output_total, expand_total, contract_total = (
+        lax.optimization_barrier(
+            (grad_tokens_0, attend_total, output_total, expand_total, contract_total)
+        )
+    )
+    input_grad = jnp.where(on_first, grad_tokens_0, grad_tokens_1).astype(jnp.float32)
+    input_grad = input_grad.reshape(1, 2, 1, 64, 1024)
     mlp_own = lax.dynamic_slice_in_dim(got_contract[65], shard * 64, 64, 0)
     biases_grad = jnp.stack(
         [
@@ -670,9 +682,9 @@
     return (
         layer_output,
         input_grad,
-        totals[:, :, :3072],
-        totals[:, :, 3072:4096],
-        totals[:, :, 4096:],
+        attend_total,
+        output_total,
+        expand_total,
         contract_total,
         biases_grad[None],
         got_contract[None, 64, :256],

time: 540 us -> 530 us (0.981)
    ppermute x3, waiting for transfers between devices: 24.5 us -> 0.87 us  [the longest x1 0.86 us: on_device(): grad_tokens_0 = lax.ppermute(rounded, 'section', [(1, 0)])]
    ppermute x1, waiting for transfers between devices: 0.01 us -> 7.2 us  [on_device(): take_0 = lax.ppermute(part_0, 'section', [(1, 0)])]
    ppermute x1, waiting for transfers between devices: 4.99 us -> 10.8 us  [on_device(): take_1 = lax.ppermute(part_1, 'section', [(0, 1)])]
    all_to_all x11, waiting for transfers between devices: 117 us -> 123 us  [exchange(): return lax.all_to_all(value, axes, 0, 0, tiled=True)]
  transfers between devices with their start and end apart: 31 -> 31, of which waited for: 21 -> 22; matrix products, arithmetic and copies ran while one was open for 14% -> 16% of each run, Pallas kernels for 14% -> 14%
where the time goes in v8:
time: 530 us; the launch traced here: 519 us
  waiting for transfers between devices  197 us (37%)
  starting transfers between devices  91 us (17%)
  Pallas kernels  73.2 us (14%)
  local copies, waits for them, and re-layouts  49 us (9%)
  blocking collectives  41.7 us (8%)
  matrix products  27.4 us (5%)
  other arithmetic  24.6 us (5%)
  between operations  15.5 us (3%)
    all_to_all x11, waiting for transfers between devices, exchange(): return lax.all_to_all(value, axes, 0, 0, tiled=True)  123 us
    all_to_all x11, starting transfers between devices, exchange(): return lax.all_to_all(value, axes, 0, 0, tiled=True)  68.9 us
    all_to_all x2, blocking collectives, exchange(): return lax.all_to_all(value, axes, 0, 0, tiled=True)  41.7 us
    all_gather x1, waiting for transfers between devices, on_device(): lax.all_gather(quarter, REST, axis=0, tiled=False).reshape(16, 576, 1024)  40.8 us
    pallas_call x2, Pallas kernels, block_back(): pl.pallas_call(backward_kernel, grid=(PARTS + 1,), in_specs=[full(128, 10...  28.3 us
    pallas_call x2, Pallas kernels, block_forward(): pl.pallas_call(forward_kernel, grid=(PARTS + 1,), in_specs=[full(128, 102...  23.1 us
    unnamed x96, local copies, waits for them, and re-layouts  18.2 us
    dot_general x5, matrix products, transposed_times(): lax.dot_general(left, right, (((0,), (0,)), ((), ())), preferred_element_...  11.6 us
  transfers between devices with their start and end apart: 31, of which 22 were waited for; matrix products, arithmetic and copies ran while one was open for 16% of the time, Pallas kernels for 14%

profile of v8, /device:TPU:1, one launch (start us, length us, event | category | flops | bytes accessed | tf_op | source)
XLA Modules:
  0.0 519.3 jit_solution(3403350224504545257)
XLA Ops:
  18.8 9.6 %all-to-all-start = ((bf16[32,80,192]{2,1,0:T(8,128)(2,1)}), bf16[32,80,192]{2,1,0:T(8,128)(2,1)S(1)}, u32[]{:S(2)}, u32[]{:S(2)}) async-start(bf16[32,80,192]{2,1,0:T(8,128)(2,1)} %bitcast.5), calls=%async_computation | async-start | bytes 2621440 | tf_op jit(solution)/shard_map/head_weights/all_to_all | solution.py:37
  31.3 19.0 %all-to-all-done = bf16[32,80,192]{2,1,0:T(8,128)(2,1)S(1)} async-done(((bf16[32,80,192]{2,1,0:T(8,128)(2,1)}), bf16[32,80,192]{2,1,0:T(8,128)(2,1)S(1)}, u32[]{:S(2)}, u32[]{:S(2)}) %all-to-all-start) | async-done | bytes 983072 | tf_op jit(solution)/shard_map/head_weights/all_to_all | solution.py:37
  51.4 4.7 all-to-all-start.1
  56.5 23.7 %all-to-all-done.1 = bf16[16,32,1024]{2,1,0:T(8,128)(2,1)S(1)} async-done(((bf16[16,32,1024]{2,1,0:T(8,128)(2,1)}), bf16[16,32,1024]{2,1,0:T(8,128)(2,1)S(1)}, u32[]{:S(2)}, u32[]{:S(2)}) %all-to-all-start.1) | async-done | bytes 1048608 | tf_op jit(solution)/shard_map/sequence_tokens/all_to_all | solution.py:37
  98.4 11.4 %all-to-all-done.2 = bf16[32,32,128]{2,1,0:T(8,128)(2,1)S(1)} async-done(((bf16[32,32,128]{2,1,0:T(8,128)(2,1)}), bf16[32,32,128]{2,1,0:T(8,128)(2,1)S(1)}, u32[]{:S(2)}, u32[]{:S(2)}) %all-to-all-start.2) | async-done | bytes 262176 | tf_op jit(solution)/shard_map/context_out/all_to_all | solution.py:37
  109.8 40.8 %all-gather.15.cloned.1.call-done = bf16[9216,1024]{1,0:T(8,128)(2,1)} async-done(((bf16[144,1024]{1,0:T(8,128)(2,1)}), bf16[9216,1024]{1,0:T(8,128)(2,1)}) %all-gather.15.cloned.1.call-update) | async-done | bytes 18874384 | tf_op jit(solution)/shard_map/gather_block_weights/all_gather | solution.py:461
  150.5 12.0 %block_0.1 = (bf16[128,1024]{1,0:T(8,128)(2,1)S(1)}, f32[128,1024]{1,0:T(8,128)}, bf16[128,1024]{1,0:T(8,128)(2,1)}, f32[128,4096]{1,0:T(8,128)}, f32[128,1024]{1,0:T(8,128)}, /*index=5*/bf16[128,1024]{1,0:T(8,128)(2,1)}) custom-call(bf16[128,1024]{1,0:T(8,128)(2,1)S(1)} %bitcast.252, bf16[2,2,4,2,32,128]{5,4,3,2,1,0:T(8,128)(2,1)S(1)} %bitcast.253, ...), custom_call_target="tpu_custom_call" | custom-call | flops 2415919104 | bytes 25165824 | tf_op jit(solution)/shard_map/block_0/pallas_call | solution.py:197
  164.8 5.5 %collective-permute-done.2 = bf16[128,1024]{1,0:T(8,128)(2,1)S(1)} collective-permute-done((bf16[128,1024]{1,0:T(8,128)(2,1)S(1)}, bf16[128,1024]{1,0:T(8,128)(2,1)S(1)}, u32[]{:S(2)}, u32[]{:S(2)}) %collective-permute-start.2) | collective-permute-done | bytes 262176 | tf_op jit(solution)/shard_map/to_next_section/ppermute | solution.py:529
  171.2 25.1 %all_to_all.65 = bf16[16,32,1024]{2,1,0:T(8,128)(2,1)S(1)} all-to-all(bf16[16,32,1024]{2,1,0:T(8,128)(2,1)S(1)} %bitcast.274), channel_id=1, replica_groups=mesh['section'=2,'shard'=16,'replica'=4] {'shard'}, dimensions={0} | all-to-all | bytes 2097152 | tf_op jit(solution)/shard_map/sequence_tokens/all_to_all | solution.py:37
  206.7 16.6 %all_to_all.66 = bf16[32,32,128]{2,1,0:T(8,128)(2,1)S(1)} all-to-all(bf16[32,32,128]{2,1,0:T(8,128)(2,1)S(1)} %bitcast.296), channel_id=1, replica_groups=mesh['section'=2,'shard'=16,'replica'=4] {'section','shard'}, dimensions={0} | all-to-all | bytes 524288 | tf_op jit(solution)/shard_map/context_out/all_to_all | solution.py:37
  223.3 11.1 %block_1.1 = (bf16[128,1024]{1,0:T(8,128)(2,1)}, f32[128,1024]{1,0:T(8,128)S(1)}, bf16[128,1024]{1,0:T(8,128)(2,1)S(1)}, f32[128,4096]{1,0:T(8,128)S(1)}, f32[12...) custom-call(bf16[128,1024]{1,0:T(8,128)(2,1)S(1)} %copy-done.5, ...), custom_call_target="tpu_custom_call" | custom-call | flops 2415919104 | bytes 25165824 | tf_op jit(solution)/shard_map/block_1/pallas_call | solution.py:197
  235.8 14.3 %block_back_1.1 = (f32[128,1024]{1,0:T(8,128)}, bf16[128,1024]{1,0:T(8,128)(2,1)}, bf16[2,2,4,2,64,128]{5,4,3,2,1,0:T(8,128)(2,1)S(1)}, f32[8,1024]{1,0:T(8,128)}) custom-call(bf16[128,1024]{1,0:T(8,128)(2,1)S(1)} %bitcast.255, bf16[16,576,1024]{2,1,0:T(8,128)(2,1)} %bitcast.264, bf16[16,576,1024]{2,1,0:T(8,128)(2,1)} %bitcast.265, ...), custom_call_target="tpu_custom_call" | custom-call | flops 2415919104 | bytes 25165824 | tf_op jit(solution)/shard_map/block_back_1/pallas_call | solution.py:292
  252.2 8.9 %all-to-all-start.5 = ((bf16[32,64,128]{2,1,0:T(8,128)(2,1)}), bf16[32,64,128]{2,1,0:T(8,128)(2,1)S(1)}, u32[]{:S(2)}, u32[]{:S(2)}) async-start(bf16[32,64,128]{2,1,0:T(8,128)(2,1)} %bitcast.257), calls=%async_computation.5 | async-start | bytes 1048576 | tf_op jit(solution)/shard_map/grad_context_in/all_to_all | solution.py:37
  262.7 10.6 %all-to-all-done.5.got = bf16[32,64,128]{2,1,0:T(8,128)(2,1)S(1)} async-done(((bf16[32,64,128]{2,1,0:T(8,128)(2,1)}), bf16[32,64,128]{2,1,0:T(8,128)(2,1)S(1)}, u32[]{:S(2)}, u32[]{:S(2)}) %all-to-all-start.5) | async-done | bytes 524320 | tf_op jit(solution)/shard_map/grad_context_in/all_to_all | solution.py:37
  277.2 5.5 %attention_back.2 = bf16[1024,192]{1,0:T(8,128)(2,1)S(1)} custom-call(s32[1]{0:T(128)} %bitcast.45.core, bf16[1024,192]{1,0:T(8,128)(2,1)S(1)} %copy-done.23, f32[1024,1]{1,0:T(8,128)S(1)} %copy-done.12, bf16[1024,1]{1,0:T(8,128)(2,1)S(1)} %select_n.401.seg_rows, bf16[1,1024]{1,0:T(2,128)(2,1)S(1)} %select_n.370.seg_columns, bf16[32,64,128]{2,1,0:T(8,128)(2,1)S(1)} %copy-done.10), custom_call_target="tpu_custom_call" | custom-call | flops 671088640 | bytes 2097152 | tf_op jit(solution)/shard_map/attention_back/pallas_call | solution.py:410
  290.3 5.2 all-to-all-start.6
  296.0 13.8 %all-to-all-done.6 = bf16[32,32,384]{2,1,0:T(8,128)(2,1)} async-done(((bf16[32,32,384]{2,1,0:T(8,128)(2,1)}), bf16[32,32,384]{2,1,0:T(8,128)(2,1)}, u32[]{:S(2)}, u32[]{:S(2)}) %all-to-all-start.6) | async-done | bytes 786464 | tf_op jit(solution)/shard_map/grad_tokens_1/all_to_all | solution.py:37
  309.8 5.5 %grad_tokens_1.1 = bf16[128,1024]{1,0:T(8,128)(2,1)S(1)} custom-call(bf16[2,2,4,2,32,384]{5,4,3,2,1,0:T(8,128)(2,1)} %bitcast.53.got, bf16[1024,3072]{1,0:T(8,128)(2,1)} %all-gather.7.cloned.1.call-done.weight, f32[128,1024]{1,0:T(8,128)} %collective-permute-done.5.grad_residual), custom_call_target="tpu_custom_call" | custom-call | flops 805306368 | bytes 8388608 | tf_op jit(solution)/shard_map/grad_tokens_1/pallas_call | solution.py:345
  318.1 14.1 %block_back_0.1 = (f32[128,1024]{1,0:T(8,128)}, bf16[128,1024]{1,0:T(8,128)(2,1)S(1)}, bf16[2,2,4,2,64,128]{5,4,3,2,1,0:T(8,128)(2,1)S(1)}, f32[8,1024]{1,0:T(8,128)S(1)}) custom-call(bf16[128,1024]{1,0:T(8,128)(2,1)S(1)} %get-tuple-element.60.grad, bf16[16,576,1024]{2,1,0:T(8,128)(2,1)} %bitcast.267, bf16[16,576,1024]{2,1,0:T(8,128)(2,1)} %bitcast.268, ...), custom_call_target="tpu_custom_call" | custom-call | flops 2415919104 | bytes 25165824 | tf_op jit(solution)/shard_map/block_back_0/pallas_call | solution.py:292
  343.6 7.7 %all-to-all-done.7.got = bf16[32,64,128]{2,1,0:T(8,128)(2,1)S(1)} async-done(((bf16[32,64,128]{2,1,0:T(8,128)(2,1)}), bf16[32,64,128]{2,1,0:T(8,128)(2,1)S(1)}, u32[]{:S(2)}, u32[]{:S(2)}) %all-to-all-start.7) | async-done | bytes 524320 | tf_op jit(solution)/shard_map/grad_context_in/all_to_all | solution.py:37
  351.3 6.3 %all-to-all-start.8 = ((bf16[64,16,512]{2,1,0:T(8,128)(2,1)}), bf16[64,16,512]{2,1,0:T(8,128)(2,1)S(1)}, u32[]{:S(2)}, u32[]{:S(2)}) async-start(bf16[64,16,512]{2,1,0:T(8,128)(2,1)} %bitcast.57), calls=%async_computation.8 | async-start | bytes 2097152 | tf_op jit(solution)/shard_map/sum_output_grad/all_to_all | solution.py:37
  370.2 5.5 %attention_back.3 = bf16[1024,192]{1,0:T(8,128)(2,1)S(1)} custom-call(s32[1]{0:T(128)} %bitcast.45.core, bf16[1024,192]{1,0:T(8,128)(2,1)S(1)} %copy-done.21, f32[1024,1]{1,0:T(8,128)S(1)} %copy.180.log_totals, bf16[1024,1]{1,0:T(8,128)(2,1)S(1)} %copy-done.19, bf16[1,1024]{1,0:T(2,128)(2,1)S(1)} %select_n.370.seg_columns, ...), custom_call_target="tpu_custom_call" | custom-call | flops 671088640 | bytes 2097152 | tf_op jit(solution)/shard_map/attention_back/pallas_call | solution.py:410
  378.7 10.8 %collective-permute-done.9 = bf16[1040,192]{0,1:T(8,128)(2,1)} collective-permute-done((bf16[1040,192]{0,1:T(8,128)(2,1)}, bf16[1040,192]{0,1:T(8,128)(2,1)}, u32[]{:S(2)}, u32[]{:S(2)}) %collective-permute-start.9) | collective-permute-done | bytes 399392 | tf_op jit(solution)/shard_map/swap_attend_grad/ppermute | solution.py:572
  391.7 4.8 convolution_add_fusion
  397.7 7.2 %collective-permute-done.10 = bf16[1040,192]{0,1:T(8,128)(2,1)} collective-permute-done((bf16[1040,192]{0,1:T(8,128)(2,1)}, bf16[1040,192]{0,1:T(8,128)(2,1)}, u32[]{:S(2)}, u32[]{:S(2)}) %collective-permute-start.10) | collective-permute-done | bytes 399392 | tf_op jit(solution)/shard_map/swap_attend_grad/ppermute | solution.py:587
  408.1 11.4 %all-to-all-start.9 = ((bf16[64,16,512]{2,1,0:T(8,128)(2,1)}), bf16[64,16,512]{2,1,0:T(8,128)(2,1)S(1)}, u32[]{:S(2)}, u32[]{:S(2)}) async-start(bf16[64,16,512]{2,1,0:T(8,128)(2,1)} %bitcast.62), calls=%async_computation.9 | async-start | bytes 2097152 | tf_op jit(solution)/shard_map/sum_attend_grad/all_to_all | solution.py:37
  419.5 5.4 %fusion.50 = (bf16[256]{0:T(256)(128)(2,1)S(1)}, bf16[2048,256]{1,0:T(8,128)(2,1)S(1)}) fusion(f32[2048,256]{1,0:T(8,128)} %convolution_add_fusion, bf16[2048,1024]{1,0:T(8,128)(2,1)} %all-gather.11.cloned.1.call-done, bf16[1,256,1024]{2,1,0:T(8,128)(2,1)S(1)} %copy-done.33), kind=kOutput, calls=%fused_computation.167 | convolution fusion | flops 1079508736 | bytes 7864832 | tf_op jit(solution)/shard_map/block_weight_grads/dot_general | solution.py:25
  438.0 7.7 %all-to-all-start.10 = ((bf16[64,16,256]{2,1,0:T(8,128)(2,1)}), bf16[64,16,256]{2,1,0:T(8,128)(2,1)S(1)}, u32[]{:S(2)}, u32[]{:S(2)}) async-start(bf16[64,16,256]{2,1,0:T(8,128)(2,1)} %bitcast.71), calls=%async_computation.10 | async-start | bytes 1048576 | tf_op jit(solution)/shard_map/sum_expand_grad/all_to_all | solution.py:37
  446.5 12.5 %all-to-all-done.10 = bf16[64,16,256]{2,1,0:T(8,128)(2,1)S(1)} async-done(((bf16[64,16,256]{2,1,0:T(8,128)(2,1)}), bf16[64,16,256]{2,1,0:T(8,128)(2,1)S(1)}, u32[]{:S(2)}, u32[]{:S(2)}) %all-to-all-start.10) | async-done | bytes 524320 | tf_op jit(solution)/shard_map/sum_expand_grad/all_to_all | solution.py:37
  462.7 9.5 %all-to-all-done.11 = bf16[4,80,1024]{2,1,0:T(8,128)(2,1)S(1)} async-done(((bf16[4,80,1024]{2,1,0:T(8,128)(2,1)}), bf16[4,80,1024]{2,1,0:T(8,128)(2,1)S(1)}, u32[]{:S(2)}, u32[]{:S(2)}) %all-to-all-start.11) | async-done | bytes 655392 | tf_op jit(solution)/shard_map/sum_contract/all_to_all | solution.py:37
  485.0 11.5 %all-to-all-done.12 = bf16[32,32,384]{2,1,0:T(8,128)(2,1)S(1)} async-done(((bf16[32,32,384]{2,1,0:T(8,128)(2,1)}), bf16[32,32,384]{2,1,0:T(8,128)(2,1)S(1)}, u32[]{:S(2)}, u32[]{:S(2)}) %all-to-all-start.12) | async-done | bytes 786464 | tf_op jit(solution)/shard_map/grad_tokens_0/all_to_all | solution.py:37
  496.5 5.2 %grad_tokens_0.1 = bf16[128,1024]{1,0:T(8,128)(2,1)S(1)} custom-call(bf16[2,2,4,2,32,384]{5,4,3,2,1,0:T(8,128)(2,1)S(1)} %bitcast.250, bf16[1024,3072]{1,0:T(8,128)(2,1)} %all-gather.7.cloned.1.call-done.weight, f32[128,1024]{1,0:T(8,128)S(1)} %convert_element_type.200.grad_residual), custom_call_target="tpu_custom_call" | custom-call | flops 805306368 | bytes 8388608 | tf_op jit(solution)/shard_map/grad_tokens_0/pallas_call | solution.py:345
  (327 shorter events, 141.2 us)
Async XLA Ops:
  7.2 143.4 %all-gather.15.cloned.1.call-start = ((), (), s32[]{:S(2)}) async-start(), calls=%async_computation.17 | async-start | bytes 19169280 | tf_op jit(solution)/shard_map/gather_block_weights/all_gather | solution.py:461
  18.8 31.5 %copy-start = (bf16[2,1,64,1024]{3,2,1,0:T(8,128)(2,1)S(1)}, bf16[2,1,64,1024]{3,2,1,0:T(8,128)(2,1)}, u32[]{:S(2)}) copy-start(bf16[2,1,64,1024]{3,2,1,0:T(8,128)(2,1)} %param.10) | copy-start | bytes 786436
  18.8 31.5 %all-to-all-start = ((bf16[32,80,192]{2,1,0:T(8,128)(2,1)}), bf16[32,80,192]{2,1,0:T(8,128)(2,1)S(1)}, u32[]{:S(2)}, u32[]{:S(2)}) async-start(bf16[32,80,192]{2,1,0:T(8,128)(2,1)} %bitcast.5), calls=%async_computation | async-start | bytes 2621440 | tf_op jit(solution)/shard_map/head_weights/all_to_all | solution.py:37
  29.8 132.7 %collective-permute-start.7 = (bf16[64,3072]{1,0:T(8,128)(2,1)}, bf16[64,3072]{1,0:T(8,128)(2,1)}, u32[]{:S(2)}, u32[]{:S(2)}) collective-permute-start(bf16[64,3072]{1,0:T(8,128)(2,1)} %reshape.440), channel_id=1, source_target_pairs={{0,64},{64,0},{1,65},{65,1},{2,66},{66,2},{3,67},{67,3},{4,68},{68... | collective-permute-start | bytes 1179656 | tf_op jit(solution)/shard_map/gather_attend_weight/ppermute | solution.py:533
  51.4 28.8 %all-to-all-start.1 = ((bf16[16,32,1024]{2,1,0:T(8,128)(2,1)}), bf16[16,32,1024]{2,1,0:T(8,128)(2,1)S(1)}, u32[]{:S(2)}, u32[]{:S(2)}) async-start(bf16[16,32,1024]{2,1,0:T(8,128)(2,1)} %bitcast.273), calls=%async_computation.1 | async-start | bytes 2097152 | tf_op jit(solution)/shard_map/sequence_tokens/all_to_all | solution.py:37
  80.2 4.3 collective-permute-start
  91.5 1.4 collective-permute-start.1
  93.8 16.0 %all-to-all-start.2 = ((bf16[32,32,128]{2,1,0:T(8,128)(2,1)}), bf16[32,32,128]{2,1,0:T(8,128)(2,1)S(1)}, u32[]{:S(2)}, u32[]{:S(2)}) async-start(bf16[32,32,128]{2,1,0:T(8,128)(2,1)} %bitcast.22), calls=%async_computation.2 | async-start | bytes 524288 | tf_op jit(solution)/shard_map/context_out/all_to_all | solution.py:37
  97.7 212.1 %all-gather.7.cloned.1.call-start = ((), (), s32[]{:S(2)}) async-start(), calls=%async_computation.13 | async-start | bytes 6684672 | tf_op jit(solution)/shard_map/gather_attend_weight/all_gather | solution.py:535
  162.5 229.2 %all-gather.9.cloned.1.call-start = ((), (), s32[]{:S(2)}) async-start(), calls=%async_computation.14 | async-start | bytes 4456448 | tf_op jit(solution)/shard_map/gather_first/all_gather | solution.py:543
  162.6 7.7 %collective-permute-start.2 = (bf16[128,1024]{1,0:T(8,128)(2,1)S(1)}, bf16[128,1024]{1,0:T(8,128)(2,1)S(1)}, u32[]{:S(2)}, u32[]{:S(2)}) collective-permute-start(bf16[128,1024]{1,0:T(8,128)(2,1)S(1)} %get-tuple-element.50), channel_id=1, source_target_pairs={{0,64},{1,65},{2,66},{3,67},{4,68},{5,69},{6,70},{7,71},{8,72},{9,... | collective-permute-start | bytes 786440 | tf_op jit(solution)/shard_map/to_next_section/ppermute | solution.py:529
  196.3 2.7 collective-permute-start.3
  205.0 1.4 collective-permute-start.4
  250.9 23.2 %collective-permute-start.5 = (f32[128,1024]{1,0:T(8,128)}, f32[128,1024]{1,0:T(8,128)}, u32[]{:S(2)}, u32[]{:S(2)}) collective-permute-start(f32[128,1024]{1,0:T(8,128)} %get-tuple-element.56), channel_id=1, source_target_pairs={{64,0},{65,1},{66,2},{67,3},{68,4},{69,5},{70,6},{71,7},{72,8},{73... | collective-permute-start | bytes 1572872 | tf_op jit(solution)/shard_map/residual_to_other_section/ppermute | solution.py:551
  252.2 21.1 %all-to-all-start.5 = ((bf16[32,64,128]{2,1,0:T(8,128)(2,1)}), bf16[32,64,128]{2,1,0:T(8,128)(2,1)S(1)}, u32[]{:S(2)}, u32[]{:S(2)}) async-start(bf16[32,64,128]{2,1,0:T(8,128)(2,1)} %bitcast.257), calls=%async_computation.5 | async-start | bytes 1048576 | tf_op jit(solution)/shard_map/grad_context_in/all_to_all | solution.py:37
  282.8 2.7 collective-permute-start.6
  290.3 19.5 %all-to-all-start.6 = ((bf16[32,32,384]{2,1,0:T(8,128)(2,1)}), bf16[32,32,384]{2,1,0:T(8,128)(2,1)}, u32[]{:S(2)}, u32[]{:S(2)}) async-start(bf16[32,32,384]{2,1,0:T(8,128)(2,1)} %bitcast.277), calls=%async_computation.6 | async-start | bytes 1572864 | tf_op jit(solution)/shard_map/grad_tokens_1/all_to_all | solution.py:37
  295.5 124.0 %all-gather.11.cloned.1.call-start = ((), (), s32[]{:S(2)}) async-start(), calls=%async_computation.15 | async-start | bytes 4456448 | tf_op jit(solution)/shard_map/gather_grad_mlp/all_gather | solution.py:560
  335.5 4.3 collective-permute-start.8
  335.8 15.5 %all-to-all-start.7 = ((bf16[32,64,128]{2,1,0:T(8,128)(2,1)}), bf16[32,64,128]{2,1,0:T(8,128)(2,1)S(1)}, u32[]{:S(2)}, u32[]{:S(2)}) async-start(bf16[32,64,128]{2,1,0:T(8,128)(2,1)} %bitcast.256), calls=%async_computation.7 | async-start | bytes 1048576 | tf_op jit(solution)/shard_map/grad_context_in/all_to_all | solution.py:37
  351.3 24.8 %all-to-all-start.8 = ((bf16[64,16,512]{2,1,0:T(8,128)(2,1)}), bf16[64,16,512]{2,1,0:T(8,128)(2,1)S(1)}, u32[]{:S(2)}, u32[]{:S(2)}) async-start(bf16[64,16,512]{2,1,0:T(8,128)(2,1)} %bitcast.57), calls=%async_computation.8 | async-start | bytes 2097152 | tf_op jit(solution)/shard_map/sum_output_grad/all_to_all | solution.py:37
  357.8 77.2 %collective-permute-start.11 = (bf16[128,1024]{1,0:T(8,128)(2,1)S(1)}, bf16[128,1024]{1,0:T(8,128)(2,1)}, u32[]{:S(2)}, u32[]{:S(2)}) collective-permute-start(bf16[128,1024]{1,0:T(8,128)(2,1)S(1)} %copy-done.14), channel_id=1, source_target_pairs={{0,64},{1,65},{2,66},{3,67},{4,68},{5,69},{6,70},{7,71},{8,72},{9,... | collective-permute-start | bytes 786440 | tf_op jit(solution)/shard_map/residual_to_other_section/ppermute | solution.py:566
  360.5 74.5 %collective-permute-start.12 = (bf16[128,1024]{1,0:T(8,128)(2,1)S(1)}, bf16[128,1024]{1,0:T(8,128)(2,1)}, u32[]{:S(2)}, u32[]{:S(2)}) collective-permute-start(bf16[128,1024]{1,0:T(8,128)(2,1)S(1)} %copy-done.7), channel_id=1, source_target_pairs={{0,64},{1,65},{2,66},{3,67},{4,68},{5,69},{6,70},{7,71},{8,72},{9,... | collective-permute-start | bytes 786440 | tf_op jit(solution)/shard_map/grad_tokens_1/ppermute | solution.py:555
  366.0 23.6 %collective-permute-start.9 = (bf16[1040,192]{0,1:T(8,128)(2,1)}, bf16[1040,192]{0,1:T(8,128)(2,1)}, u32[]{:S(2)}, u32[]{:S(2)}) collective-permute-start(bf16[1040,192]{0,1:T(8,128)(2,1)} %fusion.25), channel_id=1, source_target_pairs={{0,64},{1,65},{2,66},{3,67},{4,68},{5,69},{6,70},{7,71},{8,72},{9,... | collective-permute-start | bytes 1198088 | tf_op jit(solution)/shard_map/swap_attend_grad/ppermute | solution.py:572
  390.4 14.5 %collective-permute-start.10 = (bf16[1040,192]{0,1:T(8,128)(2,1)}, bf16[1040,192]{0,1:T(8,128)(2,1)}, u32[]{:S(2)}, u32[]{:S(2)}) collective-permute-start(bf16[1040,192]{0,1:T(8,128)(2,1)} %get-tuple-element.152), channel_id=1, source_target_pairs={{64,0},{65,1},{66,2},{67,3},{68,4},{69,5},{70,6},{71,7},{72,8},{73... | collective-permute-start | bytes 1198088 | tf_op jit(solution)/shard_map/swap_attend_grad/ppermute | solution.py:587
  408.1 29.9 %all-to-all-start.9 = ((bf16[64,16,512]{2,1,0:T(8,128)(2,1)}), bf16[64,16,512]{2,1,0:T(8,128)(2,1)S(1)}, u32[]{:S(2)}, u32[]{:S(2)}) async-start(bf16[64,16,512]{2,1,0:T(8,128)(2,1)} %bitcast.62), calls=%async_computation.9 | async-start | bytes 2097152 | tf_op jit(solution)/shard_map/sum_attend_grad/all_to_all | solution.py:37
  438.0 21.0 %all-to-all-start.10 = ((bf16[64,16,256]{2,1,0:T(8,128)(2,1)}), bf16[64,16,256]{2,1,0:T(8,128)(2,1)S(1)}, u32[]{:S(2)}, u32[]{:S(2)}) async-start(bf16[64,16,256]{2,1,0:T(8,128)(2,1)} %bitcast.71), calls=%async_computation.10 | async-start | bytes 1048576 | tf_op jit(solution)/shard_map/sum_expand_grad/all_to_all | solution.py:37
  459.0 13.2 %all-to-all-start.11 = ((bf16[4,80,1024]{2,1,0:T(8,128)(2,1)}), bf16[4,80,1024]{2,1,0:T(8,128)(2,1)S(1)}, u32[]{:S(2)}, u32[]{:S(2)}) async-start(bf16[4,80,1024]{2,1,0:T(8,128)(2,1)} %pad_maximum_fusion.3), calls=%async_computation.11 | async-start | bytes 1310720 | tf_op jit(solution)/shard_map/sum_contract/all_to_all | solution.py:37
  462.5 40.5 %all-gather.13.cloned.1.call-start = ((), (), s32[]{:S(2)}) async-start(), calls=%async_computation.16 | async-start | bytes 1966080 | tf_op jit(solution)/shard_map/gather_weight_grads/all_gather | solution.py:657
  473.2 3.4 collective-permute-start.13
  478.2 18.3 %all-to-all-start.12 = ((bf16[32,32,384]{2,1,0:T(8,128)(2,1)}), bf16[32,32,384]{2,1,0:T(8,128)(2,1)S(1)}, u32[]{:S(2)}, u32[]{:S(2)}) async-start(bf16[32,32,384]{2,1,0:T(8,128)(2,1)} %bitcast.80), calls=%async_computation.12 | async-start | bytes 1572864 | tf_op jit(solution)/shard_map/grad_tokens_0/all_to_all | solution.py:37
  501.7 9.7 %collective-permute-start.14 = (bf16[128,1024]{1,0:T(8,128)(2,1)S(1)}, bf16[128,1024]{1,0:T(8,128)(2,1)S(1)}, u32[]{:S(2)}, u32[]{:S(2)}) collective-permute-start(bf16[128,1024]{1,0:T(8,128)(2,1)S(1)} %grad_tokens_0.1), channel_id=1, source_target_pairs={{64,0},{65,1},{66,2},{67,3},{68,4},{69,5},{70,6},{71,7},{72,8},{73... | collective-permute-start | bytes 786440 | tf_op jit(solution)/shard_map/grad_tokens_0/ppermute | solution.py:655
  (38 other events, 232.8 us)
Sparse Core Ops, SparseCore 0:
  13.9 136.5 all-gather.14
  162.7 72.8 all-gather.6
  238.0 54.5 all-gather.8
  317.2 60.9 all-gather.10
  473.3 23.7 all-gather.12

commit v9 on v8

--- a/solution.py
+++ b/solution.py
@@ -552,7 +552,7 @@
     grad_packed_1, arrived_1 = attention_back(1, grad_context, kept_1, arrived_1)
     with jax.named_scope("grad_tokens_1"):
         rounded = grad_tokens(send_tokens(grad_packed_1, 3), other_attend, arrived_1)
-        grad_tokens_1 = lax.ppermute(rounded, "section", [(0, 1)])
+        rounded_1 = rounded
     own_grad = jnp.where(on_first, rounded, last_grad)
     with jax.named_scope("gather_grad_mlp"):
         grad_mlp = normed_back(own_grad.astype(jnp.float32), saved[3], params[5:6])[0].astype(LOW)
@@ -562,8 +562,6 @@
         grad_residual, grad_attn, grad_context, norm_sums = block_back(
             own_grad, saved, gathered, params
         )
-    with jax.named_scope("residual_to_other_section"):
-        arrived_0 = lax.ppermute(grad_attn, "section", [(0, 1)])
     late_tokens, late_packed, late_gathered, grad_context = lax.optimization_barrier(
         (kept_1[0], grad_packed_1, gathered, grad_context)
     )
@@ -601,7 +599,10 @@
         vectors = vectors.astype(LOW)
     with jax.named_scope("sum_attend_grad"):
         parts = jnp.concatenate([attend_grad, vectors], 1)
+        parts, late_attn, late_rounded = lax.optimization_barrier((parts, grad_attn, rounded_1))
         got = exchange(parts.reshape(64, 16, 512), REST)
+        arrived_0 = lax.ppermute(late_attn, "section", [(0, 1)])
+        grad_tokens_1 = lax.ppermute(late_rounded, "section", [(0, 1)])
     with jax.named_scope("block_weight_grads"):
         expand_part = lax.dynamic_slice(
             late_gathered, (0, 320 + shard // 4 * 64, shard % 4 * 256), (16, 64, 256)

time: 530 us -> 525 us (level)
  waiting for transfers between devices: 197 us -> 191 us
    ppermute x1, waiting for transfers between devices: 10.8 us -> 0.01 us  [on_device(): take_1 = lax.ppermute(part_1, 'section', [(0, 1)])]
    unnamed x96 -> x104, local copies, waits for them, and re-layouts: 18.2 us -> 19 us
  transfers between devices with their start and end apart: 31 -> 31, of which waited for: 22 -> 21; matrix products, arithmetic and copies ran while one was open for 16% -> 15% of each run, Pallas kernels for 14% -> 14%
where the time goes in v9:
time: 525 us; the launch traced here: 515 us
  waiting for transfers between devices  191 us (36%)
  starting transfers between devices  94.3 us (18%)
  Pallas kernels  73.1 us (14%)
  local copies, waits for them, and re-layouts  49.8 us (9%)
  blocking collectives  41.7 us (8%)
  matrix products  27.4 us (5%)
  other arithmetic  21.6 us (4%)
  between operations  15.6 us (3%)
    all_to_all x11, waiting for transfers between devices, exchange(): return lax.all_to_all(value, axes, 0, 0, tiled=True)  125 us
    all_to_all x11, starting transfers between devices, exchange(): return lax.all_to_all(value, axes, 0, 0, tiled=True)  73.6 us
    all_to_all x2, blocking collectives, exchange(): return lax.all_to_all(value, axes, 0, 0, tiled=True)  41.7 us
    all_gather x1, waiting for transfers between devices, on_device(): lax.all_gather(quarter, REST, axis=0, tiled=False).reshape(16, 576, 1024)  40.8 us
    pallas_call x2, Pallas kernels, block_back(): pl.pallas_call(backward_kernel, grid=(PARTS + 1,), in_specs=[full(128, 10...  28.3 us
    pallas_call x2, Pallas kernels, block_forward(): pl.pallas_call(forward_kernel, grid=(PARTS + 1,), in_specs=[full(128, 102...  23.1 us
    unnamed x104, local copies, waits for them, and re-layouts  19 us
    dot_general x5, matrix products, transposed_times(): lax.dot_general(left, right, (((0,), (0,)), ((), ())), preferred_element_...  11.6 us
  transfers between devices with their start and end apart: 31, of which 21 were waited for; matrix products, arithmetic and copies ran while one was open for 15% of the time, Pallas kernels for 14%

profile of v9, /device:TPU:1, one launch (start us, length us, event | category | flops | bytes accessed | tf_op | source)
XLA Modules:
  0.0 514.6 jit_solution(6321587112173931276)
XLA Ops:
  18.9 9.6 %all-to-all-start = ((bf16[32,80,192]{2,1,0:T(8,128)(2,1)}), bf16[32,80,192]{2,1,0:T(8,128)(2,1)S(1)}, u32[]{:S(2)}, u32[]{:S(2)}) async-start(bf16[32,80,192]{2,1,0:T(8,128)(2,1)} %bitcast.5), calls=%async_computation | async-start | bytes 2621440 | tf_op jit(solution)/shard_map/head_weights/all_to_all | solution.py:37
  31.4 19.0 %all-to-all-done = bf16[32,80,192]{2,1,0:T(8,128)(2,1)S(1)} async-done(((bf16[32,80,192]{2,1,0:T(8,128)(2,1)}), bf16[32,80,192]{2,1,0:T(8,128)(2,1)S(1)}, u32[]{:S(2)}, u32[]{:S(2)}) %all-to-all-start) | async-done | bytes 983072 | tf_op jit(solution)/shard_map/head_weights/all_to_all | solution.py:37
  51.4 4.7 all-to-all-start.1
  56.5 23.7 %all-to-all-done.1 = bf16[16,32,1024]{2,1,0:T(8,128)(2,1)S(1)} async-done(((bf16[16,32,1024]{2,1,0:T(8,128)(2,1)}), bf16[16,32,1024]{2,1,0:T(8,128)(2,1)S(1)}, u32[]{:S(2)}, u32[]{:S(2)}) %all-to-all-start.1) | async-done | bytes 1048608 | tf_op jit(solution)/shard_map/sequence_tokens/all_to_all | solution.py:37
  98.4 11.4 %all-to-all-done.2 = bf16[32,32,128]{2,1,0:T(8,128)(2,1)S(1)} async-done(((bf16[32,32,128]{2,1,0:T(8,128)(2,1)}), bf16[32,32,128]{2,1,0:T(8,128)(2,1)S(1)}, u32[]{:S(2)}, u32[]{:S(2)}) %all-to-all-start.2) | async-done | bytes 262176 | tf_op jit(solution)/shard_map/context_out/all_to_all | solution.py:37
  109.8 40.8 %all-gather.15.cloned.1.call-done = bf16[9216,1024]{1,0:T(8,128)(2,1)} async-done(((bf16[144,1024]{1,0:T(8,128)(2,1)}), bf16[9216,1024]{1,0:T(8,128)(2,1)}) %all-gather.15.cloned.1.call-update) | async-done | bytes 18874384 | tf_op jit(solution)/shard_map/gather_block_weights/all_gather | solution.py:461
  150.5 12.0 %block_0.1 = (bf16[128,1024]{1,0:T(8,128)(2,1)S(1)}, f32[128,1024]{1,0:T(8,128)}, bf16[128,1024]{1,0:T(8,128)(2,1)}, f32[128,4096]{1,0:T(8,128)}, f32[128,1024]{1,0:T(8,128)}, /*index=5*/bf16[128,1024]{1,0:T(8,128)(2,1)}) custom-call(bf16[128,1024]{1,0:T(8,128)(2,1)S(1)} %bitcast.252, bf16[2,2,4,2,32,128]{5,4,3,2,1,0:T(8,128)(2,1)S(1)} %bitcast.253, ...), custom_call_target="tpu_custom_call" | custom-call | flops 2415919104 | bytes 25165824 | tf_op jit(solution)/shard_map/block_0/pallas_call | solution.py:197
  164.9 5.5 %collective-permute-done.2 = bf16[128,1024]{1,0:T(8,128)(2,1)S(1)} collective-permute-done((bf16[128,1024]{1,0:T(8,128)(2,1)S(1)}, bf16[128,1024]{1,0:T(8,128)(2,1)S(1)}, u32[]{:S(2)}, u32[]{:S(2)}) %collective-permute-start.2) | collective-permute-done | bytes 262176 | tf_op jit(solution)/shard_map/to_next_section/ppermute | solution.py:529
  171.2 25.1 %all_to_all.65 = bf16[16,32,1024]{2,1,0:T(8,128)(2,1)S(1)} all-to-all(bf16[16,32,1024]{2,1,0:T(8,128)(2,1)S(1)} %bitcast.274), channel_id=1, replica_groups=mesh['section'=2,'shard'=16,'replica'=4] {'shard'}, dimensions={0} | all-to-all | bytes 2097152 | tf_op jit(solution)/shard_map/sequence_tokens/all_to_all | solution.py:37
  206.6 16.6 %all_to_all.66 = bf16[32,32,128]{2,1,0:T(8,128)(2,1)S(1)} all-to-all(bf16[32,32,128]{2,1,0:T(8,128)(2,1)S(1)} %bitcast.296), channel_id=1, replica_groups=mesh['section'=2,'shard'=16,'replica'=4] {'section','shard'}, dimensions={0} | all-to-all | bytes 524288 | tf_op jit(solution)/shard_map/context_out/all_to_all | solution.py:37
  223.3 11.1 %block_1.1 = (bf16[128,1024]{1,0:T(8,128)(2,1)}, f32[128,1024]{1,0:T(8,128)S(1)}, bf16[128,1024]{1,0:T(8,128)(2,1)S(1)}, f32[128,4096]{1,0:T(8,128)S(1)}, f32[12...) custom-call(bf16[128,1024]{1,0:T(8,128)(2,1)S(1)} %copy-done.5, ...), custom_call_target="tpu_custom_call" | custom-call | flops 2415919104 | bytes 25165824 | tf_op jit(solution)/shard_map/block_1/pallas_call | solution.py:197
  235.8 14.2 %block_back_1.1 = (f32[128,1024]{1,0:T(8,128)}, bf16[128,1024]{1,0:T(8,128)(2,1)}, bf16[2,2,4,2,64,128]{5,4,3,2,1,0:T(8,128)(2,1)S(1)}, f32[8,1024]{1,0:T(8,128)}) custom-call(bf16[128,1024]{1,0:T(8,128)(2,1)S(1)} %bitcast.255, bf16[16,576,1024]{2,1,0:T(8,128)(2,1)} %bitcast.264, bf16[16,576,1024]{2,1,0:T(8,128)(2,1)} %bitcast.265, ...), custom_call_target="tpu_custom_call" | custom-call | flops 2415919104 | bytes 25165824 | tf_op jit(solution)/shard_map/block_back_1/pallas_call | solution.py:292
  252.1 8.9 %all-to-all-start.5 = ((bf16[32,64,128]{2,1,0:T(8,128)(2,1)}), bf16[32,64,128]{2,1,0:T(8,128)(2,1)S(1)}, u32[]{:S(2)}, u32[]{:S(2)}) async-start(bf16[32,64,128]{2,1,0:T(8,128)(2,1)} %bitcast.257), calls=%async_computation.5 | async-start | bytes 1048576 | tf_op jit(solution)/shard_map/grad_context_in/all_to_all | solution.py:37
  262.7 10.5 %all-to-all-done.5.got = bf16[32,64,128]{2,1,0:T(8,128)(2,1)S(1)} async-done(((bf16[32,64,128]{2,1,0:T(8,128)(2,1)}), bf16[32,64,128]{2,1,0:T(8,128)(2,1)S(1)}, u32[]{:S(2)}, u32[]{:S(2)}) %all-to-all-start.5) | async-done | bytes 524320 | tf_op jit(solution)/shard_map/grad_context_in/all_to_all | solution.py:37
  277.2 5.5 %attention_back.2 = bf16[1024,192]{1,0:T(8,128)(2,1)S(1)} custom-call(s32[1]{0:T(128)} %bitcast.45.core, bf16[1024,192]{1,0:T(8,128)(2,1)S(1)} %copy-done.23, f32[1024,1]{1,0:T(8,128)S(1)} %copy-done.12, bf16[1024,1]{1,0:T(8,128)(2,1)S(1)} %select_n.401.seg_rows, bf16[1,1024]{1,0:T(2,128)(2,1)S(1)} %select_n.370.seg_columns, bf16[32,64,128]{2,1,0:T(8,128)(2,1)S(1)} %copy-done.10), custom_call_target="tpu_custom_call" | custom-call | flops 671088640 | bytes 2097152 | tf_op jit(solution)/shard_map/attention_back/pallas_call | solution.py:410
  290.3 5.1 all-to-all-start.6
  295.9 13.8 %all-to-all-done.6 = bf16[32,32,384]{2,1,0:T(8,128)(2,1)} async-done(((bf16[32,32,384]{2,1,0:T(8,128)(2,1)}), bf16[32,32,384]{2,1,0:T(8,128)(2,1)}, u32[]{:S(2)}, u32[]{:S(2)}) %all-to-all-start.6) | async-done | bytes 786464 | tf_op jit(solution)/shard_map/grad_tokens_1/all_to_all | solution.py:37
  309.7 5.5 %grad_tokens_1.1 = bf16[128,1024]{1,0:T(8,128)(2,1)S(1)} custom-call(bf16[2,2,4,2,32,384]{5,4,3,2,1,0:T(8,128)(2,1)} %bitcast.53.got, bf16[1024,3072]{1,0:T(8,128)(2,1)} %all-gather.7.cloned.1.call-done.weight, f32[128,1024]{1,0:T(8,128)} %collective-permute-done.5.grad_residual), custom_call_target="tpu_custom_call" | custom-call | flops 805306368 | bytes 8388608 | tf_op jit(solution)/shard_map/grad_tokens_1/pallas_call | solution.py:345
  318.0 14.1 %block_back_0.1 = (f32[128,1024]{1,0:T(8,128)}, bf16[128,1024]{1,0:T(8,128)(2,1)S(1)}, bf16[2,2,4,2,64,128]{5,4,3,2,1,0:T(8,128)(2,1)S(1)}, f32[8,1024]{1,0:T(8,128)S(1)}) custom-call(bf16[128,1024]{1,0:T(8,128)(2,1)S(1)} %get-tuple-element.63.grad, bf16[16,576,1024]{2,1,0:T(8,128)(2,1)} %bitcast.267, bf16[16,576,1024]{2,1,0:T(8,128)(2,1)} %bitcast.268, ...), custom_call_target="tpu_custom_call" | custom-call | flops 2415919104 | bytes 25165824 | tf_op jit(solution)/shard_map/block_back_0/pallas_call | solution.py:292
  343.2 7.7 %all-to-all-done.7.got = bf16[32,64,128]{2,1,0:T(8,128)(2,1)S(1)} async-done(((bf16[32,64,128]{2,1,0:T(8,128)(2,1)}), bf16[32,64,128]{2,1,0:T(8,128)(2,1)S(1)}, u32[]{:S(2)}, u32[]{:S(2)}) %all-to-all-start.7) | async-done | bytes 524320 | tf_op jit(solution)/shard_map/grad_context_in/all_to_all | solution.py:37
  350.9 6.3 %all-to-all-start.8 = ((bf16[64,16,512]{2,1,0:T(8,128)(2,1)}), bf16[64,16,512]{2,1,0:T(8,128)(2,1)S(1)}, u32[]{:S(2)}, u32[]{:S(2)}) async-start(bf16[64,16,512]{2,1,0:T(8,128)(2,1)} %bitcast.57), calls=%async_computation.8 | async-start | bytes 2097152 | tf_op jit(solution)/shard_map/sum_output_grad/all_to_all | solution.py:37
  365.7 5.5 %attention_back.3 = bf16[1024,192]{1,0:T(8,128)(2,1)S(1)} custom-call(s32[1]{0:T(128)} %bitcast.45.core, bf16[1024,192]{1,0:T(8,128)(2,1)S(1)} %copy-done.21, f32[1024,1]{1,0:T(8,128)S(1)} %copy.180.log_totals, bf16[1024,1]{1,0:T(8,128)(2,1)S(1)} %copy-done.19, bf16[1,1024]{1,0:T(2,128)(2,1)S(1)} %select_n.370.seg_columns, ...), custom_call_target="tpu_custom_call" | custom-call | flops 671088640 | bytes 2097152 | tf_op jit(solution)/shard_map/attention_back/pallas_call | solution.py:410
  380.7 4.8 convolution_add_fusion
  386.6 6.2 %collective-permute-done.10 = bf16[1040,192]{0,1:T(8,128)(2,1)S(1)} collective-permute-done((bf16[1040,192]{0,1:T(8,128)(2,1)}, bf16[1040,192]{0,1:T(8,128)(2,1)S(1)}, u32[]{:S(2)}, u32[]{:S(2)}) %collective-permute-start.10) | collective-permute-done | bytes 399392 | tf_op jit(solution)/shard_map/swap_attend_grad/ppermute | solution.py:585
  395.1 11.8 %all-to-all-start.9 = ((bf16[64,16,512]{2,1,0:T(8,128)(2,1)}), bf16[64,16,512]{2,1,0:T(8,128)(2,1)S(1)}, u32[]{:S(2)}, u32[]{:S(2)}) async-start(bf16[64,16,512]{2,1,0:T(8,128)(2,1)} %bitcast.62), calls=%async_computation.9 | async-start | bytes 2097152 | tf_op jit(solution)/shard_map/sum_attend_grad/all_to_all | solution.py:37
  409.6 5.4 %fusion.50 = (bf16[256]{0:T(256)(128)(2,1)S(1)}, bf16[2048,256]{1,0:T(8,128)(2,1)S(1)}) fusion(f32[2048,256]{1,0:T(8,128)} %convolution_add_fusion, bf16[2048,1024]{1,0:T(8,128)(2,1)} %all-gather.11.cloned.1.call-done, bf16[1,256,1024]{2,1,0:T(8,128)(2,1)S(1)} %copy-done.33), kind=kOutput, calls=%fused_computation.167 | convolution fusion | flops 1079508736 | bytes 7864832 | tf_op jit(solution)/shard_map/block_weight_grads/dot_general | solution.py:25
  429.3 11.2 %all-to-all-start.10 = ((bf16[64,16,256]{2,1,0:T(8,128)(2,1)}), bf16[64,16,256]{2,1,0:T(8,128)(2,1)S(1)}, u32[]{:S(2)}, u32[]{:S(2)}) async-start(bf16[64,16,256]{2,1,0:T(8,128)(2,1)} %bitcast.71), calls=%async_computation.10 | async-start | bytes 1048576 | tf_op jit(solution)/shard_map/sum_expand_grad/all_to_all | solution.py:37
  441.3 12.5 %all-to-all-done.10 = bf16[64,16,256]{2,1,0:T(8,128)(2,1)S(1)} async-done(((bf16[64,16,256]{2,1,0:T(8,128)(2,1)}), bf16[64,16,256]{2,1,0:T(8,128)(2,1)S(1)}, u32[]{:S(2)}, u32[]{:S(2)}) %all-to-all-start.10) | async-done | bytes 524320 | tf_op jit(solution)/shard_map/sum_expand_grad/all_to_all | solution.py:37
  457.4 9.5 %all-to-all-done.11 = bf16[4,80,1024]{2,1,0:T(8,128)(2,1)S(1)} async-done(((bf16[4,80,1024]{2,1,0:T(8,128)(2,1)}), bf16[4,80,1024]{2,1,0:T(8,128)(2,1)S(1)}, u32[]{:S(2)}, u32[]{:S(2)}) %all-to-all-start.11) | async-done | bytes 655392 | tf_op jit(solution)/shard_map/sum_contract/all_to_all | solution.py:37
  472.9 4.7 all-to-all-start.12
  479.6 12.3 %all-to-all-done.12 = bf16[32,32,384]{2,1,0:T(8,128)(2,1)S(1)} async-done(((bf16[32,32,384]{2,1,0:T(8,128)(2,1)}), bf16[32,32,384]{2,1,0:T(8,128)(2,1)S(1)}, u32[]{:S(2)}, u32[]{:S(2)}) %all-to-all-start.12) | async-done | bytes 786464 | tf_op jit(solution)/shard_map/grad_tokens_0/all_to_all | solution.py:37
  491.9 5.2 %grad_tokens_0.1 = bf16[128,1024]{1,0:T(8,128)(2,1)S(1)} custom-call(bf16[2,2,4,2,32,384]{5,4,3,2,1,0:T(8,128)(2,1)S(1)} %bitcast.250, bf16[1024,3072]{1,0:T(8,128)(2,1)} %all-gather.7.cloned.1.call-done.weight, f32[128,1024]{1,0:T(8,128)S(1)} %convert_element_type.200.grad_residual), custom_call_target="tpu_custom_call" | custom-call | flops 805306368 | bytes 8388608 | tf_op jit(solution)/shard_map/grad_tokens_0/pallas_call | solution.py:345
  (335 shorter events, 138.9 us)
Async XLA Ops:
  7.2 143.4 %all-gather.15.cloned.1.call-start = ((), (), s32[]{:S(2)}) async-start(), calls=%async_computation.17 | async-start | bytes 19169280 | tf_op jit(solution)/shard_map/gather_block_weights/all_gather | solution.py:461
  18.9 31.5 %copy-start = (bf16[2,1,64,1024]{3,2,1,0:T(8,128)(2,1)S(1)}, bf16[2,1,64,1024]{3,2,1,0:T(8,128)(2,1)}, u32[]{:S(2)}) copy-start(bf16[2,1,64,1024]{3,2,1,0:T(8,128)(2,1)} %param.10) | copy-start | bytes 786436
  18.9 31.5 %all-to-all-start = ((bf16[32,80,192]{2,1,0:T(8,128)(2,1)}), bf16[32,80,192]{2,1,0:T(8,128)(2,1)S(1)}, u32[]{:S(2)}, u32[]{:S(2)}) async-start(bf16[32,80,192]{2,1,0:T(8,128)(2,1)} %bitcast.5), calls=%async_computation | async-start | bytes 2621440 | tf_op jit(solution)/shard_map/head_weights/all_to_all | solution.py:37
  29.8 132.7 %collective-permute-start.7 = (bf16[64,3072]{1,0:T(8,128)(2,1)}, bf16[64,3072]{1,0:T(8,128)(2,1)}, u32[]{:S(2)}, u32[]{:S(2)}) collective-permute-start(bf16[64,3072]{1,0:T(8,128)(2,1)} %reshape.440), channel_id=1, source_target_pairs={{0,64},{64,0},{1,65},{65,1},{2,66},{66,2},{3,67},{67,3},{4,68},{68... | collective-permute-start | bytes 1179656 | tf_op jit(solution)/shard_map/gather_attend_weight/ppermute | solution.py:533
  51.4 28.8 %all-to-all-start.1 = ((bf16[16,32,1024]{2,1,0:T(8,128)(2,1)}), bf16[16,32,1024]{2,1,0:T(8,128)(2,1)S(1)}, u32[]{:S(2)}, u32[]{:S(2)}) async-start(bf16[16,32,1024]{2,1,0:T(8,128)(2,1)} %bitcast.273), calls=%async_computation.1 | async-start | bytes 2097152 | tf_op jit(solution)/shard_map/sequence_tokens/all_to_all | solution.py:37
  80.2 4.3 collective-permute-start
  91.5 1.4 collective-permute-start.1
  93.8 16.0 %all-to-all-start.2 = ((bf16[32,32,128]{2,1,0:T(8,128)(2,1)}), bf16[32,32,128]{2,1,0:T(8,128)(2,1)S(1)}, u32[]{:S(2)}, u32[]{:S(2)}) async-start(bf16[32,32,128]{2,1,0:T(8,128)(2,1)} %bitcast.22), calls=%async_computation.2 | async-start | bytes 524288 | tf_op jit(solution)/shard_map/context_out/all_to_all | solution.py:37
  97.7 212.0 %all-gather.7.cloned.1.call-start = ((), (), s32[]{:S(2)}) async-start(), calls=%async_computation.13 | async-start | bytes 6684672 | tf_op jit(solution)/shard_map/gather_attend_weight/all_gather | solution.py:535
  162.5 218.1 %all-gather.9.cloned.1.call-start = ((), (), s32[]{:S(2)}) async-start(), calls=%async_computation.14 | async-start | bytes 4456448 | tf_op jit(solution)/shard_map/gather_first/all_gather | solution.py:543
  162.6 7.7 %collective-permute-start.2 = (bf16[128,1024]{1,0:T(8,128)(2,1)S(1)}, bf16[128,1024]{1,0:T(8,128)(2,1)S(1)}, u32[]{:S(2)}, u32[]{:S(2)}) collective-permute-start(bf16[128,1024]{1,0:T(8,128)(2,1)S(1)} %get-tuple-element.53), channel_id=1, source_target_pairs={{0,64},{1,65},{2,66},{3,67},{4,68},{5,69},{6,70},{7,71},{8,72},{9,... | collective-permute-start | bytes 786440 | tf_op jit(solution)/shard_map/to_next_section/ppermute | solution.py:529
  196.3 2.7 collective-permute-start.3
  205.0 1.4 collective-permute-start.4
  250.9 23.2 %collective-permute-start.5 = (f32[128,1024]{1,0:T(8,128)}, f32[128,1024]{1,0:T(8,128)}, u32[]{:S(2)}, u32[]{:S(2)}) collective-permute-start(f32[128,1024]{1,0:T(8,128)} %get-tuple-element.59), channel_id=1, source_target_pairs={{64,0},{65,1},{66,2},{67,3},{68,4},{69,5},{70,6},{71,7},{72,8},{73... | collective-permute-start | bytes 1572872 | tf_op jit(solution)/shard_map/residual_to_other_section/ppermute | solution.py:551
  252.1 21.1 %all-to-all-start.5 = ((bf16[32,64,128]{2,1,0:T(8,128)(2,1)}), bf16[32,64,128]{2,1,0:T(8,128)(2,1)S(1)}, u32[]{:S(2)}, u32[]{:S(2)}) async-start(bf16[32,64,128]{2,1,0:T(8,128)(2,1)} %bitcast.257), calls=%async_computation.5 | async-start | bytes 1048576 | tf_op jit(solution)/shard_map/grad_context_in/all_to_all | solution.py:37
  282.7 2.7 collective-permute-start.6
  290.3 19.4 %all-to-all-start.6 = ((bf16[32,32,384]{2,1,0:T(8,128)(2,1)}), bf16[32,32,384]{2,1,0:T(8,128)(2,1)}, u32[]{:S(2)}, u32[]{:S(2)}) async-start(bf16[32,32,384]{2,1,0:T(8,128)(2,1)} %bitcast.277), calls=%async_computation.6 | async-start | bytes 1572864 | tf_op jit(solution)/shard_map/grad_tokens_1/all_to_all | solution.py:37
  295.4 114.1 %all-gather.11.cloned.1.call-start = ((), (), s32[]{:S(2)}) async-start(), calls=%async_computation.15 | async-start | bytes 4456448 | tf_op jit(solution)/shard_map/gather_grad_mlp/all_gather | solution.py:560
  335.1 4.3 collective-permute-start.8
  335.5 15.4 %all-to-all-start.7 = ((bf16[32,64,128]{2,1,0:T(8,128)(2,1)}), bf16[32,64,128]{2,1,0:T(8,128)(2,1)S(1)}, u32[]{:S(2)}, u32[]{:S(2)}) async-start(bf16[32,64,128]{2,1,0:T(8,128)(2,1)} %bitcast.256), calls=%async_computation.7 | async-start | bytes 1048576 | tf_op jit(solution)/shard_map/grad_context_in/all_to_all | solution.py:37
  350.9 24.9 %all-to-all-start.8 = ((bf16[64,16,512]{2,1,0:T(8,128)(2,1)}), bf16[64,16,512]{2,1,0:T(8,128)(2,1)S(1)}, u32[]{:S(2)}, u32[]{:S(2)}) async-start(bf16[64,16,512]{2,1,0:T(8,128)(2,1)} %bitcast.57), calls=%async_computation.8 | async-start | bytes 2097152 | tf_op jit(solution)/shard_map/sum_output_grad/all_to_all | solution.py:37
  360.9 17.5 %collective-permute-start.9 = (bf16[1040,192]{0,1:T(8,128)(2,1)}, bf16[1040,192]{0,1:T(8,128)(2,1)}, u32[]{:S(2)}, u32[]{:S(2)}) collective-permute-start(bf16[1040,192]{0,1:T(8,128)(2,1)} %fusion.25), channel_id=1, source_target_pairs={{0,64},{1,65},{2,66},{3,67},{4,68},{5,69},{6,70},{7,71},{8,72},{9,... | collective-permute-start | bytes 1198088 | tf_op jit(solution)/shard_map/swap_attend_grad/ppermute | solution.py:570
  379.3 13.5 %collective-permute-start.10 = (bf16[1040,192]{0,1:T(8,128)(2,1)}, bf16[1040,192]{0,1:T(8,128)(2,1)S(1)}, u32[]{:S(2)}, u32[]{:S(2)}) collective-permute-start(bf16[1040,192]{0,1:T(8,128)(2,1)} %get-tuple-element.158), channel_id=1, source_target_pairs={{64,0},{65,1},{66,2},{67,3},{68,4},{69,5},{70,6},{71,7},{72,8},{73... | collective-permute-start | bytes 1198088 | tf_op jit(solution)/shard_map/swap_attend_grad/ppermute | solution.py:585
  395.1 34.2 %all-to-all-start.9 = ((bf16[64,16,512]{2,1,0:T(8,128)(2,1)}), bf16[64,16,512]{2,1,0:T(8,128)(2,1)S(1)}, u32[]{:S(2)}, u32[]{:S(2)}) async-start(bf16[64,16,512]{2,1,0:T(8,128)(2,1)} %bitcast.62), calls=%async_computation.9 | async-start | bytes 2097152 | tf_op jit(solution)/shard_map/sum_attend_grad/all_to_all | solution.py:37
  406.9 18.2 %collective-permute-start.11 = (bf16[128,1024]{1,0:T(8,128)(2,1)S(1)}, bf16[128,1024]{1,0:T(8,128)(2,1)S(1)}, u32[]{:S(2)}, u32[]{:S(2)}) collective-permute-start(bf16[128,1024]{1,0:T(8,128)(2,1)S(1)} %copy-done.14), channel_id=1, source_target_pairs={{0,64},{1,65},{2,66},{3,67},{4,68},{5,69},{6,70},{7,71},{8,72},{9,... | collective-permute-start | bytes 786440 | tf_op jit(solution)/shard_map/sum_attend_grad/ppermute | solution.py:604
  408.2 21.0 %collective-permute-start.12 = (bf16[128,1024]{1,0:T(8,128)(2,1)S(1)}, bf16[128,1024]{1,0:T(8,128)(2,1)S(1)}, u32[]{:S(2)}, u32[]{:S(2)}) collective-permute-start(bf16[128,1024]{1,0:T(8,128)(2,1)S(1)} %copy-done.7), channel_id=1, source_target_pairs={{0,64},{1,65},{2,66},{3,67},{4,68},{5,69},{6,70},{7,71},{8,72},{9,... | collective-permute-start | bytes 786440 | tf_op jit(solution)/shard_map/sum_attend_grad/ppermute | solution.py:605
  429.3 24.5 %all-to-all-start.10 = ((bf16[64,16,256]{2,1,0:T(8,128)(2,1)}), bf16[64,16,256]{2,1,0:T(8,128)(2,1)S(1)}, u32[]{:S(2)}, u32[]{:S(2)}) async-start(bf16[64,16,256]{2,1,0:T(8,128)(2,1)} %bitcast.71), calls=%async_computation.10 | async-start | bytes 1048576 | tf_op jit(solution)/shard_map/sum_expand_grad/all_to_all | solution.py:37
  453.8 13.2 %all-to-all-start.11 = ((bf16[4,80,1024]{2,1,0:T(8,128)(2,1)}), bf16[4,80,1024]{2,1,0:T(8,128)(2,1)S(1)}, u32[]{:S(2)}, u32[]{:S(2)}) async-start(bf16[4,80,1024]{2,1,0:T(8,128)(2,1)} %pad_maximum_fusion.3), calls=%async_computation.11 | async-start | bytes 1310720 | tf_op jit(solution)/shard_map/sum_contract/all_to_all | solution.py:37
  457.2 41.2 %all-gather.13.cloned.1.call-start = ((), (), s32[]{:S(2)}) async-start(), calls=%async_computation.16 | async-start | bytes 1966080 | tf_op jit(solution)/shard_map/gather_weight_grads/all_gather | solution.py:658
  467.9 3.4 collective-permute-start.13
  472.9 19.0 %all-to-all-start.12 = ((bf16[32,32,384]{2,1,0:T(8,128)(2,1)}), bf16[32,32,384]{2,1,0:T(8,128)(2,1)S(1)}, u32[]{:S(2)}, u32[]{:S(2)}) async-start(bf16[32,32,384]{2,1,0:T(8,128)(2,1)} %bitcast.80), calls=%async_computation.12 | async-start | bytes 1572864 | tf_op jit(solution)/shard_map/grad_tokens_0/all_to_all | solution.py:37
  497.1 9.6 %collective-permute-start.14 = (bf16[128,1024]{1,0:T(8,128)(2,1)S(1)}, bf16[128,1024]{1,0:T(8,128)(2,1)S(1)}, u32[]{:S(2)}, u32[]{:S(2)}) collective-permute-start(bf16[128,1024]{1,0:T(8,128)(2,1)S(1)} %grad_tokens_0.1), channel_id=1, source_target_pairs={{64,0},{65,1},{66,2},{67,3},{68,4},{69,5},{70,6},{71,7},{72,8},{73... | collective-permute-start | bytes 786440 | tf_op jit(solution)/shard_map/grad_tokens_0/ppermute | solution.py:656
  (42 other events, 261.7 us)
Sparse Core Ops, SparseCore 0:
  13.9 136.5 all-gather.14
  162.7 72.8 all-gather.6
  238.0 54.4 all-gather.8
  317.1 60.8 all-gather.10
  468.0 24.7 all-gather.12

commit v10 on v9

--- a/solution.py
+++ b/solution.py
@@ -330,7 +330,7 @@
 
     @pl.when(step == 0)
     def start():
-        total[...] = grad_residual[...] + product
+        total[...] = grad_residual[...].astype(jnp.float32) + product
 
     @pl.when(step > 0)
     def proceed():
@@ -544,11 +544,11 @@
 
     last_grad = cotangent.reshape(128, 1024)
     with jax.named_scope("block_back_1"):
-        grad_residual, unused, grad_context, unused = block_back(
+        unused, grad_attn_1, grad_context, unused = block_back(
             last_grad, saved, gathered, params
         )
     with jax.named_scope("residual_to_other_section"):
-        arrived_1 = lax.ppermute(grad_residual, "section", [(1, 0)])
+        arrived_1 = lax.ppermute(grad_attn_1, "section", [(1, 0)])
     grad_packed_1, arrived_1 = attention_back(1, grad_context, kept_1, arrived_1)
     with jax.named_scope("grad_tokens_1"):
         rounded = grad_tokens(send_tokens(grad_packed_1, 3), other_attend, arrived_1)
@@ -628,11 +628,11 @@
             [contract_grad.reshape(4, 64, 1024), jnp.broadcast_to(extra, (4, 16, 1024))], 1
         )
     with jax.named_scope("sum_expand_grad"):
-        got, expand_grad, rows, arrived_0, grad_tokens_1 = lax.optimization_barrier(
-            (got, expand_grad, rows, arrived_0, grad_tokens_1)
-        )
+        got, expand_grad, rows = lax.optimization_barrier((got, expand_grad, rows))
         expand_got = exchange(expand_grad.reshape(64, 16, 256), REST)
-        expand_got, rows = lax.optimization_barrier((expand_got, rows))
+        expand_got, rows, arrived_0, grad_tokens_1 = lax.optimization_barrier(
+            (expand_got, rows, arrived_0, grad_tokens_1)
+        )
     with jax.named_scope("sum_contract"):
         got_contract = exchange(rows, "replica").astype(jnp.float32).sum(0)
     with jax.named_scope("sum_attend_grad"):
@@ -650,9 +650,7 @@
         owned = jnp.concatenate([got_attend, got_output, got_expand, *contract_rows], 1)
     with jax.named_scope("grad_tokens_0"):
         late_packed, owned = lax.optimization_barrier((grad_packed, owned))
-        rounded = grad_tokens(
-            send_tokens(late_packed, 3), other_attend, arrived_0.astype(jnp.float32)
-        )
+        rounded = grad_tokens(send_tokens(late_packed, 3), other_attend, arrived_0)
         grad_tokens_0 = lax.ppermute(rounded, "section", [(1, 0)])
     with jax.named_scope("gather_weight_grads"):
         totals = lax.all_gather(owned, "replica", axis=0, tiled=True)

time: 525 us -> 530 us (level)
    all_to_all x11, waiting for transfers between devices: 125 us -> 103 us  [exchange(): return lax.all_to_all(value, axes, 0, 0, tiled=True)]
    ppermute x1, waiting for transfers between devices: 0.01 us -> 11.4 us  [on_device(): arrived_1 = lax.ppermute(grad_attn_1, 'section', [(1, 0)])]
    ppermute x1, waiting for transfers between devices: 0.01 us -> 6.59 us  [on_device(): arrived_0 = lax.ppermute(late_attn, 'section', [(0, 1)])]
    unnamed x104 -> x100, local copies, waits for them, and re-layouts: 19 us -> 21.5 us
  transfers between devices with their start and end apart: 31 -> 31, of which waited for: 21 -> 22; matrix products, arithmetic and copies ran while one was open for 15% -> 15% of each run, Pallas kernels for 14% -> 14%
where the time goes in v10:
time: 530 us; the launch traced here: 520 us
  waiting for transfers between devices  188 us (35%)
  starting transfers between devices  97.4 us (18%)
  Pallas kernels  73 us (14%)
  local copies, waits for them, and re-layouts  53 us (10%)
  blocking collectives  41.7 us (8%)
  matrix products  28.2 us (5%)
  other arithmetic  22.6 us (4%)
  between operations  15.4 us (3%)
    all_to_all x11, waiting for transfers between devices, exchange(): return lax.all_to_all(value, axes, 0, 0, tiled=True)  103 us
    all_to_all x11, starting transfers between devices, exchange(): return lax.all_to_all(value, axes, 0, 0, tiled=True)  75.4 us
    all_to_all x2, blocking collectives, exchange(): return lax.all_to_all(value, axes, 0, 0, tiled=True)  41.7 us
    all_gather x1, waiting for transfers between devices, on_device(): lax.all_gather(quarter, REST, axis=0, tiled=False).reshape(16, 576, 1024)  40.8 us
    pallas_call x2, Pallas kernels, block_back(): pl.pallas_call(backward_kernel, grid=(PARTS + 1,), in_specs=[full(128, 10...  28.3 us
    pallas_call x2, Pallas kernels, block_forward(): pl.pallas_call(forward_kernel, grid=(PARTS + 1,), in_specs=[full(128, 102...  23.1 us
    unnamed x100, local copies, waits for them, and re-layouts  21.5 us
    dot_general x5, matrix products, transposed_times(): lax.dot_general(left, right, (((0,), (0,)), ((), ())), preferred_element_...  11.7 us
  transfers between devices with their start and end apart: 31, of which 22 were waited for; matrix products, arithmetic and copies ran while one was open for 15% of the time, Pallas kernels for 14%

profile of v10, /device:TPU:1, one launch (start us, length us, event | category | flops | bytes accessed | tf_op | source)
XLA Modules:
  0.0 519.5 jit_solution(8273115962372232738)
XLA Ops:
  18.9 9.6 %all-to-all-start = ((bf16[32,80,192]{2,1,0:T(8,128)(2,1)}), bf16[32,80,192]{2,1,0:T(8,128)(2,1)S(1)}, u32[]{:S(2)}, u32[]{:S(2)}) async-start(bf16[32,80,192]{2,1,0:T(8,128)(2,1)} %bitcast.5), calls=%async_computation | async-start | bytes 2621440 | tf_op jit(solution)/shard_map/head_weights/all_to_all | solution.py:37
  31.4 19.0 %all-to-all-done = bf16[32,80,192]{2,1,0:T(8,128)(2,1)S(1)} async-done(((bf16[32,80,192]{2,1,0:T(8,128)(2,1)}), bf16[32,80,192]{2,1,0:T(8,128)(2,1)S(1)}, u32[]{:S(2)}, u32[]{:S(2)}) %all-to-all-start) | async-done | bytes 983072 | tf_op jit(solution)/shard_map/head_weights/all_to_all | solution.py:37
  56.5 23.7 %all-to-all-done.1 = bf16[16,32,1024]{2,1,0:T(8,128)(2,1)S(1)} async-done(((bf16[16,32,1024]{2,1,0:T(8,128)(2,1)}), bf16[16,32,1024]{2,1,0:T(8,128)(2,1)S(1)}, u32[]{:S(2)}, u32[]{:S(2)}) %all-to-all-start.1) | async-done | bytes 1048608 | tf_op jit(solution)/shard_map/sequence_tokens/all_to_all | solution.py:37
  98.4 11.4 %all-to-all-done.2 = bf16[32,32,128]{2,1,0:T(8,128)(2,1)S(1)} async-done(((bf16[32,32,128]{2,1,0:T(8,128)(2,1)}), bf16[32,32,128]{2,1,0:T(8,128)(2,1)S(1)}, u32[]{:S(2)}, u32[]{:S(2)}) %all-to-all-start.2) | async-done | bytes 262176 | tf_op jit(solution)/shard_map/context_out/all_to_all | solution.py:37
  109.8 40.8 %all-gather.15.cloned.1.call-done = bf16[9216,1024]{1,0:T(8,128)(2,1)} async-done(((bf16[144,1024]{1,0:T(8,128)(2,1)}), bf16[9216,1024]{1,0:T(8,128)(2,1)}) %all-gather.15.cloned.1.call-update) | async-done | bytes 18874384 | tf_op jit(solution)/shard_map/gather_block_weights/all_gather | solution.py:461
  150.5 12.0 %block_0.1 = (bf16[128,1024]{1,0:T(8,128)(2,1)S(1)}, f32[128,1024]{1,0:T(8,128)}, bf16[128,1024]{1,0:T(8,128)(2,1)}, f32[128,4096]{1,0:T(8,128)}, f32[128,1024]{1,0:T(8,128)}, /*index=5*/bf16[128,1024]{1,0:T(8,128)(2,1)}) custom-call(bf16[128,1024]{1,0:T(8,128)(2,1)S(1)} %bitcast.252, bf16[2,2,4,2,32,128]{5,4,3,2,1,0:T(8,128)(2,1)S(1)} %bitcast.253, ...), custom_call_target="tpu_custom_call" | custom-call | flops 2415919104 | bytes 25165824 | tf_op jit(solution)/shard_map/block_0/pallas_call | solution.py:197
  164.8 5.5 %collective-permute-done.2 = bf16[128,1024]{1,0:T(8,128)(2,1)S(1)} collective-permute-done((bf16[128,1024]{1,0:T(8,128)(2,1)S(1)}, bf16[128,1024]{1,0:T(8,128)(2,1)S(1)}, u32[]{:S(2)}, u32[]{:S(2)}) %collective-permute-start.2) | collective-permute-done | bytes 262176 | tf_op jit(solution)/shard_map/to_next_section/ppermute | solution.py:529
  171.2 25.1 %all_to_all.65 = bf16[16,32,1024]{2,1,0:T(8,128)(2,1)S(1)} all-to-all(bf16[16,32,1024]{2,1,0:T(8,128)(2,1)S(1)} %bitcast.274), channel_id=1, replica_groups=mesh['section'=2,'shard'=16,'replica'=4] {'shard'}, dimensions={0} | all-to-all | bytes 2097152 | tf_op jit(solution)/shard_map/sequence_tokens/all_to_all | solution.py:37
  206.6 16.6 %all_to_all.66 = bf16[32,32,128]{2,1,0:T(8,128)(2,1)S(1)} all-to-all(bf16[32,32,128]{2,1,0:T(8,128)(2,1)S(1)} %bitcast.296), channel_id=1, replica_groups=mesh['section'=2,'shard'=16,'replica'=4] {'section','shard'}, dimensions={0} | all-to-all | bytes 524288 | tf_op jit(solution)/shard_map/context_out/all_to_all | solution.py:37
  223.3 11.1 %block_1.1 = (bf16[128,1024]{1,0:T(8,128)(2,1)}, f32[128,1024]{1,0:T(8,128)S(1)}, bf16[128,1024]{1,0:T(8,128)(2,1)S(1)}, f32[128,4096]{1,0:T(8,128)S(1)}, f32[12...) custom-call(bf16[128,1024]{1,0:T(8,128)(2,1)S(1)} %copy-done.5, ...), custom_call_target="tpu_custom_call" | custom-call | flops 2415919104 | bytes 25165824 | tf_op jit(solution)/shard_map/block_1/pallas_call | solution.py:197
  235.8 14.2 %block_back_1.1 = (f32[128,1024]{1,0:T(8,128)}, bf16[128,1024]{1,0:T(8,128)(2,1)S(1)}, bf16[2,2,4,2,64,128]{5,4,3,2,1,0:T(8,128)(2,1)S(1)}, f32[8,1024]{1,0:T(8,128)}) custom-call(bf16[128,1024]{1,0:T(8,128)(2,1)S(1)} %bitcast.255, bf16[16,576,1024]{2,1,0:T(8,128)(2,1)} %bitcast.264, bf16[16,576,1024]{2,1,0:T(8,128)(2,1)} %bitcast.265, ...), custom_call_target="tpu_custom_call" | custom-call | flops 2415919104 | bytes 25165824 | tf_op jit(solution)/shard_map/block_back_1/pallas_call | solution.py:292
  251.4 6.9 %all-to-all-start.5 = ((bf16[32,64,128]{2,1,0:T(8,128)(2,1)}), bf16[32,64,128]{2,1,0:T(8,128)(2,1)S(1)}, u32[]{:S(2)}, u32[]{:S(2)}) async-start(bf16[32,64,128]{2,1,0:T(8,128)(2,1)} %bitcast.257), calls=%async_computation.5 | async-start | bytes 1048576 | tf_op jit(solution)/shard_map/grad_context_in/all_to_all | solution.py:37
  261.4 11.4 %collective-permute-done.5.grad_residual = bf16[128,1024]{1,0:T(8,128)(2,1)} collective-permute-done((bf16[128,1024]{1,0:T(8,128)(2,1)}, bf16[128,1024]{1,0:T(8,128)(2,1)}, u32[]{:S(2)}, u32[]{:S(2)}) %collective-permute-start.5) | collective-permute-done | bytes 262176 | tf_op jit(solution)/shard_map/residual_to_other_section/ppermute | solution.py:551
  276.7 5.5 %attention_back.2 = bf16[1024,192]{1,0:T(8,128)(2,1)S(1)} custom-call(s32[1]{0:T(128)} %bitcast.45.core, bf16[1024,192]{1,0:T(8,128)(2,1)S(1)} %copy-done.24, f32[1024,1]{1,0:T(8,128)S(1)} %copy-done.12, bf16[1024,1]{1,0:T(8,128)(2,1)S(1)} %select_n.401.seg_rows, bf16[1,1024]{1,0:T(2,128)(2,1)S(1)} %select_n.370.seg_columns, bf16[32,64,128]{2,1,0:T(8,128)(2,1)S(1)} %copy-done.10), custom_call_target="tpu_custom_call" | custom-call | flops 671088640 | bytes 2097152 | tf_op jit(solution)/shard_map/attention_back/pallas_call | solution.py:410
  290.3 6.7 %all-to-all-start.6 = ((bf16[32,32,384]{2,1,0:T(8,128)(2,1)}), bf16[32,32,384]{2,1,0:T(8,128)(2,1)}, u32[]{:S(2)}, u32[]{:S(2)}) async-start(bf16[32,32,384]{2,1,0:T(8,128)(2,1)} %bitcast.277), calls=%async_computation.6 | async-start | bytes 1572864 | tf_op jit(solution)/shard_map/grad_tokens_1/all_to_all | solution.py:37
  297.5 13.8 %all-to-all-done.6 = bf16[32,32,384]{2,1,0:T(8,128)(2,1)} async-done(((bf16[32,32,384]{2,1,0:T(8,128)(2,1)}), bf16[32,32,384]{2,1,0:T(8,128)(2,1)}, u32[]{:S(2)}, u32[]{:S(2)}) %all-to-all-start.6) | async-done | bytes 786464 | tf_op jit(solution)/shard_map/grad_tokens_1/all_to_all | solution.py:37
  311.3 5.4 %grad_tokens_1.1 = bf16[128,1024]{1,0:T(8,128)(2,1)S(1)} custom-call(bf16[2,2,4,2,32,384]{5,4,3,2,1,0:T(8,128)(2,1)} %bitcast.53.got, bf16[1024,3072]{1,0:T(8,128)(2,1)} %all-gather.7.cloned.1.call-done.weight, bf16[128,1024]{1,0:T(8,128)(2,1)} %collective-permute-done.5.grad_residual), custom_call_target="tpu_custom_call" | custom-call | flops 805306368 | bytes 8388608 | tf_op jit(solution)/shard_map/grad_tokens_1/pallas_call | solution.py:345
  319.5 14.2 %block_back_0.1 = (f32[128,1024]{1,0:T(8,128)}, bf16[128,1024]{1,0:T(8,128)(2,1)S(1)}, bf16[2,2,4,2,64,128]{5,4,3,2,1,0:T(8,128)(2,1)S(1)}, f32[8,1024]{1,0:T(8,128)S(1)}) custom-call(bf16[128,1024]{1,0:T(8,128)(2,1)S(1)} %get-tuple-element.63.grad, bf16[16,576,1024]{2,1,0:T(8,128)(2,1)} %bitcast.267, bf16[16,576,1024]{2,1,0:T(8,128)(2,1)} %bitcast.268, ...), custom_call_target="tpu_custom_call" | custom-call | flops 2415919104 | bytes 25165824 | tf_op jit(solution)/shard_map/block_back_0/pallas_call | solution.py:292
  344.7 7.7 %all-to-all-done.7.got = bf16[32,64,128]{2,1,0:T(8,128)(2,1)S(1)} async-done(((bf16[32,64,128]{2,1,0:T(8,128)(2,1)}), bf16[32,64,128]{2,1,0:T(8,128)(2,1)S(1)}, u32[]{:S(2)}, u32[]{:S(2)}) %all-to-all-start.7) | async-done | bytes 524320 | tf_op jit(solution)/shard_map/grad_context_in/all_to_all | solution.py:37
  352.5 7.1 %all-to-all-start.8 = ((bf16[64,16,512]{2,1,0:T(8,128)(2,1)}), bf16[64,16,512]{2,1,0:T(8,128)(2,1)S(1)}, u32[]{:S(2)}, u32[]{:S(2)}) async-start(bf16[64,16,512]{2,1,0:T(8,128)(2,1)} %bitcast.57), calls=%async_computation.8 | async-start | bytes 2097152 | tf_op jit(solution)/shard_map/sum_output_grad/all_to_all | solution.py:37
  368.1 5.5 %attention_back.3 = bf16[1024,192]{1,0:T(8,128)(2,1)S(1)} custom-call(s32[1]{0:T(128)} %bitcast.45.core, bf16[1024,192]{1,0:T(8,128)(2,1)S(1)} %copy-done.22, f32[1024,1]{1,0:T(8,128)S(1)} %copy.180.log_totals, bf16[1024,1]{1,0:T(8,128)(2,1)S(1)} %copy-done.19, bf16[1,1024]{1,0:T(2,128)(2,1)S(1)} %select_n.370.seg_columns, ...), custom_call_target="tpu_custom_call" | custom-call | flops 671088640 | bytes 2097152 | tf_op jit(solution)/shard_map/attention_back/pallas_call | solution.py:410
  382.9 4.8 convolution_add_fusion
  388.9 6.3 %collective-permute-done.10 = bf16[1040,192]{0,1:T(8,128)(2,1)S(1)} collective-permute-done((bf16[1040,192]{0,1:T(8,128)(2,1)}, bf16[1040,192]{0,1:T(8,128)(2,1)S(1)}, u32[]{:S(2)}, u32[]{:S(2)}) %collective-permute-start.10) | collective-permute-done | bytes 399392 | tf_op jit(solution)/shard_map/swap_attend_grad/ppermute | solution.py:585
  397.4 11.8 %all-to-all-start.9 = ((bf16[64,16,512]{2,1,0:T(8,128)(2,1)}), bf16[64,16,512]{2,1,0:T(8,128)(2,1)S(1)}, u32[]{:S(2)}, u32[]{:S(2)}) async-start(bf16[64,16,512]{2,1,0:T(8,128)(2,1)} %bitcast.62), calls=%async_computation.9 | async-start | bytes 2097152 | tf_op jit(solution)/shard_map/sum_attend_grad/all_to_all | solution.py:37
  409.2 6.0 %fusion.50 = (bf16[256]{0:T(256)(128)(2,1)S(1)}, bf16[2048,256]{1,0:T(8,128)(2,1)}) fusion(f32[2048,256]{1,0:T(8,128)} %convolution_add_fusion, bf16[2048,1024]{1,0:T(8,128)(2,1)} %all-gather.11.cloned.1.call-done, bf16[1,256,1024]{2,1,0:T(8,128)(2,1)S(1)} %copy-done.34), kind=kOutput, calls=%fused_computation.167 | convolution fusion | flops 1079508736 | bytes 7864832 | tf_op jit(solution)/shard_map/block_weight_grads/dot_general | solution.py:25
  427.7 8.3 %all-to-all-start.10 = ((bf16[64,16,256]{2,1,0:T(8,128)(2,1)}), bf16[64,16,256]{2,1,0:T(8,128)(2,1)}, u32[]{:S(2)}, u32[]{:S(2)}) async-start(bf16[64,16,256]{2,1,0:T(8,128)(2,1)} %bitcast.71), calls=%async_computation.10 | async-start | bytes 1048576 | tf_op jit(solution)/shard_map/sum_expand_grad/all_to_all | solution.py:37
  440.4 6.6 %collective-permute-done.11.grad_residual = bf16[128,1024]{1,0:T(8,128)(2,1)S(1)} collective-permute-done((bf16[128,1024]{1,0:T(8,128)(2,1)S(1)}, bf16[128,1024]{1,0:T(8,128)(2,1)S(1)}, u32[]{:S(2)}, u32[]{:S(2)}) %collective-permute-start.11) | collective-permute-done | bytes 262176 | tf_op jit(solution)/shard_map/sum_attend_grad/ppermute | solution.py:604
  447.0 5.6 %collective-permute-done.12 = bf16[128,1024]{1,0:T(8,128)(2,1)} collective-permute-done((bf16[128,1024]{1,0:T(8,128)(2,1)S(1)}, bf16[128,1024]{1,0:T(8,128)(2,1)}, u32[]{:S(2)}, u32[]{:S(2)}) %collective-permute-start.12) | collective-permute-done | bytes 262176 | tf_op jit(solution)/shard_map/sum_attend_grad/ppermute | solution.py:605
  458.6 7.9 %all-to-all-done.11 = bf16[4,80,1024]{2,1,0:T(8,128)(2,1)S(1)} async-done(((bf16[4,80,1024]{2,1,0:T(8,128)(2,1)}), bf16[4,80,1024]{2,1,0:T(8,128)(2,1)S(1)}, u32[]{:S(2)}, u32[]{:S(2)}) %all-to-all-start.11) | async-done | bytes 655392 | tf_op jit(solution)/shard_map/sum_contract/all_to_all | solution.py:37
  474.1 8.5 %all-to-all-start.12 = ((bf16[32,32,384]{2,1,0:T(8,128)(2,1)}), bf16[32,32,384]{2,1,0:T(8,128)(2,1)S(1)}, u32[]{:S(2)}, u32[]{:S(2)}) async-start(bf16[32,32,384]{2,1,0:T(8,128)(2,1)} %bitcast.80), calls=%async_computation.12 | async-start | bytes 1572864 | tf_op jit(solution)/shard_map/grad_tokens_0/all_to_all | solution.py:37
  484.5 12.4 %all-to-all-done.12 = bf16[32,32,384]{2,1,0:T(8,128)(2,1)S(1)} async-done(((bf16[32,32,384]{2,1,0:T(8,128)(2,1)}), bf16[32,32,384]{2,1,0:T(8,128)(2,1)S(1)}, u32[]{:S(2)}, u32[]{:S(2)}) %all-to-all-start.12) | async-done | bytes 786464 | tf_op jit(solution)/shard_map/grad_tokens_0/all_to_all | solution.py:37
  496.9 5.2 grad_tokens_0.1
  (330 shorter events, 147.8 us)
Async XLA Ops:
  7.2 143.4 %all-gather.15.cloned.1.call-start = ((), (), s32[]{:S(2)}) async-start(), calls=%async_computation.17 | async-start | bytes 19169280 | tf_op jit(solution)/shard_map/gather_block_weights/all_gather | solution.py:461
  18.8 31.5 %copy-start = (bf16[2,1,64,1024]{3,2,1,0:T(8,128)(2,1)S(1)}, bf16[2,1,64,1024]{3,2,1,0:T(8,128)(2,1)}, u32[]{:S(2)}) copy-start(bf16[2,1,64,1024]{3,2,1,0:T(8,128)(2,1)} %param.10) | copy-start | bytes 786436
  18.9 31.5 %all-to-all-start = ((bf16[32,80,192]{2,1,0:T(8,128)(2,1)}), bf16[32,80,192]{2,1,0:T(8,128)(2,1)S(1)}, u32[]{:S(2)}, u32[]{:S(2)}) async-start(bf16[32,80,192]{2,1,0:T(8,128)(2,1)} %bitcast.5), calls=%async_computation | async-start | bytes 2621440 | tf_op jit(solution)/shard_map/head_weights/all_to_all | solution.py:37
  29.8 132.7 %collective-permute-start.7 = (bf16[64,3072]{1,0:T(8,128)(2,1)}, bf16[64,3072]{1,0:T(8,128)(2,1)}, u32[]{:S(2)}, u32[]{:S(2)}) collective-permute-start(bf16[64,3072]{1,0:T(8,128)(2,1)} %reshape.440), channel_id=1, source_target_pairs={{0,64},{64,0},{1,65},{65,1},{2,66},{66,2},{3,67},{67,3},{4,68},{68... | collective-permute-start | bytes 1179656 | tf_op jit(solution)/shard_map/gather_attend_weight/ppermute | solution.py:533
  51.4 28.8 %all-to-all-start.1 = ((bf16[16,32,1024]{2,1,0:T(8,128)(2,1)}), bf16[16,32,1024]{2,1,0:T(8,128)(2,1)S(1)}, u32[]{:S(2)}, u32[]{:S(2)}) async-start(bf16[16,32,1024]{2,1,0:T(8,128)(2,1)} %bitcast.273), calls=%async_computation.1 | async-start | bytes 2097152 | tf_op jit(solution)/shard_map/sequence_tokens/all_to_all | solution.py:37
  80.2 4.3 collective-permute-start
  91.5 1.4 collective-permute-start.1
  93.8 16.0 %all-to-all-start.2 = ((bf16[32,32,128]{2,1,0:T(8,128)(2,1)}), bf16[32,32,128]{2,1,0:T(8,128)(2,1)S(1)}, u32[]{:S(2)}, u32[]{:S(2)}) async-start(bf16[32,32,128]{2,1,0:T(8,128)(2,1)} %bitcast.22), calls=%async_computation.2 | async-start | bytes 524288 | tf_op jit(solution)/shard_map/context_out/all_to_all | solution.py:37
  97.7 213.6 %all-gather.7.cloned.1.call-start = ((), (), s32[]{:S(2)}) async-start(), calls=%async_computation.13 | async-start | bytes 6684672 | tf_op jit(solution)/shard_map/gather_attend_weight/all_gather | solution.py:535
  162.5 220.4 %all-gather.9.cloned.1.call-start = ((), (), s32[]{:S(2)}) async-start(), calls=%async_computation.14 | async-start | bytes 4456448 | tf_op jit(solution)/shard_map/gather_first/all_gather | solution.py:543
  162.6 7.7 %collective-permute-start.2 = (bf16[128,1024]{1,0:T(8,128)(2,1)S(1)}, bf16[128,1024]{1,0:T(8,128)(2,1)S(1)}, u32[]{:S(2)}, u32[]{:S(2)}) collective-permute-start(bf16[128,1024]{1,0:T(8,128)(2,1)S(1)} %get-tuple-element.53), channel_id=1, source_target_pairs={{0,64},{1,65},{2,66},{3,67},{4,68},{5,69},{6,70},{7,71},{8,72},{9,... | collective-permute-start | bytes 786440 | tf_op jit(solution)/shard_map/to_next_section/ppermute | solution.py:529
  196.3 2.7 collective-permute-start.3
  205.0 1.4 collective-permute-start.4
  251.4 21.3 %all-to-all-start.5 = ((bf16[32,64,128]{2,1,0:T(8,128)(2,1)}), bf16[32,64,128]{2,1,0:T(8,128)(2,1)S(1)}, u32[]{:S(2)}, u32[]{:S(2)}) async-start(bf16[32,64,128]{2,1,0:T(8,128)(2,1)} %bitcast.257), calls=%async_computation.5 | async-start | bytes 1048576 | tf_op jit(solution)/shard_map/grad_context_in/all_to_all | solution.py:37
  258.4 14.4 %collective-permute-start.5 = (bf16[128,1024]{1,0:T(8,128)(2,1)}, bf16[128,1024]{1,0:T(8,128)(2,1)}, u32[]{:S(2)}, u32[]{:S(2)}) collective-permute-start(bf16[128,1024]{1,0:T(8,128)(2,1)} %copy-done.20), channel_id=1, source_target_pairs={{64,0},{65,1},{66,2},{67,3},{68,4},{69,5},{70,6},{71,7},{72,8},{73... | collective-permute-start | bytes 786440 | tf_op jit(solution)/shard_map/residual_to_other_section/ppermute | solution.py:551
  282.2 3.2 collective-permute-start.6
  290.3 21.0 %all-to-all-start.6 = ((bf16[32,32,384]{2,1,0:T(8,128)(2,1)}), bf16[32,32,384]{2,1,0:T(8,128)(2,1)}, u32[]{:S(2)}, u32[]{:S(2)}) async-start(bf16[32,32,384]{2,1,0:T(8,128)(2,1)} %bitcast.277), calls=%async_computation.6 | async-start | bytes 1572864 | tf_op jit(solution)/shard_map/grad_tokens_1/all_to_all | solution.py:37
  297.0 112.2 %all-gather.11.cloned.1.call-start = ((), (), s32[]{:S(2)}) async-start(), calls=%async_computation.15 | async-start | bytes 4456448 | tf_op jit(solution)/shard_map/gather_grad_mlp/all_gather | solution.py:560
  336.6 4.3 collective-permute-start.8
  337.0 15.4 %all-to-all-start.7 = ((bf16[32,64,128]{2,1,0:T(8,128)(2,1)}), bf16[32,64,128]{2,1,0:T(8,128)(2,1)S(1)}, u32[]{:S(2)}, u32[]{:S(2)}) async-start(bf16[32,64,128]{2,1,0:T(8,128)(2,1)} %bitcast.256), calls=%async_computation.7 | async-start | bytes 1048576 | tf_op jit(solution)/shard_map/grad_context_in/all_to_all | solution.py:37
  352.5 25.6 %all-to-all-start.8 = ((bf16[64,16,512]{2,1,0:T(8,128)(2,1)}), bf16[64,16,512]{2,1,0:T(8,128)(2,1)S(1)}, u32[]{:S(2)}, u32[]{:S(2)}) async-start(bf16[64,16,512]{2,1,0:T(8,128)(2,1)} %bitcast.57), calls=%async_computation.8 | async-start | bytes 2097152 | tf_op jit(solution)/shard_map/sum_output_grad/all_to_all | solution.py:37
  363.2 17.5 %collective-permute-start.9 = (bf16[1040,192]{0,1:T(8,128)(2,1)}, bf16[1040,192]{0,1:T(8,128)(2,1)}, u32[]{:S(2)}, u32[]{:S(2)}) collective-permute-start(bf16[1040,192]{0,1:T(8,128)(2,1)} %fusion.25), channel_id=1, source_target_pairs={{0,64},{1,65},{2,66},{3,67},{4,68},{5,69},{6,70},{7,71},{8,72},{9,... | collective-permute-start | bytes 1198088 | tf_op jit(solution)/shard_map/swap_attend_grad/ppermute | solution.py:570
  381.6 13.6 %collective-permute-start.10 = (bf16[1040,192]{0,1:T(8,128)(2,1)}, bf16[1040,192]{0,1:T(8,128)(2,1)S(1)}, u32[]{:S(2)}, u32[]{:S(2)}) collective-permute-start(bf16[1040,192]{0,1:T(8,128)(2,1)} %get-tuple-element.158), channel_id=1, source_target_pairs={{64,0},{65,1},{66,2},{67,3},{68,4},{69,5},{70,6},{71,7},{72,8},{73... | collective-permute-start | bytes 1198088 | tf_op jit(solution)/shard_map/swap_attend_grad/ppermute | solution.py:585
  397.4 30.3 %all-to-all-start.9 = ((bf16[64,16,512]{2,1,0:T(8,128)(2,1)}), bf16[64,16,512]{2,1,0:T(8,128)(2,1)S(1)}, u32[]{:S(2)}, u32[]{:S(2)}) async-start(bf16[64,16,512]{2,1,0:T(8,128)(2,1)} %bitcast.62), calls=%async_computation.9 | async-start | bytes 2097152 | tf_op jit(solution)/shard_map/sum_attend_grad/all_to_all | solution.py:37
  427.7 24.9 %all-to-all-start.10 = ((bf16[64,16,256]{2,1,0:T(8,128)(2,1)}), bf16[64,16,256]{2,1,0:T(8,128)(2,1)}, u32[]{:S(2)}, u32[]{:S(2)}) async-start(bf16[64,16,256]{2,1,0:T(8,128)(2,1)} %bitcast.71), calls=%async_computation.10 | async-start | bytes 1048576 | tf_op jit(solution)/shard_map/sum_expand_grad/all_to_all | solution.py:37
  436.0 10.9 %collective-permute-start.11 = (bf16[128,1024]{1,0:T(8,128)(2,1)S(1)}, bf16[128,1024]{1,0:T(8,128)(2,1)S(1)}, u32[]{:S(2)}, u32[]{:S(2)}) collective-permute-start(bf16[128,1024]{1,0:T(8,128)(2,1)S(1)} %copy-done.14), channel_id=1, source_target_pairs={{0,64},{1,65},{2,66},{3,67},{4,68},{5,69},{6,70},{7,71},{8,72},{9,... | collective-permute-start | bytes 786440 | tf_op jit(solution)/shard_map/sum_attend_grad/ppermute | solution.py:604
  437.4 15.2 %collective-permute-start.12 = (bf16[128,1024]{1,0:T(8,128)(2,1)S(1)}, bf16[128,1024]{1,0:T(8,128)(2,1)}, u32[]{:S(2)}, u32[]{:S(2)}) collective-permute-start(bf16[128,1024]{1,0:T(8,128)(2,1)S(1)} %copy-done.7), channel_id=1, source_target_pairs={{0,64},{1,65},{2,66},{3,67},{4,68},{5,69},{6,70},{7,71},{8,72},{9,... | collective-permute-start | bytes 786440 | tf_op jit(solution)/shard_map/sum_attend_grad/ppermute | solution.py:605
  452.6 13.9 %all-to-all-start.11 = ((bf16[4,80,1024]{2,1,0:T(8,128)(2,1)}), bf16[4,80,1024]{2,1,0:T(8,128)(2,1)S(1)}, u32[]{:S(2)}, u32[]{:S(2)}) async-start(bf16[4,80,1024]{2,1,0:T(8,128)(2,1)} %pad_maximum_fusion.3), calls=%async_computation.11 | async-start | bytes 1310720 | tf_op jit(solution)/shard_map/sum_contract/all_to_all | solution.py:37
  456.7 46.7 %all-gather.13.cloned.1.call-start = ((), (), s32[]{:S(2)}) async-start(), calls=%async_computation.16 | async-start | bytes 1966080 | tf_op jit(solution)/shard_map/gather_weight_grads/all_gather | solution.py:656
  469.1 3.3 collective-permute-start.13
  474.1 22.7 %all-to-all-start.12 = ((bf16[32,32,384]{2,1,0:T(8,128)(2,1)}), bf16[32,32,384]{2,1,0:T(8,128)(2,1)S(1)}, u32[]{:S(2)}, u32[]{:S(2)}) async-start(bf16[32,32,384]{2,1,0:T(8,128)(2,1)} %bitcast.80), calls=%async_computation.12 | async-start | bytes 1572864 | tf_op jit(solution)/shard_map/grad_tokens_0/all_to_all | solution.py:37
  502.0 9.6 %collective-permute-start.14 = (bf16[128,1024]{1,0:T(8,128)(2,1)S(1)}, bf16[128,1024]{1,0:T(8,128)(2,1)S(1)}, u32[]{:S(2)}, u32[]{:S(2)}) collective-permute-start(bf16[128,1024]{1,0:T(8,128)(2,1)S(1)} %grad_tokens_0.1), channel_id=1, source_target_pairs={{64,0},{65,1},{66,2},{67,3},{68,4},{69,5},{70,6},{71,7},{72,8},{73... | collective-permute-start | bytes 786440 | tf_op jit(solution)/shard_map/grad_tokens_0/ppermute | solution.py:654
  (40 other events, 229.1 us)
Sparse Core Ops, SparseCore 0:
  13.9 136.5 all-gather.14
  162.7 72.8 all-gather.6
  238.0 54.4 all-gather.8
  318.5 61.7 all-gather.10
  469.2 28.4 all-gather.12
